TPU v7x, 256 devices: a whole 4x4x8 slice. The times are simulated.
256 devices in a mesh: own: 8 (over z), col: 8 (over x, core), mlp: 4 (over y).
Axes of the slice: x: 4, y: 4, z: 8, core: 2. Of those that a mesh axis runs over, the one named last changes fastest.
Arguments:
- features: bfloat16 [262144, 512], P(('own', 'col')), may hold values from -6 to 6
- nbr_page: int32 [8192, 32], P(('own', 'col')), may hold values from 0 to 262143, as said below
- nbr_weight: bfloat16 [8192, 32], P(('own', 'col')), may hold values from 0.0049743652 to 0.29882812
- labels: int32 [8192], P(('own', 'col')), may hold values from 0 to 255
- w_one: bfloat16 [512, 2048], P(None, 'mlp'), may hold values from -0.25 to 0.25
- w_two: bfloat16 [2048, 256], P('mlp'), may hold values from -0.125 to 0.125
Outputs:
- grad_one: float32 [512, 2048], P(None, 'mlp')
- grad_two: float32 [2048, 256], P('mlp')
Inputs may be any that keep to these rules, and one draw needn't show every extreme that they name: `nbr_page`: page p is held by owner p // 4096 (owners numbered along own then col) at its row p % 4096. The 32 neighbours of a target are distinct pages listed in non-decreasing order of owner. Of the 4096 neighbour entries of the targets of one index of own and col, at most 128 fall on one owner; one owner receives exactly 128 entries from every index, and some owners receive none from some indices.
All inputs are finite; a program needn't handle non-finite values.
Results may differ from a plain program's by a relative error of at most 0.011.
Values may be sent and summed in bfloat16 or wider, within the bound.
No kernel may reach another device: no remote copies, remote signals or barrier semaphores. Data moves between devices by JAX's collectives and lax.ppermute only.
A program may use at most 128 MiB of HBM per device.

v0:
```python
import jax
import jax.numpy as jnp
from jax import lax
from jax.sharding import PartitionSpec as P


def body(features, nbr_page, nbr_weight, labels, w_one, w_two):
    rows_dev = features.shape[0]
    width_f = features.shape[1]
    targets = nbr_page.shape[0]
    width_k = nbr_page.shape[1]
    owners = lax.axis_size(("own", "col"))
    entries = targets * width_k
    capacity = 2 * entries // owners
    owner_ids = nbr_page // rows_dev
    local_row = nbr_page % rows_dev
    owner_range = jnp.arange(owners, dtype=jnp.int32)
    matches = (owner_ids[:, :, None] == owner_range[None, None, :]).astype(jnp.int32)
    row_count = jnp.sum(matches, axis=1)
    earlier_rows = jnp.cumsum(row_count, axis=0) - row_count
    before_owner = jnp.cumsum(row_count, axis=1) - row_count
    first_slot = earlier_rows - before_owner + owner_range[None, :] * capacity
    slot_ids = (
        jnp.sum(matches * first_slot[:, None, :], axis=2)
        + jnp.arange(width_k, dtype=jnp.int32)[None, :]
    )
    flat_slot = slot_ids.reshape(-1)
    requests = jnp.zeros((owners * capacity,), jnp.int32).at[flat_slot].set(local_row.reshape(-1))
    requests = requests.reshape(owners, capacity)
    asked_rows = lax.all_to_all(requests, ("own", "col"), split_axis=0, concat_axis=0, tiled=True)
    fetched = features[asked_rows]
    returned = lax.all_to_all(fetched, ("own", "col"), split_axis=0, concat_axis=0, tiled=True)
    received = returned.reshape(owners * capacity, width_f)
    contract_first = (((0,), (0,)), ((), ()))
    target_ids = jnp.broadcast_to(
        jnp.arange(targets, dtype=jnp.int32)[:, None], (targets, width_k)
    ).reshape(-1)
    spread = (
        jnp.zeros((targets, owners * capacity), jnp.bfloat16)
        .at[target_ids, flat_slot]
        .set(nbr_weight.reshape(-1))
    )
    pre_act = jnp.dot(received, w_one, preferred_element_type=jnp.float32)
    active = jnp.maximum(pre_act, 0.0).astype(jnp.bfloat16)
    hidden = jnp.dot(spread, active, preferred_element_type=jnp.float32).astype(jnp.bfloat16)
    partial_logits = jnp.dot(hidden, w_two, preferred_element_type=jnp.float32)
    logits = lax.psum(partial_logits, "mlp")
    exponent = jnp.exp(logits)
    probability = exponent / jnp.sum(exponent, axis=1, keepdims=True)
    classes = w_two.shape[1]
    onehot_label = (labels[:, None] == jnp.arange(classes, dtype=jnp.int32)[None, :]).astype(
        jnp.float32
    )
    d_logits = (probability - onehot_label).astype(jnp.bfloat16)
    grad_two = lax.dot_general(hidden, d_logits, contract_first, preferred_element_type=jnp.float32)
    d_hidden = lax.dot_general(
        d_logits, w_two, (((1,), (1,)), ((), ())), preferred_element_type=jnp.float32
    ).astype(jnp.bfloat16)
    positive = (pre_act > 0).astype(jnp.float32)
    scattered = lax.dot_general(
        spread, d_hidden, contract_first, preferred_element_type=jnp.float32
    )
    d_pre = (scattered * positive).astype(jnp.bfloat16)
    grad_one = lax.dot_general(received, d_pre, contract_first, preferred_element_type=jnp.float32)
    grad_one, grad_two = lax.psum((grad_one, grad_two), ("own", "col"))
    return (grad_one, grad_two)


def solution(mesh):
    placed = (
        P(("own", "col"), None),
        P(("own", "col"), None),
        P(("own", "col"), None),
        P(("own", "col")),
        P(None, "mlp"),
        P("mlp", None),
    )
    return jax.shard_map(
        body,
        mesh=mesh,
        in_specs=placed,
        out_specs=(P(None, "mlp"), P("mlp", None)),
        check_vma=False,
    )
```

profile of v0, /device:TPU:1, one launch (start us, length us, event | category | flops | bytes accessed | tf_op | source)
XLA Modules:
  0.0 550.5 jit_solution(711926448814235918)
XLA Ops:
  7.2 0.0 copy-start
  7.2 0.8 add_select_fusion
  8.0 0.1 convert_reduce_fusion
  8.1 0.1 copy.16
  8.2 0.1 reduce_window_sum.23
  8.3 0.1 copy.18
  8.4 0.1 copy.22
  8.5 0.1 reshape.163
  8.6 0.2 reduce_window_sum.22
  8.8 0.1 copy.20
  8.8 0.2 select_reduce_fusion
  9.1 0.1 copy.21
  9.2 0.1 add.85
  9.3 0.1 reshape.145
  9.4 15.5 %scatter_custom_fusion = s32[8192]{0:T(1024)S(1)} fusion(s32[4096]{0:T(1024)S(1)} %bitcast.22, s32[4096]{0:T(1024)S(1)} %reshape.163, s32[]{:T(128)} %constant.41.clone.1), kind=kCustom, calls=%fused_computation.34 | custom fusion | bytes 32772 | tf_op jit(solution)/shard_map/scatter | solution.py:28
  25.0 22.2 %all_to_all.17 = s32[64,1,128]{2,1,0:T(1,128)S(1)} all-to-all(s32[64,1,128]{2,1,0:T(1,128)S(1)} %bitcast.23), channel_id=1, replica_groups=mesh['own'=8,'col'=8,'mlp'=4] {'own','col'}, dimensions={0} | all-to-all | bytes 65536 | tf_op jit(solution)/shard_map/all_to_all | solution.py:30
  47.2 36.5 %gather_fusion = bf16[8192,512]{1,0:T(8,128)(2,1)} fusion(bf16[4096,512]{1,0:T(8,128)(2,1)} %param.6, s32[8192]{0:T(1024)S(1)} %fusion.7), kind=kCustom, calls=%fused_computation | custom fusion | bytes 16809984 | tf_op jit(solution)/shard_map/gather | solution.py:31
  83.7 0.0 copy-start.4
  83.7 0.0 copy-start.7
  83.7 0.0 copy-start.6
  83.7 5.9 %all-to-all-start.1 = ((bf16[64,128,512]{2,1,0:T(8,128)(2,1)}), bf16[64,128,512]{2,1,0:T(8,128)(2,1)}, u32[]{:S(2)}, u32[]{:S(2)}) async-start(bf16[64,128,512]{2,1,0:T(8,128)(2,1)} %bitcast.21), calls=%async_computation.1 | async-start | bytes 16777216 | tf_op jit(solution)/shard_map/all_to_all | solution.py:32
  89.6 0.0 all-reduce.4.cloned.1.call-start
  89.7 0.0 copy-done.4
  89.7 0.1 copy.23
  89.8 0.1 reshape.169
  89.9 0.0 copy-done.7
  89.9 0.1 multiply_reduce_fusion
  90.0 0.0 copy-done.6
  90.0 0.1 and_reduce_fusion
  90.2 30.4 %scatter_custom_fusion.1 = bf16[1048576]{0:T(1024)(128)(2,1)} fusion(s32[4096]{0:T(1024)S(1)} %broadcast_select_fusion, bf16[4096]{0:T(1024)(128)(2,1)S(1)} %reshape.169, bf16[]{:T(256)} %constant.50.clone.1), kind=kCustom, calls=%fused_computation.10 | custom fusion | bytes 2097154
  120.5 2.8 reshape.150
  123.4 149.1 %all-to-all-done.1 = bf16[64,128,512]{2,1,0:T(8,128)(2,1)} async-done(((bf16[64,128,512]{2,1,0:T(8,128)(2,1)}), bf16[64,128,512]{2,1,0:T(8,128)(2,1)}, u32[]{:S(2)}, u32[]{:S(2)}) %all-to-all-start.1) | async-done | bytes 8388640 | tf_op jit(solution)/shard_map/all_to_all | solution.py:32
  272.5 0.0 copy-done
  272.5 7.1 %fusion.15 = f32[8192,512]{1,0:T(8,128)S(1)} fusion(bf16[8192,512]{1,0:T(8,128)(2,1)} %bitcast.5, bf16[512,512]{1,0:T(8,128)(2,1)S(1)} %copy-done), kind=kOutput, calls=%fused_computation.43 | convolution fusion | flops 4294967296 | bytes 25690112 | tf_op jit(solution)/shard_map/dot_general | solution.py:43
  279.6 0.0 copy-start.1
  279.6 0.0 copy-start.3
  279.6 0.0 copy-start.5
  279.6 1.6 fusion.3
  281.2 4.1 copy-done.1
  285.3 0.0 copy-done.3
  285.3 0.8 fusion.16
  286.1 0.0 all-reduce.4.cloned.1.call-update
  286.2 0.0 all-reduce.6.cloned.1.call-start
  286.2 44.8 %all-reduce.4.cloned.1.call-done = f32[128,256]{1,0:T(8,128)} async-done(((f32[128,256]{1,0:T(8,128)}), f32[128,256]{1,0:T(8,128)}) %all-reduce.4.cloned.1.call-update) | async-done | bytes 131088 | tf_op jit(solution)/shard_map/psum | solution.py:47
  331.0 1.0 exponential_reduce_fusion
  332.1 0.0 copy-done.5
  332.1 1.1 convolution_convert_fusion
  333.2 0.0 copy-start.2
  333.2 16.1 %fusion.2 = f32[512,512]{1,0:T(8,128)} fusion(bf16[8192,512]{1,0:T(8,128)(2,1)} %bitcast.5, f32[8192,512]{1,0:T(8,128)} %copy-done.1, bf16[128,8192]{1,0:T(8,128)(2,1)S(1)} %reshape.150, bf16[128,512]{1,0:T(8,128)(2,1)S(1)} %convolution_convert_fusion), kind=kOutput, calls=%fused_computation.7 | convolution fusion | flops 5381292032 | bytes 28442624 | tf_op jit(solution)/shard_map/dot_general | solution.py:64
  349.3 0.0 copy-done.2
  349.3 1.1 fusion.14
  350.4 0.0 all-reduce.6.cloned.1.call-update
  350.4 189.1 %all-reduce.6.cloned.1.call-done = (f32[512,512]{1,0:T(8,128)}, f32[512,256]{1,0:T(8,128)}) async-done(((f32[512,512]{1,0:T(8,128)}, f32[512,256]{1,0:T(8,128)}), (f32[512,512]{1,0:T(8,128)}, f32[512,256]{1,0:T(8,128)})) %all-reduce.6.cloned.1.call-update) | async-done | bytes 1572880 | tf_op jit(solution)/shard_map/psum | solution.py:65
  539.5 2.3 copy.27
  541.8 1.9 copy.28
  (7 shorter events, 0.1 us)
Async XLA Ops:
  7.2 265.3 %copy-start = (bf16[512,512]{1,0:T(8,128)(2,1)S(1)}, bf16[512,512]{1,0:T(8,128)(2,1)}, u32[]{:S(2)}) copy-start(bf16[512,512]{1,0:T(8,128)(2,1)} %param.10) | copy-start | bytes 1572868
  83.7 6.0 %copy-start.4 = (bf16[128,32]{0,1:T(8,128)(2,1)S(1)}, bf16[128,32]{0,1:T(8,128)(2,1)}, u32[]{:S(2)}) copy-start(bf16[128,32]{0,1:T(8,128)(2,1)} %param.8) | copy-start | bytes 24580
  83.7 6.2 %copy-start.7 = (s32[2]{0:T(128)S(1)}, s32[2]{0:T(128)}, u32[]{:S(2)}) copy-start(s32[2]{0:T(128)} %constant.51) | copy-start | bytes 28
  83.7 6.3 %copy-start.6 = (s32[2]{0:T(128)S(1)}, s32[2]{0:T(128)}, u32[]{:S(2)}) copy-start(s32[2]{0:T(128)} %constant.54) | copy-start | bytes 28
  83.7 188.8 %all-to-all-start.1 = ((bf16[64,128,512]{2,1,0:T(8,128)(2,1)}), bf16[64,128,512]{2,1,0:T(8,128)(2,1)}, u32[]{:S(2)}, u32[]{:S(2)}) async-start(bf16[64,128,512]{2,1,0:T(8,128)(2,1)} %bitcast.21), calls=%async_computation.1 | async-start | bytes 16777216 | tf_op jit(solution)/shard_map/all_to_all | solution.py:32
  89.6 241.4 %all-reduce.4.cloned.1.call-start = ((), (), s32[]{:S(2)}) async-start(), calls=%async_computation.2 | async-start | bytes 262144 | tf_op jit(solution)/shard_map/psum | solution.py:47
  279.6 5.7 %copy-start.1 = (f32[8192,512]{1,0:T(8,128)}, f32[8192,512]{1,0:T(8,128)S(1)}, u32[]{:S(2)}) copy-start(f32[8192,512]{1,0:T(8,128)S(1)} %fusion.15) | copy-start | bytes 50331652
  279.6 5.7 %copy-start.3 = (bf16[512,256]{1,0:T(8,128)(2,1)S(1)}, bf16[512,256]{1,0:T(8,128)(2,1)}, u32[]{:S(2)}) copy-start(bf16[512,256]{1,0:T(8,128)(2,1)} %param.11) | copy-start | bytes 786436
  279.6 52.5 %copy-start.5 = (s32[128]{0:T(128)S(1)}, s32[128]{0:T(128)}, u32[]{:S(2)}) copy-start(s32[128]{0:T(128)} %param.9) | copy-start | bytes 1540
  286.2 253.4 %all-reduce.6.cloned.1.call-start = ((), (), s32[]{:S(2)}) async-start(), calls=%async_computation.3 | async-start | bytes 3145728 | tf_op jit(solution)/shard_map/psum | solution.py:65
  333.2 16.1 %copy-start.2 = (f32[128,256]{1,0:T(8,128)S(1)}, f32[128,256]{1,0:T(8,128)}, u32[]{:S(2)}) copy-start(f32[128,256]{1,0:T(8,128)} %all-reduce.4.cloned.1.call-done) | copy-start | bytes 393220
Sparse Core Ops, SparseCore 0:
  286.3 44.7 all-reduce.3
  350.6 188.9 all-reduce.5
where the time goes:
time: 552 us; the launch traced here: 551 us
  waiting for transfers between devices  383 us (69%)
  local copies, waits for them, and re-layouts  94.5 us (17%)
  matrix products  27.8 us (5%)
  blocking collectives  22.2 us (4%)
  between operations  14.3 us (3%)
  starting transfers between devices  6.01 us (1%)
    psum x1, waiting for transfers between devices, body(): grad_one, grad_two = lax.psum((grad_one, grad_two), ('own', 'col'))  189 us
    all_to_all x1, waiting for transfers between devices, body(): lax.all_to_all(fetched, ('own', 'col'), split_axis=0, concat_axis=0, tile...  149 us
    psum x1, waiting for transfers between devices, body(): logits = lax.psum(partial_logits, 'mlp')  44.8 us
    unnamed x20, local copies, waits for them, and re-layouts  38.8 us
    gather x1, local copies, waits for them, and re-layouts, body(): fetched = features[asked_rows]  36.5 us
    all_to_all x1, blocking collectives, body(): lax.all_to_all(requests, ('own', 'col'), split_axis=0, concat_axis=0, til...  22.2 us
    dot_general x1, matrix products, body(): lax.dot_general(received, d_pre, contract_first, preferred_element_type=j...  16.1 us
    scatter x1, local copies, waits for them, and re-layouts, body(): jnp.zeros((owners * capacity,), jnp.int32).at[flat_slot]  15.5 us
  transfers between devices with their start and end apart: 3, of which 3 were waited for; matrix products, arithmetic and copies ran while one was open for 6% of the time, Pallas kernels for 0%

commit v1 on v0

v1 whole, which is shorter than its diff:
```python
import jax
import jax.numpy as jnp
from jax import lax
from jax.sharding import PartitionSpec as P

BF = jnp.bfloat16
F32 = jnp.float32


def dot(a, b, ca=1, cb=0):
    return lax.dot_general(a, b, (((ca,), (cb,)), ((), ())), preferred_element_type=F32)


def exchange(x, axes, groups=None):
    return lax.all_to_all(
        x, axes, split_axis=0, concat_axis=0, tiled=True, axis_index_groups=groups
    )


def body(features, nbr_page, nbr_weight, labels, w_one, w_two):
    rows_dev, width_f = features.shape
    targets, width_k = nbr_page.shape
    own_n, col_n, mlp_n = (lax.axis_size(a) for a in ("own", "col", "mlp"))
    owners = own_n * col_n
    entries = targets * width_k
    capacity = 2 * entries // owners
    share = capacity // mlp_n
    quarter = targets // mlp_n
    units, classes = w_two.shape
    me = lax.axis_index("mlp")
    core = lax.axis_index("col") % 2

    w_one_all = lax.all_gather(w_one, "mlp")
    w_two_all = lax.all_gather(w_two, "mlp", tiled=True)

    owner_range = jnp.arange(owners, dtype=jnp.int32)
    owner_ids = nbr_page // rows_dev
    local_row = nbr_page % rows_dev
    matches = owner_ids[:, :, None] == owner_range[None, None, :]
    row_count = jnp.sum(matches.astype(F32), axis=1)
    t_range = jnp.arange(targets)
    earlier = dot((t_range[:, None] > t_range[None, :]).astype(BF), row_count.astype(BF))
    before = dot(row_count.astype(BF), (owner_range[:, None] < owner_range[None, :]).astype(BF))
    first_slot = earlier - before
    slot_ids = (
        jnp.sum(matches.astype(F32) * first_slot[:, None, :], axis=2).astype(jnp.int32)
        + jnp.arange(width_k, dtype=jnp.int32)[None, :]
    )
    by_owner = matches.astype(BF).reshape(entries, owners)
    in_slot = slot_ids[:, :, None] == jnp.arange(capacity, dtype=jnp.int32)[None, None, :]

    def place(values):
        spread_out = jnp.where(in_slot, values.astype(BF)[:, :, None], jnp.zeros((), BF))
        return dot(by_owner, spread_out.reshape(entries, capacity), 0, 0)

    requests = (place(local_row // 64) * 64.0 + place(local_row % 64)).astype(jnp.int32)
    slot_weight = place(nbr_weight)
    slot_target = place(jnp.broadcast_to(t_range[:, None], (targets, width_k)))

    asked = exchange(requests, ("own", "col"))
    asked = lax.dynamic_slice_in_dim(asked, me * share, share, 1)
    fetched = features[asked]
    received = exchange(fetched, ("own", "col")).reshape(owners * share, width_f)

    my_weight = lax.dynamic_slice_in_dim(slot_weight, me * share, share, 1).reshape(1, -1)
    my_target = lax.dynamic_slice_in_dim(slot_target, me * share, share, 1).reshape(1, -1)
    spread = jnp.where(
        my_target.astype(jnp.int32) == t_range[:, None].astype(jnp.int32), my_weight, 0.0
    ).astype(BF)

    active = [
        jnp.maximum(dot(received, w_one_all[j]), 0.0).astype(BF) for j in range(mlp_n)
    ]
    partial_hidden = jnp.concatenate([dot(spread, a).astype(BF) for a in active], axis=1)
    parts = exchange(partial_hidden.reshape(mlp_n, quarter, mlp_n * units), "mlp")
    hidden = jnp.sum(parts.astype(F32), axis=0).astype(BF)
    logits = dot(hidden, w_two_all)
    exponent = jnp.exp(logits)
    probability = exponent / jnp.sum(exponent, axis=1, keepdims=True)
    my_labels = lax.dynamic_slice_in_dim(labels, me * quarter, quarter, 0)
    onehot = (my_labels[:, None] == jnp.arange(classes, dtype=jnp.int32)[None, :]).astype(F32)
    d_logits = (probability - onehot).astype(BF)
    send = jnp.stack(
        [
            jnp.concatenate([hidden[:, j * units : (j + 1) * units], d_logits], axis=1)
            for j in range(mlp_n)
        ]
    )
    got = exchange(send, "mlp").reshape(targets, units + classes)
    hidden_all = got[:, :units]
    d_logits_all = got[:, units:]

    grad_two = dot(hidden_all, d_logits_all, 0, 0)
    d_hidden = dot(d_logits_all, w_two_all, 1, 1).astype(BF)
    grads = []
    for j in range(mlp_n):
        scattered = dot(spread, d_hidden[:, j * units : (j + 1) * units], 0, 0)
        d_pre = jnp.where(active[j] > 0, scattered, 0.0).astype(BF)
        grads.append(dot(received, d_pre, 0, 0))
    grad_one = jnp.stack(grads)

    half = width_f // 2
    pairs = [(i, i ^ 1) for i in range(col_n)]

    def halves(x, axis):
        size = x.shape[axis] // 2
        mine = lax.dynamic_slice_in_dim(x, core * size, size, axis)
        other = lax.dynamic_slice_in_dim(x, (1 - core) * size, size, axis).astype(BF)
        return mine + lax.ppermute(other, "col", pairs).astype(F32)

    grad_one = halves(grad_one, 1).astype(BF)
    grad_two = halves(grad_two, 0)
    grad_one = jnp.sum(exchange(grad_one, "mlp").reshape(mlp_n, half, units).astype(F32), axis=0)
    both = jnp.concatenate([grad_one, grad_two], axis=1).astype(BF)
    chips = owners // 2
    groups = [[2 * i + c for i in range(chips)] for c in (0, 1)]
    width = units + classes
    both = exchange(both.reshape(chips, half // chips, width), ("own", "col"), groups)
    both = jnp.sum(both.astype(F32), axis=0).astype(BF)
    both = jnp.broadcast_to(both[None], (chips, half // chips, width))
    both = exchange(both, ("own", "col"), groups).reshape(half, width)
    other = lax.ppermute(both, "col", pairs)
    low = jnp.where(core == 0, both, other)
    high = jnp.where(core == 0, other, both)
    both = jnp.concatenate([low, high], axis=0).astype(F32)
    return both[:, :units], both[:, units:]


def solution(mesh):
    placed = (
        P(("own", "col"), None),
        P(("own", "col"), None),
        P(("own", "col"), None),
        P(("own", "col")),
        P(None, "mlp"),
        P("mlp", None),
    )
    return jax.shard_map(
        body,
        mesh=mesh,
        in_specs=placed,
        out_specs=(P(None, "mlp"), P("mlp", None)),
        check_vma=False,
    )
```

time: 552 us -> 237 us (0.43)
  waiting for transfers between devices: 383 us -> 87.1 us
  local copies, waits for them, and re-layouts: 94.5 us -> 19.1 us
  starting transfers between devices: 6.01 us -> 38 us
  blocking collectives: 22.2 us -> 36.6 us
  other arithmetic: 2.71 us -> 9.57 us
    psum x2 -> x0, waiting for transfers between devices: 234 us -> none  [the longest x1 189 us: body(): grad_one, grad_two = lax.psum((grad_one, grad_two), ('own', 'col'))]
    all_to_all x1 -> x5, waiting for transfers between devices: 149 us -> 46.5 us  [exchange(): lax.all_to_all(x, axes, split_axis=0, concat_axis=0, tiled=True, axis_ind...]
    all_gather x0 -> x2, waiting for transfers between devices: none -> 34.6 us  [the longest x1 34.5 us: body(): w_one_all = lax.all_gather(w_one, 'mlp')]
    unnamed x20 -> x18, local copies, waits for them, and re-layouts: 38.8 us -> 5.2 us
    gather x1, local copies, waits for them, and re-layouts: 36.5 us -> 11.9 us  [body(): fetched = features[asked]]
    all_to_all x1 -> x5, starting transfers between devices: 5.92 us -> 29 us  [exchange(): lax.all_to_all(x, axes, split_axis=0, concat_axis=0, tiled=True, axis_ind...]
    scatter x2 -> x0, local copies, waits for them, and re-layouts: 18.4 us -> none  [the longest x1 15.5 us: body(): jnp.zeros((owners * capacity,), jnp.int32).at[flat_slot]]
    all_to_all x1 -> x2, blocking collectives: 22.2 us -> 36.6 us  [exchange(): lax.all_to_all(x, axes, split_axis=0, concat_axis=0, tiled=True, axis_ind...]
  transfers between devices with their start and end apart: 3 -> 10, of which waited for: 3 -> 9; matrix products, arithmetic and copies ran while one was open for 6% -> 4% of each run, Pallas kernels for 0% -> 0%
where the time goes in v1:
time: 237 us; the launch traced here: 236 us
  waiting for transfers between devices  87.1 us (37%)
  starting transfers between devices  38 us (16%)
  blocking collectives  36.6 us (15%)
  matrix products  31.7 us (13%)
  local copies, waits for them, and re-layouts  19.1 us (8%)
  between operations  14.4 us (6%)
  other arithmetic  9.57 us (4%)
    all_to_all x5, waiting for transfers between devices, exchange(): lax.all_to_all(x, axes, split_axis=0, concat_axis=0, tiled=True, axis_ind...  46.5 us
    all_to_all x2, blocking collectives, exchange(): lax.all_to_all(x, axes, split_axis=0, concat_axis=0, tiled=True, axis_ind...  36.6 us
    all_gather x1, waiting for transfers between devices, body(): w_one_all = lax.all_gather(w_one, 'mlp')  34.5 us
    dot_general x21, matrix products, dot(): lax.dot_general(a, b, (((ca,), (cb,)), ((), ())), preferred_element_type=...  31.7 us
    all_to_all x5, starting transfers between devices, exchange(): lax.all_to_all(x, axes, split_axis=0, concat_axis=0, tiled=True, axis_ind...  29 us
    gather x1, local copies, waits for them, and re-layouts, body(): fetched = features[asked]  11.9 us
    ppermute x2, starting transfers between devices, halves(): return mine + lax.ppermute(other, 'col', pairs).astype(F32)  5.33 us
    unnamed x18, local copies, waits for them, and re-layouts  5.2 us
  transfers between devices with their start and end apart: 10, of which 9 were waited for; matrix products, arithmetic and copies ran while one was open for 4% of the time, Pallas kernels for 0%

profile of v1, /device:TPU:1, one launch (start us, length us, event | category | flops | bytes accessed | tf_op | source)
XLA Modules:
  0.0 236.4 jit_solution(8797949230184321179)
XLA Ops:
  7.2 0.8 fusion.97
  7.9 0.1 convert_reduce_fusion
  8.0 0.1 fusion.90
  8.2 0.2 convolution_subtract_fusion
  8.4 0.2 select_reduce_fusion
  8.6 0.5 convolution_bitcast_fusion.2
  9.1 1.1 fusion.14
  10.2 13.0 %all-to-all-start = ((s32[64,1,128]{2,1,0:T(1,128)}), s32[64,1,128]{2,1,0:T(1,128)S(1)}, u32[]{:S(2)}, u32[]{:S(2)}) async-start(s32[64,1,128]{2,1,0:T(1,128)} %bitcast.3), calls=%async_computation | async-start | bytes 65536 | tf_op jit(solution)/shard_map/all_to_all | solution.py:15
  23.2 9.3 %all-to-all-done = s32[64,1,128]{2,1,0:T(1,128)S(1)} async-done(((s32[64,1,128]{2,1,0:T(1,128)}), s32[64,1,128]{2,1,0:T(1,128)S(1)}, u32[]{:S(2)}, u32[]{:S(2)}) %all-to-all-start) | async-done | bytes 32800 | tf_op jit(solution)/shard_map/all_to_all | solution.py:15
  32.5 0.1 constant_dynamic-slice_fusion.1
  32.7 11.9 %gather_fusion = bf16[2048,512]{1,0:T(8,128)(2,1)} fusion(bf16[4096,512]{1,0:T(8,128)(2,1)} %param.6, s32[2048]{0:T(1024)S(1)} %broadcast_clamp_fusion), kind=kCustom, calls=%fused_computation | custom fusion | bytes 4202496 | tf_op jit(solution)/shard_map/gather | solution.py:62
  44.7 4.8 %all-to-all-start.1 = ((bf16[64,32,512]{2,1,0:T(8,128)(2,1)}), bf16[64,32,512]{2,1,0:T(8,128)(2,1)S(1)}, u32[]{:S(2)}, u32[]{:S(2)}) async-start(bf16[64,32,512]{2,1,0:T(8,128)(2,1)} %bitcast.5), calls=%async_computation.1 | async-start | bytes 4194304 | tf_op jit(solution)/shard_map/all_to_all | solution.py:15
  49.5 0.7 all-gather.6.cloned.1.call-update
  50.3 0.7 all-gather.4.cloned.1.call-update
  51.0 0.4 convolution_bitcast_fusion.1
  51.4 0.1 copy.22
  51.6 0.4 convolution_bitcast_fusion
  52.1 0.1 copy.23
  52.2 0.1 broadcast_in_dim.83
  52.3 34.5 %all-gather.6.cloned.1.call-done = bf16[2048,512]{1,0:T(8,128)(2,1)} async-done(((bf16[512,512]{1,0:T(8,128)(2,1)}), bf16[2048,512]{1,0:T(8,128)(2,1)}) %all-gather.6.cloned.1.call-update) | async-done | bytes 2097168 | tf_op jit(solution)/shard_map/all_gather | solution.py:33
  86.8 12.4 %all-to-all-done.1 = bf16[64,32,512]{2,1,0:T(8,128)(2,1)S(1)} async-done(((bf16[64,32,512]{2,1,0:T(8,128)(2,1)}), bf16[64,32,512]{2,1,0:T(8,128)(2,1)S(1)}, u32[]{:S(2)}, u32[]{:S(2)}) %all-to-all-start.1) | async-done | bytes 2097184 | tf_op jit(solution)/shard_map/all_to_all | solution.py:15
  99.2 2.3 maximum_convert_fusion.1
  101.5 0.4 convolution_convert_fusion.2
  102.0 1.9 copy-done.2
  103.9 1.2 maximum_convert_fusion.2
  105.1 0.4 convolution_convert_fusion.3
  105.6 1.2 maximum_convert_fusion.3
  106.9 1.3 copy-done.8
  108.2 0.4 convolution_convert_fusion.4
  108.6 1.3 maximum_convert_fusion
  109.9 0.4 convolution_convert_fusion.1
  110.4 1.0 pad_maximum_fusion.1
  111.4 4.2 %all-to-all-start.2 = ((bf16[4,32,2048]{2,1,0:T(8,128)(2,1)}), bf16[4,32,2048]{2,1,0:T(8,128)(2,1)S(1)}, u32[]{:S(2)}, u32[]{:S(2)}) async-start(bf16[4,32,2048]{2,1,0:T(8,128)(2,1)} %bitcast.9), calls=%async_computation.2 | async-start | bytes 1048576 | tf_op jit(solution)/shard_map/all_to_all | solution.py:15
  115.6 6.9 %all-to-all-done.2 = bf16[4,32,2048]{2,1,0:T(8,128)(2,1)S(1)} async-done(((bf16[4,32,2048]{2,1,0:T(8,128)(2,1)}), bf16[4,32,2048]{2,1,0:T(8,128)(2,1)S(1)}, u32[]{:S(2)}, u32[]{:S(2)}) %all-to-all-start.2) | async-done | bytes 524320 | tf_op jit(solution)/shard_map/all_to_all | solution.py:15
  122.5 0.1 reduce_sum.62
  122.6 1.7 fusion.126
  124.4 0.1 subtract_convert_fusion
  124.5 0.7 pad_maximum_fusion.3
  125.2 3.5 %all-to-all-start.3 = ((bf16[4,32,768]{2,1,0:T(8,128)(2,1)}), bf16[4,32,768]{2,1,0:T(8,128)(2,1)S(1)}, u32[]{:S(2)}, u32[]{:S(2)}) async-start(bf16[4,32,768]{2,1,0:T(8,128)(2,1)} %pad_maximum_fusion.3), calls=%async_computation.3 | async-start | bytes 393216 | tf_op jit(solution)/shard_map/all_to_all | solution.py:15
  128.8 4.9 %all-to-all-done.3 = bf16[4,32,768]{2,1,0:T(8,128)(2,1)S(1)} async-done(((bf16[4,32,768]{2,1,0:T(8,128)(2,1)}), bf16[4,32,768]{2,1,0:T(8,128)(2,1)S(1)}, u32[]{:S(2)}, u32[]{:S(2)}) %all-to-all-start.3) | async-done | bytes 196640 | tf_op jit(solution)/shard_map/all_to_all | solution.py:15
  133.7 1.3 convolution_convert_fusion
  135.0 3.7 %fusion.11 = f32[1,512,512]{2,1,0:T(8,128)S(1)} fusion(bf16[2048,512]{1,0:T(8,128)(2,1)S(1)} %bitcast.67, bf16[2048,512]{1,0:T(8,128)(2,1)} %copy-done.8, bf16[2048]{0:T(1024)(128)(2,1)S(1)} %broadcast_in_dim.83, s32[2048]{0:T(1024)S(1)} %convert_element_type.126, bf16[128,2048]{1,0:T(8,128)(2,1)} %convolution_convert_fusion), kind=kOutput, calls=%fused_computation.25 | convolution fusion | flops 1345847296 | bytes 5386240 | tf_op jit(solution)/shard_map/dot_general | solution.py:11
  138.7 4.7 %fusion.10 = f32[1,512,512]{2,1,0:T(8,128)} fusion(bf16[2048,512]{1,0:T(8,128)(2,1)S(1)} %bitcast.68, bf16[2048,512]{1,0:T(8,128)(2,1)} %copy-done.7, bf16[2048]{0:T(1024)(128)(2,1)S(1)} %broadcast_in_dim.83, s32[2048]{0:T(1024)S(1)} %convert_element_type.126, bf16[128,2048]{1,0:T(8,128)(2,1)} %convolution_convert_fusion), kind=kOutput, calls=%fused_computation.24 | convolution fusion | flops 1345847296 | bytes 5386240 | tf_op jit(solution)/shard_map/dot_general | solution.py:11
  143.4 4.7 %fusion.9 = f32[1,512,512]{2,1,0:T(8,128)} fusion(bf16[2048,512]{1,0:T(8,128)(2,1)S(1)} %bitcast.69, bf16[2048,512]{1,0:T(8,128)(2,1)} %copy-done.5, bf16[2048]{0:T(1024)(128)(2,1)S(1)} %broadcast_in_dim.83, s32[2048]{0:T(1024)S(1)} %convert_element_type.126, bf16[128,2048]{1,0:T(8,128)(2,1)} %convolution_convert_fusion), kind=kOutput, calls=%fused_computation.23 | convolution fusion | flops 1345847296 | bytes 5386240 | tf_op jit(solution)/shard_map/dot_general | solution.py:11
  148.1 4.7 %fusion.8 = f32[1,512,512]{2,1,0:T(8,128)} fusion(bf16[2048,512]{1,0:T(8,128)(2,1)S(1)} %bitcast.70, bf16[2048,512]{1,0:T(8,128)(2,1)} %copy-done.6, bf16[2048]{0:T(1024)(128)(2,1)S(1)} %broadcast_in_dim.83, s32[2048]{0:T(1024)S(1)} %convert_element_type.126, bf16[128,2048]{1,0:T(8,128)(2,1)} %convolution_convert_fusion), kind=kOutput, calls=%fused_computation.22 | convolution fusion | flops 1345847296 | bytes 5386240 | tf_op jit(solution)/shard_map/dot_general | solution.py:11
  152.8 2.3 pad_maximum_fusion
  155.1 1.9 copy-done
  157.0 0.1 dynamic-slice_convert_fusion
  157.2 4.9 %collective-permute-start = (bf16[4,256,512]{2,1,0:T(8,128)(2,1)S(1)}, bf16[4,256,512]{2,1,0:T(8,128)(2,1)S(1)}, u32[]{:S(2)}, u32[]{:S(2)}) collective-permute-start(bf16[4,256,512]{2,1,0:T(8,128)(2,1)S(1)} %dynamic-slice_convert_fusion), channel_id=1, source_target_pairs={{0,4},{4,0},{8,12},{12,8},{16,20},{20,16},{24,28},{28,24},{1,5},{5... | collective-permute-start | bytes 3145736 | tf_op jit(solution)/shard_map/ppermute | solution.py:109
  162.0 2.3 collective-permute-done
  164.3 2.9 %add_convert_fusion = bf16[4,256,512]{2,1,0:T(8,128)(2,1)} fusion(bf16[4,256,512]{2,1,0:T(8,128)(2,1)S(1)} %collective-permute-done, f32[4,512,512]{2,1,0:T(8,128)} %copy-done, s32[]{:T(128)S(6)} %select_n.106), kind=kLoop, calls=%fused_computation.11 | loop fusion | flops 1572864 | bytes 4194308 | tf_op jit(solution)/shard_map/convert_element_type | solution.py:111
  167.2 3.5 %all-to-all-start.4 = ((bf16[4,256,512]{2,1,0:T(8,128)(2,1)}), bf16[4,256,512]{2,1,0:T(8,128)(2,1)S(1)}, u32[]{:S(2)}, u32[]{:S(2)}) async-start(bf16[4,256,512]{2,1,0:T(8,128)(2,1)} %add_convert_fusion), calls=%async_computation.4 | async-start | bytes 2097152 | tf_op jit(solution)/shard_map/all_to_all | solution.py:15
  170.7 0.2 fusion.80
  171.0 0.5 collective-permute-start.1
  171.5 1.0 collective-permute-done.1
  172.5 13.0 %all-to-all-done.4 = bf16[4,256,512]{2,1,0:T(8,128)(2,1)S(1)} async-done(((bf16[4,256,512]{2,1,0:T(8,128)(2,1)}), bf16[4,256,512]{2,1,0:T(8,128)(2,1)S(1)}, u32[]{:S(2)}, u32[]{:S(2)}) %all-to-all-start.4) | async-done | bytes 1048608 | tf_op jit(solution)/shard_map/all_to_all | solution.py:15
  185.6 0.2 reduce.2
  185.8 18.8 %all_to_all.39 = bf16[32,8,768]{2,1,0:T(8,128)(2,1)S(1)} all-to-all(bf16[32,8,768]{2,1,0:T(8,128)(2,1)S(1)} %pad_maximum_fusion.2), channel_id=1, replica_groups={{0,8,16,24,32,40,48,56,64,72,80,88,96,104,112,120,128,136,144,152,160,1..., dimensions={0} | all-to-all | bytes 786432 | tf_op jit(solution)/shard_map/all_to_all | solution.py:15
  204.7 17.8 %all_to_all.40 = bf16[32,8,768]{2,1,0:T(8,128)(2,1)S(1)} all-to-all(bf16[32,8,768]{2,1,0:T(8,128)(2,1)S(1)} %broadcast_in_dim.86), channel_id=1, replica_groups={{0,8,16,24,32,40,48,56,64,72,80,88,96,104,112,120,128,136,144,152,160,1..., dimensions={0} | all-to-all | bytes 786432 | tf_op jit(solution)/shard_map/all_to_all | solution.py:15
  222.6 3.6 %collective-permute-start.2 = (bf16[256,768]{1,0:T(8,128)(2,1)S(1)}, bf16[256,768]{1,0:T(8,128)(2,1)S(1)}, u32[]{:S(2)}, u32[]{:S(2)}) collective-permute-start(bf16[256,768]{1,0:T(8,128)(2,1)S(1)} %bitcast.71), channel_id=1, source_target_pairs={{0,4},{4,0},{8,12},{12,8},{16,20},{20,16},{24,28},{28,24},{1,5},{5... | collective-permute-start | bytes 1179656 | tf_op jit(solution)/shard_map/ppermute | solution.py:122
  226.1 1.3 collective-permute-done.2
  227.5 0.8 maximum_convert_fusion.5
  228.4 0.1 maximum_convert_fusion.4
  228.5 1.1 slice.84
  (35 shorter events, 0.7 us)
Async XLA Ops:
  10.2 22.3 %all-to-all-start = ((s32[64,1,128]{2,1,0:T(1,128)}), s32[64,1,128]{2,1,0:T(1,128)S(1)}, u32[]{:S(2)}, u32[]{:S(2)}) async-start(s32[64,1,128]{2,1,0:T(1,128)} %bitcast.3), calls=%async_computation | async-start | bytes 65536 | tf_op jit(solution)/shard_map/all_to_all | solution.py:15
  44.7 54.5 %all-to-all-start.1 = ((bf16[64,32,512]{2,1,0:T(8,128)(2,1)}), bf16[64,32,512]{2,1,0:T(8,128)(2,1)S(1)}, u32[]{:S(2)}, u32[]{:S(2)}) async-start(bf16[64,32,512]{2,1,0:T(8,128)(2,1)} %bitcast.5), calls=%async_computation.1 | async-start | bytes 4194304 | tf_op jit(solution)/shard_map/all_to_all | solution.py:15
  49.5 2.1 copy-start.3
  49.5 37.3 %all-gather.6.cloned.1.call-start = ((), (), s32[]{:S(2)}) async-start(), calls=%async_computation.8 | async-start | bytes 2621440 | tf_op jit(solution)/shard_map/all_gather | solution.py:33
  50.2 72.4 %all-gather.4.cloned.1.call-start = ((), (), s32[]{:S(2)}) async-start(), calls=%async_computation.7 | async-start | bytes 1310720 | tf_op jit(solution)/shard_map/all_gather | solution.py:34
  101.5 3.6 %copy-start.5 = (bf16[2048,512]{1,0:T(8,128)(2,1)}, bf16[2048,512]{1,0:T(8,128)(2,1)S(1)}, u32[]{:S(2)}) copy-start(bf16[2048,512]{1,0:T(8,128)(2,1)S(1)} %maximum_convert_fusion.1) | copy-start | bytes 6291460
  101.5 2.4 copy-start.2
  105.1 1.7 copy-start.7
  106.8 1.3 copy-start.8
  109.9 1.5 copy-start.6
  109.9 5.7 %copy-start.4 = (s32[128]{0:T(128)S(1)}, s32[128]{0:T(128)}, u32[]{:S(2)}) copy-start(s32[128]{0:T(128)} %param.9) | copy-start | bytes 1540
  111.4 11.1 %all-to-all-start.2 = ((bf16[4,32,2048]{2,1,0:T(8,128)(2,1)}), bf16[4,32,2048]{2,1,0:T(8,128)(2,1)S(1)}, u32[]{:S(2)}, u32[]{:S(2)}) async-start(bf16[4,32,2048]{2,1,0:T(8,128)(2,1)} %bitcast.9), calls=%async_computation.2 | async-start | bytes 1048576 | tf_op jit(solution)/shard_map/all_to_all | solution.py:15
  122.6 11.1 %copy-start.1 = (bf16[2048,256]{1,0:T(8,128)(2,1)S(1)}, bf16[2048,256]{1,0:T(8,128)(2,1)}, u32[]{:S(2)}) copy-start(bf16[2048,256]{1,0:T(8,128)(2,1)} %all-gather.4.cloned.1.call-done) | copy-start | bytes 3145732
  125.2 8.5 %all-to-all-start.3 = ((bf16[4,32,768]{2,1,0:T(8,128)(2,1)}), bf16[4,32,768]{2,1,0:T(8,128)(2,1)S(1)}, u32[]{:S(2)}, u32[]{:S(2)}) async-start(bf16[4,32,768]{2,1,0:T(8,128)(2,1)} %pad_maximum_fusion.3), calls=%async_computation.3 | async-start | bytes 393216 | tf_op jit(solution)/shard_map/all_to_all | solution.py:15
  155.1 2.0 copy-start
  157.2 7.2 %collective-permute-start = (bf16[4,256,512]{2,1,0:T(8,128)(2,1)S(1)}, bf16[4,256,512]{2,1,0:T(8,128)(2,1)S(1)}, u32[]{:S(2)}, u32[]{:S(2)}) collective-permute-start(bf16[4,256,512]{2,1,0:T(8,128)(2,1)S(1)} %dynamic-slice_convert_fusion), channel_id=1, source_target_pairs={{0,4},{4,0},{8,12},{12,8},{16,20},{20,16},{24,28},{28,24},{1,5},{5... | collective-permute-start | bytes 3145736 | tf_op jit(solution)/shard_map/ppermute | solution.py:109
  167.2 18.3 %all-to-all-start.4 = ((bf16[4,256,512]{2,1,0:T(8,128)(2,1)}), bf16[4,256,512]{2,1,0:T(8,128)(2,1)S(1)}, u32[]{:S(2)}, u32[]{:S(2)}) async-start(bf16[4,256,512]{2,1,0:T(8,128)(2,1)} %add_convert_fusion), calls=%async_computation.4 | async-start | bytes 2097152 | tf_op jit(solution)/shard_map/all_to_all | solution.py:15
  171.0 1.4 collective-permute-start.1
  222.6 4.9 %collective-permute-start.2 = (bf16[256,768]{1,0:T(8,128)(2,1)S(1)}, bf16[256,768]{1,0:T(8,128)(2,1)S(1)}, u32[]{:S(2)}, u32[]{:S(2)}) collective-permute-start(bf16[256,768]{1,0:T(8,128)(2,1)S(1)} %bitcast.71), channel_id=1, source_target_pairs={{0,4},{4,0},{8,12},{12,8},{16,20},{20,16},{24,28},{28,24},{1,5},{5... | collective-permute-start | bytes 1179656 | tf_op jit(solution)/shard_map/ppermute | solution.py:122
Sparse Core Ops, SparseCore 0:
  52.1 34.6 all-gather.5
  88.6 25.6 all-gather.3

commit v2 on v1

--- a/solution.py
+++ b/solution.py
@@ -25,13 +25,19 @@
     entries = targets * width_k
     capacity = 2 * entries // owners
     share = capacity // mlp_n
-    quarter = targets // mlp_n
     units, classes = w_two.shape
     me = lax.axis_index("mlp")
     core = lax.axis_index("col") % 2
 
-    w_one_all = lax.all_gather(w_one, "mlp")
-    w_two_all = lax.all_gather(w_two, "mlp", tiled=True)
+    def to_mlp(x, step):
+        return lax.ppermute(x, "mlp", [(j, (j + step) % mlp_n) for j in range(mlp_n)])
+
+    steps = (2, 1, 3, 0)
+    w_both = jnp.concatenate([w_one, w_two], axis=1)
+    w_ones, w_twos = {0: w_one}, {0: w_two}
+    for step in steps[:-1]:
+        w_got = to_mlp(w_both, -step)
+        w_ones[step], w_twos[step] = w_got[:, :units], w_got[:, units:]
 
     owner_range = jnp.arange(owners, dtype=jnp.int32)
     owner_ids = nbr_page // rows_dev
@@ -67,50 +73,47 @@
     spread = jnp.where(
         my_target.astype(jnp.int32) == t_range[:, None].astype(jnp.int32), my_weight, 0.0
     ).astype(BF)
+    spread, spread_t = lax.optimization_barrier((spread, spread.T))
 
-    active = [
-        jnp.maximum(dot(received, w_one_all[j]), 0.0).astype(BF) for j in range(mlp_n)
-    ]
-    partial_hidden = jnp.concatenate([dot(spread, a).astype(BF) for a in active], axis=1)
-    parts = exchange(partial_hidden.reshape(mlp_n, quarter, mlp_n * units), "mlp")
-    hidden = jnp.sum(parts.astype(F32), axis=0).astype(BF)
-    logits = dot(hidden, w_two_all)
+    active, hidden = {}, 0.0
+    for step in steps:
+        active[step] = lax.optimization_barrier(
+            jnp.maximum(dot(received, w_ones[step]), 0.0).astype(BF)
+        )
+        part = dot(spread, active[step])
+        hidden += to_mlp(part.astype(BF), step).astype(F32) if step else part
+    hidden = hidden.astype(BF)
+    half = width_f // 2
+    own_half = jnp.where(core == 0, received[:, :half], received[:, half:])
+    other_half = jnp.where(core == 0, received[:, half:], received[:, :half])
+    own_half, other_half = lax.optimization_barrier((own_half.T, other_half.T))
+
+    part = dot(hidden, w_two)
+    logits = part
+    for step in steps[:-1]:
+        logits += to_mlp(part, step)
     exponent = jnp.exp(logits)
     probability = exponent / jnp.sum(exponent, axis=1, keepdims=True)
-    my_labels = lax.dynamic_slice_in_dim(labels, me * quarter, quarter, 0)
-    onehot = (my_labels[:, None] == jnp.arange(classes, dtype=jnp.int32)[None, :]).astype(F32)
+    onehot = (labels[:, None] == jnp.arange(classes, dtype=jnp.int32)[None, :]).astype(F32)
     d_logits = (probability - onehot).astype(BF)
-    send = jnp.stack(
-        [
-            jnp.concatenate([hidden[:, j * units : (j + 1) * units], d_logits], axis=1)
-            for j in range(mlp_n)
-        ]
-    )
-    got = exchange(send, "mlp").reshape(targets, units + classes)
-    hidden_all = got[:, :units]
-    d_logits_all = got[:, units:]
 
-    grad_two = dot(hidden_all, d_logits_all, 0, 0)
-    d_hidden = dot(d_logits_all, w_two_all, 1, 1).astype(BF)
-    grads = []
-    for j in range(mlp_n):
-        scattered = dot(spread, d_hidden[:, j * units : (j + 1) * units], 0, 0)
-        d_pre = jnp.where(active[j] > 0, scattered, 0.0).astype(BF)
-        grads.append(dot(received, d_pre, 0, 0))
-    grad_one = jnp.stack(grads)
-
-    half = width_f // 2
     pairs = [(i, i ^ 1) for i in range(col_n)]
 
-    def halves(x, axis):
-        size = x.shape[axis] // 2
-        mine = lax.dynamic_slice_in_dim(x, core * size, size, axis)
-        other = lax.dynamic_slice_in_dim(x, (1 - core) * size, size, axis).astype(BF)
-        return mine + lax.ppermute(other, "col", pairs).astype(F32)
+    def partner(x):
+        return lax.ppermute(x, "col", pairs)
 
-    grad_one = halves(grad_one, 1).astype(BF)
-    grad_two = halves(grad_two, 0)
-    grad_one = jnp.sum(exchange(grad_one, "mlp").reshape(mlp_n, half, units).astype(F32), axis=0)
+    grad_two = dot(hidden, d_logits, 0, 0)
+    mine = lax.dynamic_slice_in_dim(grad_two, core * (units // 2), units // 2, 0)
+    other = lax.dynamic_slice_in_dim(grad_two, (1 - core) * (units // 2), units // 2, 0)
+    grad_two = mine + partner(other.astype(BF)).astype(F32)
+    grad_one = 0.0
+    for step in steps:
+        d_hidden = dot(d_logits, w_twos[step], 1, 1).astype(BF)
+        d_pre = jnp.where(active[step] > 0, dot(spread_t, d_hidden), 0.0).astype(BF)
+        d_pre = lax.optimization_barrier(d_pre)
+        other = partner(dot(other_half, d_pre).astype(BF))
+        mine = dot(own_half, d_pre) + other.astype(F32)
+        grad_one += to_mlp(mine.astype(BF), step).astype(F32) if step else mine
     both = jnp.concatenate([grad_one, grad_two], axis=1).astype(BF)
     chips = owners // 2
     groups = [[2 * i + c for i in range(chips)] for c in (0, 1)]
@@ -119,7 +122,7 @@
     both = jnp.sum(both.astype(F32), axis=0).astype(BF)
     both = jnp.broadcast_to(both[None], (chips, half // chips, width))
     both = exchange(both, ("own", "col"), groups).reshape(half, width)
-    other = lax.ppermute(both, "col", pairs)
+    other = partner(both)
     low = jnp.where(core == 0, both, other)
     high = jnp.where(core == 0, other, both)
     both = jnp.concatenate([low, high], axis=0).astype(F32)

time: 237 us -> 211 us (0.89)
  waiting for transfers between devices: 87.1 us -> 63.9 us
  between operations: 14.4 us -> 1.11 us
  matrix products: 31.7 us -> 41.3 us
  starting transfers between devices: 38 us -> 46.5 us
  other arithmetic: 9.57 us -> 5.48 us
  local copies, waits for them, and re-layouts: 19.1 us -> 16.2 us
    all_gather x2 -> x0, waiting for transfers between devices: 34.6 us -> none  [the longest x1 34.5 us: body(): w_one_all = lax.all_gather(w_one, 'mlp')]
    ppermute x3 -> x18, waiting for transfers between devices: 4.62 us -> 26.8 us  [the longest x12 25.5 us: to_mlp(): lax.ppermute(x, 'mlp', [(j, (j + step) % mlp_n) for j in range(mlp_n)])]
    ppermute x3 -> x18, starting transfers between devices: 8.9 us -> 28.6 us  [the longest x12 18 us: to_mlp(): lax.ppermute(x, 'mlp', [(j, (j + step) % mlp_n) for j in range(mlp_n)])]
    all_to_all x5 -> x2, starting transfers between devices: 29 us -> 17.9 us  [exchange(): lax.all_to_all(x, axes, split_axis=0, concat_axis=0, tiled=True, axis_ind...]
    dot_general x21 -> x28, matrix products: 31.7 us -> 41.3 us  [dot(): lax.dot_general(a, b, (((ca,), (cb,)), ((), ())), preferred_element_type=...]
    all_to_all x5 -> x2, waiting for transfers between devices: 46.5 us -> 37 us  [exchange(): lax.all_to_all(x, axes, split_axis=0, concat_axis=0, tiled=True, axis_ind...]
    unnamed x18 -> x37, local copies, waits for them, and re-layouts: 5.2 us -> 1.76 us
    another operation x3 -> x0, other arithmetic: 3.02 us -> none  [the longest x1 2.3 us: body(): grad_one = jnp.stack(grads)]
  transfers between devices with their start and end apart: 10 -> 20, of which waited for: 9 -> 9; matrix products, arithmetic and copies ran while one was open for 4% -> 16% of each run, Pallas kernels for 0% -> 0%
where the time goes in v2:
time: 211 us
  waiting for transfers between devices  63.9 us (30%)
  starting transfers between devices  46.5 us (22%)
  matrix products  41.3 us (20%)
  blocking collectives  36.1 us (17%)
  local copies, waits for them, and re-layouts  16.2 us (8%)
  other arithmetic  5.48 us (3%)
    dot_general x28, matrix products, dot(): lax.dot_general(a, b, (((ca,), (cb,)), ((), ())), preferred_element_type=...  41.3 us
    all_to_all x2, waiting for transfers between devices, exchange(): lax.all_to_all(x, axes, split_axis=0, concat_axis=0, tiled=True, axis_ind...  37 us
    all_to_all x2, blocking collectives, exchange(): lax.all_to_all(x, axes, split_axis=0, concat_axis=0, tiled=True, axis_ind...  36.1 us
    ppermute x12, waiting for transfers between devices, to_mlp(): lax.ppermute(x, 'mlp', [(j, (j + step) % mlp_n) for j in range(mlp_n)])  25.5 us
    ppermute x12, starting transfers between devices, to_mlp(): lax.ppermute(x, 'mlp', [(j, (j + step) % mlp_n) for j in range(mlp_n)])  18 us
    all_to_all x2, starting transfers between devices, exchange(): lax.all_to_all(x, axes, split_axis=0, concat_axis=0, tiled=True, axis_ind...  17.9 us
    gather x1, local copies, waits for them, and re-layouts, body(): fetched = features[asked]  12 us
    ppermute x6, starting transfers between devices, partner(): return lax.ppermute(x, 'col', pairs)  10.5 us
  transfers between devices with their start and end apart: 20, of which 9 were waited for; matrix products, arithmetic and copies ran while one was open for 16% of the time, Pallas kernels for 0%

profile of v2, /device:TPU:1, one launch (start us, length us, event | category | flops | bytes accessed | tf_op | source)
XLA Modules:
  0.0 210.5 jit_solution(4162440619022226232)
XLA Ops:
  0.6 0.8 fusion.39
  2.1 0.5 convolution_bitcast_fusion.2
  2.6 1.1 fusion.6
  3.7 13.0 %all-to-all-start = ((s32[64,1,128]{2,1,0:T(1,128)}), s32[64,1,128]{2,1,0:T(1,128)S(1)}, u32[]{:S(2)}, u32[]{:S(2)}) async-start(s32[64,1,128]{2,1,0:T(1,128)} %bitcast.3), calls=%async_computation | async-start | bytes 65536 | tf_op jit(solution)/shard_map/all_to_all | solution.py:15
  16.7 9.3 %all-to-all-done = s32[64,1,128]{2,1,0:T(1,128)S(1)} async-done(((s32[64,1,128]{2,1,0:T(1,128)}), s32[64,1,128]{2,1,0:T(1,128)S(1)}, u32[]{:S(2)}, u32[]{:S(2)}) %all-to-all-start) | async-done | bytes 32800 | tf_op jit(solution)/shard_map/all_to_all | solution.py:15
  26.2 12.0 %gather_fusion = bf16[2048,512]{1,0:T(8,128)(2,1)} fusion(bf16[4096,512]{1,0:T(8,128)(2,1)} %param.6, s32[2048]{0:T(1024)S(1)} %broadcast_clamp_fusion), kind=kCustom, calls=%fused_computation | custom fusion | bytes 4202496 | tf_op jit(solution)/shard_map/gather | solution.py:68
  38.2 4.9 %all-to-all-start.1 = ((bf16[64,32,512]{2,1,0:T(8,128)(2,1)}), bf16[64,32,512]{2,1,0:T(8,128)(2,1)S(1)}, u32[]{:S(2)}, u32[]{:S(2)}) async-start(bf16[64,32,512]{2,1,0:T(8,128)(2,1)} %bitcast.5), calls=%async_computation.1 | async-start | bytes 4194304 | tf_op jit(solution)/shard_map/all_to_all | solution.py:15
  43.2 0.8 constant_dynamic-update-slice_fusion.1
  44.0 0.7 constant_dynamic-update-slice_fusion
  44.7 2.9 %collective-permute-start = (bf16[512,768]{1,0:T(8,128)(2,1)}, bf16[512,768]{1,0:T(8,128)(2,1)}, u32[]{:S(2)}, u32[]{:S(2)}) collective-permute-start(bf16[512,768]{1,0:T(8,128)(2,1)} %constant_dynamic-update-slice_fusion), channel_id=1, source_target_pairs={{0,2},{1,3},{2,0},{3,1},{4,6},{5,7},{6,4},{7,5},{8,10},{9,11},{10,... | collective-permute-start | bytes 2359304 | tf_op jit(solution)/shard_map/ppermute | solution.py:33
  47.6 0.8 collective-permute-start.2
  48.4 0.7 collective-permute-start.4
  49.1 0.4 convolution_bitcast_fusion.1
  49.7 0.4 convolution_bitcast_fusion
  50.4 1.4 select_convert_fusion.4
  51.9 13.2 %collective-permute-done = bf16[512,768]{1,0:T(8,128)(2,1)} collective-permute-done((bf16[512,768]{1,0:T(8,128)(2,1)}, bf16[512,768]{1,0:T(8,128)(2,1)}, u32[]{:S(2)}, u32[]{:S(2)}) %collective-permute-start) | collective-permute-done | bytes 786464 | tf_op jit(solution)/shard_map/ppermute | solution.py:33
  65.1 27.7 %all-to-all-done.1 = bf16[64,32,512]{2,1,0:T(8,128)(2,1)S(1)} async-done(((bf16[64,32,512]{2,1,0:T(8,128)(2,1)}), bf16[64,32,512]{2,1,0:T(8,128)(2,1)S(1)}, u32[]{:S(2)}, u32[]{:S(2)}) %all-to-all-start.1) | async-done | bytes 2097184 | tf_op jit(solution)/shard_map/all_to_all | solution.py:15
  92.9 2.3 %maximum_convert_fusion.3 = bf16[2048,512]{1,0:T(8,128)(2,1)S(1)} fusion(bf16[2048,512]{1,0:T(8,128)(2,1)S(1)} %bitcast.72, bf16[512,768]{1,0:T(8,128)(2,1)} %collective-permute-done), kind=kOutput, calls=%fused_computation.8 | convolution fusion | flops 1075838976 | bytes 4718592 | tf_op jit(solution)/shard_map/dot_general | solution.py:11
  95.2 0.5 convolution_convert_fusion.6
  95.6 3.0 %collective-permute-start.1 = (bf16[128,512]{1,0:T(8,128)(2,1)S(1)}, bf16[128,512]{1,0:T(8,128)(2,1)S(1)}, u32[]{:S(2)}, u32[]{:S(2)}) collective-permute-start(bf16[128,512]{1,0:T(8,128)(2,1)S(1)} %convolution_convert_fusion.6), channel_id=1, source_target_pairs={{0,2},{1,3},{2,0},{3,1},{4,6},{5,7},{6,4},{7,5},{8,10},{9,11},{10,... | collective-permute-start | bytes 393224 | tf_op jit(solution)/shard_map/ppermute | solution.py:33
  98.6 2.3 %maximum_convert_fusion.2 = bf16[2048,512]{1,0:T(8,128)(2,1)S(1)} fusion(bf16[2048,512]{1,0:T(8,128)(2,1)S(1)} %bitcast.73, bf16[512,768]{1,0:T(8,128)(2,1)} %collective-permute-done.2), kind=kOutput, calls=%fused_computation.7 | convolution fusion | flops 1075838976 | bytes 4718592 | tf_op jit(solution)/shard_map/dot_general | solution.py:11
  100.9 0.4 convolution_convert_fusion.5
  101.4 0.7 collective-permute-start.3
  102.1 2.3 %maximum_convert_fusion.1 = bf16[2048,512]{1,0:T(8,128)(2,1)S(1)} fusion(bf16[2048,512]{1,0:T(8,128)(2,1)S(1)} %bitcast.74, bf16[512,768]{1,0:T(8,128)(2,1)} %collective-permute-done.4), kind=kOutput, calls=%fused_computation.6 | convolution fusion | flops 1075838976 | bytes 4718592 | tf_op jit(solution)/shard_map/dot_general | solution.py:11
  104.4 0.4 convolution_convert_fusion.4
  104.8 0.9 copy-done.5
  105.7 2.3 %collective-permute-start.5 = (bf16[128,512]{1,0:T(8,128)(2,1)S(1)}, bf16[128,512]{1,0:T(8,128)(2,1)S(1)}, u32[]{:S(2)}, u32[]{:S(2)}) collective-permute-start(bf16[128,512]{1,0:T(8,128)(2,1)S(1)} %convolution_convert_fusion.4), channel_id=1, source_target_pairs={{0,3},{1,0},{2,1},{3,2},{4,7},{5,4},{6,5},{7,6},{8,11},{9,8},{10,9... | collective-permute-start | bytes 393224 | tf_op jit(solution)/shard_map/ppermute | solution.py:33
  108.0 1.2 maximum_convert_fusion
  109.2 0.7 collective-permute-done.5
  109.9 0.5 add_convert_fusion.5
  110.6 1.7 collective-permute-start.6
  112.3 2.1 collective-permute-start.7
  114.3 0.6 collective-permute-start.8
  115.0 1.5 select_bitcast_fusion
  116.4 1.0 collective-permute-done.7
  117.4 0.8 collective-permute-done.8
  118.3 4.0 %select_convert_fusion = bf16[2048,512]{1,0:T(8,128)(2,1)} fusion(bf16[2048,512]{1,0:T(8,128)(2,1)} %copy-done, bf16[2048,128]{1,0:T(8,128)(2,1)S(1)} %copy-done.11, bf16[512,256]{1,0:T(8,128)(2,1)S(1)} %copy-done.9, f32[128,256]{1,0:T(8,128)S(1)} %get-tuple-element.11, s32[128]{0:T(128)S(1)} %copy-done.12, f32[128]{0:T(128)S(1)} %get-tuple-element.10), kind=kOutput, calls=%fused_computation.1 | convolution fusion | flops 307462144 | bytes 5112832 | tf_op jit(solution)/shard_map/dot_general | solution.py:11
  122.3 3.2 %select_convert_fusion.3 = bf16[2048,512]{1,0:T(8,128)(2,1)} fusion(bf16[2048,512]{1,0:T(8,128)(2,1)S(1)} %copy-done.2, bf16[2048,128]{1,0:T(8,128)(2,1)S(1)} %copy-done.11, bf16[512,768]{1,0:T(8,128)(2,1)} %collective-permute-done, f32[128,256]{1,0:T(8,128)S(1)} %get-tuple-element.11, s32[128]{0:T(128)S(1)} %copy-done.12, f32[128]{0:T(128)S(1)} %get-tuple-element.10), kind=kOutput, calls=%fused_computation.4 | convolution fusion | flops 307462144 | bytes 5112832 | tf_op jit(solution)/shard_map/dot_general | solution.py:11
  125.6 3.5 %convolution_convert_fusion.3 = bf16[256,512]{1,0:T(8,128)(2,1)} fusion(bf16[256,2048]{0,1:T(8,128)(2,1)} %get-tuple-element.9, bf16[2048,512]{1,0:T(8,128)(2,1)} %select_convert_fusion.3), kind=kOutput, calls=%fused_computation.17 | convolution fusion | flops 537001984 | bytes 3407872 | tf_op jit(solution)/shard_map/dot_general | solution.py:11
  129.1 5.6 %collective-permute-start.9 = (bf16[256,512]{1,0:T(8,128)(2,1)}, bf16[256,512]{1,0:T(8,128)(2,1)}, u32[]{:S(2)}, u32[]{:S(2)}) collective-permute-start(bf16[256,512]{1,0:T(8,128)(2,1)} %convolution_convert_fusion.3), channel_id=1, source_target_pairs={{0,4},{4,0},{8,12},{12,8},{16,20},{20,16},{24,28},{28,24},{1,5},{5... | collective-permute-start | bytes 786440 | tf_op jit(solution)/shard_map/ppermute | solution.py:103
  134.7 3.3 %select_convert_fusion.2 = bf16[2048,512]{1,0:T(8,128)(2,1)} fusion(bf16[2048,512]{1,0:T(8,128)(2,1)S(1)} %copy-done.4, bf16[2048,128]{1,0:T(8,128)(2,1)S(1)} %copy-done.11, bf16[512,768]{1,0:T(8,128)(2,1)} %collective-permute-done.2, f32[128,256]{1,0:T(8,128)S(1)} %get-tuple-element.11, s32[128]{0:T(128)S(1)} %copy-done.12, f32[128]{0:T(128)S(1)} %get-tuple-element.10), kind=kOutput, calls=%fused_computation.3 | convolution fusion | flops 307462144 | bytes 5112832 | tf_op jit(solution)/shard_map/dot_general | solution.py:11
  138.0 3.5 %convolution_convert_fusion.2 = bf16[256,512]{1,0:T(8,128)(2,1)} fusion(bf16[256,2048]{0,1:T(8,128)(2,1)} %get-tuple-element.9, bf16[2048,512]{1,0:T(8,128)(2,1)} %select_convert_fusion.2), kind=kOutput, calls=%fused_computation.16 | convolution fusion | flops 537001984 | bytes 3407872 | tf_op jit(solution)/shard_map/dot_general | solution.py:11
  141.5 3.2 %select_convert_fusion.1 = bf16[2048,512]{1,0:T(8,128)(2,1)} fusion(bf16[2048,512]{1,0:T(8,128)(2,1)S(1)} %copy-done.6, bf16[2048,128]{1,0:T(8,128)(2,1)S(1)} %copy-done.11, bf16[512,768]{1,0:T(8,128)(2,1)} %collective-permute-done.4, f32[128,256]{1,0:T(8,128)S(1)} %get-tuple-element.11, s32[128]{0:T(128)S(1)} %copy-done.12, f32[128]{0:T(128)S(1)} %get-tuple-element.10), kind=kOutput, calls=%fused_computation.2 | convolution fusion | flops 307462144 | bytes 5112832 | tf_op jit(solution)/shard_map/dot_general | solution.py:11
  144.6 2.8 %convolution_convert_fusion.1 = bf16[256,512]{1,0:T(8,128)(2,1)S(1)} fusion(bf16[256,2048]{0,1:T(8,128)(2,1)} %get-tuple-element.9, bf16[2048,512]{1,0:T(8,128)(2,1)} %select_convert_fusion.1), kind=kOutput, calls=%fused_computation.15 | convolution fusion | flops 537001984 | bytes 3407872 | tf_op jit(solution)/shard_map/dot_general | solution.py:11
  147.4 0.6 collective-permute-start.13
  148.0 0.7 convolution_convert_fusion
  148.8 0.3 collective-permute-start.15
  149.1 0.3 fusion.52
  149.5 0.6 collective-permute-start.16
  150.0 1.7 add_convert_fusion.3
  151.8 0.5 collective-permute-start.10
  152.3 0.7 add_convert_fusion.2
  153.0 2.0 collective-permute-start.12
  155.0 0.7 add_convert_fusion.1
  155.8 0.8 collective-permute-start.14
  156.6 0.7 fusion.54
  157.4 3.9 %collective-permute-done.10 = bf16[256,512]{1,0:T(8,128)(2,1)S(1)} collective-permute-done((bf16[256,512]{1,0:T(8,128)(2,1)S(1)}, bf16[256,512]{1,0:T(8,128)(2,1)S(1)}, u32[]{:S(2)}, u32[]{:S(2)}) %collective-permute-start.10) | collective-permute-done | bytes 262176 | tf_op jit(solution)/shard_map/ppermute | solution.py:33
  161.3 6.0 %collective-permute-done.12 = bf16[256,512]{1,0:T(8,128)(2,1)S(1)} collective-permute-done((bf16[256,512]{1,0:T(8,128)(2,1)S(1)}, bf16[256,512]{1,0:T(8,128)(2,1)S(1)}, u32[]{:S(2)}, u32[]{:S(2)}) %collective-permute-start.12) | collective-permute-done | bytes 262176 | tf_op jit(solution)/shard_map/ppermute | solution.py:33
  167.5 18.4 %all_to_all.24 = bf16[32,8,768]{2,1,0:T(8,128)(2,1)S(1)} all-to-all(bf16[32,8,768]{2,1,0:T(8,128)(2,1)S(1)} %pad_maximum_fusion), channel_id=1, replica_groups={{0,8,16,24,32,40,48,56,64,72,80,88,96,104,112,120,128,136,144,152,160,1..., dimensions={0} | all-to-all | bytes 786432 | tf_op jit(solution)/shard_map/all_to_all | solution.py:15
  185.9 17.7 %all_to_all.25 = bf16[32,8,768]{2,1,0:T(8,128)(2,1)S(1)} all-to-all(bf16[32,8,768]{2,1,0:T(8,128)(2,1)S(1)} %broadcast_in_dim.92), channel_id=1, replica_groups={{0,8,16,24,32,40,48,56,64,72,80,88,96,104,112,120,128,136,144,152,160,1..., dimensions={0} | all-to-all | bytes 786432 | tf_op jit(solution)/shard_map/all_to_all | solution.py:15
  203.7 3.4 %collective-permute-start.17 = (bf16[256,768]{1,0:T(8,128)(2,1)S(1)}, bf16[256,768]{1,0:T(8,128)(2,1)S(1)}, u32[]{:S(2)}, u32[]{:S(2)}) collective-permute-start(bf16[256,768]{1,0:T(8,128)(2,1)S(1)} %bitcast.77), channel_id=1, source_target_pairs={{0,4},{4,0},{8,12},{12,8},{16,20},{20,16},{24,28},{28,24},{1,5},{5... | collective-permute-start | bytes 1179656 | tf_op jit(solution)/shard_map/ppermute | solution.py:103
  207.0 1.3 collective-permute-done.17
  208.4 0.8 maximum_convert_fusion.5
  209.4 1.1 slice.52
  (74 shorter events, 2.3 us)
Async XLA Ops:
  3.7 22.3 %all-to-all-start = ((s32[64,1,128]{2,1,0:T(1,128)}), s32[64,1,128]{2,1,0:T(1,128)S(1)}, u32[]{:S(2)}, u32[]{:S(2)}) async-start(s32[64,1,128]{2,1,0:T(1,128)} %bitcast.3), calls=%async_computation | async-start | bytes 65536 | tf_op jit(solution)/shard_map/all_to_all | solution.py:15
  38.2 4.9 %copy-start.10 = (bf16[512,512]{1,0:T(8,128)(2,1)S(1)}, bf16[512,512]{1,0:T(8,128)(2,1)}, u32[]{:S(2)}) copy-start(bf16[512,512]{1,0:T(8,128)(2,1)} %param.10) | copy-start | bytes 1572868
  38.2 5.8 %copy-start.9 = (bf16[512,256]{1,0:T(8,128)(2,1)S(1)}, bf16[512,256]{1,0:T(8,128)(2,1)}, u32[]{:S(2)}) copy-start(bf16[512,256]{1,0:T(8,128)(2,1)} %param.11) | copy-start | bytes 786436
  38.2 54.6 %all-to-all-start.1 = ((bf16[64,32,512]{2,1,0:T(8,128)(2,1)}), bf16[64,32,512]{2,1,0:T(8,128)(2,1)S(1)}, u32[]{:S(2)}, u32[]{:S(2)}) async-start(bf16[64,32,512]{2,1,0:T(8,128)(2,1)} %bitcast.5), calls=%async_computation.1 | async-start | bytes 4194304 | tf_op jit(solution)/shard_map/all_to_all | solution.py:15
  43.2 6.6 %copy-start.13 = (bf16[128,32]{0,1:T(8,128)(2,1)S(1)}, bf16[128,32]{0,1:T(8,128)(2,1)}, u32[]{:S(2)}) copy-start(bf16[128,32]{0,1:T(8,128)(2,1)} %param.8) | copy-start | bytes 24580
  44.7 20.4 %collective-permute-start = (bf16[512,768]{1,0:T(8,128)(2,1)}, bf16[512,768]{1,0:T(8,128)(2,1)}, u32[]{:S(2)}, u32[]{:S(2)}) collective-permute-start(bf16[512,768]{1,0:T(8,128)(2,1)} %constant_dynamic-update-slice_fusion), channel_id=1, source_target_pairs={{0,2},{1,3},{2,0},{3,1},{4,6},{5,7},{6,4},{7,5},{8,10},{9,11},{10,... | collective-permute-start | bytes 2359304 | tf_op jit(solution)/shard_map/ppermute | solution.py:33
  47.6 51.0 %collective-permute-start.2 = (bf16[512,768]{1,0:T(8,128)(2,1)}, bf16[512,768]{1,0:T(8,128)(2,1)}, u32[]{:S(2)}, u32[]{:S(2)}) collective-permute-start(bf16[512,768]{1,0:T(8,128)(2,1)} %constant_dynamic-update-slice_fusion), channel_id=1, source_target_pairs={{0,3},{1,0},{2,1},{3,2},{4,7},{5,4},{6,5},{7,6},{8,11},{9,8},{10,9... | collective-permute-start | bytes 2359304 | tf_op jit(solution)/shard_map/ppermute | solution.py:33
  48.4 53.6 %collective-permute-start.4 = (bf16[512,768]{1,0:T(8,128)(2,1)}, bf16[512,768]{1,0:T(8,128)(2,1)}, u32[]{:S(2)}, u32[]{:S(2)}) collective-permute-start(bf16[512,768]{1,0:T(8,128)(2,1)} %constant_dynamic-update-slice_fusion), channel_id=1, source_target_pairs={{0,1},{1,2},{2,3},{3,0},{4,5},{5,6},{6,7},{7,4},{8,9},{9,10},{10,1... | collective-permute-start | bytes 2359304 | tf_op jit(solution)/shard_map/ppermute | solution.py:33
  95.2 5.8 %copy-start.1 = (bf16[2048,512]{1,0:T(8,128)(2,1)}, bf16[2048,512]{1,0:T(8,128)(2,1)S(1)}, u32[]{:S(2)}) copy-start(bf16[2048,512]{1,0:T(8,128)(2,1)S(1)} %maximum_convert_fusion.3) | copy-start | bytes 6291460
  95.6 13.6 %collective-permute-start.1 = (bf16[128,512]{1,0:T(8,128)(2,1)S(1)}, bf16[128,512]{1,0:T(8,128)(2,1)S(1)}, u32[]{:S(2)}, u32[]{:S(2)}) collective-permute-start(bf16[128,512]{1,0:T(8,128)(2,1)S(1)} %convolution_convert_fusion.6), channel_id=1, source_target_pairs={{0,2},{1,3},{2,0},{3,1},{4,6},{5,7},{6,4},{7,5},{8,10},{9,11},{10,... | collective-permute-start | bytes 393224 | tf_op jit(solution)/shard_map/ppermute | solution.py:33
  100.9 3.4 %copy-start.3 = (bf16[2048,512]{1,0:T(8,128)(2,1)}, bf16[2048,512]{1,0:T(8,128)(2,1)S(1)}, u32[]{:S(2)}) copy-start(bf16[2048,512]{1,0:T(8,128)(2,1)S(1)} %maximum_convert_fusion.2) | copy-start | bytes 6291460
  101.4 7.8 %collective-permute-start.3 = (bf16[128,512]{1,0:T(8,128)(2,1)S(1)}, bf16[128,512]{1,0:T(8,128)(2,1)S(1)}, u32[]{:S(2)}, u32[]{:S(2)}) collective-permute-start(bf16[128,512]{1,0:T(8,128)(2,1)S(1)} %convolution_convert_fusion.5), channel_id=1, source_target_pairs={{0,1},{1,2},{2,3},{3,0},{4,5},{5,6},{6,7},{7,4},{8,9},{9,10},{10,1... | collective-permute-start | bytes 393224 | tf_op jit(solution)/shard_map/ppermute | solution.py:33
  104.4 1.3 copy-start.5
  105.7 4.2 %collective-permute-start.5 = (bf16[128,512]{1,0:T(8,128)(2,1)S(1)}, bf16[128,512]{1,0:T(8,128)(2,1)S(1)}, u32[]{:S(2)}, u32[]{:S(2)}) collective-permute-start(bf16[128,512]{1,0:T(8,128)(2,1)S(1)} %convolution_convert_fusion.4), channel_id=1, source_target_pairs={{0,3},{1,0},{2,1},{3,2},{4,7},{5,4},{6,5},{7,6},{8,11},{9,8},{10,9... | collective-permute-start | bytes 393224 | tf_op jit(solution)/shard_map/ppermute | solution.py:33
  109.2 7.2 %copy-start = (bf16[2048,512]{1,0:T(8,128)(2,1)}, bf16[2048,512]{1,0:T(8,128)(2,1)S(1)}, u32[]{:S(2)}) copy-start(bf16[2048,512]{1,0:T(8,128)(2,1)S(1)} %maximum_convert_fusion) | copy-start | bytes 6291460
  110.6 7.7 %copy-start.11 = (bf16[2048,128]{1,0:T(8,128)(2,1)S(1)}, bf16[2048,128]{1,0:T(8,128)(2,1)}, u32[]{:S(2)}) copy-start(bf16[2048,128]{1,0:T(8,128)(2,1)} %select_convert_fusion.4) | copy-start | bytes 1572868
  110.6 7.7 %copy-start.12 = (s32[128]{0:T(128)S(1)}, s32[128]{0:T(128)}, u32[]{:S(2)}) copy-start(s32[128]{0:T(128)} %param.9) | copy-start | bytes 1540
  110.6 5.8 %collective-permute-start.6 = (f32[128,256]{1,0:T(8,128)S(1)}, f32[128,256]{1,0:T(8,128)S(1)}, u32[]{:S(2)}, u32[]{:S(2)}) collective-permute-start(f32[128,256]{1,0:T(8,128)S(1)} %fusion.53), channel_id=1, source_target_pairs={{0,2},{1,3},{2,0},{3,1},{4,6},{5,7},{6,4},{7,5},{8,10},{9,11},{10,... | collective-permute-start | bytes 393224 | tf_op jit(solution)/shard_map/ppermute | solution.py:33
  112.3 5.1 %collective-permute-start.7 = (f32[128,256]{1,0:T(8,128)S(1)}, f32[128,256]{1,0:T(8,128)S(1)}, u32[]{:S(2)}, u32[]{:S(2)}) collective-permute-start(f32[128,256]{1,0:T(8,128)S(1)} %fusion.53), channel_id=1, source_target_pairs={{0,1},{1,2},{2,3},{3,0},{4,5},{5,6},{6,7},{7,4},{8,9},{9,10},{10,1... | collective-permute-start | bytes 393224 | tf_op jit(solution)/shard_map/ppermute | solution.py:33
  114.3 3.8 %collective-permute-start.8 = (f32[128,256]{1,0:T(8,128)S(1)}, f32[128,256]{1,0:T(8,128)S(1)}, u32[]{:S(2)}, u32[]{:S(2)}) collective-permute-start(f32[128,256]{1,0:T(8,128)S(1)} %fusion.53), channel_id=1, source_target_pairs={{0,3},{1,0},{2,1},{3,2},{4,7},{5,4},{6,5},{7,6},{8,11},{9,8},{10,9... | collective-permute-start | bytes 393224 | tf_op jit(solution)/shard_map/ppermute | solution.py:33
  118.3 4.0 %copy-start.2 = (bf16[2048,512]{1,0:T(8,128)(2,1)S(1)}, bf16[2048,512]{1,0:T(8,128)(2,1)}, u32[]{:S(2)}) copy-start(bf16[2048,512]{1,0:T(8,128)(2,1)} %copy-done.1) | copy-start | bytes 6291460
  125.6 9.2 %copy-start.4 = (bf16[2048,512]{1,0:T(8,128)(2,1)S(1)}, bf16[2048,512]{1,0:T(8,128)(2,1)}, u32[]{:S(2)}) copy-start(bf16[2048,512]{1,0:T(8,128)(2,1)} %copy-done.3) | copy-start | bytes 6291460
  129.1 21.0 %collective-permute-start.9 = (bf16[256,512]{1,0:T(8,128)(2,1)}, bf16[256,512]{1,0:T(8,128)(2,1)}, u32[]{:S(2)}, u32[]{:S(2)}) collective-permute-start(bf16[256,512]{1,0:T(8,128)(2,1)} %convolution_convert_fusion.3), channel_id=1, source_target_pairs={{0,4},{4,0},{8,12},{12,8},{16,20},{20,16},{24,28},{28,24},{1,5},{5... | collective-permute-start | bytes 786440 | tf_op jit(solution)/shard_map/ppermute | solution.py:103
  138.0 3.5 %copy-start.6 = (bf16[2048,512]{1,0:T(8,128)(2,1)S(1)}, bf16[2048,512]{1,0:T(8,128)(2,1)}, u32[]{:S(2)}) copy-start(bf16[2048,512]{1,0:T(8,128)(2,1)} %copy-done.5) | copy-start | bytes 6291460
  141.5 10.8 %collective-permute-start.11 = (bf16[256,512]{1,0:T(8,128)(2,1)}, bf16[256,512]{1,0:T(8,128)(2,1)S(1)}, u32[]{:S(2)}, u32[]{:S(2)}) collective-permute-start(bf16[256,512]{1,0:T(8,128)(2,1)} %convolution_convert_fusion.2), channel_id=1, source_target_pairs={{0,4},{4,0},{8,12},{12,8},{16,20},{20,16},{24,28},{28,24},{1,5},{5... | collective-permute-start | bytes 786440 | tf_op jit(solution)/shard_map/ppermute | solution.py:103
  144.6 3.4 %copy-start.8 = (bf16[256,2048]{0,1:T(8,128)(2,1)S(1)}, bf16[256,2048]{0,1:T(8,128)(2,1)}, u32[]{:S(2)}) copy-start(bf16[256,2048]{0,1:T(8,128)(2,1)} %get-tuple-element.9) | copy-start | bytes 3145732
  144.6 3.4 %copy-start.14 = (bf16[2048,512]{1,0:T(8,128)(2,1)S(1)}, bf16[2048,512]{1,0:T(8,128)(2,1)}, u32[]{:S(2)}) copy-start(bf16[2048,512]{1,0:T(8,128)(2,1)} %select_convert_fusion) | copy-start | bytes 6291460
  147.4 2.6 %copy-start.7 = (bf16[256,2048]{0,1:T(8,128)(2,1)S(1)}, bf16[256,2048]{0,1:T(8,128)(2,1)}, u32[]{:S(2)}) copy-start(bf16[256,2048]{0,1:T(8,128)(2,1)} %get-tuple-element.6) | copy-start | bytes 3145732
  147.4 2.6 %copy-start.17 = (bf16[2048,512]{1,0:T(8,128)(2,1)S(1)}, bf16[2048,512]{1,0:T(8,128)(2,1)}, u32[]{:S(2)}) copy-start(bf16[2048,512]{1,0:T(8,128)(2,1)} %select_convert_fusion.3) | copy-start | bytes 6291460
  147.4 7.6 %collective-permute-start.13 = (bf16[256,512]{1,0:T(8,128)(2,1)S(1)}, bf16[256,512]{1,0:T(8,128)(2,1)S(1)}, u32[]{:S(2)}, u32[]{:S(2)}) collective-permute-start(bf16[256,512]{1,0:T(8,128)(2,1)S(1)} %convolution_convert_fusion.1), channel_id=1, source_target_pairs={{0,4},{4,0},{8,12},{12,8},{16,20},{20,16},{24,28},{28,24},{1,5},{5... | collective-permute-start | bytes 786440 | tf_op jit(solution)/shard_map/ppermute | solution.py:103
  148.8 8.6 %collective-permute-start.15 = (bf16[256,512]{1,0:T(8,128)(2,1)S(1)}, bf16[256,512]{1,0:T(8,128)(2,1)S(1)}, u32[]{:S(2)}, u32[]{:S(2)}) collective-permute-start(bf16[256,512]{1,0:T(8,128)(2,1)S(1)} %convolution_convert_fusion), channel_id=1, source_target_pairs={{0,4},{4,0},{8,12},{12,8},{16,20},{20,16},{24,28},{28,24},{1,5},{5... | collective-permute-start | bytes 786440 | tf_op jit(solution)/shard_map/ppermute | solution.py:103
  149.4 2.9 %copy-start.16 = (bf16[2048,512]{1,0:T(8,128)(2,1)S(1)}, bf16[2048,512]{1,0:T(8,128)(2,1)}, u32[]{:S(2)}) copy-start(bf16[2048,512]{1,0:T(8,128)(2,1)} %select_convert_fusion.2) | copy-start | bytes 6291460
  149.5 7.9 %collective-permute-start.16 = (bf16[256,256]{1,0:T(8,128)(2,1)S(1)}, bf16[256,256]{1,0:T(8,128)(2,1)S(1)}, u32[]{:S(2)}, u32[]{:S(2)}) collective-permute-start(bf16[256,256]{1,0:T(8,128)(2,1)S(1)} %dynamic-slice_convert_fusion), channel_id=1, source_target_pairs={{0,4},{4,0},{8,12},{12,8},{16,20},{20,16},{24,28},{28,24},{1,5},{5... | collective-permute-start | bytes 393224 | tf_op jit(solution)/shard_map/ppermute | solution.py:103
  151.8 3.3 %copy-start.15 = (bf16[2048,512]{1,0:T(8,128)(2,1)S(1)}, bf16[2048,512]{1,0:T(8,128)(2,1)}, u32[]{:S(2)}) copy-start(bf16[2048,512]{1,0:T(8,128)(2,1)} %select_convert_fusion.1) | copy-start | bytes 6291460
  151.8 9.5 %collective-permute-start.10 = (bf16[256,512]{1,0:T(8,128)(2,1)S(1)}, bf16[256,512]{1,0:T(8,128)(2,1)S(1)}, u32[]{:S(2)}, u32[]{:S(2)}) collective-permute-start(bf16[256,512]{1,0:T(8,128)(2,1)S(1)} %add_convert_fusion.3), channel_id=1, source_target_pairs={{0,2},{1,3},{2,0},{3,1},{4,6},{5,7},{6,4},{7,5},{8,10},{9,11},{10,... | collective-permute-start | bytes 786440 | tf_op jit(solution)/shard_map/ppermute | solution.py:33
  153.0 14.2 %collective-permute-start.12 = (bf16[256,512]{1,0:T(8,128)(2,1)S(1)}, bf16[256,512]{1,0:T(8,128)(2,1)S(1)}, u32[]{:S(2)}, u32[]{:S(2)}) collective-permute-start(bf16[256,512]{1,0:T(8,128)(2,1)S(1)} %add_convert_fusion.2), channel_id=1, source_target_pairs={{0,1},{1,2},{2,3},{3,0},{4,5},{5,6},{6,7},{7,4},{8,9},{9,10},{10,1... | collective-permute-start | bytes 786440 | tf_op jit(solution)/shard_map/ppermute | solution.py:33
  155.8 11.5 %collective-permute-start.14 = (bf16[256,512]{1,0:T(8,128)(2,1)S(1)}, bf16[256,512]{1,0:T(8,128)(2,1)S(1)}, u32[]{:S(2)}, u32[]{:S(2)}) collective-permute-start(bf16[256,512]{1,0:T(8,128)(2,1)S(1)} %add_convert_fusion.1), channel_id=1, source_target_pairs={{0,3},{1,0},{2,1},{3,2},{4,7},{5,4},{6,5},{7,6},{8,11},{9,8},{10,9... | collective-permute-start | bytes 786440 | tf_op jit(solution)/shard_map/ppermute | solution.py:33
  203.7 4.7 %collective-permute-start.17 = (bf16[256,768]{1,0:T(8,128)(2,1)S(1)}, bf16[256,768]{1,0:T(8,128)(2,1)S(1)}, u32[]{:S(2)}, u32[]{:S(2)}) collective-permute-start(bf16[256,768]{1,0:T(8,128)(2,1)S(1)} %bitcast.77), channel_id=1, source_target_pairs={{0,4},{4,0},{8,12},{12,8},{16,20},{20,16},{24,28},{28,24},{1,5},{5... | collective-permute-start | bytes 1179656 | tf_op jit(solution)/shard_map/ppermute | solution.py:103

commit v3 on v2

--- a/solution.py
+++ b/solution.py
@@ -1,6 +1,8 @@
 import jax
 import jax.numpy as jnp
 from jax import lax
+from jax.experimental import pallas as pl
+from jax.experimental.pallas import tpu as pltpu
 from jax.sharding import PartitionSpec as P
 
 BF = jnp.bfloat16
@@ -15,6 +17,107 @@
     return lax.all_to_all(
         x, axes, split_axis=0, concat_axis=0, tiled=True, axis_index_groups=groups
     )
+
+
+def middle(parts, labels, hidden, w_twos, core):
+    count = len(parts)
+    targets, classes = parts[0].shape
+    units = hidden.shape[1]
+    half = units // 2
+
+    def kernel(core_ref, *refs):
+        part_refs, refs = refs[:count], refs[count:]
+        labels_ref, hidden_ref = refs[:2]
+        w_refs, refs = refs[2 : 2 + count], refs[2 + count :]
+        own_ref, other_ref = refs[:2]
+        d_hidden_refs = refs[2:]
+        logits = part_refs[0][...]
+        for part in part_refs[1:]:
+            logits += part[...]
+        exponent = jnp.exp(logits)
+        probability = exponent / jnp.sum(exponent, axis=1, keepdims=True)
+        ids = lax.broadcasted_iota(jnp.int32, (targets, classes), 1)
+        onehot = (labels_ref[...] == ids).astype(F32)
+        d_logits = (probability - onehot).astype(BF)
+        for w_ref, out in zip(w_refs, d_hidden_refs):
+            out[...] = dot(d_logits, w_ref[...], 1, 1).astype(BF)
+        both = dot(hidden_ref[...], d_logits, 0, 0)
+        swap = core_ref[0] != 0
+        low, high = both[:half], both[half:]
+        own_ref[...] = jnp.where(swap, high, low)
+        other_ref[...] = jnp.where(swap, low, high).astype(BF)
+
+    vmem = pl.BlockSpec(memory_space=pltpu.VMEM)
+    return pl.pallas_call(
+        kernel,
+        out_shape=[
+            jax.ShapeDtypeStruct((half, classes), F32),
+            jax.ShapeDtypeStruct((half, classes), BF),
+        ]
+        + [jax.ShapeDtypeStruct((targets, units), BF)] * count,
+        in_specs=[pl.BlockSpec(memory_space=pltpu.SMEM)] + [vmem] * (2 * count + 2),
+        out_specs=[vmem] * (2 + count),
+        compiler_params=pltpu.CompilerParams(vmem_limit_bytes=24 * 2**20),
+        cost_estimate=pl.CostEstimate(
+            flops=2 * targets * classes * units * (count + 1),
+            bytes_accessed=4 * 2**20,
+            transcendentals=targets * classes,
+        ),
+    )(core, *parts, labels, hidden, *w_twos)
+
+
+def backward(spread_t, d_hidden, active, rows_t):
+    slots, targets = spread_t.shape
+    units = d_hidden.shape[1]
+    width_f = rows_t.shape[0]
+    half = width_f // 2
+    block = 512
+    steps = slots // block
+
+    def kernel(spread_ref, d_hidden_ref, active_ref, rows_ref, own_ref, other_ref, total):
+        step = pl.program_id(0)
+        scattered = dot(spread_ref[...], d_hidden_ref[...]).astype(BF)
+        d_pre = jnp.where(active_ref[...] > 0, scattered, jnp.zeros_like(scattered))
+        term = dot(rows_ref[...], d_pre)
+
+        @pl.when(step == 0)
+        def _():
+            total[...] = term
+
+        @pl.when(step > 0)
+        def _():
+            total[...] += term
+
+        @pl.when(step == steps - 1)
+        def _():
+            own_ref[...] = total[:half]
+            other_ref[...] = total[half:].astype(BF)
+
+    return pl.pallas_call(
+        kernel,
+        out_shape=[
+            jax.ShapeDtypeStruct((half, units), F32),
+            jax.ShapeDtypeStruct((half, units), BF),
+        ],
+        grid=(steps,),
+        in_specs=[
+            pl.BlockSpec((block, targets), lambda i: (i, 0)),
+            pl.BlockSpec((targets, units), lambda i: (0, 0)),
+            pl.BlockSpec((block, units), lambda i: (i, 0)),
+            pl.BlockSpec((width_f, block), lambda i: (0, i)),
+        ],
+        out_specs=[
+            pl.BlockSpec((half, units), lambda i: (0, 0)),
+            pl.BlockSpec((half, units), lambda i: (0, 0)),
+        ],
+        scratch_shapes=[pltpu.VMEM((width_f, units), F32)],
+        compiler_params=pltpu.CompilerParams(vmem_limit_bytes=24 * 2**20),
+        cost_estimate=pl.CostEstimate(
+            flops=2 * slots * units * (width_f + 2 * targets),
+            bytes_accessed=2 * slots * (width_f + units + targets),
+            transcendentals=0,
+        ),
+    )(spread_t, d_hidden, active, rows_t)
 
 
 def body(features, nbr_page, nbr_weight, labels, w_one, w_two):
@@ -86,33 +189,24 @@
     half = width_f // 2
     own_half = jnp.where(core == 0, received[:, :half], received[:, half:])
     other_half = jnp.where(core == 0, received[:, half:], received[:, :half])
-    own_half, other_half = lax.optimization_barrier((own_half.T, other_half.T))
+    rows_t = jnp.concatenate([own_half, other_half], axis=1).T
 
     part = dot(hidden, w_two)
-    logits = part
-    for step in steps[:-1]:
-        logits += to_mlp(part, step)
-    exponent = jnp.exp(logits)
-    probability = exponent / jnp.sum(exponent, axis=1, keepdims=True)
-    onehot = (labels[:, None] == jnp.arange(classes, dtype=jnp.int32)[None, :]).astype(F32)
-    d_logits = (probability - onehot).astype(BF)
+    parts = [part] + [to_mlp(part, step) for step in steps[:-1]]
 
     pairs = [(i, i ^ 1) for i in range(col_n)]
 
     def partner(x):
         return lax.ppermute(x, "col", pairs)
 
-    grad_two = dot(hidden, d_logits, 0, 0)
-    mine = lax.dynamic_slice_in_dim(grad_two, core * (units // 2), units // 2, 0)
-    other = lax.dynamic_slice_in_dim(grad_two, (1 - core) * (units // 2), units // 2, 0)
-    grad_two = mine + partner(other.astype(BF)).astype(F32)
+    mine, other, *d_hidden = middle(
+        parts, labels[:, None], hidden, [w_twos[s] for s in steps], core.reshape(1)
+    )
+    grad_two = mine + partner(other).astype(F32)
     grad_one = 0.0
-    for step in steps:
-        d_hidden = dot(d_logits, w_twos[step], 1, 1).astype(BF)
-        d_pre = jnp.where(active[step] > 0, dot(spread_t, d_hidden), 0.0).astype(BF)
-        d_pre = lax.optimization_barrier(d_pre)
-        other = partner(dot(other_half, d_pre).astype(BF))
-        mine = dot(own_half, d_pre) + other.astype(F32)
+    for step, d_slice in zip(steps, d_hidden):
+        mine, other = backward(spread_t, d_slice, active[step], rows_t)
+        mine += partner(other).astype(F32)
         grad_one += to_mlp(mine.astype(BF), step).astype(F32) if step else mine
     both = jnp.concatenate([grad_one, grad_two], axis=1).astype(BF)
     chips = owners // 2

time: 211 us -> 209 us (level)
  matrix products: 41.3 us -> 20.7 us
  Pallas kernels: 0 us -> 13 us
  local copies, waits for them, and re-layouts: 16.2 us -> 26.1 us
  starting transfers between devices: 46.5 us -> 42.5 us
    dot_general x28 -> x15, matrix products: 41.3 us -> 20.7 us  [dot(): lax.dot_general(a, b, (((ca,), (cb,)), ((), ())), preferred_element_type=...]
    all_to_all x2, waiting for transfers between devices: 37 us -> 18.3 us  [exchange(): lax.all_to_all(x, axes, split_axis=0, concat_axis=0, tiled=True, axis_ind...]
    ppermute x12, waiting for transfers between devices: 25.5 us -> 43.4 us  [to_mlp(): lax.ppermute(x, 'mlp', [(j, (j + step) % mlp_n) for j in range(mlp_n)])]
    pallas_call x0 -> x5, Pallas kernels: none -> 13 us  [the longest x4 12.5 us: backward(): pl.pallas_call(kernel, out_shape=[jax.ShapeDtypeStruct((half, units), F32...]
    unnamed x37 -> x33, local copies, waits for them, and re-layouts: 1.76 us -> 7.31 us
    slice x0 -> x4, local copies, waits for them, and re-layouts: none -> 4.34 us  [the longest x3 2.9 us: body(): w_ones[step], w_twos[step] = (w_got[:, :units], w_got[:, units:])]
    ppermute x12, starting transfers between devices: 18 us -> 15.5 us  [to_mlp(): lax.ppermute(x, 'mlp', [(j, (j + step) % mlp_n) for j in range(mlp_n)])]
  transfers between devices with their start and end apart: 20 -> 20, of which waited for: 9 -> 9; matrix products, arithmetic and copies ran while one was open for 16% -> 12% of each run, Pallas kernels for 0% -> 6%
where the time goes in v3:
time: 209 us
  waiting for transfers between devices  63 us (30%)
  starting transfers between devices  42.5 us (20%)
  blocking collectives  35.3 us (17%)
  local copies, waits for them, and re-layouts  26.1 us (12%)
  matrix products  20.7 us (10%)
  Pallas kernels  13 us (6%)
  other arithmetic  7 us (3%)
    ppermute x12, waiting for transfers between devices, to_mlp(): lax.ppermute(x, 'mlp', [(j, (j + step) % mlp_n) for j in range(mlp_n)])  43.4 us
    all_to_all x2, blocking collectives, exchange(): lax.all_to_all(x, axes, split_axis=0, concat_axis=0, tiled=True, axis_ind...  35.3 us
    dot_general x15, matrix products, dot(): lax.dot_general(a, b, (((ca,), (cb,)), ((), ())), preferred_element_type=...  20.7 us
    all_to_all x2, waiting for transfers between devices, exchange(): lax.all_to_all(x, axes, split_axis=0, concat_axis=0, tiled=True, axis_ind...  18.3 us
    all_to_all x2, starting transfers between devices, exchange(): lax.all_to_all(x, axes, split_axis=0, concat_axis=0, tiled=True, axis_ind...  17.9 us
    ppermute x12, starting transfers between devices, to_mlp(): lax.ppermute(x, 'mlp', [(j, (j + step) % mlp_n) for j in range(mlp_n)])  15.5 us
    pallas_call x4, Pallas kernels, backward(): pl.pallas_call(kernel, out_shape=[jax.ShapeDtypeStruct((half, units), F32...  12.5 us
    gather x1, local copies, waits for them, and re-layouts, body(): fetched = features[asked]  11.9 us
  transfers between devices with their start and end apart: 20, of which 9 were waited for; matrix products, arithmetic and copies ran while one was open for 12% of the time, Pallas kernels for 6%

profile of v3, /device:TPU:1, one launch (start us, length us, event | category | flops | bytes accessed | tf_op | source)
XLA Modules:
  0.0 208.7 jit_solution(253141546492278457)
XLA Ops:
  0.6 0.8 fusion.33
  1.6 0.2 convolution_subtract_fusion
  2.1 1.3 convolution_bitcast_fusion.2
  3.4 1.9 fusion.6
  5.3 13.0 %all-to-all-start = ((s32[64,1,128]{2,1,0:T(1,128)}), s32[64,1,128]{2,1,0:T(1,128)S(1)}, u32[]{:S(2)}, u32[]{:S(2)}) async-start(s32[64,1,128]{2,1,0:T(1,128)} %bitcast.6), calls=%async_computation | async-start | bytes 65536 | tf_op jit(solution)/shard_map/all_to_all | solution.py:17
  18.3 9.3 %all-to-all-done = s32[64,1,128]{2,1,0:T(1,128)S(1)} async-done(((s32[64,1,128]{2,1,0:T(1,128)}), s32[64,1,128]{2,1,0:T(1,128)S(1)}, u32[]{:S(2)}, u32[]{:S(2)}) %all-to-all-start) | async-done | bytes 32800 | tf_op jit(solution)/shard_map/all_to_all | solution.py:17
  27.8 11.9 %gather_fusion = bf16[2048,512]{1,0:T(8,128)(2,1)} fusion(bf16[4096,512]{1,0:T(8,128)(2,1)} %param.6, s32[2048]{0:T(1024)S(1)} %broadcast_clamp_fusion), kind=kCustom, calls=%fused_computation | custom fusion | bytes 4202496 | tf_op jit(solution)/shard_map/gather | solution.py:171
  39.7 4.9 %all-to-all-start.1 = ((bf16[64,32,512]{2,1,0:T(8,128)(2,1)}), bf16[64,32,512]{2,1,0:T(8,128)(2,1)S(1)}, u32[]{:S(2)}, u32[]{:S(2)}) async-start(bf16[64,32,512]{2,1,0:T(8,128)(2,1)} %bitcast.8), calls=%async_computation.1 | async-start | bytes 4194304 | tf_op jit(solution)/shard_map/all_to_all | solution.py:17
  44.7 0.8 constant_dynamic-update-slice_fusion.1
  45.5 0.7 constant_dynamic-update-slice_fusion
  46.3 1.3 collective-permute-start.4
  47.6 1.4 collective-permute-start.2
  49.0 1.6 collective-permute-start
  50.6 1.8 convolution_bitcast_fusion
  52.7 1.4 convolution_bitcast_fusion.1
  54.4 1.4 select_convert_fusion.spread_ref
  55.8 0.9 select_convert_fusion.1
  56.7 9.7 %collective-permute-done.4 = bf16[512,768]{1,0:T(8,128)(2,1)} collective-permute-done((bf16[512,768]{1,0:T(8,128)(2,1)}, bf16[512,768]{1,0:T(8,128)(2,1)}, u32[]{:S(2)}, u32[]{:S(2)}) %collective-permute-start.4) | collective-permute-done | bytes 786464 | tf_op jit(solution)/shard_map/ppermute | solution.py:136
  66.4 1.0 slice.49.refs_8_
  67.4 1.0 slice.48.refs_7_
  68.4 16.0 %collective-permute-done = bf16[512,768]{1,0:T(8,128)(2,1)} collective-permute-done((bf16[512,768]{1,0:T(8,128)(2,1)}, bf16[512,768]{1,0:T(8,128)(2,1)}, u32[]{:S(2)}, u32[]{:S(2)}) %collective-permute-start) | collective-permute-done | bytes 786464 | tf_op jit(solution)/shard_map/ppermute | solution.py:136
  84.4 1.0 slice.47.refs_6_
  85.4 9.0 %all-to-all-done.1 = bf16[64,32,512]{2,1,0:T(8,128)(2,1)S(1)} async-done(((bf16[64,32,512]{2,1,0:T(8,128)(2,1)}), bf16[64,32,512]{2,1,0:T(8,128)(2,1)S(1)}, u32[]{:S(2)}, u32[]{:S(2)}) %all-to-all-start.1) | async-done | bytes 2097184 | tf_op jit(solution)/shard_map/all_to_all | solution.py:17
  94.4 1.4 copy-done.8
  95.8 1.4 fusion.45
  97.2 3.0 %maximum_convert_fusion.1.active_ref = bf16[2048,512]{1,0:T(8,128)(2,1)S(1)} fusion(bf16[2048,512]{1,0:T(8,128)(2,1)} %bitcast.51, bf16[512,768]{1,0:T(8,128)(2,1)} %collective-permute-done.4), kind=kOutput, calls=%fused_computation.2 | convolution fusion | flops 1075838976 | bytes 4718592 | tf_op jit(solution)/shard_map/dot_general | solution.py:13
  100.2 1.1 convolution_convert_fusion
  101.3 2.7 %collective-permute-start.5 = (bf16[128,512]{1,0:T(8,128)(2,1)}, bf16[128,512]{1,0:T(8,128)(2,1)S(1)}, u32[]{:S(2)}, u32[]{:S(2)}) collective-permute-start(bf16[128,512]{1,0:T(8,128)(2,1)} %convolution_convert_fusion), channel_id=1, source_target_pairs={{0,3},{1,0},{2,1},{3,2},{4,7},{5,4},{6,5},{7,6},{8,11},{9,8},{10,9... | collective-permute-start | bytes 393224 | tf_op jit(solution)/shard_map/ppermute | solution.py:136
  104.1 2.3 %maximum_convert_fusion.2.active_ref = bf16[2048,512]{1,0:T(8,128)(2,1)S(1)} fusion(bf16[2048,512]{1,0:T(8,128)(2,1)S(1)} %bitcast.52, bf16[512,768]{1,0:T(8,128)(2,1)} %collective-permute-done.2), kind=kOutput, calls=%fused_computation.3 | convolution fusion | flops 1075838976 | bytes 4718592 | tf_op jit(solution)/shard_map/dot_general | solution.py:13
  106.4 1.4 convolution_convert_fusion.1
  107.8 2.3 %maximum_convert_fusion.3.active_ref = bf16[2048,512]{1,0:T(8,128)(2,1)S(1)} fusion(bf16[2048,512]{1,0:T(8,128)(2,1)S(1)} %bitcast.53, bf16[512,768]{1,0:T(8,128)(2,1)} %collective-permute-done), kind=kOutput, calls=%fused_computation.4 | convolution fusion | flops 1075838976 | bytes 4718592 | tf_op jit(solution)/shard_map/dot_general | solution.py:13
  110.1 1.1 convolution_convert_fusion.2
  111.2 2.4 %collective-permute-start.1 = (bf16[128,512]{1,0:T(8,128)(2,1)}, bf16[128,512]{1,0:T(8,128)(2,1)}, u32[]{:S(2)}, u32[]{:S(2)}) collective-permute-start(bf16[128,512]{1,0:T(8,128)(2,1)} %convolution_convert_fusion.2), channel_id=1, source_target_pairs={{0,2},{1,3},{2,0},{3,1},{4,6},{5,7},{6,4},{7,5},{8,10},{9,11},{10,... | collective-permute-start | bytes 393224 | tf_op jit(solution)/shard_map/ppermute | solution.py:136
  113.6 2.3 %copy.29 = bf16[2048,256]{0,1:T(8,128)(2,1)} copy(bf16[2048,256]{1,0:T(8,128)(2,1)} %get-tuple-element.36) | data formatting | bytes 2097152
  116.0 2.3 %copy.30 = bf16[2048,256]{0,1:T(8,128)(2,1)} copy(bf16[2048,256]{1,0:T(8,128)(2,1)} %get-tuple-element.37) | data formatting | bytes 2097152
  118.2 1.8 broadcast_select_fusion.1
  120.1 0.4 copy-done.10
  120.5 1.2 maximum_convert_fusion.active_ref
  121.8 1.4 add_convert_fusion.5.refs_5_
  123.4 1.1 collective-permute-start.8
  124.5 0.4 collective-permute-start.7
  124.9 1.1 collective-permute-start.6
  126.1 0.2 maximum_bitcast_fusion.rows_ref
  126.3 1.0 collective-permute-done.8.refs_3_
  127.3 3.7 %collective-permute-done.7.refs_2_ = f32[128,256]{1,0:T(8,128)S(1)} collective-permute-done((f32[128,256]{1,0:T(8,128)S(1)}, f32[128,256]{1,0:T(8,128)S(1)}, u32[]{:S(2)}, u32[]{:S(2)}) %collective-permute-start.7) | collective-permute-done | bytes 131104 | tf_op jit(solution)/shard_map/ppermute | solution.py:136
  131.0 0.6 shard_map.77
  131.5 4.3 %collective-permute-start.16 = (bf16[256,256]{1,0:T(8,128)(2,1)S(1)}, bf16[256,256]{1,0:T(8,128)(2,1)S(1)}, u32[]{:S(2)}, u32[]{:S(2)}) collective-permute-start(bf16[256,256]{1,0:T(8,128)(2,1)S(1)} %get-tuple-element.33), channel_id=1, source_target_pairs={{0,4},{4,0},{8,12},{12,8},{16,20},{20,16},{24,28},{28,24},{1,5},{5... | collective-permute-start | bytes 393224 | tf_op jit(solution)/shard_map/ppermute | solution.py:200
  135.8 3.1 %shard_map.80 = (f32[256,512]{1,0:T(8,128)S(1)}, bf16[256,512]{1,0:T(8,128)(2,1)S(1)}) custom-call(bf16[2048,128]{1,0:T(8,128)(2,1)S(1)} %copy-done.5, bf16[128,512]{1,0:T(8,128)(2,1)S(1)} %get-tuple-element.26.d_hidden_ref, bf16[2048,512]{1,0:T(8,128)(2,1)S(1)} %copy-done.2, bf16[512,2048]{1,0:T(8,128)(2,1)S(1)} %maximum_bitcast_fusion.rows_ref), custom_call_target="tpu_custom_call" | custom-call | flops 1610612736 | bytes 4718592 | tf_op jit(solution)/shard_map/pallas_call | solution.py:96
  139.0 3.1 %shard_map.79 = (f32[256,512]{1,0:T(8,128)S(1)}, bf16[256,512]{1,0:T(8,128)(2,1)S(1)}) custom-call(bf16[2048,128]{1,0:T(8,128)(2,1)S(1)} %copy-done.5, bf16[128,512]{1,0:T(8,128)(2,1)S(1)} %get-tuple-element.23.d_hidden_ref, bf16[2048,512]{1,0:T(8,128)(2,1)S(1)} %copy-done.4, bf16[512,2048]{1,0:T(8,128)(2,1)S(1)} %maximum_bitcast_fusion.rows_ref), custom_call_target="tpu_custom_call" | custom-call | flops 1610612736 | bytes 4718592 | tf_op jit(solution)/shard_map/pallas_call | solution.py:96
  142.2 0.5 collective-permute-start.11
  142.7 3.1 %shard_map.81 = (f32[256,512]{1,0:T(8,128)S(1)}, bf16[256,512]{1,0:T(8,128)(2,1)S(1)}) custom-call(bf16[2048,128]{1,0:T(8,128)(2,1)S(1)} %copy-done.5, bf16[128,512]{1,0:T(8,128)(2,1)S(1)} %get-tuple-element.29.d_hidden_ref, bf16[2048,512]{1,0:T(8,128)(2,1)S(1)} %maximum_convert_fusion.active_ref, bf16[512,2048]{1,0:T(8,128)(2,1)S(1)} %maximum_bitcast_fusion.rows_ref), custom_call_target="tpu_custom_call" | custom-call | flops 1610612736 | bytes 4718592 | tf_op jit(solution)/shard_map/pallas_call | solution.py:96
  145.8 3.1 %shard_map.78 = (f32[256,512]{1,0:T(8,128)S(1)}, bf16[256,512]{1,0:T(8,128)(2,1)S(1)}) custom-call(bf16[2048,128]{1,0:T(8,128)(2,1)S(1)} %copy-done.5, bf16[128,512]{1,0:T(8,128)(2,1)S(1)} %get-tuple-element.20.d_hidden_ref, bf16[2048,512]{1,0:T(8,128)(2,1)S(1)} %maximum_convert_fusion.3.active_ref, bf16[512,2048]{1,0:T(8,128)(2,1)S(1)} %maximum_bitcast_fusion.rows_ref), custom_call_target="tpu_custom_call" | custom-call | flops 1610612736 | bytes 4718592 | tf_op jit(solution)/shard_map/pallas_call | solution.py:96
  148.9 0.2 collective-permute-start.15
  149.1 0.4 collective-permute-start.9
  149.6 2.0 collective-permute-start.14
  151.8 1.3 collective-permute-start.10
  153.1 4.4 %collective-permute-done.14 = bf16[256,512]{1,0:T(8,128)(2,1)S(1)} collective-permute-done((bf16[256,512]{1,0:T(8,128)(2,1)S(1)}, bf16[256,512]{1,0:T(8,128)(2,1)S(1)}, u32[]{:S(2)}, u32[]{:S(2)}) %collective-permute-start.14) | collective-permute-done | bytes 262176 | tf_op jit(solution)/shard_map/ppermute | solution.py:136
  157.6 8.5 %collective-permute-done.12 = bf16[256,512]{1,0:T(8,128)(2,1)S(1)} collective-permute-done((bf16[256,512]{1,0:T(8,128)(2,1)S(1)}, bf16[256,512]{1,0:T(8,128)(2,1)S(1)}, u32[]{:S(2)}, u32[]{:S(2)}) %collective-permute-start.12) | collective-permute-done | bytes 262176 | tf_op jit(solution)/shard_map/ppermute | solution.py:136
  166.3 17.4 %all_to_all.24 = bf16[32,8,768]{2,1,0:T(8,128)(2,1)S(1)} all-to-all(bf16[32,8,768]{2,1,0:T(8,128)(2,1)S(1)} %pad_maximum_fusion), channel_id=1, replica_groups={{0,8,16,24,32,40,48,56,64,72,80,88,96,104,112,120,128,136,144,152,160,1..., dimensions={0} | all-to-all | bytes 786432 | tf_op jit(solution)/shard_map/all_to_all | solution.py:17
  183.8 17.9 %all_to_all.25 = bf16[32,8,768]{2,1,0:T(8,128)(2,1)S(1)} all-to-all(bf16[32,8,768]{2,1,0:T(8,128)(2,1)S(1)} %broadcast_in_dim.88), channel_id=1, replica_groups={{0,8,16,24,32,40,48,56,64,72,80,88,96,104,112,120,128,136,144,152,160,1..., dimensions={0} | all-to-all | bytes 786432 | tf_op jit(solution)/shard_map/all_to_all | solution.py:17
  201.7 3.5 %collective-permute-start.17 = (bf16[256,768]{1,0:T(8,128)(2,1)S(1)}, bf16[256,768]{1,0:T(8,128)(2,1)S(1)}, u32[]{:S(2)}, u32[]{:S(2)}) collective-permute-start(bf16[256,768]{1,0:T(8,128)(2,1)S(1)} %bitcast.55), channel_id=1, source_target_pairs={{0,4},{4,0},{8,12},{12,8},{16,20},{20,16},{24,28},{28,24},{1,5},{5... | collective-permute-start | bytes 1179656 | tf_op jit(solution)/shard_map/ppermute | solution.py:200
  205.2 1.3 collective-permute-done.17
  206.6 0.8 maximum_convert_fusion.5
  207.6 1.1 slice.52
  (69 shorter events, 2.4 us)
Async XLA Ops:
  5.3 22.3 %all-to-all-start = ((s32[64,1,128]{2,1,0:T(1,128)}), s32[64,1,128]{2,1,0:T(1,128)S(1)}, u32[]{:S(2)}, u32[]{:S(2)}) async-start(s32[64,1,128]{2,1,0:T(1,128)} %bitcast.6), calls=%async_computation | async-start | bytes 65536 | tf_op jit(solution)/shard_map/all_to_all | solution.py:17
  39.7 5.0 %copy-start.11 = (bf16[512,512]{1,0:T(8,128)(2,1)S(1)}, bf16[512,512]{1,0:T(8,128)(2,1)}, u32[]{:S(2)}) copy-start(bf16[512,512]{1,0:T(8,128)(2,1)} %param.10) | copy-start | bytes 1572868
  39.7 5.8 %copy-start = (bf16[512,256]{1,0:T(8,128)(2,1)S(1)}, bf16[512,256]{1,0:T(8,128)(2,1)}, u32[]{:S(2)}) copy-start(bf16[512,256]{1,0:T(8,128)(2,1)} %refs_9_.1) | copy-start | bytes 786436
  39.7 10.9 %copy-start.14 = (bf16[128,32]{0,1:T(8,128)(2,1)S(1)}, bf16[128,32]{0,1:T(8,128)(2,1)}, u32[]{:S(2)}) copy-start(bf16[128,32]{0,1:T(8,128)(2,1)} %param.8) | copy-start | bytes 24580
  39.7 54.7 %all-to-all-start.1 = ((bf16[64,32,512]{2,1,0:T(8,128)(2,1)}), bf16[64,32,512]{2,1,0:T(8,128)(2,1)S(1)}, u32[]{:S(2)}, u32[]{:S(2)}) async-start(bf16[64,32,512]{2,1,0:T(8,128)(2,1)} %bitcast.8), calls=%async_computation.1 | async-start | bytes 4194304 | tf_op jit(solution)/shard_map/all_to_all | solution.py:17
  46.3 20.2 %collective-permute-start.4 = (bf16[512,768]{1,0:T(8,128)(2,1)}, bf16[512,768]{1,0:T(8,128)(2,1)}, u32[]{:S(2)}, u32[]{:S(2)}) collective-permute-start(bf16[512,768]{1,0:T(8,128)(2,1)} %constant_dynamic-update-slice_fusion), channel_id=1, source_target_pairs={{0,1},{1,2},{2,3},{3,0},{4,5},{5,6},{6,7},{7,4},{8,9},{9,10},{10,1... | collective-permute-start | bytes 2359304 | tf_op jit(solution)/shard_map/ppermute | solution.py:136
  47.6 19.9 %collective-permute-start.2 = (bf16[512,768]{1,0:T(8,128)(2,1)}, bf16[512,768]{1,0:T(8,128)(2,1)}, u32[]{:S(2)}, u32[]{:S(2)}) collective-permute-start(bf16[512,768]{1,0:T(8,128)(2,1)} %constant_dynamic-update-slice_fusion), channel_id=1, source_target_pairs={{0,3},{1,0},{2,1},{3,2},{4,7},{5,4},{6,5},{7,6},{8,11},{9,8},{10,9... | collective-permute-start | bytes 2359304 | tf_op jit(solution)/shard_map/ppermute | solution.py:136
  49.0 35.4 %collective-permute-start = (bf16[512,768]{1,0:T(8,128)(2,1)}, bf16[512,768]{1,0:T(8,128)(2,1)}, u32[]{:S(2)}, u32[]{:S(2)}) collective-permute-start(bf16[512,768]{1,0:T(8,128)(2,1)} %constant_dynamic-update-slice_fusion), channel_id=1, source_target_pairs={{0,2},{1,3},{2,0},{3,1},{4,6},{5,7},{6,4},{7,5},{8,10},{9,11},{10,... | collective-permute-start | bytes 2359304 | tf_op jit(solution)/shard_map/ppermute | solution.py:136
  50.6 3.6 %copy-start.13 = (s32[128]{0:T(128)S(1)}, s32[128]{0:T(128)}, u32[]{:S(2)}) copy-start(s32[128]{0:T(128)} %param.9) | copy-start | bytes 1540
  94.4 1.4 copy-start.8
  97.2 3.0 %copy-start.6 = (bf16[128,2048]{1,0:T(8,128)(2,1)S(1)}, bf16[128,2048]{1,0:T(8,128)(2,1)}, u32[]{:S(2)}) copy-start(bf16[128,2048]{1,0:T(8,128)(2,1)} %select_convert_fusion.1) | copy-start | bytes 1572868
  100.2 6.2 %copy-start.1 = (bf16[2048,512]{1,0:T(8,128)(2,1)}, bf16[2048,512]{1,0:T(8,128)(2,1)S(1)}, u32[]{:S(2)}) copy-start(bf16[2048,512]{1,0:T(8,128)(2,1)S(1)} %maximum_convert_fusion.1.active_ref) | copy-start | bytes 6291460
  100.2 3.9 %copy-start.9 = (bf16[64,32,512]{2,1,0:T(8,128)(2,1)S(1)}, bf16[64,32,512]{2,1,0:T(8,128)(2,1)}, u32[]{:S(2)}) copy-start(bf16[64,32,512]{2,1,0:T(8,128)(2,1)} %copy-done.8) | copy-start | bytes 6291460
  101.3 20.4 %collective-permute-start.5 = (bf16[128,512]{1,0:T(8,128)(2,1)}, bf16[128,512]{1,0:T(8,128)(2,1)S(1)}, u32[]{:S(2)}, u32[]{:S(2)}) collective-permute-start(bf16[128,512]{1,0:T(8,128)(2,1)} %convolution_convert_fusion), channel_id=1, source_target_pairs={{0,3},{1,0},{2,1},{3,2},{4,7},{5,4},{6,5},{7,6},{8,11},{9,8},{10,9... | collective-permute-start | bytes 393224 | tf_op jit(solution)/shard_map/ppermute | solution.py:136
  106.4 3.7 %copy-start.3 = (bf16[2048,512]{1,0:T(8,128)(2,1)}, bf16[2048,512]{1,0:T(8,128)(2,1)S(1)}, u32[]{:S(2)}) copy-start(bf16[2048,512]{1,0:T(8,128)(2,1)S(1)} %maximum_convert_fusion.2.active_ref) | copy-start | bytes 6291460
  107.8 14.0 %collective-permute-start.3 = (bf16[128,512]{1,0:T(8,128)(2,1)}, bf16[128,512]{1,0:T(8,128)(2,1)S(1)}, u32[]{:S(2)}, u32[]{:S(2)}) collective-permute-start(bf16[128,512]{1,0:T(8,128)(2,1)} %convolution_convert_fusion.1), channel_id=1, source_target_pairs={{0,1},{1,2},{2,3},{3,0},{4,5},{5,6},{6,7},{7,4},{8,9},{9,10},{10,1... | collective-permute-start | bytes 393224 | tf_op jit(solution)/shard_map/ppermute | solution.py:136
  111.2 10.6 %collective-permute-start.1 = (bf16[128,512]{1,0:T(8,128)(2,1)}, bf16[128,512]{1,0:T(8,128)(2,1)}, u32[]{:S(2)}, u32[]{:S(2)}) collective-permute-start(bf16[128,512]{1,0:T(8,128)(2,1)} %convolution_convert_fusion.2), channel_id=1, source_target_pairs={{0,2},{1,3},{2,0},{3,1},{4,6},{5,7},{6,4},{7,5},{8,10},{9,11},{10,... | collective-permute-start | bytes 393224 | tf_op jit(solution)/shard_map/ppermute | solution.py:136
  118.2 2.2 %copy-start.10 = (bf16[64,32,512]{2,1,0:T(8,128)(2,1)S(1)}, bf16[64,32,512]{2,1,0:T(8,128)(2,1)}, u32[]{:S(2)}) copy-start(bf16[64,32,512]{2,1,0:T(8,128)(2,1)} %copy-done.8) | copy-start | bytes 6291460
  118.2 2.3 %copy-start.12 = (bf16[512,512]{1,0:T(8,128)(2,1)S(1)}, bf16[512,512]{1,0:T(8,128)(2,1)}, u32[]{:S(2)}) copy-start(bf16[512,512]{1,0:T(8,128)(2,1)} %param.10) | copy-start | bytes 1572868
  120.5 1.3 copy-start.7
  123.4 3.9 %collective-permute-start.8 = (f32[128,256]{1,0:T(8,128)S(1)}, f32[128,256]{1,0:T(8,128)S(1)}, u32[]{:S(2)}, u32[]{:S(2)}) collective-permute-start(f32[128,256]{1,0:T(8,128)S(1)} %fusion.46.refs_0_), channel_id=1, source_target_pairs={{0,3},{1,0},{2,1},{3,2},{4,7},{5,4},{6,5},{7,6},{8,11},{9,8},{10,9... | collective-permute-start | bytes 393224 | tf_op jit(solution)/shard_map/ppermute | solution.py:136
  124.5 6.4 %collective-permute-start.7 = (f32[128,256]{1,0:T(8,128)S(1)}, f32[128,256]{1,0:T(8,128)S(1)}, u32[]{:S(2)}, u32[]{:S(2)}) collective-permute-start(f32[128,256]{1,0:T(8,128)S(1)} %fusion.46.refs_0_), channel_id=1, source_target_pairs={{0,1},{1,2},{2,3},{3,0},{4,5},{5,6},{6,7},{7,4},{8,9},{9,10},{10,1... | collective-permute-start | bytes 393224 | tf_op jit(solution)/shard_map/ppermute | solution.py:136
  124.9 6.0 %collective-permute-start.6 = (f32[128,256]{1,0:T(8,128)S(1)}, f32[128,256]{1,0:T(8,128)S(1)}, u32[]{:S(2)}, u32[]{:S(2)}) collective-permute-start(f32[128,256]{1,0:T(8,128)S(1)} %fusion.46.refs_0_), channel_id=1, source_target_pairs={{0,2},{1,3},{2,0},{3,1},{4,6},{5,7},{6,4},{7,5},{8,10},{9,11},{10,... | collective-permute-start | bytes 393224 | tf_op jit(solution)/shard_map/ppermute | solution.py:136
  126.0 9.8 %copy-start.2 = (bf16[2048,512]{1,0:T(8,128)(2,1)S(1)}, bf16[2048,512]{1,0:T(8,128)(2,1)}, u32[]{:S(2)}) copy-start(bf16[2048,512]{1,0:T(8,128)(2,1)} %copy-done.1) | copy-start | bytes 6291460
  126.1 9.8 %copy-start.5 = (bf16[2048,128]{1,0:T(8,128)(2,1)S(1)}, bf16[2048,128]{1,0:T(8,128)(2,1)}, u32[]{:S(2)}) copy-start(bf16[2048,128]{1,0:T(8,128)(2,1)} %select_convert_fusion.spread_ref) | copy-start | bytes 1572868
  131.5 21.6 %collective-permute-start.16 = (bf16[256,256]{1,0:T(8,128)(2,1)S(1)}, bf16[256,256]{1,0:T(8,128)(2,1)S(1)}, u32[]{:S(2)}, u32[]{:S(2)}) collective-permute-start(bf16[256,256]{1,0:T(8,128)(2,1)S(1)} %get-tuple-element.33), channel_id=1, source_target_pairs={{0,4},{4,0},{8,12},{12,8},{16,20},{20,16},{24,28},{28,24},{1,5},{5... | collective-permute-start | bytes 393224 | tf_op jit(solution)/shard_map/ppermute | solution.py:200
  135.8 3.1 %copy-start.4 = (bf16[2048,512]{1,0:T(8,128)(2,1)S(1)}, bf16[2048,512]{1,0:T(8,128)(2,1)}, u32[]{:S(2)}) copy-start(bf16[2048,512]{1,0:T(8,128)(2,1)} %copy-done.3) | copy-start | bytes 6291460
  142.1 7.4 %collective-permute-start.13 = (bf16[256,512]{1,0:T(8,128)(2,1)S(1)}, bf16[256,512]{1,0:T(8,128)(2,1)S(1)}, u32[]{:S(2)}, u32[]{:S(2)}) collective-permute-start(bf16[256,512]{1,0:T(8,128)(2,1)S(1)} %get-tuple-element.28), channel_id=1, source_target_pairs={{0,4},{4,0},{8,12},{12,8},{16,20},{20,16},{24,28},{28,24},{1,5},{5... | collective-permute-start | bytes 786440 | tf_op jit(solution)/shard_map/ppermute | solution.py:200
  142.2 9.3 %collective-permute-start.11 = (bf16[256,512]{1,0:T(8,128)(2,1)S(1)}, bf16[256,512]{1,0:T(8,128)(2,1)S(1)}, u32[]{:S(2)}, u32[]{:S(2)}) collective-permute-start(bf16[256,512]{1,0:T(8,128)(2,1)S(1)} %get-tuple-element.25), channel_id=1, source_target_pairs={{0,4},{4,0},{8,12},{12,8},{16,20},{20,16},{24,28},{28,24},{1,5},{5... | collective-permute-start | bytes 786440 | tf_op jit(solution)/shard_map/ppermute | solution.py:200
  148.9 4.2 %collective-permute-start.15 = (bf16[256,512]{1,0:T(8,128)(2,1)S(1)}, bf16[256,512]{1,0:T(8,128)(2,1)S(1)}, u32[]{:S(2)}, u32[]{:S(2)}) collective-permute-start(bf16[256,512]{1,0:T(8,128)(2,1)S(1)} %get-tuple-element.31), channel_id=1, source_target_pairs={{0,4},{4,0},{8,12},{12,8},{16,20},{20,16},{24,28},{28,24},{1,5},{5... | collective-permute-start | bytes 786440 | tf_op jit(solution)/shard_map/ppermute | solution.py:200
  149.1 2.6 %collective-permute-start.9 = (bf16[256,512]{1,0:T(8,128)(2,1)S(1)}, bf16[256,512]{1,0:T(8,128)(2,1)S(1)}, u32[]{:S(2)}, u32[]{:S(2)}) collective-permute-start(bf16[256,512]{1,0:T(8,128)(2,1)S(1)} %get-tuple-element.22), channel_id=1, source_target_pairs={{0,4},{4,0},{8,12},{12,8},{16,20},{20,16},{24,28},{28,24},{1,5},{5... | collective-permute-start | bytes 786440 | tf_op jit(solution)/shard_map/ppermute | solution.py:200
  149.6 7.9 %collective-permute-start.14 = (bf16[256,512]{1,0:T(8,128)(2,1)S(1)}, bf16[256,512]{1,0:T(8,128)(2,1)S(1)}, u32[]{:S(2)}, u32[]{:S(2)}) collective-permute-start(bf16[256,512]{1,0:T(8,128)(2,1)S(1)} %add_convert_fusion.1), channel_id=1, source_target_pairs={{0,3},{1,0},{2,1},{3,2},{4,7},{5,4},{6,5},{7,6},{8,11},{9,8},{10,9... | collective-permute-start | bytes 786440 | tf_op jit(solution)/shard_map/ppermute | solution.py:136
  151.6 14.4 %collective-permute-start.12 = (bf16[256,512]{1,0:T(8,128)(2,1)S(1)}, bf16[256,512]{1,0:T(8,128)(2,1)S(1)}, u32[]{:S(2)}, u32[]{:S(2)}) collective-permute-start(bf16[256,512]{1,0:T(8,128)(2,1)S(1)} %add_convert_fusion.2), channel_id=1, source_target_pairs={{0,1},{1,2},{2,3},{3,0},{4,5},{5,6},{6,7},{7,4},{8,9},{9,10},{10,1... | collective-permute-start | bytes 786440 | tf_op jit(solution)/shard_map/ppermute | solution.py:136
  151.8 14.3 %collective-permute-start.10 = (bf16[256,512]{1,0:T(8,128)(2,1)S(1)}, bf16[256,512]{1,0:T(8,128)(2,1)S(1)}, u32[]{:S(2)}, u32[]{:S(2)}) collective-permute-start(bf16[256,512]{1,0:T(8,128)(2,1)S(1)} %add_convert_fusion.3), channel_id=1, source_target_pairs={{0,2},{1,3},{2,0},{3,1},{4,6},{5,7},{6,4},{7,5},{8,10},{9,11},{10,... | collective-permute-start | bytes 786440 | tf_op jit(solution)/shard_map/ppermute | solution.py:136
  201.7 4.9 %collective-permute-start.17 = (bf16[256,768]{1,0:T(8,128)(2,1)S(1)}, bf16[256,768]{1,0:T(8,128)(2,1)S(1)}, u32[]{:S(2)}, u32[]{:S(2)}) collective-permute-start(bf16[256,768]{1,0:T(8,128)(2,1)S(1)} %bitcast.55), channel_id=1, source_target_pairs={{0,4},{4,0},{8,12},{12,8},{16,20},{20,16},{24,28},{28,24},{1,5},{5... | collective-permute-start | bytes 1179656 | tf_op jit(solution)/shard_map/ppermute | solution.py:200

commit v4 on v3

--- a/solution.py
+++ b/solution.py
@@ -19,7 +19,7 @@
     )
 
 
-def middle(parts, labels, hidden, w_twos, core):
+def middle(parts, labels, hidden, w_boths, core):
     count = len(parts)
     targets, classes = parts[0].shape
     units = hidden.shape[1]
@@ -40,7 +40,7 @@
         onehot = (labels_ref[...] == ids).astype(F32)
         d_logits = (probability - onehot).astype(BF)
         for w_ref, out in zip(w_refs, d_hidden_refs):
-            out[...] = dot(d_logits, w_ref[...], 1, 1).astype(BF)
+            out[...] = dot(d_logits, w_ref[:, units:], 1, 1).astype(BF)
         both = dot(hidden_ref[...], d_logits, 0, 0)
         swap = core_ref[0] != 0
         low, high = both[:half], both[half:]
@@ -63,7 +63,52 @@
             bytes_accessed=4 * 2**20,
             transcendentals=targets * classes,
         ),
-    )(core, *parts, labels, hidden, *w_twos)
+    )(core, *parts, labels, hidden, *w_boths)
+
+
+VMEM = pl.BlockSpec(memory_space=pltpu.VMEM)
+SMEM = pl.BlockSpec(memory_space=pltpu.SMEM)
+
+
+def forward(rows, w_both, spread, core, out_type, turn):
+    slots, width_f = rows.shape
+    targets = spread.shape[0]
+    units = width_f
+    half = width_f // 2
+    block = 512
+
+    def kernel(core_ref, rows_ref, w_ref, spread_ref, active_ref, hidden_ref, *turned):
+        mine = pl.multiple_of(core_ref[0] * half, half)
+        other = pl.multiple_of((1 - core_ref[0]) * half, half)
+
+        @pl.loop(0, slots // block)
+        def _(i):
+            at = pl.ds(pl.multiple_of(i * block, block), block)
+            value = rows_ref[at, :]
+            active_ref[at, :] = jnp.maximum(dot(value, w_ref[:, :units]), 0.0).astype(BF)
+            for ref in turned:
+                flat = value.T
+                ref[pl.ds(mine, half), at] = flat[:half]
+                ref[pl.ds(other, half), at] = flat[half:]
+
+        hidden_ref[...] = dot(spread_ref[...], active_ref[...]).astype(out_type)
+
+    shapes = [
+        jax.ShapeDtypeStruct((slots, units), BF),
+        jax.ShapeDtypeStruct((targets, units), out_type),
+    ] + [jax.ShapeDtypeStruct((width_f, slots), BF)] * turn
+    return pl.pallas_call(
+        kernel,
+        out_shape=shapes,
+        in_specs=[SMEM] + [VMEM] * 3,
+        out_specs=[VMEM] * len(shapes),
+        compiler_params=pltpu.CompilerParams(vmem_limit_bytes=24 * 2**20),
+        cost_estimate=pl.CostEstimate(
+            flops=2 * slots * units * (width_f + targets),
+            bytes_accessed=2 * slots * (width_f + units + targets),
+            transcendentals=0,
+        ),
+    )(core, rows, w_both, spread)
 
 
 def backward(spread_t, d_hidden, active, rows_t):
@@ -71,27 +116,17 @@
     units = d_hidden.shape[1]
     width_f = rows_t.shape[0]
     half = width_f // 2
-    block = 512
-    steps = slots // block
-
-    def kernel(spread_ref, d_hidden_ref, active_ref, rows_ref, own_ref, other_ref, total):
-        step = pl.program_id(0)
-        scattered = dot(spread_ref[...], d_hidden_ref[...]).astype(BF)
-        d_pre = jnp.where(active_ref[...] > 0, scattered, jnp.zeros_like(scattered))
-        term = dot(rows_ref[...], d_pre)
-
-        @pl.when(step == 0)
-        def _():
-            total[...] = term
-
-        @pl.when(step > 0)
-        def _():
-            total[...] += term
-
-        @pl.when(step == steps - 1)
-        def _():
-            own_ref[...] = total[:half]
-            other_ref[...] = total[half:].astype(BF)
+    block = 256
+
+    def kernel(spread_ref, d_hidden_ref, active_ref, rows_ref, own_ref, other_ref):
+        @pl.loop(0, units // block)
+        def _(i):
+            at = pl.ds(pl.multiple_of(i * block, block), block)
+            scattered = dot(spread_ref[...], d_hidden_ref[:, at]).astype(BF)
+            d_pre = jnp.where(active_ref[:, at] > 0, scattered, jnp.zeros_like(scattered))
+            total = dot(rows_ref[...], d_pre)
+            own_ref[:, at] = total[:half]
+            other_ref[:, at] = total[half:].astype(BF)
 
     return pl.pallas_call(
         kernel,
@@ -99,22 +134,12 @@
             jax.ShapeDtypeStruct((half, units), F32),
             jax.ShapeDtypeStruct((half, units), BF),
         ],
-        grid=(steps,),
-        in_specs=[
-            pl.BlockSpec((block, targets), lambda i: (i, 0)),
-            pl.BlockSpec((targets, units), lambda i: (0, 0)),
-            pl.BlockSpec((block, units), lambda i: (i, 0)),
-            pl.BlockSpec((width_f, block), lambda i: (0, i)),
-        ],
-        out_specs=[
-            pl.BlockSpec((half, units), lambda i: (0, 0)),
-            pl.BlockSpec((half, units), lambda i: (0, 0)),
-        ],
-        scratch_shapes=[pltpu.VMEM((width_f, units), F32)],
+        in_specs=[VMEM] * 4,
+        out_specs=[VMEM] * 2,
         compiler_params=pltpu.CompilerParams(vmem_limit_bytes=24 * 2**20),
         cost_estimate=pl.CostEstimate(
-            flops=2 * slots * units * (width_f + 2 * targets),
-            bytes_accessed=2 * slots * (width_f + units + targets),
+            flops=2 * units,
+            bytes_accessed=2 * units,
             transcendentals=0,
         ),
     )(spread_t, d_hidden, active, rows_t)
@@ -137,10 +162,9 @@
 
     steps = (2, 1, 3, 0)
     w_both = jnp.concatenate([w_one, w_two], axis=1)
-    w_ones, w_twos = {0: w_one}, {0: w_two}
+    w_boths = {0: w_both}
     for step in steps[:-1]:
-        w_got = to_mlp(w_both, -step)
-        w_ones[step], w_twos[step] = w_got[:, :units], w_got[:, units:]
+        w_boths[step] = to_mlp(w_both, -step)
 
     owner_range = jnp.arange(owners, dtype=jnp.int32)
     owner_ids = nbr_page // rows_dev
@@ -178,18 +202,17 @@
     ).astype(BF)
     spread, spread_t = lax.optimization_barrier((spread, spread.T))
 
+    core_id = core.reshape(1)
     active, hidden = {}, 0.0
     for step in steps:
-        active[step] = lax.optimization_barrier(
-            jnp.maximum(dot(received, w_ones[step]), 0.0).astype(BF)
+        out = F32 if step == 0 else BF
+        active[step], part, *turned = forward(
+            received, w_boths[step], spread, core_id, out, step == 0
         )
-        part = dot(spread, active[step])
-        hidden += to_mlp(part.astype(BF), step).astype(F32) if step else part
+        hidden += to_mlp(part, step).astype(F32) if step else part
     hidden = hidden.astype(BF)
     half = width_f // 2
-    own_half = jnp.where(core == 0, received[:, :half], received[:, half:])
-    other_half = jnp.where(core == 0, received[:, half:], received[:, :half])
-    rows_t = jnp.concatenate([own_half, other_half], axis=1).T
+    (rows_t,) = turned
 
     part = dot(hidden, w_two)
     parts = [part] + [to_mlp(part, step) for step in steps[:-1]]
@@ -200,14 +223,21 @@
         return lax.ppermute(x, "col", pairs)
 
     mine, other, *d_hidden = middle(
-        parts, labels[:, None], hidden, [w_twos[s] for s in steps], core.reshape(1)
-    )
-    grad_two = mine + partner(other).astype(F32)
-    grad_one = 0.0
-    for step, d_slice in zip(steps, d_hidden):
+        parts, labels[:, None], hidden, [w_boths[s] for s in steps], core_id
+    )
+    own_two, other_two = mine, other
+    sums = []
+    for i, step in enumerate(steps):
+        d_slice = d_hidden[i]
+        if i >= 2:
+            d_slice, sums[i - 2] = lax.optimization_barrier((d_slice, sums[i - 2]))
         mine, other = backward(spread_t, d_slice, active[step], rows_t)
         mine += partner(other).astype(F32)
-        grad_one += to_mlp(mine.astype(BF), step).astype(F32) if step else mine
+        sums.append(mine.astype(BF) if step else mine)
+    grad_two = own_two + partner(other_two).astype(F32)
+    grad_one = sums[-1]
+    for step, value in zip(steps[:-1], sums):
+        grad_one += to_mlp(value, step).astype(F32)
     both = jnp.concatenate([grad_one, grad_two], axis=1).astype(BF)
     chips = owners // 2
     groups = [[2 * i + c for i in range(chips)] for c in (0, 1)]

time: 209 us -> 206 us (0.986)
  matrix products: 20.7 us -> 7.6 us
  Pallas kernels: 13 us -> 24.8 us
  other arithmetic: 7 us -> 4.27 us
    all_to_all x2, waiting for transfers between devices: 18.3 us -> 37.6 us  [exchange(): lax.all_to_all(x, axes, split_axis=0, concat_axis=0, tiled=True, axis_ind...]
    ppermute x12, waiting for transfers between devices: 43.4 us -> 25.4 us  [to_mlp(): lax.ppermute(x, 'mlp', [(j, (j + step) % mlp_n) for j in range(mlp_n)])]
    dot_general x15 -> x7, matrix products: 20.7 us -> 7.6 us  [dot(): lax.dot_general(a, b, (((ca,), (cb,)), ((), ())), preferred_element_type=...]
    pallas_call x0 -> x4, Pallas kernels: none -> 12.3 us  [forward(): pl.pallas_call(kernel, out_shape=shapes, in_specs=[SMEM] + [VMEM] * 3, ou...]
    slice x4 -> x0, local copies, waits for them, and re-layouts: 4.34 us -> none  [the longest x3 2.9 us: body(): w_ones[step], w_twos[step] = (w_got[:, :units], w_got[:, units:])]
    unnamed x33 -> x35, local copies, waits for them, and re-layouts: 7.31 us -> 10.4 us
    pallas_call x4, Pallas kernels: 12.5 us -> 10.1 us  [backward(): pl.pallas_call(kernel, out_shape=[jax.ShapeDtypeStruct((half, units), F32...]
  transfers between devices with their start and end apart: 20 -> 20, of which waited for: 9 -> 9; matrix products, arithmetic and copies ran while one was open for 12% -> 4% of each run, Pallas kernels for 6% -> 10%
where the time goes in v4:
time: 206 us
  waiting for transfers between devices  64.4 us (31%)
  starting transfers between devices  42.9 us (21%)
  blocking collectives  36 us (17%)
  local copies, waits for them, and re-layouts  24.8 us (12%)
  Pallas kernels  24.8 us (12%)
  matrix products  7.6 us (4%)
  other arithmetic  4.27 us (2%)
    all_to_all x2, waiting for transfers between devices, exchange(): lax.all_to_all(x, axes, split_axis=0, concat_axis=0, tiled=True, axis_ind...  37.6 us
    all_to_all x2, blocking collectives, exchange(): lax.all_to_all(x, axes, split_axis=0, concat_axis=0, tiled=True, axis_ind...  36 us
    ppermute x12, waiting for transfers between devices, to_mlp(): lax.ppermute(x, 'mlp', [(j, (j + step) % mlp_n) for j in range(mlp_n)])  25.4 us
    all_to_all x2, starting transfers between devices, exchange(): lax.all_to_all(x, axes, split_axis=0, concat_axis=0, tiled=True, axis_ind...  17.9 us
    ppermute x12, starting transfers between devices, to_mlp(): lax.ppermute(x, 'mlp', [(j, (j + step) % mlp_n) for j in range(mlp_n)])  15.8 us
    pallas_call x4, Pallas kernels, forward(): pl.pallas_call(kernel, out_shape=shapes, in_specs=[SMEM] + [VMEM] * 3, ou...  12.3 us
    gather x1, local copies, waits for them, and re-layouts, body(): fetched = features[asked]  11.9 us
    unnamed x35, local copies, waits for them, and re-layouts  10.4 us
  transfers between devices with their start and end apart: 20, of which 9 were waited for; matrix products, arithmetic and copies ran while one was open for 4% of the time, Pallas kernels for 10%

profile of v4, /device:TPU:1, one launch (start us, length us, event | category | flops | bytes accessed | tf_op | source)
XLA Modules:
  0.0 205.8 jit_solution(17473337548138449404)
XLA Ops:
  0.6 0.8 fusion.30
  1.5 0.1 fusion.29
  1.6 0.2 convolution_subtract_fusion
  1.9 0.2 select_reduce_fusion
  2.1 1.3 convolution_bitcast_fusion.2
  3.4 1.9 fusion.6
  5.3 13.0 %all-to-all-start = ((s32[64,1,128]{2,1,0:T(1,128)}), s32[64,1,128]{2,1,0:T(1,128)S(1)}, u32[]{:S(2)}, u32[]{:S(2)}) async-start(s32[64,1,128]{2,1,0:T(1,128)} %bitcast.6), calls=%async_computation | async-start | bytes 65536 | tf_op jit(solution)/shard_map/all_to_all | solution.py:17
  18.3 9.3 %all-to-all-done = s32[64,1,128]{2,1,0:T(1,128)S(1)} async-done(((s32[64,1,128]{2,1,0:T(1,128)}), s32[64,1,128]{2,1,0:T(1,128)S(1)}, u32[]{:S(2)}, u32[]{:S(2)}) %all-to-all-start) | async-done | bytes 32800 | tf_op jit(solution)/shard_map/all_to_all | solution.py:17
  27.6 0.1 constant_dynamic-slice_fusion
  27.8 11.9 %gather_fusion = bf16[2048,512]{1,0:T(8,128)(2,1)} fusion(bf16[4096,512]{1,0:T(8,128)(2,1)} %param.6, s32[2048]{0:T(1024)S(1)} %broadcast_clamp_fusion), kind=kCustom, calls=%fused_computation | custom fusion | bytes 4202496 | tf_op jit(solution)/shard_map/gather | solution.py:195
  39.7 4.9 %all-to-all-start.1 = ((bf16[64,32,512]{2,1,0:T(8,128)(2,1)}), bf16[64,32,512]{2,1,0:T(8,128)(2,1)S(1)}, u32[]{:S(2)}, u32[]{:S(2)}) async-start(bf16[64,32,512]{2,1,0:T(8,128)(2,1)} %bitcast.39), calls=%async_computation.1 | async-start | bytes 4194304 | tf_op jit(solution)/shard_map/all_to_all | solution.py:17
  44.7 1.1 constant_dynamic-update-slice_fusion.1
  45.8 3.0 %collective-permute-start = (bf16[512,768]{1,0:T(8,128)(2,1)S(1)}, bf16[512,768]{1,0:T(8,128)(2,1)}, u32[]{:S(2)}, u32[]{:S(2)}) collective-permute-start(bf16[512,768]{1,0:T(8,128)(2,1)S(1)} %constant_dynamic-update-slice_fusion.w_ref.refs_9_), channel_id=1, source_target_pairs={{0,2},{1,3},{2,0},{3,1},{4,6},{5,7},{6,4},{7,5},{8,10},{9,11},{10,... | collective-permute-start | bytes 2359304 | tf_op jit(solution)/shard_map/ppermute | solution.py:161
  48.8 0.8 collective-permute-start.2
  49.6 0.7 collective-permute-start.4
  50.3 1.4 convolution_bitcast_fusion.1
  51.8 1.8 convolution_bitcast_fusion
  53.9 0.7 select_convert_fusion.spread_ref
  54.6 0.9 select_convert_fusion.1.spread_ref
  55.5 10.6 %collective-permute-done.w_ref.refs_6_ = bf16[512,768]{1,0:T(8,128)(2,1)} collective-permute-done((bf16[512,768]{1,0:T(8,128)(2,1)S(1)}, bf16[512,768]{1,0:T(8,128)(2,1)}, u32[]{:S(2)}, u32[]{:S(2)}) %collective-permute-start) | collective-permute-done | bytes 786464 | tf_op jit(solution)/shard_map/ppermute | solution.py:161
  66.1 28.3 %all-to-all-done.1 = bf16[64,32,512]{2,1,0:T(8,128)(2,1)S(1)} async-done(((bf16[64,32,512]{2,1,0:T(8,128)(2,1)}), bf16[64,32,512]{2,1,0:T(8,128)(2,1)S(1)}, u32[]{:S(2)}, u32[]{:S(2)}) %all-to-all-start.1) | async-done | bytes 2097184 | tf_op jit(solution)/shard_map/all_to_all | solution.py:17
  94.4 1.4 copy-done.10
  95.8 3.3 %shard_map.77 = (bf16[2048,512]{1,0:T(8,128)(2,1)S(1)}, bf16[128,512]{1,0:T(8,128)(2,1)S(1)}) custom-call(s32[1]{0:T(128)} %bitcast.2.core_ref, bf16[2048,512]{1,0:T(8,128)(2,1)S(1)} %bitcast.35, bf16[512,768]{1,0:T(8,128)(2,1)} %collective-permute-done.w_ref.refs_6_, bf16[128,2048]{1,0:T(8,128)(2,1)S(1)} %copy-done.10), custom_call_target="tpu_custom_call" | custom-call | flops 1342177280 | bytes 4718592 | tf_op jit(solution)/shard_map/pallas_call | solution.py:100
  99.1 1.4 copy-done.4
  100.5 2.9 %collective-permute-start.1 = (bf16[128,512]{1,0:T(8,128)(2,1)S(1)}, bf16[128,512]{1,0:T(8,128)(2,1)S(1)}, u32[]{:S(2)}, u32[]{:S(2)}) collective-permute-start(bf16[128,512]{1,0:T(8,128)(2,1)S(1)} %get-tuple-element.33), channel_id=1, source_target_pairs={{0,2},{1,3},{2,0},{3,1},{4,6},{5,7},{6,4},{7,5},{8,10},{9,11},{10,... | collective-permute-start | bytes 393224 | tf_op jit(solution)/shard_map/ppermute | solution.py:161
  103.4 3.3 %shard_map.78 = (bf16[2048,512]{1,0:T(8,128)(2,1)S(1)}, bf16[128,512]{1,0:T(8,128)(2,1)S(1)}) custom-call(s32[1]{0:T(128)} %bitcast.2.core_ref, bf16[2048,512]{1,0:T(8,128)(2,1)S(1)} %bitcast.36, bf16[512,768]{1,0:T(8,128)(2,1)} %collective-permute-done.2.w_ref.refs_7_, bf16[128,2048]{1,0:T(8,128)(2,1)S(1)} %copy-done.10), custom_call_target="tpu_custom_call" | custom-call | flops 1342177280 | bytes 4718592 | tf_op jit(solution)/shard_map/pallas_call | solution.py:100
  106.8 1.3 copy-done.6
  108.1 0.4 collective-permute-start.3
  108.5 3.3 %shard_map.79 = (bf16[2048,512]{1,0:T(8,128)(2,1)S(1)}, bf16[128,512]{1,0:T(8,128)(2,1)S(1)}) custom-call(s32[1]{0:T(128)} %bitcast.2.core_ref, bf16[2048,512]{1,0:T(8,128)(2,1)S(1)} %bitcast.37, bf16[512,768]{1,0:T(8,128)(2,1)} %collective-permute-done.4.w_ref.refs_8_, bf16[128,2048]{1,0:T(8,128)(2,1)S(1)} %copy-done.10), custom_call_target="tpu_custom_call" | custom-call | flops 1342177280 | bytes 4718592 | tf_op jit(solution)/shard_map/pallas_call | solution.py:100
  111.9 1.3 copy-done.2
  113.2 2.3 %collective-permute-start.5 = (bf16[128,512]{1,0:T(8,128)(2,1)S(1)}, bf16[128,512]{1,0:T(8,128)(2,1)S(1)}, u32[]{:S(2)}, u32[]{:S(2)}) collective-permute-start(bf16[128,512]{1,0:T(8,128)(2,1)S(1)} %get-tuple-element.35), channel_id=1, source_target_pairs={{0,3},{1,0},{2,1},{3,2},{4,7},{5,4},{6,5},{7,6},{8,11},{9,8},{10,9... | collective-permute-start | bytes 393224 | tf_op jit(solution)/shard_map/ppermute | solution.py:161
  115.5 1.6 copy-done.9
  117.1 2.3 %shard_map.80 = (bf16[2048,512]{1,0:T(8,128)(2,1)S(1)}, f32[128,512]{1,0:T(8,128)S(1)}, bf16[512,2048]{1,0:T(8,128)(2,1)S(1)}) custom-call(s32[1]{0:T(128)} %bitcast.2.core_ref, bf16[2048,512]{1,0:T(8,128)(2,1)S(1)} %bitcast.38, bf16[512,768]{1,0:T(8,128)(2,1)S(1)} %constant_dynamic-update-slice_fusion.w_ref.refs_9_, bf16[128,2048]{1,0:T(8,128)(2,1)S(1)} %copy-done.11), custom_call_target="tpu_custom_call" | custom-call | flops 1342177280 | bytes 4718592 | tf_op jit(solution)/shard_map/pallas_call | solution.py:100
  119.4 1.4 copy-done
  120.9 0.8 fusion.42.refs_0_
  121.8 0.6 collective-permute-start.7
  122.3 2.1 %collective-permute-start.8 = (f32[128,256]{1,0:T(8,128)}, f32[128,256]{1,0:T(8,128)}, u32[]{:S(2)}, u32[]{:S(2)}) collective-permute-start(f32[128,256]{1,0:T(8,128)} %fusion.42.refs_0_), channel_id=1, source_target_pairs={{0,3},{1,0},{2,1},{3,2},{4,7},{5,4},{6,5},{7,6},{8,11},{9,8},{10,9... | collective-permute-start | bytes 393224 | tf_op jit(solution)/shard_map/ppermute | solution.py:161
  124.4 0.7 copy.21.refs_4_
  125.2 2.3 %collective-permute-done.6.refs_1_ = f32[128,256]{1,0:T(8,128)} collective-permute-done((f32[128,256]{1,0:T(8,128)}, f32[128,256]{1,0:T(8,128)}, u32[]{:S(2)}, u32[]{:S(2)}) %collective-permute-start.6) | collective-permute-done | bytes 131104 | tf_op jit(solution)/shard_map/ppermute | solution.py:161
  127.5 1.0 collective-permute-done.7.refs_2_
  128.5 0.8 copy-done.12
  129.3 2.4 %shard_map.81 = (f32[256,256]{1,0:T(8,128)S(1)}, bf16[256,256]{1,0:T(8,128)(2,1)S(1)}, bf16[128,512]{1,0:T(8,128)(2,1)S(1)}, bf16[128,512]{1,0:T(8,128)(2,1)S(1)...) custom-call(s32[1]{0:T(128)} %bitcast.2.core_ref, f32[128,256]{1,0:T(8,128)} %fusion.42.refs_0_, ...), custom_call_target="tpu_custom_call" | custom-call | flops 167772160 | bytes 4194304 | tf_op jit(solution)/shard_map/pallas_call | solution.py:51
  131.8 2.5 %shard_map.84 = (f32[256,512]{1,0:T(8,128)S(1)}, bf16[256,512]{1,0:T(8,128)(2,1)S(1)}) custom-call(bf16[2048,128]{1,0:T(8,128)(2,1)S(1)} %select_convert_fusion.spread_ref, bf16[128,512]{1,0:T(8,128)(2,1)S(1)} %get-tuple-element.48.d_hidden_ref, bf16[2048,512]{1,0:T(8,128)(2,1)S(1)} %copy-done.5, bf16[512,2048]{1,0:T(8,128)(2,1)S(1)} %get-tuple-element.40.rows_ref), custom_call_target="tpu_custom_call" | custom-call | flops 1024 | bytes 1024 | tf_op jit(solution)/shard_map/pallas_call | solution.py:131
  134.3 4.3 %collective-permute-start.11 = (bf16[256,512]{1,0:T(8,128)(2,1)S(1)}, bf16[256,512]{1,0:T(8,128)(2,1)S(1)}, u32[]{:S(2)}, u32[]{:S(2)}) collective-permute-start(bf16[256,512]{1,0:T(8,128)(2,1)S(1)} %get-tuple-element.51), channel_id=1, source_target_pairs={{0,4},{4,0},{8,12},{12,8},{16,20},{20,16},{24,28},{28,24},{1,5},{5... | collective-permute-start | bytes 786440 | tf_op jit(solution)/shard_map/ppermute | solution.py:223
  138.6 2.5 %shard_map.82 = (f32[256,512]{1,0:T(8,128)S(1)}, bf16[256,512]{1,0:T(8,128)(2,1)S(1)}) custom-call(bf16[2048,128]{1,0:T(8,128)(2,1)S(1)} %select_convert_fusion.spread_ref, bf16[128,512]{1,0:T(8,128)(2,1)S(1)} %get-tuple-element.38.d_hidden_ref, bf16[2048,512]{1,0:T(8,128)(2,1)S(1)} %copy-done.7, bf16[512,2048]{1,0:T(8,128)(2,1)S(1)} %get-tuple-element.40.rows_ref), custom_call_target="tpu_custom_call" | custom-call | flops 1024 | bytes 1024 | tf_op jit(solution)/shard_map/pallas_call | solution.py:131
  141.1 0.1 collective-permute-start.9
  141.4 2.5 %shard_map.85 = (f32[256,512]{1,0:T(8,128)S(1)}, bf16[256,512]{1,0:T(8,128)(2,1)S(1)}) custom-call(bf16[2048,128]{1,0:T(8,128)(2,1)S(1)} %select_convert_fusion.spread_ref, bf16[128,512]{1,0:T(8,128)(2,1)S(1)} %get-tuple-element.54.d_hidden_ref, bf16[2048,512]{1,0:T(8,128)(2,1)S(1)} %copy-done.3, bf16[512,2048]{1,0:T(8,128)(2,1)S(1)} %get-tuple-element.40.rows_ref), custom_call_target="tpu_custom_call" | custom-call | flops 1024 | bytes 1024 | tf_op jit(solution)/shard_map/pallas_call | solution.py:131
  143.9 0.6 collective-permute-start.14
  144.4 0.3 collective-permute-start.16
  144.9 2.5 %shard_map.83 = (f32[256,512]{1,0:T(8,128)S(1)}, bf16[256,512]{1,0:T(8,128)(2,1)S(1)}) custom-call(bf16[2048,128]{1,0:T(8,128)(2,1)S(1)} %select_convert_fusion.spread_ref, bf16[128,512]{1,0:T(8,128)(2,1)S(1)} %get-tuple-element.43.d_hidden_ref, bf16[2048,512]{1,0:T(8,128)(2,1)S(1)} %copy-done.1, bf16[512,2048]{1,0:T(8,128)(2,1)S(1)} %get-tuple-element.40.rows_ref), custom_call_target="tpu_custom_call" | custom-call | flops 1024 | bytes 1024 | tf_op jit(solution)/shard_map/pallas_call | solution.py:131
  147.4 0.3 collective-permute-start.10
  147.7 0.6 collective-permute-start.13
  148.2 2.1 %collective-permute-start.12 = (bf16[256,512]{1,0:T(8,128)(2,1)S(1)}, bf16[256,512]{1,0:T(8,128)(2,1)S(1)}, u32[]{:S(2)}, u32[]{:S(2)}) collective-permute-start(bf16[256,512]{1,0:T(8,128)(2,1)S(1)} %add_convert_fusion.2), channel_id=1, source_target_pairs={{0,2},{1,3},{2,0},{3,1},{4,6},{5,7},{6,4},{7,5},{8,10},{9,11},{10,... | collective-permute-start | bytes 786440 | tf_op jit(solution)/shard_map/ppermute | solution.py:161
  150.5 0.3 collective-permute-start.15
  150.8 5.6 %collective-permute-done.13 = bf16[256,512]{1,0:T(8,128)(2,1)S(1)} collective-permute-done((bf16[256,512]{1,0:T(8,128)(2,1)S(1)}, bf16[256,512]{1,0:T(8,128)(2,1)S(1)}, u32[]{:S(2)}, u32[]{:S(2)}) %collective-permute-start.13) | collective-permute-done | bytes 262176 | tf_op jit(solution)/shard_map/ppermute | solution.py:161
  156.4 5.7 %collective-permute-done.12 = bf16[256,512]{1,0:T(8,128)(2,1)S(1)} collective-permute-done((bf16[256,512]{1,0:T(8,128)(2,1)S(1)}, bf16[256,512]{1,0:T(8,128)(2,1)S(1)}, u32[]{:S(2)}, u32[]{:S(2)}) %collective-permute-start.12) | collective-permute-done | bytes 262176 | tf_op jit(solution)/shard_map/ppermute | solution.py:161
  162.1 0.2 collective-permute-done.15
  162.4 0.2 fusion.27
  162.6 17.9 %all_to_all.24 = bf16[32,8,768]{2,1,0:T(8,128)(2,1)S(1)} all-to-all(bf16[32,8,768]{2,1,0:T(8,128)(2,1)S(1)} %pad_maximum_fusion), channel_id=1, replica_groups={{0,8,16,24,32,40,48,56,64,72,80,88,96,104,112,120,128,136,144,152,160,1..., dimensions={0} | all-to-all | bytes 786432 | tf_op jit(solution)/shard_map/all_to_all | solution.py:17
  180.6 18.1 %all_to_all.25 = bf16[32,8,768]{2,1,0:T(8,128)(2,1)S(1)} all-to-all(bf16[32,8,768]{2,1,0:T(8,128)(2,1)S(1)} %broadcast_in_dim.88), channel_id=1, replica_groups={{0,8,16,24,32,40,48,56,64,72,80,88,96,104,112,120,128,136,144,152,160,1..., dimensions={0} | all-to-all | bytes 786432 | tf_op jit(solution)/shard_map/all_to_all | solution.py:17
  198.7 3.6 %collective-permute-start.17 = (bf16[256,768]{1,0:T(8,128)(2,1)S(1)}, bf16[256,768]{1,0:T(8,128)(2,1)S(1)}, u32[]{:S(2)}, u32[]{:S(2)}) collective-permute-start(bf16[256,768]{1,0:T(8,128)(2,1)S(1)} %bitcast.40), channel_id=1, source_target_pairs={{0,4},{4,0},{8,12},{12,8},{16,20},{20,16},{24,28},{28,24},{1,5},{5... | collective-permute-start | bytes 1179656 | tf_op jit(solution)/shard_map/ppermute | solution.py:223
  202.3 1.3 collective-permute-done.17
  203.7 0.8 maximum_convert_fusion.1
  204.7 1.1 slice.10
  (62 shorter events, 1.3 us)
Async XLA Ops:
  5.3 22.3 %all-to-all-start = ((s32[64,1,128]{2,1,0:T(1,128)}), s32[64,1,128]{2,1,0:T(1,128)S(1)}, u32[]{:S(2)}, u32[]{:S(2)}) async-start(s32[64,1,128]{2,1,0:T(1,128)} %bitcast.6), calls=%async_computation | async-start | bytes 65536 | tf_op jit(solution)/shard_map/all_to_all | solution.py:17
  39.7 6.0 %copy-start.13 = (bf16[512,256]{1,0:T(8,128)(2,1)S(1)}, bf16[512,256]{1,0:T(8,128)(2,1)}, u32[]{:S(2)}) copy-start(bf16[512,256]{1,0:T(8,128)(2,1)} %param.11) | copy-start | bytes 786436
  39.7 54.6 %all-to-all-start.1 = ((bf16[64,32,512]{2,1,0:T(8,128)(2,1)}), bf16[64,32,512]{2,1,0:T(8,128)(2,1)S(1)}, u32[]{:S(2)}, u32[]{:S(2)}) async-start(bf16[64,32,512]{2,1,0:T(8,128)(2,1)} %bitcast.39), calls=%async_computation.1 | async-start | bytes 4194304 | tf_op jit(solution)/shard_map/all_to_all | solution.py:17
  44.7 7.2 %copy-start.16 = (bf16[128,32]{0,1:T(8,128)(2,1)S(1)}, bf16[128,32]{0,1:T(8,128)(2,1)}, u32[]{:S(2)}) copy-start(bf16[128,32]{0,1:T(8,128)(2,1)} %param.8) | copy-start | bytes 24580
  45.8 20.3 %collective-permute-start = (bf16[512,768]{1,0:T(8,128)(2,1)S(1)}, bf16[512,768]{1,0:T(8,128)(2,1)}, u32[]{:S(2)}, u32[]{:S(2)}) collective-permute-start(bf16[512,768]{1,0:T(8,128)(2,1)S(1)} %constant_dynamic-update-slice_fusion.w_ref.refs_9_), channel_id=1, source_target_pairs={{0,2},{1,3},{2,0},{3,1},{4,6},{5,7},{6,4},{7,5},{8,10},{9,11},{10,... | collective-permute-start | bytes 2359304 | tf_op jit(solution)/shard_map/ppermute | solution.py:161
  48.8 54.6 %collective-permute-start.2 = (bf16[512,768]{1,0:T(8,128)(2,1)S(1)}, bf16[512,768]{1,0:T(8,128)(2,1)}, u32[]{:S(2)}, u32[]{:S(2)}) collective-permute-start(bf16[512,768]{1,0:T(8,128)(2,1)S(1)} %constant_dynamic-update-slice_fusion.w_ref.refs_9_), channel_id=1, source_target_pairs={{0,3},{1,0},{2,1},{3,2},{4,7},{5,4},{6,5},{7,6},{8,11},{9,8},{10,9... | collective-permute-start | bytes 2359304 | tf_op jit(solution)/shard_map/ppermute | solution.py:161
  49.6 58.9 %collective-permute-start.4 = (bf16[512,768]{1,0:T(8,128)(2,1)S(1)}, bf16[512,768]{1,0:T(8,128)(2,1)}, u32[]{:S(2)}, u32[]{:S(2)}) collective-permute-start(bf16[512,768]{1,0:T(8,128)(2,1)S(1)} %constant_dynamic-update-slice_fusion.w_ref.refs_9_), channel_id=1, source_target_pairs={{0,1},{1,2},{2,3},{3,0},{4,5},{5,6},{6,7},{7,4},{8,9},{9,10},{10,1... | collective-permute-start | bytes 2359304 | tf_op jit(solution)/shard_map/ppermute | solution.py:161
  94.4 14.1 %copy-start.8 = (bf16[64,32,512]{2,1,0:T(8,128)(2,1)}, bf16[64,32,512]{2,1,0:T(8,128)(2,1)S(1)}, u32[]{:S(2)}) copy-start(bf16[64,32,512]{2,1,0:T(8,128)(2,1)S(1)} %all-to-all-done.1) | copy-start | bytes 6291460
  94.4 1.4 copy-start.10
  99.1 1.4 copy-start.4
  100.5 20.3 %collective-permute-start.1 = (bf16[128,512]{1,0:T(8,128)(2,1)S(1)}, bf16[128,512]{1,0:T(8,128)(2,1)S(1)}, u32[]{:S(2)}, u32[]{:S(2)}) collective-permute-start(bf16[128,512]{1,0:T(8,128)(2,1)S(1)} %get-tuple-element.33), channel_id=1, source_target_pairs={{0,2},{1,3},{2,0},{3,1},{4,6},{5,7},{6,4},{7,5},{8,10},{9,11},{10,... | collective-permute-start | bytes 393224 | tf_op jit(solution)/shard_map/ppermute | solution.py:161
  106.8 1.3 copy-start.6
  108.1 7.4 %copy-start.11 = (bf16[128,2048]{1,0:T(8,128)(2,1)S(1)}, bf16[128,2048]{1,0:T(8,128)(2,1)}, u32[]{:S(2)}) copy-start(bf16[128,2048]{1,0:T(8,128)(2,1)} %select_convert_fusion.1.spread_ref) | copy-start | bytes 1572868
  108.1 12.7 %collective-permute-start.3 = (bf16[128,512]{1,0:T(8,128)(2,1)S(1)}, bf16[128,512]{1,0:T(8,128)(2,1)S(1)}, u32[]{:S(2)}, u32[]{:S(2)}) collective-permute-start(bf16[128,512]{1,0:T(8,128)(2,1)S(1)} %get-tuple-element.34), channel_id=1, source_target_pairs={{0,1},{1,2},{2,3},{3,0},{4,5},{5,6},{6,7},{7,4},{8,9},{9,10},{10,1... | collective-permute-start | bytes 393224 | tf_op jit(solution)/shard_map/ppermute | solution.py:161
  111.9 1.4 copy-start.2
  113.2 7.6 %collective-permute-start.5 = (bf16[128,512]{1,0:T(8,128)(2,1)S(1)}, bf16[128,512]{1,0:T(8,128)(2,1)S(1)}, u32[]{:S(2)}, u32[]{:S(2)}) collective-permute-start(bf16[128,512]{1,0:T(8,128)(2,1)S(1)} %get-tuple-element.35), channel_id=1, source_target_pairs={{0,3},{1,0},{2,1},{3,2},{4,7},{5,4},{6,5},{7,6},{8,11},{9,8},{10,9... | collective-permute-start | bytes 393224 | tf_op jit(solution)/shard_map/ppermute | solution.py:161
  115.5 1.6 copy-start.9
  117.1 3.8 %copy-start.14 = (bf16[512,256]{1,0:T(8,128)(2,1)S(1)}, bf16[512,256]{1,0:T(8,128)(2,1)}, u32[]{:S(2)}) copy-start(bf16[512,256]{1,0:T(8,128)(2,1)} %param.11) | copy-start | bytes 786436
  117.1 7.3 %copy-start.15 = (s32[128]{0:T(128)S(1)}, s32[128]{0:T(128)}, u32[]{:S(2)}) copy-start(s32[128]{0:T(128)} %param.9) | copy-start | bytes 1540
  119.4 1.4 copy-start
  121.7 5.7 %collective-permute-start.6 = (f32[128,256]{1,0:T(8,128)}, f32[128,256]{1,0:T(8,128)}, u32[]{:S(2)}, u32[]{:S(2)}) collective-permute-start(f32[128,256]{1,0:T(8,128)} %fusion.42.refs_0_), channel_id=1, source_target_pairs={{0,2},{1,3},{2,0},{3,1},{4,6},{5,7},{6,4},{7,5},{8,10},{9,11},{10,... | collective-permute-start | bytes 393224 | tf_op jit(solution)/shard_map/ppermute | solution.py:161
  121.8 6.7 %collective-permute-start.7 = (f32[128,256]{1,0:T(8,128)}, f32[128,256]{1,0:T(8,128)}, u32[]{:S(2)}, u32[]{:S(2)}) collective-permute-start(f32[128,256]{1,0:T(8,128)} %fusion.42.refs_0_), channel_id=1, source_target_pairs={{0,1},{1,2},{2,3},{3,0},{4,5},{5,6},{6,7},{7,4},{8,9},{9,10},{10,1... | collective-permute-start | bytes 393224 | tf_op jit(solution)/shard_map/ppermute | solution.py:161
  122.3 6.2 %collective-permute-start.8 = (f32[128,256]{1,0:T(8,128)}, f32[128,256]{1,0:T(8,128)}, u32[]{:S(2)}, u32[]{:S(2)}) collective-permute-start(f32[128,256]{1,0:T(8,128)} %fusion.42.refs_0_), channel_id=1, source_target_pairs={{0,3},{1,0},{2,1},{3,2},{4,7},{5,4},{6,5},{7,6},{8,11},{9,8},{10,9... | collective-permute-start | bytes 393224 | tf_op jit(solution)/shard_map/ppermute | solution.py:161
  125.2 6.6 %copy-start.5 = (bf16[2048,512]{1,0:T(8,128)(2,1)S(1)}, bf16[2048,512]{1,0:T(8,128)(2,1)}, u32[]{:S(2)}) copy-start(bf16[2048,512]{1,0:T(8,128)(2,1)} %copy-done.4) | copy-start | bytes 6291460
  128.5 0.8 copy-start.12
  131.8 6.9 %copy-start.7 = (bf16[2048,512]{1,0:T(8,128)(2,1)S(1)}, bf16[2048,512]{1,0:T(8,128)(2,1)}, u32[]{:S(2)}) copy-start(bf16[2048,512]{1,0:T(8,128)(2,1)} %copy-done.6) | copy-start | bytes 6291460
  134.3 7.0 %collective-permute-start.11 = (bf16[256,512]{1,0:T(8,128)(2,1)S(1)}, bf16[256,512]{1,0:T(8,128)(2,1)S(1)}, u32[]{:S(2)}, u32[]{:S(2)}) collective-permute-start(bf16[256,512]{1,0:T(8,128)(2,1)S(1)} %get-tuple-element.51), channel_id=1, source_target_pairs={{0,4},{4,0},{8,12},{12,8},{16,20},{20,16},{24,28},{28,24},{1,5},{5... | collective-permute-start | bytes 786440 | tf_op jit(solution)/shard_map/ppermute | solution.py:223
  138.6 2.7 %copy-start.3 = (bf16[2048,512]{1,0:T(8,128)(2,1)S(1)}, bf16[2048,512]{1,0:T(8,128)(2,1)}, u32[]{:S(2)}) copy-start(bf16[2048,512]{1,0:T(8,128)(2,1)} %copy-done.2) | copy-start | bytes 6291460
  141.1 3.6 %collective-permute-start.9 = (bf16[256,512]{1,0:T(8,128)(2,1)S(1)}, bf16[256,512]{1,0:T(8,128)(2,1)S(1)}, u32[]{:S(2)}, u32[]{:S(2)}) collective-permute-start(bf16[256,512]{1,0:T(8,128)(2,1)S(1)} %get-tuple-element.42), channel_id=1, source_target_pairs={{0,4},{4,0},{8,12},{12,8},{16,20},{20,16},{24,28},{28,24},{1,5},{5... | collective-permute-start | bytes 786440 | tf_op jit(solution)/shard_map/ppermute | solution.py:223
  141.3 3.5 %copy-start.1 = (bf16[2048,512]{1,0:T(8,128)(2,1)S(1)}, bf16[2048,512]{1,0:T(8,128)(2,1)}, u32[]{:S(2)}) copy-start(bf16[2048,512]{1,0:T(8,128)(2,1)} %copy-done) | copy-start | bytes 6291460
  143.9 6.5 %collective-permute-start.14 = (bf16[256,512]{1,0:T(8,128)(2,1)S(1)}, bf16[256,512]{1,0:T(8,128)(2,1)S(1)}, u32[]{:S(2)}, u32[]{:S(2)}) collective-permute-start(bf16[256,512]{1,0:T(8,128)(2,1)S(1)} %get-tuple-element.57), channel_id=1, source_target_pairs={{0,4},{4,0},{8,12},{12,8},{16,20},{20,16},{24,28},{28,24},{1,5},{5... | collective-permute-start | bytes 786440 | tf_op jit(solution)/shard_map/ppermute | solution.py:223
  144.4 6.4 %collective-permute-start.16 = (bf16[256,256]{1,0:T(8,128)(2,1)S(1)}, bf16[256,256]{1,0:T(8,128)(2,1)S(1)}, u32[]{:S(2)}, u32[]{:S(2)}) collective-permute-start(bf16[256,256]{1,0:T(8,128)(2,1)S(1)} %get-tuple-element.59), channel_id=1, source_target_pairs={{0,4},{4,0},{8,12},{12,8},{16,20},{20,16},{24,28},{28,24},{1,5},{5... | collective-permute-start | bytes 393224 | tf_op jit(solution)/shard_map/ppermute | solution.py:223
  147.4 3.4 %collective-permute-start.10 = (bf16[256,512]{1,0:T(8,128)(2,1)S(1)}, bf16[256,512]{1,0:T(8,128)(2,1)S(1)}, u32[]{:S(2)}, u32[]{:S(2)}) collective-permute-start(bf16[256,512]{1,0:T(8,128)(2,1)S(1)} %get-tuple-element.46), channel_id=1, source_target_pairs={{0,4},{4,0},{8,12},{12,8},{16,20},{20,16},{24,28},{28,24},{1,5},{5... | collective-permute-start | bytes 786440 | tf_op jit(solution)/shard_map/ppermute | solution.py:223
  147.7 8.8 %collective-permute-start.13 = (bf16[256,512]{1,0:T(8,128)(2,1)S(1)}, bf16[256,512]{1,0:T(8,128)(2,1)S(1)}, u32[]{:S(2)}, u32[]{:S(2)}) collective-permute-start(bf16[256,512]{1,0:T(8,128)(2,1)S(1)} %add_convert_fusion.3), channel_id=1, source_target_pairs={{0,1},{1,2},{2,3},{3,0},{4,5},{5,6},{6,7},{7,4},{8,9},{9,10},{10,1... | collective-permute-start | bytes 786440 | tf_op jit(solution)/shard_map/ppermute | solution.py:161
  148.2 13.9 %collective-permute-start.12 = (bf16[256,512]{1,0:T(8,128)(2,1)S(1)}, bf16[256,512]{1,0:T(8,128)(2,1)S(1)}, u32[]{:S(2)}, u32[]{:S(2)}) collective-permute-start(bf16[256,512]{1,0:T(8,128)(2,1)S(1)} %add_convert_fusion.2), channel_id=1, source_target_pairs={{0,2},{1,3},{2,0},{3,1},{4,6},{5,7},{6,4},{7,5},{8,10},{9,11},{10,... | collective-permute-start | bytes 786440 | tf_op jit(solution)/shard_map/ppermute | solution.py:161
  150.5 11.9 %collective-permute-start.15 = (bf16[256,512]{1,0:T(8,128)(2,1)S(1)}, bf16[256,512]{1,0:T(8,128)(2,1)S(1)}, u32[]{:S(2)}, u32[]{:S(2)}) collective-permute-start(bf16[256,512]{1,0:T(8,128)(2,1)S(1)} %add_convert_fusion.1), channel_id=1, source_target_pairs={{0,3},{1,0},{2,1},{3,2},{4,7},{5,4},{6,5},{7,6},{8,11},{9,8},{10,9... | collective-permute-start | bytes 786440 | tf_op jit(solution)/shard_map/ppermute | solution.py:161
  198.7 5.0 %collective-permute-start.17 = (bf16[256,768]{1,0:T(8,128)(2,1)S(1)}, bf16[256,768]{1,0:T(8,128)(2,1)S(1)}, u32[]{:S(2)}, u32[]{:S(2)}) collective-permute-start(bf16[256,768]{1,0:T(8,128)(2,1)S(1)} %bitcast.40), channel_id=1, source_target_pairs={{0,4},{4,0},{8,12},{12,8},{16,20},{20,16},{24,28},{28,24},{1,5},{5... | collective-permute-start | bytes 1179656 | tf_op jit(solution)/shard_map/ppermute | solution.py:223

commit v5 on v4

--- a/solution.py
+++ b/solution.py
@@ -19,6 +19,11 @@
     )
 
 
+VMEM = pl.BlockSpec(memory_space=pltpu.VMEM)
+SMEM = pl.BlockSpec(memory_space=pltpu.SMEM)
+HBM = pl.BlockSpec(memory_space=pltpu.HBM)
+
+
 def middle(parts, labels, hidden, w_boths, core):
     count = len(parts)
     targets, classes = parts[0].shape
@@ -30,7 +35,14 @@
         labels_ref, hidden_ref = refs[:2]
         w_refs, refs = refs[2 : 2 + count], refs[2 + count :]
         own_ref, other_ref = refs[:2]
-        d_hidden_refs = refs[2:]
+        d_hidden_refs = refs[2 : 2 + count]
+        w_all, sems = refs[2 + count :]
+        copies = [
+            pltpu.make_async_copy(w_refs[i].at[:, pl.ds(units, classes)], w_all.at[i], sems.at[i])
+            for i in range(count)
+        ]
+        for copy in copies:
+            copy.start()
         logits = part_refs[0][...]
         for part in part_refs[1:]:
             logits += part[...]
@@ -39,15 +51,15 @@
         ids = lax.broadcasted_iota(jnp.int32, (targets, classes), 1)
         onehot = (labels_ref[...] == ids).astype(F32)
         d_logits = (probability - onehot).astype(BF)
-        for w_ref, out in zip(w_refs, d_hidden_refs):
-            out[...] = dot(d_logits, w_ref[:, units:], 1, 1).astype(BF)
         both = dot(hidden_ref[...], d_logits, 0, 0)
         swap = core_ref[0] != 0
         low, high = both[:half], both[half:]
         own_ref[...] = jnp.where(swap, high, low)
         other_ref[...] = jnp.where(swap, low, high).astype(BF)
-
-    vmem = pl.BlockSpec(memory_space=pltpu.VMEM)
+        for i in range(count):
+            copies[i].wait()
+            d_hidden_refs[i][...] = dot(d_logits, w_all[i], 1, 1).astype(BF)
+
     return pl.pallas_call(
         kernel,
         out_shape=[
@@ -55,8 +67,12 @@
             jax.ShapeDtypeStruct((half, classes), BF),
         ]
         + [jax.ShapeDtypeStruct((targets, units), BF)] * count,
-        in_specs=[pl.BlockSpec(memory_space=pltpu.SMEM)] + [vmem] * (2 * count + 2),
-        out_specs=[vmem] * (2 + count),
+        in_specs=[SMEM] + [VMEM] * (count + 2) + [HBM] * count,
+        out_specs=[VMEM] * (2 + count),
+        scratch_shapes=[
+            pltpu.VMEM((count, units, classes), BF),
+            pltpu.SemaphoreType.DMA((count,)),
+        ],
         compiler_params=pltpu.CompilerParams(vmem_limit_bytes=24 * 2**20),
         cost_estimate=pl.CostEstimate(
             flops=2 * targets * classes * units * (count + 1),
@@ -66,49 +82,84 @@
     )(core, *parts, labels, hidden, *w_boths)
 
 
-VMEM = pl.BlockSpec(memory_space=pltpu.VMEM)
-SMEM = pl.BlockSpec(memory_space=pltpu.SMEM)
-
-
-def forward(rows, w_both, spread, core, out_type, turn):
+def forward(rows, w_boths, spread, core, out_type, turn):
     slots, width_f = rows.shape
     targets = spread.shape[0]
     units = width_f
     half = width_f // 2
     block = 512
-
-    def kernel(core_ref, rows_ref, w_ref, spread_ref, active_ref, hidden_ref, *turned):
+    count = len(w_boths)
+
+    def kernel(core_ref, rows_ref, spread_ref, *refs):
+        w_refs, refs = refs[:count], refs[count:]
+        active_refs, refs = refs[:count], refs[count:]
+        hidden_refs, refs = refs[:count], refs[count:]
+        turned_refs, refs = refs[:turn], refs[turn:]
+        w_all, active_all, spread_all, w_sems, out_sems, spread_sem = refs[:6]
+        turned, turned_sems = refs[6 : 6 + turn], refs[6 + turn :]
+        for i in range(count):
+            pltpu.make_async_copy(
+                w_refs[i].at[:, pl.ds(0, units)], w_all.at[i], w_sems.at[i]
+            ).start()
+        spread_copy = pltpu.make_async_copy(spread_ref, spread_all, spread_sem)
+        spread_copy.start()
         mine = pl.multiple_of(core_ref[0] * half, half)
         other = pl.multiple_of((1 - core_ref[0]) * half, half)
-
-        @pl.loop(0, slots // block)
-        def _(i):
-            at = pl.ds(pl.multiple_of(i * block, block), block)
-            value = rows_ref[at, :]
-            active_ref[at, :] = jnp.maximum(dot(value, w_ref[:, :units]), 0.0).astype(BF)
-            for ref in turned:
-                flat = value.T
-                ref[pl.ds(mine, half), at] = flat[:half]
-                ref[pl.ds(other, half), at] = flat[half:]
-
-        hidden_ref[...] = dot(spread_ref[...], active_ref[...]).astype(out_type)
-
-    shapes = [
-        jax.ShapeDtypeStruct((slots, units), BF),
-        jax.ShapeDtypeStruct((targets, units), out_type),
-    ] + [jax.ShapeDtypeStruct((width_f, slots), BF)] * turn
+        for i in range(count):
+            pltpu.make_async_copy(
+                w_refs[i].at[:, pl.ds(0, units)], w_all.at[i], w_sems.at[i]
+            ).wait()
+
+            @pl.loop(0, slots // block)
+            def _(j, i=i):
+                at = pl.ds(pl.multiple_of(j * block, block), block)
+                value = rows_ref[at, :]
+                active_all[i, at, :] = jnp.maximum(dot(value, w_all[i]), 0.0).astype(BF)
+                if i == count - 1:
+                    for ref in turned:
+                        flat = value.T
+                        ref[pl.ds(mine, half), at] = flat[:half]
+                        ref[pl.ds(other, half), at] = flat[half:]
+
+            pltpu.make_async_copy(active_all.at[i], active_refs[i], out_sems.at[i]).start()
+            if i == count - 1:
+                for source, target, sem in zip(turned, turned_refs, turned_sems):
+                    pltpu.make_async_copy(source, target, sem).start()
+            if i == 0:
+                spread_copy.wait()
+            hidden_refs[i][...] = dot(spread_all[...], active_all[i]).astype(out_type)
+        for i in range(count):
+            pltpu.make_async_copy(active_all.at[i], active_refs[i], out_sems.at[i]).wait()
+        for source, target, sem in zip(turned, turned_refs, turned_sems):
+            pltpu.make_async_copy(source, target, sem).wait()
+
+    shapes = (
+        [pltpu.HBM((slots, units), BF)] * count
+        + [jax.ShapeDtypeStruct((targets, units), out_type)] * count
+        + [pltpu.HBM((width_f, slots), BF)] * turn
+    )
     return pl.pallas_call(
         kernel,
         out_shape=shapes,
-        in_specs=[SMEM] + [VMEM] * 3,
-        out_specs=[VMEM] * len(shapes),
+        in_specs=[SMEM, VMEM, HBM] + [HBM] * count,
+        out_specs=[HBM] * count + [VMEM] * count + [HBM] * turn,
+        scratch_shapes=[
+            pltpu.VMEM((count, width_f, units), BF),
+            pltpu.VMEM((count, slots, units), BF),
+            pltpu.VMEM((targets, slots), BF),
+            pltpu.SemaphoreType.DMA((count,)),
+            pltpu.SemaphoreType.DMA((count,)),
+            pltpu.SemaphoreType.DMA,
+        ]
+        + [pltpu.VMEM((width_f, slots), BF)] * turn
+        + [pltpu.SemaphoreType.DMA] * turn,
         compiler_params=pltpu.CompilerParams(vmem_limit_bytes=24 * 2**20),
         cost_estimate=pl.CostEstimate(
-            flops=2 * slots * units * (width_f + targets),
+            flops=2 * count * slots * units * (width_f + targets),
             bytes_accessed=2 * slots * (width_f + units + targets),
             transcendentals=0,
         ),
-    )(core, rows, w_both, spread)
+    )(core, rows, *(pltpu.with_memory_space_constraint(x, pltpu.HBM) for x in (spread, *w_boths)))
 
 
 def backward(spread_t, d_hidden, active, rows_t):
@@ -203,16 +254,15 @@
     spread, spread_t = lax.optimization_barrier((spread, spread.T))
 
     core_id = core.reshape(1)
-    active, hidden = {}, 0.0
-    for step in steps:
-        out = F32 if step == 0 else BF
-        active[step], part, *turned = forward(
-            received, w_boths[step], spread, core_id, out, step == 0
-        )
-        hidden += to_mlp(part, step).astype(F32) if step else part
+    first = steps[:-1]
+    out = forward(received, [w_boths[s] for s in first], spread, core_id, BF, 0)
+    active = dict(zip(first, out))
+    shares = [to_mlp(part, step) for part, step in zip(out[len(first) :], first)]
+    active[0], hidden, rows_t = forward(received, [w_both], spread, core_id, F32, 1)
+    for share_in in shares:
+        hidden += share_in.astype(F32)
     hidden = hidden.astype(BF)
     half = width_f // 2
-    (rows_t,) = turned
 
     part = dot(hidden, w_two)
     parts = [part] + [to_mlp(part, step) for step in steps[:-1]]
@@ -226,18 +276,22 @@
         parts, labels[:, None], hidden, [w_boths[s] for s in steps], core_id
     )
     own_two, other_two = mine, other
-    sums = []
+    grad_one, arrived = [], []
     for i, step in enumerate(steps):
         d_slice = d_hidden[i]
-        if i >= 2:
-            d_slice, sums[i - 2] = lax.optimization_barrier((d_slice, sums[i - 2]))
+        if i == 2:
+            d_slice, grad_one[0] = lax.optimization_barrier((d_slice, grad_one[0]))
+            arrived.append(to_mlp(grad_one[0], steps[0]))
+        if i == 3:
+            arrived += [to_mlp(g, s) for g, s in zip(grad_one[1:], steps[1:])]
+            d_slice, arrived[0] = lax.optimization_barrier((d_slice, arrived[0]))
         mine, other = backward(spread_t, d_slice, active[step], rows_t)
         mine += partner(other).astype(F32)
-        sums.append(mine.astype(BF) if step else mine)
+        grad_one.append(mine.astype(BF) if step else mine)
     grad_two = own_two + partner(other_two).astype(F32)
-    grad_one = sums[-1]
-    for step, value in zip(steps[:-1], sums):
-        grad_one += to_mlp(value, step).astype(F32)
+    grad_one = grad_one[-1]
+    for value in arrived:
+        grad_one += value.astype(F32)
     both = jnp.concatenate([grad_one, grad_two], axis=1).astype(BF)
     chips = owners // 2
     groups = [[2 * i + c for i in range(chips)] for c in (0, 1)]

time: 206 us -> 203 us (0.985)
  local copies, waits for them, and re-layouts: 24.8 us -> 18 us
  starting transfers between devices: 42.9 us -> 45 us
    all_to_all x2, waiting for transfers between devices: 37.6 us -> 19.8 us  [exchange(): lax.all_to_all(x, axes, split_axis=0, concat_axis=0, tiled=True, axis_ind...]
    ppermute x12, waiting for transfers between devices: 25.4 us -> 41.8 us  [to_mlp(): lax.ppermute(x, 'mlp', [(j, (j + step) % mlp_n) for j in range(mlp_n)])]
    unnamed x35 -> x25, local copies, waits for them, and re-layouts: 10.4 us -> 3.55 us
    pallas_call x4 -> x2, Pallas kernels: 12.3 us -> 13.5 us  [forward(): pl.pallas_call(kernel, out_shape=shapes, in_specs=[SMEM, VMEM, HBM] + [HB...]
  transfers between devices with their start and end apart: 20 -> 20, of which waited for: 9 -> 11; matrix products, arithmetic and copies ran while one was open for 4% -> 4% of each run, Pallas kernels for 10% -> 6%
where the time goes in v5:
time: 203 us; the launch traced here: 202 us
  waiting for transfers between devices  63 us (31%)
  starting transfers between devices  45 us (22%)
  blocking collectives  36.9 us (18%)
  Pallas kernels  26.7 us (13%)
  local copies, waits for them, and re-layouts  18 us (9%)
  matrix products  7.6 us (4%)
  other arithmetic  4.27 us (2%)
    ppermute x12, waiting for transfers between devices, to_mlp(): lax.ppermute(x, 'mlp', [(j, (j + step) % mlp_n) for j in range(mlp_n)])  41.8 us
    all_to_all x2, blocking collectives, exchange(): lax.all_to_all(x, axes, split_axis=0, concat_axis=0, tiled=True, axis_ind...  36.9 us
    all_to_all x2, waiting for transfers between devices, exchange(): lax.all_to_all(x, axes, split_axis=0, concat_axis=0, tiled=True, axis_ind...  19.8 us
    all_to_all x2, starting transfers between devices, exchange(): lax.all_to_all(x, axes, split_axis=0, concat_axis=0, tiled=True, axis_ind...  17.9 us
    ppermute x12, starting transfers between devices, to_mlp(): lax.ppermute(x, 'mlp', [(j, (j + step) % mlp_n) for j in range(mlp_n)])  16 us
    pallas_call x2, Pallas kernels, forward(): pl.pallas_call(kernel, out_shape=shapes, in_specs=[SMEM, VMEM, HBM] + [HB...  13.5 us
    gather x1, local copies, waits for them, and re-layouts, body(): fetched = features[asked]  12 us
    ppermute x6, starting transfers between devices, partner(): return lax.ppermute(x, 'col', pairs)  11.1 us
  transfers between devices with their start and end apart: 20, of which 11 were waited for; matrix products, arithmetic and copies ran while one was open for 4% of the time, Pallas kernels for 6%

profile of v5, /device:TPU:1, one launch (start us, length us, event | category | flops | bytes accessed | tf_op | source)
XLA Modules:
  0.0 202.4 jit_solution(5598618330969931523)
XLA Ops:
  0.6 0.8 fusion.30
  1.4 0.1 convert_reduce_fusion
  1.5 0.1 fusion.29
  1.6 0.2 convolution_subtract_fusion
  1.9 0.2 select_reduce_fusion
  2.1 1.3 convolution_bitcast_fusion.2
  3.4 1.9 fusion.6
  5.3 13.0 %all-to-all-start = ((s32[64,1,128]{2,1,0:T(1,128)}), s32[64,1,128]{2,1,0:T(1,128)S(1)}, u32[]{:S(2)}, u32[]{:S(2)}) async-start(s32[64,1,128]{2,1,0:T(1,128)} %bitcast.6), calls=%async_computation | async-start | bytes 65536 | tf_op jit(solution)/shard_map/all_to_all | solution.py:17
  18.3 9.3 %all-to-all-done = s32[64,1,128]{2,1,0:T(1,128)S(1)} async-done(((s32[64,1,128]{2,1,0:T(1,128)}), s32[64,1,128]{2,1,0:T(1,128)S(1)}, u32[]{:S(2)}, u32[]{:S(2)}) %all-to-all-start) | async-done | bytes 32800 | tf_op jit(solution)/shard_map/all_to_all | solution.py:17
  27.6 0.1 constant_dynamic-slice_fusion
  27.8 12.0 %gather_fusion = bf16[2048,512]{1,0:T(8,128)(2,1)} fusion(bf16[4096,512]{1,0:T(8,128)(2,1)} %param.6, s32[2048]{0:T(1024)S(1)} %broadcast_clamp_fusion), kind=kCustom, calls=%fused_computation | custom fusion | bytes 4202496 | tf_op jit(solution)/shard_map/gather | solution.py:246
  39.8 4.9 %all-to-all-start.1 = ((bf16[64,32,512]{2,1,0:T(8,128)(2,1)}), bf16[64,32,512]{2,1,0:T(8,128)(2,1)S(1)}, u32[]{:S(2)}, u32[]{:S(2)}) async-start(bf16[64,32,512]{2,1,0:T(8,128)(2,1)} %bitcast.37), calls=%async_computation.1 | async-start | bytes 4194304 | tf_op jit(solution)/shard_map/all_to_all | solution.py:17
  44.8 1.1 constant_dynamic-update-slice_fusion.1
  45.9 3.0 %collective-permute-start = (bf16[512,768]{1,0:T(8,128)(2,1)S(1)}, bf16[512,768]{1,0:T(8,128)(2,1)}, u32[]{:S(2)}, u32[]{:S(2)}) collective-permute-start(bf16[512,768]{1,0:T(8,128)(2,1)S(1)} %constant_dynamic-update-slice_fusion.refs_0_.refs_9_), channel_id=1, source_target_pairs={{0,2},{1,3},{2,0},{3,1},{4,6},{5,7},{6,4},{7,5},{8,10},{9,11},{10,... | collective-permute-start | bytes 2359304 | tf_op jit(solution)/shard_map/ppermute | solution.py:212
  48.9 0.8 collective-permute-start.1
  49.7 0.7 collective-permute-start.2
  50.4 1.4 convolution_bitcast_fusion.1
  51.8 0.1 copy.17
  51.9 1.8 convolution_bitcast_fusion
  53.8 0.1 copy.19
  53.9 0.1 broadcast_in_dim.80
  54.0 0.7 select_convert_fusion.spread_ref
  54.7 0.9 select_convert_fusion.1.spread_ref
  55.6 10.6 %collective-permute-done.refs_0_.refs_6_ = bf16[512,768]{1,0:T(8,128)(2,1)} collective-permute-done((bf16[512,768]{1,0:T(8,128)(2,1)S(1)}, bf16[512,768]{1,0:T(8,128)(2,1)}, u32[]{:S(2)}, u32[]{:S(2)}) %collective-permute-start) | collective-permute-done | bytes 786464 | tf_op jit(solution)/shard_map/ppermute | solution.py:212
  66.2 17.2 %collective-permute-done.1.refs_1_.refs_7_ = bf16[512,768]{1,0:T(8,128)(2,1)} collective-permute-done((bf16[512,768]{1,0:T(8,128)(2,1)S(1)}, bf16[512,768]{1,0:T(8,128)(2,1)}, u32[]{:S(2)}, u32[]{:S(2)}) %collective-permute-start.1) | collective-permute-done | bytes 786464 | tf_op jit(solution)/shard_map/ppermute | solution.py:212
  83.4 0.5 collective-permute-done.2.refs_2_.refs_8_
  83.9 10.5 %all-to-all-done.1 = bf16[64,32,512]{2,1,0:T(8,128)(2,1)S(1)} async-done(((bf16[64,32,512]{2,1,0:T(8,128)(2,1)}), bf16[64,32,512]{2,1,0:T(8,128)(2,1)S(1)}, u32[]{:S(2)}, u32[]{:S(2)}) %all-to-all-start.1) | async-done | bytes 2097184 | tf_op jit(solution)/shard_map/all_to_all | solution.py:17
  94.4 8.7 %shard_map.78 = (bf16[2048,512]{1,0:T(8,128)(2,1)}, bf16[2048,512]{1,0:T(8,128)(2,1)}, bf16[2048,512]{1,0:T(8,128)(2,1)}, bf16[128,512]{1,0:T(8,128)(2,1)S(1)}, ...) custom-call(s32[1]{0:T(128)} %bitcast.2.core_ref, bf16[2048,512]{1,0:T(8,128)(2,1)S(1)} %bitcast.35, ...), custom_call_target="tpu_custom_call" | custom-call | flops 4026531840 | bytes 4718592 | tf_op jit(solution)/shard_map/pallas_call | solution.py:141
  103.1 3.0 %collective-permute-start.3 = (bf16[128,512]{1,0:T(8,128)(2,1)S(1)}, bf16[128,512]{1,0:T(8,128)(2,1)S(1)}, u32[]{:S(2)}, u32[]{:S(2)}) collective-permute-start(bf16[128,512]{1,0:T(8,128)(2,1)S(1)} %get-tuple-element.34), channel_id=1, source_target_pairs={{0,2},{1,3},{2,0},{3,1},{4,6},{5,7},{6,4},{7,5},{8,10},{9,11},{10,... | collective-permute-start | bytes 393224 | tf_op jit(solution)/shard_map/ppermute | solution.py:212
  106.1 0.4 collective-permute-start.4
  106.5 2.3 %collective-permute-start.5 = (bf16[128,512]{1,0:T(8,128)(2,1)S(1)}, bf16[128,512]{1,0:T(8,128)(2,1)S(1)}, u32[]{:S(2)}, u32[]{:S(2)}) collective-permute-start(bf16[128,512]{1,0:T(8,128)(2,1)S(1)} %get-tuple-element.36), channel_id=1, source_target_pairs={{0,3},{1,0},{2,1},{3,2},{4,7},{5,4},{6,5},{7,6},{8,11},{9,8},{10,9... | collective-permute-start | bytes 393224 | tf_op jit(solution)/shard_map/ppermute | solution.py:212
  108.8 4.8 %shard_map.77 = (bf16[2048,512]{1,0:T(8,128)(2,1)}, f32[128,512]{1,0:T(8,128)S(1)}, bf16[512,2048]{1,0:T(8,128)(2,1)}) custom-call(s32[1]{0:T(128)} %bitcast.2.core_ref, bf16[2048,512]{1,0:T(8,128)(2,1)S(1)} %bitcast.36, bf16[128,2048]{1,0:T(8,128)(2,1)} %select_convert_fusion.1.spread_ref, bf16[512,768]{1,0:T(8,128)(2,1)} %copy-done.1), custom_call_target="tpu_custom_call" | custom-call | flops 1342177280 | bytes 4718592 | tf_op jit(solution)/shard_map/pallas_call | solution.py:141
  113.8 0.8 fusion.42.refs_0_
  114.6 2.1 %collective-permute-start.7 = (f32[128,256]{1,0:T(8,128)}, f32[128,256]{1,0:T(8,128)}, u32[]{:S(2)}, u32[]{:S(2)}) collective-permute-start(f32[128,256]{1,0:T(8,128)} %fusion.42.refs_0_), channel_id=1, source_target_pairs={{0,1},{1,2},{2,3},{3,0},{4,5},{5,6},{6,7},{7,4},{8,9},{9,10},{10,1... | collective-permute-start | bytes 393224 | tf_op jit(solution)/shard_map/ppermute | solution.py:212
  116.7 0.6 collective-permute-start.8
  117.3 0.7 copy.21.refs_4_
  118.0 2.3 %collective-permute-done.6.refs_1_ = f32[128,256]{1,0:T(8,128)} collective-permute-done((f32[128,256]{1,0:T(8,128)}, f32[128,256]{1,0:T(8,128)}, u32[]{:S(2)}, u32[]{:S(2)}) %collective-permute-start.6) | collective-permute-done | bytes 131104 | tf_op jit(solution)/shard_map/ppermute | solution.py:212
  120.4 1.0 collective-permute-done.7.refs_2_
  121.4 0.8 copy-done.7
  122.2 3.1 %shard_map.79 = (f32[256,256]{1,0:T(8,128)S(1)}, bf16[256,256]{1,0:T(8,128)(2,1)S(1)}, bf16[128,512]{1,0:T(8,128)(2,1)S(1)}, bf16[128,512]{1,0:T(8,128)(2,1)S(1)...) custom-call(s32[1]{0:T(128)} %bitcast.2.core_ref, f32[128,256]{1,0:T(8,128)} %fusion.42.refs_0_, ...), custom_call_target="tpu_custom_call" | custom-call | flops 167772160 | bytes 4194304 | tf_op jit(solution)/shard_map/pallas_call | solution.py:63
  125.3 1.6 copy-done.6
  126.9 2.5 %shard_map.80 = (f32[256,512]{1,0:T(8,128)S(1)}, bf16[256,512]{1,0:T(8,128)(2,1)S(1)}) custom-call(bf16[2048,128]{1,0:T(8,128)(2,1)S(1)} %select_convert_fusion.spread_ref, bf16[128,512]{1,0:T(8,128)(2,1)S(1)} %get-tuple-element.39.d_hidden_ref, bf16[2048,512]{1,0:T(8,128)(2,1)S(1)} %copy-done.6, bf16[512,2048]{1,0:T(8,128)(2,1)S(1)} %copy-done), custom_call_target="tpu_custom_call" | custom-call | flops 1024 | bytes 1024 | tf_op jit(solution)/shard_map/pallas_call | solution.py:182
  129.4 4.5 %collective-permute-start.9 = (bf16[256,512]{1,0:T(8,128)(2,1)S(1)}, bf16[256,512]{1,0:T(8,128)(2,1)S(1)}, u32[]{:S(2)}, u32[]{:S(2)}) collective-permute-start(bf16[256,512]{1,0:T(8,128)(2,1)S(1)} %get-tuple-element.43), channel_id=1, source_target_pairs={{0,4},{4,0},{8,12},{12,8},{16,20},{20,16},{24,28},{28,24},{1,5},{5... | collective-permute-start | bytes 786440 | tf_op jit(solution)/shard_map/ppermute | solution.py:273
  134.0 2.5 %shard_map.82 = (f32[256,512]{1,0:T(8,128)S(1)}, bf16[256,512]{1,0:T(8,128)(2,1)S(1)}) custom-call(bf16[2048,128]{1,0:T(8,128)(2,1)S(1)} %select_convert_fusion.spread_ref, bf16[128,512]{1,0:T(8,128)(2,1)S(1)} %get-tuple-element.50.d_hidden_ref, bf16[2048,512]{1,0:T(8,128)(2,1)S(1)} %copy-done.5, bf16[512,2048]{1,0:T(8,128)(2,1)S(1)} %copy-done), custom_call_target="tpu_custom_call" | custom-call | flops 1024 | bytes 1024 | tf_op jit(solution)/shard_map/pallas_call | solution.py:182
  136.5 0.1 collective-permute-start.12
  136.7 0.8 collective-permute-start.10
  137.5 2.5 %shard_map.83 = (f32[256,512]{1,0:T(8,128)S(1)}, bf16[256,512]{1,0:T(8,128)(2,1)S(1)}) custom-call(bf16[2048,128]{1,0:T(8,128)(2,1)S(1)} %select_convert_fusion.spread_ref, bf16[128,512]{1,0:T(8,128)(2,1)S(1)} %get-tuple-element.54.d_hidden_ref, bf16[2048,512]{1,0:T(8,128)(2,1)S(1)} %copy-done.4, bf16[512,2048]{1,0:T(8,128)(2,1)S(1)} %copy-done), custom_call_target="tpu_custom_call" | custom-call | flops 1024 | bytes 1024 | tf_op jit(solution)/shard_map/pallas_call | solution.py:182
  140.0 0.9 collective-permute-start.14
  140.9 0.1 collective-permute-start.16
  141.0 1.5 collective-permute-start.13
  142.5 3.1 %collective-permute-done.10 = bf16[256,512]{1,0:T(8,128)(2,1)S(1)} collective-permute-done((bf16[256,512]{1,0:T(8,128)(2,1)S(1)}, bf16[256,512]{1,0:T(8,128)(2,1)S(1)}, u32[]{:S(2)}, u32[]{:S(2)}) %collective-permute-start.10) | collective-permute-done | bytes 262176 | tf_op jit(solution)/shard_map/ppermute | solution.py:212
  145.7 2.5 %shard_map.81 = (f32[256,512]{1,0:T(8,128)S(1)}, bf16[256,512]{1,0:T(8,128)(2,1)S(1)}) custom-call(bf16[2048,128]{1,0:T(8,128)(2,1)S(1)} %select_convert_fusion.spread_ref, bf16[128,512]{1,0:T(8,128)(2,1)S(1)} %get-tuple-element.45.d_hidden_ref, bf16[2048,512]{1,0:T(8,128)(2,1)S(1)} %copy-done.3, bf16[512,2048]{1,0:T(8,128)(2,1)S(1)} %copy-done), custom_call_target="tpu_custom_call" | custom-call | flops 1024 | bytes 1024 | tf_op jit(solution)/shard_map/pallas_call | solution.py:182
  148.2 2.1 %collective-permute-start.11 = (bf16[256,512]{1,0:T(8,128)(2,1)S(1)}, bf16[256,512]{1,0:T(8,128)(2,1)S(1)}, u32[]{:S(2)}, u32[]{:S(2)}) collective-permute-start(bf16[256,512]{1,0:T(8,128)(2,1)S(1)} %get-tuple-element.48), channel_id=1, source_target_pairs={{0,4},{4,0},{8,12},{12,8},{16,20},{20,16},{24,28},{28,24},{1,5},{5... | collective-permute-start | bytes 786440 | tf_op jit(solution)/shard_map/ppermute | solution.py:273
  150.4 0.9 collective-permute-start.15
  151.4 0.8 collective-permute-done.13
  152.1 6.3 %collective-permute-done.15 = bf16[256,512]{1,0:T(8,128)(2,1)S(1)} collective-permute-done((bf16[256,512]{1,0:T(8,128)(2,1)S(1)}, bf16[256,512]{1,0:T(8,128)(2,1)S(1)}, u32[]{:S(2)}, u32[]{:S(2)}) %collective-permute-start.15) | collective-permute-done | bytes 262176 | tf_op jit(solution)/shard_map/ppermute | solution.py:212
  158.4 0.2 fusion.27
  158.6 19.3 %all_to_all.24 = bf16[32,8,768]{2,1,0:T(8,128)(2,1)S(1)} all-to-all(bf16[32,8,768]{2,1,0:T(8,128)(2,1)S(1)} %pad_maximum_fusion), channel_id=1, replica_groups={{0,8,16,24,32,40,48,56,64,72,80,88,96,104,112,120,128,136,144,152,160,1..., dimensions={0} | all-to-all | bytes 786432 | tf_op jit(solution)/shard_map/all_to_all | solution.py:17
  178.0 17.6 %all_to_all.25 = bf16[32,8,768]{2,1,0:T(8,128)(2,1)S(1)} all-to-all(bf16[32,8,768]{2,1,0:T(8,128)(2,1)S(1)} %broadcast_in_dim.88), channel_id=1, replica_groups={{0,8,16,24,32,40,48,56,64,72,80,88,96,104,112,120,128,136,144,152,160,1..., dimensions={0} | all-to-all | bytes 786432 | tf_op jit(solution)/shard_map/all_to_all | solution.py:17
  195.6 3.3 %collective-permute-start.17 = (bf16[256,768]{1,0:T(8,128)(2,1)S(1)}, bf16[256,768]{1,0:T(8,128)(2,1)S(1)}, u32[]{:S(2)}, u32[]{:S(2)}) collective-permute-start(bf16[256,768]{1,0:T(8,128)(2,1)S(1)} %bitcast.38), channel_id=1, source_target_pairs={{0,4},{4,0},{8,12},{12,8},{16,20},{20,16},{24,28},{28,24},{1,5},{5... | collective-permute-start | bytes 1179656 | tf_op jit(solution)/shard_map/ppermute | solution.py:273
  198.9 1.3 collective-permute-done.17
  200.3 0.8 maximum_convert_fusion.1
  201.2 0.1 maximum_convert_fusion
  201.3 1.1 slice.10
  (50 shorter events, 0.8 us)
Async XLA Ops:
  5.3 22.3 %all-to-all-start = ((s32[64,1,128]{2,1,0:T(1,128)}), s32[64,1,128]{2,1,0:T(1,128)S(1)}, u32[]{:S(2)}, u32[]{:S(2)}) async-start(s32[64,1,128]{2,1,0:T(1,128)} %bitcast.6), calls=%async_computation | async-start | bytes 65536 | tf_op jit(solution)/shard_map/all_to_all | solution.py:17
  39.8 6.0 %copy-start.8 = (bf16[512,256]{1,0:T(8,128)(2,1)S(1)}, bf16[512,256]{1,0:T(8,128)(2,1)}, u32[]{:S(2)}) copy-start(bf16[512,256]{1,0:T(8,128)(2,1)} %param.11) | copy-start | bytes 786436
  39.8 54.6 %all-to-all-start.1 = ((bf16[64,32,512]{2,1,0:T(8,128)(2,1)}), bf16[64,32,512]{2,1,0:T(8,128)(2,1)S(1)}, u32[]{:S(2)}, u32[]{:S(2)}) async-start(bf16[64,32,512]{2,1,0:T(8,128)(2,1)} %bitcast.37), calls=%async_computation.1 | async-start | bytes 4194304 | tf_op jit(solution)/shard_map/all_to_all | solution.py:17
  44.7 7.2 %copy-start.11 = (bf16[128,32]{0,1:T(8,128)(2,1)S(1)}, bf16[128,32]{0,1:T(8,128)(2,1)}, u32[]{:S(2)}) copy-start(bf16[128,32]{0,1:T(8,128)(2,1)} %param.8) | copy-start | bytes 24580
  45.9 7.9 %copy-start.1 = (bf16[512,768]{1,0:T(8,128)(2,1)}, bf16[512,768]{1,0:T(8,128)(2,1)S(1)}, u32[]{:S(2)}) copy-start(bf16[512,768]{1,0:T(8,128)(2,1)S(1)} %constant_dynamic-update-slice_fusion.refs_0_.refs_9_) | copy-start | bytes 2359300
  45.9 20.3 %collective-permute-start = (bf16[512,768]{1,0:T(8,128)(2,1)S(1)}, bf16[512,768]{1,0:T(8,128)(2,1)}, u32[]{:S(2)}, u32[]{:S(2)}) collective-permute-start(bf16[512,768]{1,0:T(8,128)(2,1)S(1)} %constant_dynamic-update-slice_fusion.refs_0_.refs_9_), channel_id=1, source_target_pairs={{0,2},{1,3},{2,0},{3,1},{4,6},{5,7},{6,4},{7,5},{8,10},{9,11},{10,... | collective-permute-start | bytes 2359304 | tf_op jit(solution)/shard_map/ppermute | solution.py:212
  48.9 34.5 %collective-permute-start.1 = (bf16[512,768]{1,0:T(8,128)(2,1)S(1)}, bf16[512,768]{1,0:T(8,128)(2,1)}, u32[]{:S(2)}, u32[]{:S(2)}) collective-permute-start(bf16[512,768]{1,0:T(8,128)(2,1)S(1)} %constant_dynamic-update-slice_fusion.refs_0_.refs_9_), channel_id=1, source_target_pairs={{0,3},{1,0},{2,1},{3,2},{4,7},{5,4},{6,5},{7,6},{8,11},{9,8},{10,9... | collective-permute-start | bytes 2359304 | tf_op jit(solution)/shard_map/ppermute | solution.py:212
  49.7 34.2 %collective-permute-start.2 = (bf16[512,768]{1,0:T(8,128)(2,1)S(1)}, bf16[512,768]{1,0:T(8,128)(2,1)}, u32[]{:S(2)}, u32[]{:S(2)}) collective-permute-start(bf16[512,768]{1,0:T(8,128)(2,1)S(1)} %constant_dynamic-update-slice_fusion.refs_0_.refs_9_), channel_id=1, source_target_pairs={{0,1},{1,2},{2,3},{3,0},{4,5},{5,6},{6,7},{7,4},{8,9},{9,10},{10,1... | collective-permute-start | bytes 2359304 | tf_op jit(solution)/shard_map/ppermute | solution.py:212
  103.1 10.5 %collective-permute-start.3 = (bf16[128,512]{1,0:T(8,128)(2,1)S(1)}, bf16[128,512]{1,0:T(8,128)(2,1)S(1)}, u32[]{:S(2)}, u32[]{:S(2)}) collective-permute-start(bf16[128,512]{1,0:T(8,128)(2,1)S(1)} %get-tuple-element.34), channel_id=1, source_target_pairs={{0,2},{1,3},{2,0},{3,1},{4,6},{5,7},{6,4},{7,5},{8,10},{9,11},{10,... | collective-permute-start | bytes 393224 | tf_op jit(solution)/shard_map/ppermute | solution.py:212
  106.1 7.5 %collective-permute-start.4 = (bf16[128,512]{1,0:T(8,128)(2,1)S(1)}, bf16[128,512]{1,0:T(8,128)(2,1)S(1)}, u32[]{:S(2)}, u32[]{:S(2)}) collective-permute-start(bf16[128,512]{1,0:T(8,128)(2,1)S(1)} %get-tuple-element.35), channel_id=1, source_target_pairs={{0,1},{1,2},{2,3},{3,0},{4,5},{5,6},{6,7},{7,4},{8,9},{9,10},{10,1... | collective-permute-start | bytes 393224 | tf_op jit(solution)/shard_map/ppermute | solution.py:212
  106.5 7.2 %copy-start.9 = (bf16[512,256]{1,0:T(8,128)(2,1)S(1)}, bf16[512,256]{1,0:T(8,128)(2,1)}, u32[]{:S(2)}) copy-start(bf16[512,256]{1,0:T(8,128)(2,1)} %param.11) | copy-start | bytes 786436
  106.5 10.8 %copy-start.10 = (s32[128]{0:T(128)S(1)}, s32[128]{0:T(128)}, u32[]{:S(2)}) copy-start(s32[128]{0:T(128)} %param.9) | copy-start | bytes 1540
  106.5 14.9 %copy-start.2 = (bf16[512,768]{1,0:T(8,128)(2,1)S(1)}, bf16[512,768]{1,0:T(8,128)(2,1)}, u32[]{:S(2)}) copy-start(bf16[512,768]{1,0:T(8,128)(2,1)} %copy-done.1) | copy-start | bytes 2359300
  106.5 7.2 %collective-permute-start.5 = (bf16[128,512]{1,0:T(8,128)(2,1)S(1)}, bf16[128,512]{1,0:T(8,128)(2,1)S(1)}, u32[]{:S(2)}, u32[]{:S(2)}) collective-permute-start(bf16[128,512]{1,0:T(8,128)(2,1)S(1)} %get-tuple-element.36), channel_id=1, source_target_pairs={{0,3},{1,0},{2,1},{3,2},{4,7},{5,4},{6,5},{7,6},{8,11},{9,8},{10,9... | collective-permute-start | bytes 393224 | tf_op jit(solution)/shard_map/ppermute | solution.py:212
  114.6 10.7 %copy-start = (bf16[512,2048]{1,0:T(8,128)(2,1)S(1)}, bf16[512,2048]{1,0:T(8,128)(2,1)}, u32[]{:S(2)}) copy-start(bf16[512,2048]{1,0:T(8,128)(2,1)} %get-tuple-element.41.rows_ref) | copy-start | bytes 6291460
  114.6 5.7 %collective-permute-start.6 = (f32[128,256]{1,0:T(8,128)}, f32[128,256]{1,0:T(8,128)}, u32[]{:S(2)}, u32[]{:S(2)}) collective-permute-start(f32[128,256]{1,0:T(8,128)} %fusion.42.refs_0_), channel_id=1, source_target_pairs={{0,2},{1,3},{2,0},{3,1},{4,6},{5,7},{6,4},{7,5},{8,10},{9,11},{10,... | collective-permute-start | bytes 393224 | tf_op jit(solution)/shard_map/ppermute | solution.py:212
  114.6 6.7 %collective-permute-start.7 = (f32[128,256]{1,0:T(8,128)}, f32[128,256]{1,0:T(8,128)}, u32[]{:S(2)}, u32[]{:S(2)}) collective-permute-start(f32[128,256]{1,0:T(8,128)} %fusion.42.refs_0_), channel_id=1, source_target_pairs={{0,1},{1,2},{2,3},{3,0},{4,5},{5,6},{6,7},{7,4},{8,9},{9,10},{10,1... | collective-permute-start | bytes 393224 | tf_op jit(solution)/shard_map/ppermute | solution.py:212
  116.7 4.6 %collective-permute-start.8 = (f32[128,256]{1,0:T(8,128)}, f32[128,256]{1,0:T(8,128)}, u32[]{:S(2)}, u32[]{:S(2)}) collective-permute-start(f32[128,256]{1,0:T(8,128)} %fusion.42.refs_0_), channel_id=1, source_target_pairs={{0,3},{1,0},{2,1},{3,2},{4,7},{5,4},{6,5},{7,6},{8,11},{9,8},{10,9... | collective-permute-start | bytes 393224 | tf_op jit(solution)/shard_map/ppermute | solution.py:212
  121.4 0.8 copy-start.7
  125.3 1.6 copy-start.6
  126.9 7.1 %copy-start.5 = (bf16[2048,512]{1,0:T(8,128)(2,1)S(1)}, bf16[2048,512]{1,0:T(8,128)(2,1)}, u32[]{:S(2)}) copy-start(bf16[2048,512]{1,0:T(8,128)(2,1)} %get-tuple-element.51.active_ref) | copy-start | bytes 6291460
  129.4 7.2 %collective-permute-start.9 = (bf16[256,512]{1,0:T(8,128)(2,1)S(1)}, bf16[256,512]{1,0:T(8,128)(2,1)S(1)}, u32[]{:S(2)}, u32[]{:S(2)}) collective-permute-start(bf16[256,512]{1,0:T(8,128)(2,1)S(1)} %get-tuple-element.43), channel_id=1, source_target_pairs={{0,4},{4,0},{8,12},{12,8},{16,20},{20,16},{24,28},{28,24},{1,5},{5... | collective-permute-start | bytes 786440 | tf_op jit(solution)/shard_map/ppermute | solution.py:273
  134.0 3.5 %copy-start.4 = (bf16[2048,512]{1,0:T(8,128)(2,1)S(1)}, bf16[2048,512]{1,0:T(8,128)(2,1)}, u32[]{:S(2)}) copy-start(bf16[2048,512]{1,0:T(8,128)(2,1)} %get-tuple-element.55.active_ref) | copy-start | bytes 6291460
  136.5 4.5 %collective-permute-start.12 = (bf16[256,512]{1,0:T(8,128)(2,1)S(1)}, bf16[256,512]{1,0:T(8,128)(2,1)S(1)}, u32[]{:S(2)}, u32[]{:S(2)}) collective-permute-start(bf16[256,512]{1,0:T(8,128)(2,1)S(1)} %get-tuple-element.53), channel_id=1, source_target_pairs={{0,4},{4,0},{8,12},{12,8},{16,20},{20,16},{24,28},{28,24},{1,5},{5... | collective-permute-start | bytes 786440 | tf_op jit(solution)/shard_map/ppermute | solution.py:273
  136.7 9.0 %collective-permute-start.10 = (bf16[256,512]{1,0:T(8,128)(2,1)S(1)}, bf16[256,512]{1,0:T(8,128)(2,1)S(1)}, u32[]{:S(2)}, u32[]{:S(2)}) collective-permute-start(bf16[256,512]{1,0:T(8,128)(2,1)S(1)} %add_convert_fusion.3), channel_id=1, source_target_pairs={{0,2},{1,3},{2,0},{3,1},{4,6},{5,7},{6,4},{7,5},{8,10},{9,11},{10,... | collective-permute-start | bytes 786440 | tf_op jit(solution)/shard_map/ppermute | solution.py:212
  137.5 8.2 %copy-start.3 = (bf16[2048,512]{1,0:T(8,128)(2,1)S(1)}, bf16[2048,512]{1,0:T(8,128)(2,1)}, u32[]{:S(2)}) copy-start(bf16[2048,512]{1,0:T(8,128)(2,1)} %get-tuple-element.46.active_ref) | copy-start | bytes 6291460
  140.0 10.3 %collective-permute-start.14 = (bf16[256,512]{1,0:T(8,128)(2,1)S(1)}, bf16[256,512]{1,0:T(8,128)(2,1)S(1)}, u32[]{:S(2)}, u32[]{:S(2)}) collective-permute-start(bf16[256,512]{1,0:T(8,128)(2,1)S(1)} %get-tuple-element.57), channel_id=1, source_target_pairs={{0,4},{4,0},{8,12},{12,8},{16,20},{20,16},{24,28},{28,24},{1,5},{5... | collective-permute-start | bytes 786440 | tf_op jit(solution)/shard_map/ppermute | solution.py:273
  140.9 10.5 %collective-permute-start.16 = (bf16[256,256]{1,0:T(8,128)(2,1)S(1)}, bf16[256,256]{1,0:T(8,128)(2,1)S(1)}, u32[]{:S(2)}, u32[]{:S(2)}) collective-permute-start(bf16[256,256]{1,0:T(8,128)(2,1)S(1)} %get-tuple-element.59), channel_id=1, source_target_pairs={{0,4},{4,0},{8,12},{12,8},{16,20},{20,16},{24,28},{28,24},{1,5},{5... | collective-permute-start | bytes 393224 | tf_op jit(solution)/shard_map/ppermute | solution.py:273
  141.0 11.1 %collective-permute-start.13 = (bf16[256,512]{1,0:T(8,128)(2,1)S(1)}, bf16[256,512]{1,0:T(8,128)(2,1)S(1)}, u32[]{:S(2)}, u32[]{:S(2)}) collective-permute-start(bf16[256,512]{1,0:T(8,128)(2,1)S(1)} %add_convert_fusion.2), channel_id=1, source_target_pairs={{0,1},{1,2},{2,3},{3,0},{4,5},{5,6},{6,7},{7,4},{8,9},{9,10},{10,1... | collective-permute-start | bytes 786440 | tf_op jit(solution)/shard_map/ppermute | solution.py:212
  148.2 3.9 %collective-permute-start.11 = (bf16[256,512]{1,0:T(8,128)(2,1)S(1)}, bf16[256,512]{1,0:T(8,128)(2,1)S(1)}, u32[]{:S(2)}, u32[]{:S(2)}) collective-permute-start(bf16[256,512]{1,0:T(8,128)(2,1)S(1)} %get-tuple-element.48), channel_id=1, source_target_pairs={{0,4},{4,0},{8,12},{12,8},{16,20},{20,16},{24,28},{28,24},{1,5},{5... | collective-permute-start | bytes 786440 | tf_op jit(solution)/shard_map/ppermute | solution.py:273
  150.4 8.0 %collective-permute-start.15 = (bf16[256,512]{1,0:T(8,128)(2,1)S(1)}, bf16[256,512]{1,0:T(8,128)(2,1)S(1)}, u32[]{:S(2)}, u32[]{:S(2)}) collective-permute-start(bf16[256,512]{1,0:T(8,128)(2,1)S(1)} %add_convert_fusion.1), channel_id=1, source_target_pairs={{0,3},{1,0},{2,1},{3,2},{4,7},{5,4},{6,5},{7,6},{8,11},{9,8},{10,9... | collective-permute-start | bytes 786440 | tf_op jit(solution)/shard_map/ppermute | solution.py:212
  195.6 4.7 %collective-permute-start.17 = (bf16[256,768]{1,0:T(8,128)(2,1)S(1)}, bf16[256,768]{1,0:T(8,128)(2,1)S(1)}, u32[]{:S(2)}, u32[]{:S(2)}) collective-permute-start(bf16[256,768]{1,0:T(8,128)(2,1)S(1)} %bitcast.38), channel_id=1, source_target_pairs={{0,4},{4,0},{8,12},{12,8},{16,20},{20,16},{24,28},{28,24},{1,5},{5... | collective-permute-start | bytes 1179656 | tf_op jit(solution)/shard_map/ppermute | solution.py:273

commit v6 on v5

--- a/solution.py
+++ b/solution.py
@@ -22,6 +22,106 @@
 VMEM = pl.BlockSpec(memory_space=pltpu.VMEM)
 SMEM = pl.BlockSpec(memory_space=pltpu.SMEM)
 HBM = pl.BlockSpec(memory_space=pltpu.HBM)
+
+
+def slots_of(page_t, rows_dev, owners, capacity):
+    width_k, targets = page_t.shape
+    shift = rows_dev.bit_length() - 1
+    low_bits = 6
+    low_mask = (1 << low_bits) - 1
+
+    def kernel(page_ref, request_ref, slot_ref, lhs, rhs):
+        page = page_ref[...]
+        owner = lax.shift_right_logical(page, jnp.int32(shift))
+        row = page & (rows_dev - 1)
+        high = lax.shift_right_logical(row, jnp.int32(low_bits)).astype(F32)
+        low = (row & low_mask).astype(F32)
+        owner_id = lax.broadcasted_iota(jnp.int32, (owners, targets), 0)
+        count = jnp.zeros((owners, targets), F32)
+        for k in range(width_k):
+            match = (owner[k : k + 1] == owner_id).astype(F32)
+            count += match
+            lhs[:, k * targets : (k + 1) * targets] = match.astype(BF)
+        count = count.astype(BF)
+
+        def before(size):
+            first = lax.broadcasted_iota(jnp.int32, (size, size), 0)
+            return first, lax.broadcasted_iota(jnp.int32, (size, size), 1)
+
+        first, second = before(targets)
+        earlier = dot(count, (first < second).astype(F32).astype(BF))
+        first, second = before(owners)
+        smaller = dot((second < first).astype(F32).astype(BF), count)
+        start = earlier - smaller
+        slot_id = lax.broadcasted_iota(jnp.int32, (capacity, targets), 0)
+        for k in range(width_k):
+            mine = jnp.where(owner[k : k + 1] == owner_id, start, 0.0)
+            slot = jnp.sum(mine, axis=0, keepdims=True).astype(jnp.int32) + k
+            slot_ref[k : k + 1] = slot
+            hit = slot == slot_id
+            at = slice(k * targets, (k + 1) * targets)
+            rhs[:capacity, at] = jnp.where(hit, high[k : k + 1], 0.0).astype(BF)
+            rhs[capacity:, at] = jnp.where(hit, low[k : k + 1], 0.0).astype(BF)
+        both = dot(lhs[...], rhs[...], 1, 1)
+        request = both[:, :capacity] * float(1 << low_bits) + both[:, capacity:]
+        request_ref[...] = request.astype(jnp.int32)
+
+    entries = width_k * targets
+    return pl.pallas_call(
+        kernel,
+        out_shape=[
+            jax.ShapeDtypeStruct((owners, capacity), jnp.int32),
+            jax.ShapeDtypeStruct((width_k, targets), jnp.int32),
+        ],
+        in_specs=[VMEM],
+        out_specs=[VMEM] * 2,
+        scratch_shapes=[
+            pltpu.VMEM((owners, entries), BF),
+            pltpu.VMEM((2 * capacity, entries), BF),
+        ],
+        compiler_params=pltpu.CompilerParams(vmem_limit_bytes=24 * 2**20),
+    )(page_t)
+
+
+def gather(features, asked, first_slot, share):
+    rows_dev, width_f = features.shape
+    askers = asked.shape[0]
+    chunk = 512
+    chunks = rows_dev // chunk
+
+    def kernel(first_ref, asked_ref, features_ref, out_ref, wide, narrow, sems):
+        copies = []
+        for i in range(chunks):
+            at = pl.ds(i * chunk, chunk)
+            copies.append(
+                pltpu.make_async_copy(features_ref.at[at, :], narrow.at[at, :], sems.at[i])
+            )
+        for copy in copies:
+            copy.start()
+        for i, copy in enumerate(copies):
+            copy.wait()
+            at = pl.ds(i * chunk, chunk)
+            wide[at, :] = narrow[at, :].astype(F32)
+        first = first_ref[0]
+
+        @pl.loop(0, askers)
+        def _(i):
+            rows = [wide[pl.ds(asked_ref[i, first + j], 1), :] for j in range(share)]
+            at = pl.ds(pl.multiple_of(i * share, share), share)
+            out_ref[at, :] = jnp.concatenate(rows, axis=0).astype(BF)
+
+    return pl.pallas_call(
+        kernel,
+        out_shape=jax.ShapeDtypeStruct((askers * share, width_f), BF),
+        in_specs=[SMEM, SMEM, HBM],
+        out_specs=VMEM,
+        scratch_shapes=[
+            pltpu.VMEM((rows_dev, width_f), F32),
+            pltpu.VMEM((rows_dev, width_f), BF),
+            pltpu.SemaphoreType.DMA((chunks,)),
+        ],
+        compiler_params=pltpu.CompilerParams(vmem_limit_bytes=32 * 2**20),
+    )(first_slot, asked, pltpu.with_memory_space_constraint(features, pltpu.HBM))
 
 
 def middle(parts, labels, hidden, w_boths, core):
@@ -105,26 +205,23 @@
         spread_copy.start()
         mine = pl.multiple_of(core_ref[0] * half, half)
         other = pl.multiple_of((1 - core_ref[0]) * half, half)
+        for source, target, sem in zip(turned, turned_refs, turned_sems):
+
+            @pl.loop(0, slots // block)
+            def _(j, source=source):
+                at = pl.ds(pl.multiple_of(j * block, block), block)
+                flat = rows_ref[at, :].T
+                source[pl.ds(mine, half), at] = flat[:half]
+                source[pl.ds(other, half), at] = flat[half:]
+
+            pltpu.make_async_copy(source, target, sem).start()
         for i in range(count):
             pltpu.make_async_copy(
                 w_refs[i].at[:, pl.ds(0, units)], w_all.at[i], w_sems.at[i]
             ).wait()
 
-            @pl.loop(0, slots // block)
-            def _(j, i=i):
-                at = pl.ds(pl.multiple_of(j * block, block), block)
-                value = rows_ref[at, :]
-                active_all[i, at, :] = jnp.maximum(dot(value, w_all[i]), 0.0).astype(BF)
-                if i == count - 1:
-                    for ref in turned:
-                        flat = value.T
-                        ref[pl.ds(mine, half), at] = flat[:half]
-                        ref[pl.ds(other, half), at] = flat[half:]
-
+            active_all[i] = jnp.maximum(dot(rows_ref[...], w_all[i]), 0.0).astype(BF)
             pltpu.make_async_copy(active_all.at[i], active_refs[i], out_sems.at[i]).start()
-            if i == count - 1:
-                for source, target, sem in zip(turned, turned_refs, turned_sems):
-                    pltpu.make_async_copy(source, target, sem).start()
             if i == 0:
                 spread_copy.wait()
             hidden_refs[i][...] = dot(spread_all[...], active_all[i]).astype(out_type)
@@ -162,22 +259,22 @@
     )(core, rows, *(pltpu.with_memory_space_constraint(x, pltpu.HBM) for x in (spread, *w_boths)))
 
 
-def backward(spread_t, d_hidden, active, rows_t):
+def backward(spread_t, d_hidden, active, rows_t, arrived):
     slots, targets = spread_t.shape
     units = d_hidden.shape[1]
     width_f = rows_t.shape[0]
     half = width_f // 2
-    block = 256
-
-    def kernel(spread_ref, d_hidden_ref, active_ref, rows_ref, own_ref, other_ref):
-        @pl.loop(0, units // block)
-        def _(i):
-            at = pl.ds(pl.multiple_of(i * block, block), block)
-            scattered = dot(spread_ref[...], d_hidden_ref[:, at]).astype(BF)
-            d_pre = jnp.where(active_ref[:, at] > 0, scattered, jnp.zeros_like(scattered))
-            total = dot(rows_ref[...], d_pre)
-            own_ref[:, at] = total[:half]
-            other_ref[:, at] = total[half:].astype(BF)
+
+    def kernel(spread_ref, d_hidden_ref, active_ref, rows_ref, *refs):
+        own_ref, other_ref = refs[-2:]
+        scattered = dot(spread_ref[...], d_hidden_ref[...]).astype(BF)
+        d_pre = jnp.where(active_ref[...] > 0, scattered, jnp.zeros_like(scattered))
+        total = dot(rows_ref[...], d_pre)
+        own = total[:half]
+        for ref in refs[:-2]:
+            own += ref[...].astype(F32)
+        own_ref[...] = own
+        other_ref[...] = total[half:].astype(BF)
 
     return pl.pallas_call(
         kernel,
@@ -185,7 +282,7 @@
             jax.ShapeDtypeStruct((half, units), F32),
             jax.ShapeDtypeStruct((half, units), BF),
         ],
-        in_specs=[VMEM] * 4,
+        in_specs=[VMEM] * (4 + len(arrived)),
         out_specs=[VMEM] * 2,
         compiler_params=pltpu.CompilerParams(vmem_limit_bytes=24 * 2**20),
         cost_estimate=pl.CostEstimate(
@@ -193,7 +290,7 @@
             bytes_accessed=2 * units,
             transcendentals=0,
         ),
-    )(spread_t, d_hidden, active, rows_t)
+    )(spread_t, d_hidden, active, rows_t, *arrived)
 
 
 def body(features, nbr_page, nbr_weight, labels, w_one, w_two):
@@ -217,19 +314,16 @@
     for step in steps[:-1]:
         w_boths[step] = to_mlp(w_both, -step)
 
+    requests, slot_ids = slots_of(nbr_page.T, rows_dev, owners, capacity)
+    asked = exchange(requests, ("own", "col"))
+    fetched = gather(features, asked, (me * share).reshape(1), share)
+    fetched = fetched.reshape(owners, share, width_f)
+    received = exchange(fetched, ("own", "col")).reshape(owners * share, width_f)
+
+    slot_ids = slot_ids.T
     owner_range = jnp.arange(owners, dtype=jnp.int32)
-    owner_ids = nbr_page // rows_dev
-    local_row = nbr_page % rows_dev
-    matches = owner_ids[:, :, None] == owner_range[None, None, :]
-    row_count = jnp.sum(matches.astype(F32), axis=1)
     t_range = jnp.arange(targets)
-    earlier = dot((t_range[:, None] > t_range[None, :]).astype(BF), row_count.astype(BF))
-    before = dot(row_count.astype(BF), (owner_range[:, None] < owner_range[None, :]).astype(BF))
-    first_slot = earlier - before
-    slot_ids = (
-        jnp.sum(matches.astype(F32) * first_slot[:, None, :], axis=2).astype(jnp.int32)
-        + jnp.arange(width_k, dtype=jnp.int32)[None, :]
-    )
+    matches = (nbr_page // rows_dev)[:, :, None] == owner_range[None, None, :]
     by_owner = matches.astype(BF).reshape(entries, owners)
     in_slot = slot_ids[:, :, None] == jnp.arange(capacity, dtype=jnp.int32)[None, None, :]
 
@@ -237,14 +331,8 @@
         spread_out = jnp.where(in_slot, values.astype(BF)[:, :, None], jnp.zeros((), BF))
         return dot(by_owner, spread_out.reshape(entries, capacity), 0, 0)
 
-    requests = (place(local_row // 64) * 64.0 + place(local_row % 64)).astype(jnp.int32)
     slot_weight = place(nbr_weight)
     slot_target = place(jnp.broadcast_to(t_range[:, None], (targets, width_k)))
-
-    asked = exchange(requests, ("own", "col"))
-    asked = lax.dynamic_slice_in_dim(asked, me * share, share, 1)
-    fetched = features[asked]
-    received = exchange(fetched, ("own", "col")).reshape(owners * share, width_f)
 
     my_weight = lax.dynamic_slice_in_dim(slot_weight, me * share, share, 1).reshape(1, -1)
     my_target = lax.dynamic_slice_in_dim(slot_target, me * share, share, 1).reshape(1, -1)
@@ -284,14 +372,11 @@
             arrived.append(to_mlp(grad_one[0], steps[0]))
         if i == 3:
             arrived += [to_mlp(g, s) for g, s in zip(grad_one[1:], steps[1:])]
-            d_slice, arrived[0] = lax.optimization_barrier((d_slice, arrived[0]))
-        mine, other = backward(spread_t, d_slice, active[step], rows_t)
+        mine, other = backward(spread_t, d_slice, active[step], rows_t, arrived if i == 3 else [])
         mine += partner(other).astype(F32)
         grad_one.append(mine.astype(BF) if step else mine)
     grad_two = own_two + partner(other_two).astype(F32)
     grad_one = grad_one[-1]
-    for value in arrived:
-        grad_one += value.astype(F32)
     both = jnp.concatenate([grad_one, grad_two], axis=1).astype(BF)
     chips = owners // 2
     groups = [[2 * i + c for i in range(chips)] for c in (0, 1)]

time: 203 us -> 197 us (0.970)
  local copies, waits for them, and re-layouts: 18 us -> 6.53 us
  Pallas kernels: 26.7 us -> 34.7 us
  matrix products: 7.6 us -> 1.73 us
  waiting for transfers between devices: 63 us -> 67.2 us
    pallas_call x0 -> x2, Pallas kernels: none -> 13.9 us  [the longest x1 11.7 us: gather(): pl.pallas_call(kernel, out_shape=jax.ShapeDtypeStruct((askers * share, wi...]
    gather x1 -> x0, local copies, waits for them, and re-layouts: 12 us -> none  [body(): fetched = features[asked]]
    dot_general x7 -> x3, matrix products: 7.6 us -> 1.73 us  [dot(): lax.dot_general(a, b, (((ca,), (cb,)), ((), ())), preferred_element_type=...]
    ppermute x12, waiting for transfers between devices: 41.8 us -> 44.9 us  [to_mlp(): lax.ppermute(x, 'mlp', [(j, (j + step) % mlp_n) for j in range(mlp_n)])]
    pallas_call x4, Pallas kernels: 10.1 us -> 7.06 us  [backward(): pl.pallas_call(kernel, out_shape=[jax.ShapeDtypeStruct((half, units), F32...]
    pallas_call x2, Pallas kernels: 13.5 us -> 10.7 us  [forward(): pl.pallas_call(kernel, out_shape=shapes, in_specs=[SMEM, VMEM, HBM] + [HB...]
    unnamed x25 -> x29, local copies, waits for them, and re-layouts: 3.55 us -> 4.27 us
  transfers between devices with their start and end apart: 20 -> 20, of which waited for: 11 -> 12; matrix products, arithmetic and copies ran while one was open for 4% -> 3% of each run, Pallas kernels for 6% -> 5%
where the time goes in v6:
time: 197 us; the launch traced here: 196 us
  waiting for transfers between devices  67.2 us (34%)
  starting transfers between devices  45.1 us (23%)
  blocking collectives  36.9 us (19%)
  Pallas kernels  34.7 us (18%)
  local copies, waits for them, and re-layouts  6.53 us (3%)
  other arithmetic  3.11 us (2%)
    ppermute x12, waiting for transfers between devices, to_mlp(): lax.ppermute(x, 'mlp', [(j, (j + step) % mlp_n) for j in range(mlp_n)])  44.9 us
    all_to_all x2, blocking collectives, exchange(): lax.all_to_all(x, axes, split_axis=0, concat_axis=0, tiled=True, axis_ind...  36.9 us
    all_to_all x2, waiting for transfers between devices, exchange(): lax.all_to_all(x, axes, split_axis=0, concat_axis=0, tiled=True, axis_ind...  19.8 us
    all_to_all x2, starting transfers between devices, exchange(): lax.all_to_all(x, axes, split_axis=0, concat_axis=0, tiled=True, axis_ind...  17.9 us
    ppermute x12, starting transfers between devices, to_mlp(): lax.ppermute(x, 'mlp', [(j, (j + step) % mlp_n) for j in range(mlp_n)])  16.9 us
    pallas_call x1, Pallas kernels, gather(): pl.pallas_call(kernel, out_shape=jax.ShapeDtypeStruct((askers * share, wi...  11.7 us
    pallas_call x2, Pallas kernels, forward(): pl.pallas_call(kernel, out_shape=shapes, in_specs=[SMEM, VMEM, HBM] + [HB...  10.7 us
    ppermute x6, starting transfers between devices, partner(): return lax.ppermute(x, 'col', pairs)  10.3 us
  transfers between devices with their start and end apart: 20, of which 12 were waited for; matrix products, arithmetic and copies ran while one was open for 3% of the time, Pallas kernels for 5%

profile of v6, /device:TPU:1, one launch (start us, length us, event | category | flops | bytes accessed | tf_op | source)
XLA Modules:
  0.0 196.2 jit_solution(61335674783068068)
XLA Ops:
  0.6 0.7 copy-done.8
  1.3 2.1 %shard_map.77 = (s32[64,128]{1,0:T(8,128)}, s32[32,128]{1,0:T(8,128)S(1)}) custom-call(s32[32,128]{1,0:T(8,128)S(1)} %bitcast.27), custom_call_target="tpu_custom_call" | custom-call | tf_op jit(solution)/shard_map/pallas_call | solution.py:70
  3.5 13.0 %all-to-all-start = ((s32[64,1,128]{2,1,0:T(1,128)}), s32[64,1,128]{2,1,0:T(1,128)S(1)}, u32[]{:S(2)}, u32[]{:S(2)}) async-start(s32[64,1,128]{2,1,0:T(1,128)} %bitcast.7), calls=%async_computation | async-start | bytes 65536 | tf_op jit(solution)/shard_map/all_to_all | solution.py:17
  16.5 9.3 %all-to-all-done = s32[64,1,128]{2,1,0:T(1,128)S(1)} async-done(((s32[64,1,128]{2,1,0:T(1,128)}), s32[64,1,128]{2,1,0:T(1,128)S(1)}, u32[]{:S(2)}, u32[]{:S(2)}) %all-to-all-start) | async-done | bytes 32800 | tf_op jit(solution)/shard_map/all_to_all | solution.py:17
  25.8 11.7 %shard_map.78 = bf16[2048,512]{1,0:T(8,128)(2,1)} custom-call(s32[1]{0:T(128)} %bitcast.5.first_ref, s32[64,128]{1,0:T(8,128)S(1)} %bitcast.26, bf16[4096,512]{1,0:T(8,128)(2,1)} %features_ref.1), custom_call_target="tpu_custom_call" | custom-call | tf_op jit(solution)/shard_map/pallas_call | solution.py:113
  37.5 4.9 %all-to-all-start.1 = ((bf16[64,32,512]{2,1,0:T(8,128)(2,1)}), bf16[64,32,512]{2,1,0:T(8,128)(2,1)S(1)}, u32[]{:S(2)}, u32[]{:S(2)}) async-start(bf16[64,32,512]{2,1,0:T(8,128)(2,1)} %bitcast.9), calls=%async_computation.1 | async-start | bytes 4194304 | tf_op jit(solution)/shard_map/all_to_all | solution.py:17
  42.5 1.1 constant_dynamic-update-slice_fusion.1
  43.6 3.0 %collective-permute-start = (bf16[512,768]{1,0:T(8,128)(2,1)S(1)}, bf16[512,768]{1,0:T(8,128)(2,1)}, u32[]{:S(2)}, u32[]{:S(2)}) collective-permute-start(bf16[512,768]{1,0:T(8,128)(2,1)S(1)} %constant_dynamic-update-slice_fusion.refs_0_.refs_9_), channel_id=1, source_target_pairs={{0,2},{1,3},{2,0},{3,1},{4,6},{5,7},{6,4},{7,5},{8,10},{9,11},{10,... | collective-permute-start | bytes 2359304 | tf_op jit(solution)/shard_map/ppermute | solution.py:309
  46.6 0.8 collective-permute-start.1
  47.4 0.7 collective-permute-start.2
  48.1 0.4 convolution_bitcast_fusion.1
  48.6 0.1 copy.12
  48.7 0.1 convert_element_type.67
  48.8 0.4 convolution_bitcast_fusion
  49.2 0.1 copy.13
  49.3 0.1 broadcast_in_dim.59
  49.4 0.7 select_convert_fusion.spread_ref
  50.1 0.9 select_convert_fusion.1.spread_ref
  51.0 12.9 %collective-permute-done.refs_0_.refs_6_ = bf16[512,768]{1,0:T(8,128)(2,1)} collective-permute-done((bf16[512,768]{1,0:T(8,128)(2,1)S(1)}, bf16[512,768]{1,0:T(8,128)(2,1)}, u32[]{:S(2)}, u32[]{:S(2)}) %collective-permute-start) | collective-permute-done | bytes 786464 | tf_op jit(solution)/shard_map/ppermute | solution.py:309
  63.9 17.2 %collective-permute-done.1.refs_1_.refs_7_ = bf16[512,768]{1,0:T(8,128)(2,1)} collective-permute-done((bf16[512,768]{1,0:T(8,128)(2,1)S(1)}, bf16[512,768]{1,0:T(8,128)(2,1)}, u32[]{:S(2)}, u32[]{:S(2)}) %collective-permute-start.1) | collective-permute-done | bytes 786464 | tf_op jit(solution)/shard_map/ppermute | solution.py:309
  81.1 0.5 collective-permute-done.2.refs_2_.refs_8_
  81.7 10.5 %all-to-all-done.1 = bf16[64,32,512]{2,1,0:T(8,128)(2,1)S(1)} async-done(((bf16[64,32,512]{2,1,0:T(8,128)(2,1)}), bf16[64,32,512]{2,1,0:T(8,128)(2,1)S(1)}, u32[]{:S(2)}, u32[]{:S(2)}) %all-to-all-start.1) | async-done | bytes 2097184 | tf_op jit(solution)/shard_map/all_to_all | solution.py:17
  92.2 6.9 %shard_map.80 = (bf16[2048,512]{1,0:T(8,128)(2,1)}, bf16[2048,512]{1,0:T(8,128)(2,1)}, bf16[2048,512]{1,0:T(8,128)(2,1)}, bf16[128,512]{1,0:T(8,128)(2,1)S(1)}, ...) custom-call(s32[1]{0:T(128)} %bitcast.4.core_ref, bf16[2048,512]{1,0:T(8,128)(2,1)S(1)} %bitcast.24, ...), custom_call_target="tpu_custom_call" | custom-call | flops 4026531840 | bytes 4718592 | tf_op jit(solution)/shard_map/pallas_call | solution.py:238
  99.2 3.0 %collective-permute-start.3 = (bf16[128,512]{1,0:T(8,128)(2,1)S(1)}, bf16[128,512]{1,0:T(8,128)(2,1)S(1)}, u32[]{:S(2)}, u32[]{:S(2)}) collective-permute-start(bf16[128,512]{1,0:T(8,128)(2,1)S(1)} %get-tuple-element.36), channel_id=1, source_target_pairs={{0,2},{1,3},{2,0},{3,1},{4,6},{5,7},{6,4},{7,5},{8,10},{9,11},{10,... | collective-permute-start | bytes 393224 | tf_op jit(solution)/shard_map/ppermute | solution.py:309
  102.2 0.4 collective-permute-start.4
  102.6 2.3 %collective-permute-start.5 = (bf16[128,512]{1,0:T(8,128)(2,1)S(1)}, bf16[128,512]{1,0:T(8,128)(2,1)S(1)}, u32[]{:S(2)}, u32[]{:S(2)}) collective-permute-start(bf16[128,512]{1,0:T(8,128)(2,1)S(1)} %get-tuple-element.38), channel_id=1, source_target_pairs={{0,3},{1,0},{2,1},{3,2},{4,7},{5,4},{6,5},{7,6},{8,11},{9,8},{10,9... | collective-permute-start | bytes 393224 | tf_op jit(solution)/shard_map/ppermute | solution.py:309
  104.8 3.7 %shard_map.79 = (bf16[2048,512]{1,0:T(8,128)(2,1)}, f32[128,512]{1,0:T(8,128)S(1)}, bf16[512,2048]{1,0:T(8,128)(2,1)}) custom-call(s32[1]{0:T(128)} %bitcast.4.core_ref, bf16[2048,512]{1,0:T(8,128)(2,1)S(1)} %bitcast.25, bf16[128,2048]{1,0:T(8,128)(2,1)} %select_convert_fusion.1.spread_ref, bf16[512,768]{1,0:T(8,128)(2,1)} %copy-done.1), custom_call_target="tpu_custom_call" | custom-call | flops 1342177280 | bytes 4718592 | tf_op jit(solution)/shard_map/pallas_call | solution.py:238
  108.6 0.1 add_convert_fusion.5.refs_5_
  108.7 0.8 fusion.18.refs_0_
  109.6 0.7 collective-permute-start.6
  110.3 2.5 %collective-permute-start.7 = (f32[128,256]{1,0:T(8,128)}, f32[128,256]{1,0:T(8,128)}, u32[]{:S(2)}, u32[]{:S(2)}) collective-permute-start(f32[128,256]{1,0:T(8,128)} %fusion.18.refs_0_), channel_id=1, source_target_pairs={{0,1},{1,2},{2,3},{3,0},{4,5},{5,6},{6,7},{7,4},{8,9},{9,10},{10,1... | collective-permute-start | bytes 393224 | tf_op jit(solution)/shard_map/ppermute | solution.py:309
  112.8 0.2 collective-permute-start.8
  112.9 0.7 copy.15.refs_4_
  113.7 1.6 collective-permute-done.6.refs_1_
  115.3 1.3 collective-permute-done.7.refs_2_
  116.6 0.3 collective-permute-done.8.refs_3_
  116.9 0.8 copy-done.7
  117.8 3.1 %shard_map.81 = (f32[256,256]{1,0:T(8,128)S(1)}, bf16[256,256]{1,0:T(8,128)(2,1)S(1)}, bf16[128,512]{1,0:T(8,128)(2,1)S(1)}, bf16[128,512]{1,0:T(8,128)(2,1)S(1)...) custom-call(s32[1]{0:T(128)} %bitcast.4.core_ref, f32[128,256]{1,0:T(8,128)} %fusion.18.refs_0_, ...), custom_call_target="tpu_custom_call" | custom-call | flops 167772160 | bytes 4194304 | tf_op jit(solution)/shard_map/pallas_call | solution.py:163
  120.9 1.6 copy-done.5
  122.5 1.8 shard_map.82
  124.2 4.3 %collective-permute-start.9 = (bf16[256,512]{1,0:T(8,128)(2,1)S(1)}, bf16[256,512]{1,0:T(8,128)(2,1)S(1)}, u32[]{:S(2)}, u32[]{:S(2)}) collective-permute-start(bf16[256,512]{1,0:T(8,128)(2,1)S(1)} %get-tuple-element.46), channel_id=1, source_target_pairs={{0,4},{4,0},{8,12},{12,8},{16,20},{20,16},{24,28},{28,24},{1,5},{5... | collective-permute-start | bytes 786440 | tf_op jit(solution)/shard_map/ppermute | solution.py:361
  128.6 1.8 shard_map.83
  130.3 0.1 collective-permute-start.11
  130.5 1.8 shard_map.84
  132.3 0.6 collective-permute-start.13
  132.9 0.1 add_convert_fusion.2
  133.0 0.1 collective-permute-start.12
  133.1 2.9 %collective-permute-start.10 = (bf16[256,512]{1,0:T(8,128)(2,1)S(1)}, bf16[256,512]{1,0:T(8,128)(2,1)S(1)}, u32[]{:S(2)}, u32[]{:S(2)}) collective-permute-start(bf16[256,512]{1,0:T(8,128)(2,1)S(1)} %add_convert_fusion.3), channel_id=1, source_target_pairs={{0,2},{1,3},{2,0},{3,1},{4,6},{5,7},{6,4},{7,5},{8,10},{9,11},{10,... | collective-permute-start | bytes 786440 | tf_op jit(solution)/shard_map/ppermute | solution.py:309
  136.1 0.3 collective-permute-start.14
  136.4 0.7 collective-permute-start.16
  137.1 5.1 %collective-permute-done.12.refs_1_ = bf16[256,512]{1,0:T(8,128)(2,1)S(1)} collective-permute-done((bf16[256,512]{1,0:T(8,128)(2,1)S(1)}, bf16[256,512]{1,0:T(8,128)(2,1)S(1)}, u32[]{:S(2)}, u32[]{:S(2)}) %collective-permute-start.12) | collective-permute-done | bytes 262176 | tf_op jit(solution)/shard_map/ppermute | solution.py:309
  142.2 5.9 %collective-permute-done.10.refs_0_ = bf16[256,512]{1,0:T(8,128)(2,1)S(1)} collective-permute-done((bf16[256,512]{1,0:T(8,128)(2,1)S(1)}, bf16[256,512]{1,0:T(8,128)(2,1)S(1)}, u32[]{:S(2)}, u32[]{:S(2)}) %collective-permute-start.10) | collective-permute-done | bytes 262176 | tf_op jit(solution)/shard_map/ppermute | solution.py:309
  148.1 1.8 shard_map.85
  149.9 1.2 collective-permute-start.15
  151.1 1.1 collective-permute-done.15
  152.2 0.1 fusion.12
  152.4 19.3 %all_to_all.26 = bf16[32,8,768]{2,1,0:T(8,128)(2,1)S(1)} all-to-all(bf16[32,8,768]{2,1,0:T(8,128)(2,1)S(1)} %pad_maximum_fusion), channel_id=1, replica_groups={{0,8,16,24,32,40,48,56,64,72,80,88,96,104,112,120,128,136,144,152,160,1..., dimensions={0} | all-to-all | bytes 786432 | tf_op jit(solution)/shard_map/all_to_all | solution.py:17
  171.6 0.1 reduce_sum.12
  171.7 17.6 %all_to_all.27 = bf16[32,8,768]{2,1,0:T(8,128)(2,1)S(1)} all-to-all(bf16[32,8,768]{2,1,0:T(8,128)(2,1)S(1)} %broadcast_in_dim.65), channel_id=1, replica_groups={{0,8,16,24,32,40,48,56,64,72,80,88,96,104,112,120,128,136,144,152,160,1..., dimensions={0} | all-to-all | bytes 786432 | tf_op jit(solution)/shard_map/all_to_all | solution.py:17
  189.4 3.4 %collective-permute-start.17 = (bf16[256,768]{1,0:T(8,128)(2,1)S(1)}, bf16[256,768]{1,0:T(8,128)(2,1)S(1)}, u32[]{:S(2)}, u32[]{:S(2)}) collective-permute-start(bf16[256,768]{1,0:T(8,128)(2,1)S(1)} %bitcast.30), channel_id=1, source_target_pairs={{0,4},{4,0},{8,12},{12,8},{16,20},{20,16},{24,28},{28,24},{1,5},{5... | collective-permute-start | bytes 1179656 | tf_op jit(solution)/shard_map/ppermute | solution.py:361
  192.8 1.3 collective-permute-done.17
  194.2 0.8 maximum_convert_fusion.1
  195.0 0.1 maximum_convert_fusion
  195.1 1.1 slice.8
  (44 shorter events, 0.5 us)
Async XLA Ops:
  0.6 0.7 copy-start.8
  3.5 22.3 %all-to-all-start = ((s32[64,1,128]{2,1,0:T(1,128)}), s32[64,1,128]{2,1,0:T(1,128)S(1)}, u32[]{:S(2)}, u32[]{:S(2)}) async-start(s32[64,1,128]{2,1,0:T(1,128)} %bitcast.7), calls=%async_computation | async-start | bytes 65536 | tf_op jit(solution)/shard_map/all_to_all | solution.py:17
  37.5 6.1 %copy-start.10 = (bf16[512,256]{1,0:T(8,128)(2,1)S(1)}, bf16[512,256]{1,0:T(8,128)(2,1)}, u32[]{:S(2)}) copy-start(bf16[512,256]{1,0:T(8,128)(2,1)} %param.11) | copy-start | bytes 786436
  37.5 10.6 %copy-start.9 = (s32[128,32]{0,1:T(8,128)S(1)}, s32[128,32]{0,1:T(8,128)}, u32[]{:S(2)}) copy-start(s32[128,32]{0,1:T(8,128)} %param.7) | copy-start | bytes 49156
  37.5 54.7 %all-to-all-start.1 = ((bf16[64,32,512]{2,1,0:T(8,128)(2,1)}), bf16[64,32,512]{2,1,0:T(8,128)(2,1)S(1)}, u32[]{:S(2)}, u32[]{:S(2)}) async-start(bf16[64,32,512]{2,1,0:T(8,128)(2,1)} %bitcast.9), calls=%async_computation.1 | async-start | bytes 4194304 | tf_op jit(solution)/shard_map/all_to_all | solution.py:17
  42.5 6.3 %copy-start.13 = (bf16[128,32]{0,1:T(8,128)(2,1)S(1)}, bf16[128,32]{0,1:T(8,128)(2,1)}, u32[]{:S(2)}) copy-start(bf16[128,32]{0,1:T(8,128)(2,1)} %param.8) | copy-start | bytes 24580
  43.6 5.6 %copy-start.1 = (bf16[512,768]{1,0:T(8,128)(2,1)}, bf16[512,768]{1,0:T(8,128)(2,1)S(1)}, u32[]{:S(2)}) copy-start(bf16[512,768]{1,0:T(8,128)(2,1)S(1)} %constant_dynamic-update-slice_fusion.refs_0_.refs_9_) | copy-start | bytes 2359300
  43.6 20.3 %collective-permute-start = (bf16[512,768]{1,0:T(8,128)(2,1)S(1)}, bf16[512,768]{1,0:T(8,128)(2,1)}, u32[]{:S(2)}, u32[]{:S(2)}) collective-permute-start(bf16[512,768]{1,0:T(8,128)(2,1)S(1)} %constant_dynamic-update-slice_fusion.refs_0_.refs_9_), channel_id=1, source_target_pairs={{0,2},{1,3},{2,0},{3,1},{4,6},{5,7},{6,4},{7,5},{8,10},{9,11},{10,... | collective-permute-start | bytes 2359304 | tf_op jit(solution)/shard_map/ppermute | solution.py:309
  46.6 34.5 %collective-permute-start.1 = (bf16[512,768]{1,0:T(8,128)(2,1)S(1)}, bf16[512,768]{1,0:T(8,128)(2,1)}, u32[]{:S(2)}, u32[]{:S(2)}) collective-permute-start(bf16[512,768]{1,0:T(8,128)(2,1)S(1)} %constant_dynamic-update-slice_fusion.refs_0_.refs_9_), channel_id=1, source_target_pairs={{0,3},{1,0},{2,1},{3,2},{4,7},{5,4},{6,5},{7,6},{8,11},{9,8},{10,9... | collective-permute-start | bytes 2359304 | tf_op jit(solution)/shard_map/ppermute | solution.py:309
  47.4 34.2 %collective-permute-start.2 = (bf16[512,768]{1,0:T(8,128)(2,1)S(1)}, bf16[512,768]{1,0:T(8,128)(2,1)}, u32[]{:S(2)}, u32[]{:S(2)}) collective-permute-start(bf16[512,768]{1,0:T(8,128)(2,1)S(1)} %constant_dynamic-update-slice_fusion.refs_0_.refs_9_), channel_id=1, source_target_pairs={{0,1},{1,2},{2,3},{3,0},{4,5},{5,6},{6,7},{7,4},{8,9},{9,10},{10,1... | collective-permute-start | bytes 2359304 | tf_op jit(solution)/shard_map/ppermute | solution.py:309
  99.2 9.4 %collective-permute-start.3 = (bf16[128,512]{1,0:T(8,128)(2,1)S(1)}, bf16[128,512]{1,0:T(8,128)(2,1)S(1)}, u32[]{:S(2)}, u32[]{:S(2)}) collective-permute-start(bf16[128,512]{1,0:T(8,128)(2,1)S(1)} %get-tuple-element.36), channel_id=1, source_target_pairs={{0,2},{1,3},{2,0},{3,1},{4,6},{5,7},{6,4},{7,5},{8,10},{9,11},{10,... | collective-permute-start | bytes 393224 | tf_op jit(solution)/shard_map/ppermute | solution.py:309
  102.2 6.4 %collective-permute-start.4 = (bf16[128,512]{1,0:T(8,128)(2,1)S(1)}, bf16[128,512]{1,0:T(8,128)(2,1)S(1)}, u32[]{:S(2)}, u32[]{:S(2)}) collective-permute-start(bf16[128,512]{1,0:T(8,128)(2,1)S(1)} %get-tuple-element.37), channel_id=1, source_target_pairs={{0,1},{1,2},{2,3},{3,0},{4,5},{5,6},{6,7},{7,4},{8,9},{9,10},{10,1... | collective-permute-start | bytes 393224 | tf_op jit(solution)/shard_map/ppermute | solution.py:309
  102.6 6.1 %copy-start.11 = (bf16[512,256]{1,0:T(8,128)(2,1)S(1)}, bf16[512,256]{1,0:T(8,128)(2,1)}, u32[]{:S(2)}) copy-start(bf16[512,256]{1,0:T(8,128)(2,1)} %param.11) | copy-start | bytes 786436
  102.6 10.4 %copy-start.12 = (s32[128]{0:T(128)S(1)}, s32[128]{0:T(128)}, u32[]{:S(2)}) copy-start(s32[128]{0:T(128)} %param.9) | copy-start | bytes 1540
  102.6 14.4 %copy-start.2 = (bf16[512,768]{1,0:T(8,128)(2,1)S(1)}, bf16[512,768]{1,0:T(8,128)(2,1)}, u32[]{:S(2)}) copy-start(bf16[512,768]{1,0:T(8,128)(2,1)} %copy-done.1) | copy-start | bytes 2359300
  102.6 6.1 %collective-permute-start.5 = (bf16[128,512]{1,0:T(8,128)(2,1)S(1)}, bf16[128,512]{1,0:T(8,128)(2,1)S(1)}, u32[]{:S(2)}, u32[]{:S(2)}) collective-permute-start(bf16[128,512]{1,0:T(8,128)(2,1)S(1)} %get-tuple-element.38), channel_id=1, source_target_pairs={{0,3},{1,0},{2,1},{3,2},{4,7},{5,4},{6,5},{7,6},{8,11},{9,8},{10,9... | collective-permute-start | bytes 393224 | tf_op jit(solution)/shard_map/ppermute | solution.py:309
  109.6 11.3 %copy-start = (bf16[512,2048]{1,0:T(8,128)(2,1)S(1)}, bf16[512,2048]{1,0:T(8,128)(2,1)}, u32[]{:S(2)}) copy-start(bf16[512,2048]{1,0:T(8,128)(2,1)} %get-tuple-element.41.rows_ref) | copy-start | bytes 6291460
  109.6 5.7 %collective-permute-start.6 = (f32[128,256]{1,0:T(8,128)}, f32[128,256]{1,0:T(8,128)}, u32[]{:S(2)}, u32[]{:S(2)}) collective-permute-start(f32[128,256]{1,0:T(8,128)} %fusion.18.refs_0_), channel_id=1, source_target_pairs={{0,2},{1,3},{2,0},{3,1},{4,6},{5,7},{6,4},{7,5},{8,10},{9,11},{10,... | collective-permute-start | bytes 393224 | tf_op jit(solution)/shard_map/ppermute | solution.py:309
  110.3 6.3 %collective-permute-start.7 = (f32[128,256]{1,0:T(8,128)}, f32[128,256]{1,0:T(8,128)}, u32[]{:S(2)}, u32[]{:S(2)}) collective-permute-start(f32[128,256]{1,0:T(8,128)} %fusion.18.refs_0_), channel_id=1, source_target_pairs={{0,1},{1,2},{2,3},{3,0},{4,5},{5,6},{6,7},{7,4},{8,9},{9,10},{10,1... | collective-permute-start | bytes 393224 | tf_op jit(solution)/shard_map/ppermute | solution.py:309
  112.8 4.1 %collective-permute-start.8 = (f32[128,256]{1,0:T(8,128)}, f32[128,256]{1,0:T(8,128)}, u32[]{:S(2)}, u32[]{:S(2)}) collective-permute-start(f32[128,256]{1,0:T(8,128)} %fusion.18.refs_0_), channel_id=1, source_target_pairs={{0,3},{1,0},{2,1},{3,2},{4,7},{5,4},{6,5},{7,6},{8,11},{9,8},{10,9... | collective-permute-start | bytes 393224 | tf_op jit(solution)/shard_map/ppermute | solution.py:309
  116.9 0.8 copy-start.7
  120.9 1.6 copy-start.5
  122.5 6.1 %copy-start.4 = (bf16[2048,512]{1,0:T(8,128)(2,1)S(1)}, bf16[2048,512]{1,0:T(8,128)(2,1)}, u32[]{:S(2)}) copy-start(bf16[2048,512]{1,0:T(8,128)(2,1)} %get-tuple-element.49.active_ref) | copy-start | bytes 6291460
  124.2 6.2 %collective-permute-start.9 = (bf16[256,512]{1,0:T(8,128)(2,1)S(1)}, bf16[256,512]{1,0:T(8,128)(2,1)S(1)}, u32[]{:S(2)}, u32[]{:S(2)}) collective-permute-start(bf16[256,512]{1,0:T(8,128)(2,1)S(1)} %get-tuple-element.46), channel_id=1, source_target_pairs={{0,4},{4,0},{8,12},{12,8},{16,20},{20,16},{24,28},{28,24},{1,5},{5... | collective-permute-start | bytes 786440 | tf_op jit(solution)/shard_map/ppermute | solution.py:361
  128.6 2.0 %copy-start.3 = (bf16[2048,512]{1,0:T(8,128)(2,1)S(1)}, bf16[2048,512]{1,0:T(8,128)(2,1)}, u32[]{:S(2)}) copy-start(bf16[2048,512]{1,0:T(8,128)(2,1)} %get-tuple-element.53.active_ref) | copy-start | bytes 6291460
  130.3 2.6 %collective-permute-start.11 = (bf16[256,512]{1,0:T(8,128)(2,1)S(1)}, bf16[256,512]{1,0:T(8,128)(2,1)S(1)}, u32[]{:S(2)}, u32[]{:S(2)}) collective-permute-start(bf16[256,512]{1,0:T(8,128)(2,1)S(1)} %get-tuple-element.51), channel_id=1, source_target_pairs={{0,4},{4,0},{8,12},{12,8},{16,20},{20,16},{24,28},{28,24},{1,5},{5... | collective-permute-start | bytes 786440 | tf_op jit(solution)/shard_map/ppermute | solution.py:361
  132.3 15.8 %copy-start.6 = (bf16[2048,512]{1,0:T(8,128)(2,1)S(1)}, bf16[2048,512]{1,0:T(8,128)(2,1)}, u32[]{:S(2)}) copy-start(bf16[2048,512]{1,0:T(8,128)(2,1)} %get-tuple-element.40.active_ref) | copy-start | bytes 6291460
  132.3 3.7 %collective-permute-start.13 = (bf16[256,512]{1,0:T(8,128)(2,1)S(1)}, bf16[256,512]{1,0:T(8,128)(2,1)S(1)}, u32[]{:S(2)}, u32[]{:S(2)}) collective-permute-start(bf16[256,512]{1,0:T(8,128)(2,1)S(1)} %get-tuple-element.55), channel_id=1, source_target_pairs={{0,4},{4,0},{8,12},{12,8},{16,20},{20,16},{24,28},{28,24},{1,5},{5... | collective-permute-start | bytes 786440 | tf_op jit(solution)/shard_map/ppermute | solution.py:361
  133.0 9.2 %collective-permute-start.12 = (bf16[256,512]{1,0:T(8,128)(2,1)S(1)}, bf16[256,512]{1,0:T(8,128)(2,1)S(1)}, u32[]{:S(2)}, u32[]{:S(2)}) collective-permute-start(bf16[256,512]{1,0:T(8,128)(2,1)S(1)} %add_convert_fusion.2), channel_id=1, source_target_pairs={{0,1},{1,2},{2,3},{3,0},{4,5},{5,6},{6,7},{7,4},{8,9},{9,10},{10,1... | collective-permute-start | bytes 786440 | tf_op jit(solution)/shard_map/ppermute | solution.py:309
  133.1 15.0 %collective-permute-start.10 = (bf16[256,512]{1,0:T(8,128)(2,1)S(1)}, bf16[256,512]{1,0:T(8,128)(2,1)S(1)}, u32[]{:S(2)}, u32[]{:S(2)}) collective-permute-start(bf16[256,512]{1,0:T(8,128)(2,1)S(1)} %add_convert_fusion.3), channel_id=1, source_target_pairs={{0,2},{1,3},{2,0},{3,1},{4,6},{5,7},{6,4},{7,5},{8,10},{9,11},{10,... | collective-permute-start | bytes 786440 | tf_op jit(solution)/shard_map/ppermute | solution.py:309
  136.1 12.0 %collective-permute-start.14 = (bf16[256,512]{1,0:T(8,128)(2,1)S(1)}, bf16[256,512]{1,0:T(8,128)(2,1)S(1)}, u32[]{:S(2)}, u32[]{:S(2)}) collective-permute-start(bf16[256,512]{1,0:T(8,128)(2,1)S(1)} %add_convert_fusion.1), channel_id=1, source_target_pairs={{0,3},{1,0},{2,1},{3,2},{4,7},{5,4},{6,5},{7,6},{8,11},{9,8},{10,9... | collective-permute-start | bytes 786440 | tf_op jit(solution)/shard_map/ppermute | solution.py:309
  136.4 14.7 %collective-permute-start.16 = (bf16[256,256]{1,0:T(8,128)(2,1)S(1)}, bf16[256,256]{1,0:T(8,128)(2,1)S(1)}, u32[]{:S(2)}, u32[]{:S(2)}) collective-permute-start(bf16[256,256]{1,0:T(8,128)(2,1)S(1)} %get-tuple-element.59), channel_id=1, source_target_pairs={{0,4},{4,0},{8,12},{12,8},{16,20},{20,16},{24,28},{28,24},{1,5},{5... | collective-permute-start | bytes 393224 | tf_op jit(solution)/shard_map/ppermute | solution.py:361
  149.9 2.4 %collective-permute-start.15 = (bf16[256,512]{1,0:T(8,128)(2,1)S(1)}, bf16[256,512]{1,0:T(8,128)(2,1)S(1)}, u32[]{:S(2)}, u32[]{:S(2)}) collective-permute-start(bf16[256,512]{1,0:T(8,128)(2,1)S(1)} %get-tuple-element.57), channel_id=1, source_target_pairs={{0,4},{4,0},{8,12},{12,8},{16,20},{20,16},{24,28},{28,24},{1,5},{5... | collective-permute-start | bytes 786440 | tf_op jit(solution)/shard_map/ppermute | solution.py:361
  189.4 4.7 %collective-permute-start.17 = (bf16[256,768]{1,0:T(8,128)(2,1)S(1)}, bf16[256,768]{1,0:T(8,128)(2,1)S(1)}, u32[]{:S(2)}, u32[]{:S(2)}) collective-permute-start(bf16[256,768]{1,0:T(8,128)(2,1)S(1)} %bitcast.30), channel_id=1, source_target_pairs={{0,4},{4,0},{8,12},{12,8},{16,20},{20,16},{24,28},{28,24},{1,5},{5... | collective-permute-start | bytes 1179656 | tf_op jit(solution)/shard_map/ppermute | solution.py:361

commit v7 on v6

--- a/solution.py
+++ b/solution.py
@@ -83,13 +83,14 @@
     )(page_t)
 
 
-def gather(features, asked, first_slot, share):
+def gather(features, asked):
     rows_dev, width_f = features.shape
-    askers = asked.shape[0]
+    (count,) = asked.shape
+    group = 32
     chunk = 512
     chunks = rows_dev // chunk
 
-    def kernel(first_ref, asked_ref, features_ref, out_ref, wide, narrow, sems):
+    def kernel(asked_ref, features_ref, out_ref, wide, narrow, sems):
         copies = []
         for i in range(chunks):
             at = pl.ds(i * chunk, chunk)
@@ -102,18 +103,17 @@
             copy.wait()
             at = pl.ds(i * chunk, chunk)
             wide[at, :] = narrow[at, :].astype(F32)
-        first = first_ref[0]
-
-        @pl.loop(0, askers)
+
+        @pl.loop(0, count // group)
         def _(i):
-            rows = [wide[pl.ds(asked_ref[i, first + j], 1), :] for j in range(share)]
-            at = pl.ds(pl.multiple_of(i * share, share), share)
-            out_ref[at, :] = jnp.concatenate(rows, axis=0).astype(BF)
-
-    return pl.pallas_call(
-        kernel,
-        out_shape=jax.ShapeDtypeStruct((askers * share, width_f), BF),
-        in_specs=[SMEM, SMEM, HBM],
+            base = pl.multiple_of(i * group, group)
+            rows = [wide[pl.ds(asked_ref[base + j], 1), :] for j in range(group)]
+            out_ref[pl.ds(base, group), :] = jnp.concatenate(rows, axis=0).astype(BF)
+
+    return pl.pallas_call(
+        kernel,
+        out_shape=jax.ShapeDtypeStruct((count, width_f), BF),
+        in_specs=[SMEM, HBM],
         out_specs=VMEM,
         scratch_shapes=[
             pltpu.VMEM((rows_dev, width_f), F32),
@@ -121,65 +121,67 @@
             pltpu.SemaphoreType.DMA((chunks,)),
         ],
         compiler_params=pltpu.CompilerParams(vmem_limit_bytes=32 * 2**20),
-    )(first_slot, asked, pltpu.with_memory_space_constraint(features, pltpu.HBM))
-
-
-def middle(parts, labels, hidden, w_boths, core):
+    )(asked, pltpu.with_memory_space_constraint(features, pltpu.HBM))
+
+
+def slice_grad(spread_ref, d_hidden, active_ref, rows_ref, own_ref, other_ref):
+    half = own_ref.shape[0]
+    scattered = dot(spread_ref[...], d_hidden).astype(BF)
+    d_pre = jnp.where(active_ref[...] > 0, scattered, jnp.zeros_like(scattered))
+    total = dot(rows_ref[...], d_pre)
+    own_ref[...] = total[:half]
+    other_ref[...] = total[half:].astype(BF)
+
+
+def middle(parts, labels, hidden, w_twos, core, spread_t, active, rows_t):
     count = len(parts)
     targets, classes = parts[0].shape
     units = hidden.shape[1]
     half = units // 2
+    half_f = rows_t.shape[0] // 2
 
     def kernel(core_ref, *refs):
         part_refs, refs = refs[:count], refs[count:]
         labels_ref, hidden_ref = refs[:2]
         w_refs, refs = refs[2 : 2 + count], refs[2 + count :]
-        own_ref, other_ref = refs[:2]
-        d_hidden_refs = refs[2 : 2 + count]
-        w_all, sems = refs[2 + count :]
-        copies = [
-            pltpu.make_async_copy(w_refs[i].at[:, pl.ds(units, classes)], w_all.at[i], sems.at[i])
-            for i in range(count)
-        ]
-        for copy in copies:
-            copy.start()
+        spread_ref, active_ref, rows_ref, own_ref, other_ref, own_two, other_two = refs[:7]
+        d_hidden_refs = refs[7:]
         logits = part_refs[0][...]
         for part in part_refs[1:]:
             logits += part[...]
         exponent = jnp.exp(logits)
         probability = exponent / jnp.sum(exponent, axis=1, keepdims=True)
         ids = lax.broadcasted_iota(jnp.int32, (targets, classes), 1)
-        onehot = (labels_ref[...] == ids).astype(F32)
-        d_logits = (probability - onehot).astype(BF)
+        label = jnp.broadcast_to(labels_ref[...], (targets, targets)).T[:, :1]
+        d_logits = (probability - (label == ids).astype(F32)).astype(BF)
+        d_first = dot(d_logits, w_refs[0][...], 1, 1).astype(BF)
+        for w_ref, out in zip(w_refs[1:], d_hidden_refs):
+            out[...] = dot(d_logits, w_ref[...], 1, 1).astype(BF)
+        slice_grad(spread_ref, d_first, active_ref, rows_ref, own_ref, other_ref)
         both = dot(hidden_ref[...], d_logits, 0, 0)
         swap = core_ref[0] != 0
         low, high = both[:half], both[half:]
-        own_ref[...] = jnp.where(swap, high, low)
-        other_ref[...] = jnp.where(swap, low, high).astype(BF)
-        for i in range(count):
-            copies[i].wait()
-            d_hidden_refs[i][...] = dot(d_logits, w_all[i], 1, 1).astype(BF)
+        own_two[...] = jnp.where(swap, high, low)
+        other_two[...] = jnp.where(swap, low, high).astype(BF)
 
     return pl.pallas_call(
         kernel,
         out_shape=[
+            jax.ShapeDtypeStruct((half_f, units), F32),
+            jax.ShapeDtypeStruct((half_f, units), BF),
             jax.ShapeDtypeStruct((half, classes), F32),
             jax.ShapeDtypeStruct((half, classes), BF),
         ]
-        + [jax.ShapeDtypeStruct((targets, units), BF)] * count,
-        in_specs=[SMEM] + [VMEM] * (count + 2) + [HBM] * count,
-        out_specs=[VMEM] * (2 + count),
-        scratch_shapes=[
-            pltpu.VMEM((count, units, classes), BF),
-            pltpu.SemaphoreType.DMA((count,)),
-        ],
+        + [jax.ShapeDtypeStruct((targets, units), BF)] * (count - 1),
+        in_specs=[SMEM] + [VMEM] * (2 * count + 5),
+        out_specs=[VMEM] * (3 + count),
         compiler_params=pltpu.CompilerParams(vmem_limit_bytes=24 * 2**20),
         cost_estimate=pl.CostEstimate(
             flops=2 * targets * classes * units * (count + 1),
             bytes_accessed=4 * 2**20,
             transcendentals=targets * classes,
         ),
-    )(core, *parts, labels, hidden, *w_boths)
+    )(core, *parts, labels, hidden, *w_twos, spread_t, active, rows_t)
 
 
 def forward(rows, w_boths, spread, core, out_type, turn):
@@ -259,22 +261,12 @@
     )(core, rows, *(pltpu.with_memory_space_constraint(x, pltpu.HBM) for x in (spread, *w_boths)))
 
 
-def backward(spread_t, d_hidden, active, rows_t, arrived):
-    slots, targets = spread_t.shape
+def backward(spread_t, d_hidden, active, rows_t):
     units = d_hidden.shape[1]
-    width_f = rows_t.shape[0]
-    half = width_f // 2
-
-    def kernel(spread_ref, d_hidden_ref, active_ref, rows_ref, *refs):
-        own_ref, other_ref = refs[-2:]
-        scattered = dot(spread_ref[...], d_hidden_ref[...]).astype(BF)
-        d_pre = jnp.where(active_ref[...] > 0, scattered, jnp.zeros_like(scattered))
-        total = dot(rows_ref[...], d_pre)
-        own = total[:half]
-        for ref in refs[:-2]:
-            own += ref[...].astype(F32)
-        own_ref[...] = own
-        other_ref[...] = total[half:].astype(BF)
+    half = rows_t.shape[0] // 2
+
+    def kernel(spread_ref, d_hidden_ref, *refs):
+        slice_grad(spread_ref, d_hidden_ref[...], *refs)
 
     return pl.pallas_call(
         kernel,
@@ -282,15 +274,39 @@
             jax.ShapeDtypeStruct((half, units), F32),
             jax.ShapeDtypeStruct((half, units), BF),
         ],
-        in_specs=[VMEM] * (4 + len(arrived)),
+        in_specs=[VMEM] * 4,
         out_specs=[VMEM] * 2,
         compiler_params=pltpu.CompilerParams(vmem_limit_bytes=24 * 2**20),
         cost_estimate=pl.CostEstimate(
-            flops=2 * units,
-            bytes_accessed=2 * units,
-            transcendentals=0,
+            flops=2 * units, bytes_accessed=2 * units, transcendentals=0
         ),
-    )(spread_t, d_hidden, active, rows_t, *arrived)
+    )(spread_t, d_hidden, active, rows_t)
+
+
+def outputs(own, other, core, units):
+    half, width = own.shape
+
+    def kernel(core_ref, own_ref, other_ref, one_ref, two_ref, wide, sems):
+        copies = []
+        for i, ref in enumerate((own_ref, other_ref)):
+            wide[i] = ref[...].astype(F32)
+            place = core_ref[0] if i == 0 else 1 - core_ref[0]
+            at = pl.ds(pl.multiple_of(place * half, half), half)
+            for j, (out, first) in enumerate(((one_ref, 0), (two_ref, units))):
+                source = wide.at[i, :, pl.ds(first, out.shape[1])]
+                copies.append(pltpu.make_async_copy(source, out.at[at, :], sems.at[2 * i + j]))
+                copies[-1].start()
+        for copy in copies:
+            copy.wait()
+
+    return pl.pallas_call(
+        kernel,
+        out_shape=[pltpu.HBM((2 * half, units), F32), pltpu.HBM((2 * half, width - units), F32)],
+        in_specs=[SMEM, VMEM, VMEM],
+        out_specs=[HBM, HBM],
+        scratch_shapes=[pltpu.VMEM((2, half, width), F32), pltpu.SemaphoreType.DMA((4,))],
+        compiler_params=pltpu.CompilerParams(vmem_limit_bytes=24 * 2**20),
+    )(core, own, other)
 
 
 def body(features, nbr_page, nbr_weight, labels, w_one, w_two):
@@ -316,7 +332,8 @@
 
     requests, slot_ids = slots_of(nbr_page.T, rows_dev, owners, capacity)
     asked = exchange(requests, ("own", "col"))
-    fetched = gather(features, asked, (me * share).reshape(1), share)
+    asked = lax.dynamic_slice_in_dim(asked, me * share, share, 1).reshape(-1)
+    fetched = gather(features, asked)
     fetched = fetched.reshape(owners, share, width_f)
     received = exchange(fetched, ("own", "col")).reshape(owners * share, width_f)
 
@@ -360,23 +377,35 @@
     def partner(x):
         return lax.ppermute(x, "col", pairs)
 
-    mine, other, *d_hidden = middle(
-        parts, labels[:, None], hidden, [w_boths[s] for s in steps], core_id
+    mine, other, own_two, other_two, *d_hidden = middle(
+        parts,
+        labels[None],
+        hidden,
+        [w_both[:, units:] for w_both in (w_boths[s] for s in steps)],
+        core_id,
+        spread_t,
+        active[2],
+        rows_t,
     )
-    own_two, other_two = mine, other
-    grad_one, arrived = [], []
-    for i, step in enumerate(steps):
-        d_slice = d_hidden[i]
-        if i == 2:
-            d_slice, grad_one[0] = lax.optimization_barrier((d_slice, grad_one[0]))
-            arrived.append(to_mlp(grad_one[0], steps[0]))
-        if i == 3:
-            arrived += [to_mlp(g, s) for g, s in zip(grad_one[1:], steps[1:])]
-        mine, other = backward(spread_t, d_slice, active[step], rows_t, arrived if i == 3 else [])
-        mine += partner(other).astype(F32)
-        grad_one.append(mine.astype(BF) if step else mine)
+    far = (mine + partner(other).astype(F32)).astype(BF)
+    upward, downward = to_mlp(far[: half // 2], 1), to_mlp(far[half // 2 :], -1)
+    near = {}
+    d_hidden = dict(zip(steps[1:], d_hidden))
+    for step in (1, 0, 3):
+        d_slice = d_hidden[step]
+        if step == 0:
+            d_slice, far = lax.optimization_barrier((d_slice, far))
+            upward, downward = to_mlp(far[: half // 2], 1), to_mlp(far[half // 2 :], -1)
+        if step == 3:
+            d_slice, near[1] = lax.optimization_barrier((d_slice, near[1]))
+        mine, other = backward(spread_t, d_slice, active[step], rows_t)
+        near[step] = mine + partner(other).astype(F32)
+    top, bottom = near[1][: half // 2], near[1][half // 2 :]
+    near[1] = jnp.concatenate([top + upward.astype(F32), bottom], axis=0).astype(BF)
+    top, bottom = near[3][: half // 2], near[3][half // 2 :]
+    near[3] = jnp.concatenate([top, bottom + downward.astype(F32)], axis=0).astype(BF)
+    grad_one = near[0] + to_mlp(near[1], 1).astype(F32) + to_mlp(near[3], -1).astype(F32)
     grad_two = own_two + partner(other_two).astype(F32)
-    grad_one = grad_one[-1]
     both = jnp.concatenate([grad_one, grad_two], axis=1).astype(BF)
     chips = owners // 2
     groups = [[2 * i + c for i in range(chips)] for c in (0, 1)]
@@ -386,10 +415,7 @@
     both = jnp.broadcast_to(both[None], (chips, half // chips, width))
     both = exchange(both, ("own", "col"), groups).reshape(half, width)
     other = partner(both)
-    low = jnp.where(core == 0, both, other)
-    high = jnp.where(core == 0, other, both)
-    both = jnp.concatenate([low, high], axis=0).astype(F32)
-    return both[:, :units], both[:, units:]
+    return tuple(outputs(both, other, core_id, units))
 
 
 def solution(mesh):

time: 197 us -> 185 us (0.939)
  waiting for transfers between devices: 67.2 us -> 61.5 us
  Pallas kernels: 34.7 us -> 30.3 us
    ppermute x12 -> x13, waiting for transfers between devices: 44.9 us -> 39.5 us  [to_mlp(): lax.ppermute(x, 'mlp', [(j, (j + step) % mlp_n) for j in range(mlp_n)])]
    pallas_call x2 -> x3, Pallas kernels: 14.8 us -> 12 us  [the longest x1 8.5 us: gather(): pl.pallas_call(kernel, out_shape=jax.ShapeDtypeStruct((count, width_f), B...]
    unnamed x29 -> x23, local copies, waits for them, and re-layouts: 4.27 us -> 1.59 us
    pallas_call x4 -> x3, Pallas kernels: 7.06 us -> 5.3 us  [backward(): pl.pallas_call(kernel, out_shape=[jax.ShapeDtypeStruct((half, units), F32...]
    ppermute x12 -> x13, starting transfers between devices: 16.9 us -> 18.1 us  [to_mlp(): lax.ppermute(x, 'mlp', [(j, (j + step) % mlp_n) for j in range(mlp_n)])]
  transfers between devices with their start and end apart: 20 -> 21, of which waited for: 12 -> 9; matrix products, arithmetic and copies ran while one was open for 3% -> 4% of each run, Pallas kernels for 5% -> 5%
where the time goes in v7:
time: 185 us; the launch traced here: 184 us
  waiting for transfers between devices  61.5 us (33%)
  starting transfers between devices  45.1 us (24%)
  blocking collectives  36.7 us (20%)
  Pallas kernels  30.3 us (16%)
  local copies, waits for them, and re-layouts  5.89 us (3%)
  other arithmetic  2.3 us (1%)
    ppermute x13, waiting for transfers between devices, to_mlp(): lax.ppermute(x, 'mlp', [(j, (j + step) % mlp_n) for j in range(mlp_n)])  39.5 us
    all_to_all x2, blocking collectives, exchange(): lax.all_to_all(x, axes, split_axis=0, concat_axis=0, tiled=True, axis_ind...  36.7 us
    all_to_all x2, waiting for transfers between devices, exchange(): lax.all_to_all(x, axes, split_axis=0, concat_axis=0, tiled=True, axis_ind...  19.3 us
    ppermute x13, starting transfers between devices, to_mlp(): lax.ppermute(x, 'mlp', [(j, (j + step) % mlp_n) for j in range(mlp_n)])  18.1 us
    all_to_all x2, starting transfers between devices, exchange(): lax.all_to_all(x, axes, split_axis=0, concat_axis=0, tiled=True, axis_ind...  17.9 us
    pallas_call x2, Pallas kernels, forward(): pl.pallas_call(kernel, out_shape=shapes, in_specs=[SMEM, VMEM, HBM] + [HB...  10.8 us
    ppermute x6, starting transfers between devices, partner(): return lax.ppermute(x, 'col', pairs)  9.05 us
    pallas_call x1, Pallas kernels, gather(): pl.pallas_call(kernel, out_shape=jax.ShapeDtypeStruct((count, width_f), B...  8.5 us
  transfers between devices with their start and end apart: 21, of which 9 were waited for; matrix products, arithmetic and copies ran while one was open for 4% of the time, Pallas kernels for 5%

profile of v7, /device:TPU:1, one launch (start us, length us, event | category | flops | bytes accessed | tf_op | source)
XLA Modules:
  0.0 184.1 jit_solution(4006841942976532287)
XLA Ops:
  0.6 0.0 copy-start.6
  0.6 0.7 copy-done.6
  1.3 2.1 %shard_map.77 = (s32[64,128]{1,0:T(8,128)}, s32[32,128]{1,0:T(8,128)S(1)}) custom-call(s32[32,128]{1,0:T(8,128)S(1)} %bitcast.24), custom_call_target="tpu_custom_call" | custom-call | tf_op jit(solution)/shard_map/pallas_call | solution.py:70
  3.5 13.0 %all-to-all-start = ((s32[64,1,128]{2,1,0:T(1,128)}), s32[64,1,128]{2,1,0:T(1,128)S(1)}, u32[]{:S(2)}, u32[]{:S(2)}) async-start(s32[64,1,128]{2,1,0:T(1,128)} %bitcast.6), calls=%async_computation | async-start | bytes 65536 | tf_op jit(solution)/shard_map/all_to_all | solution.py:17
  16.5 9.3 %all-to-all-done = s32[64,1,128]{2,1,0:T(1,128)S(1)} async-done(((s32[64,1,128]{2,1,0:T(1,128)}), s32[64,1,128]{2,1,0:T(1,128)S(1)}, u32[]{:S(2)}, u32[]{:S(2)}) %all-to-all-start) | async-done | bytes 32800 | tf_op jit(solution)/shard_map/all_to_all | solution.py:17
  25.8 0.2 dynamic-slice_reduce_fusion
  25.9 0.1 reshape.47.asked_ref
  26.0 8.5 %shard_map.78 = bf16[2048,512]{1,0:T(8,128)(2,1)} custom-call(s32[2048]{0:T(1024)S(1)} %reshape.47.asked_ref, bf16[4096,512]{1,0:T(8,128)(2,1)} %features_ref.1), custom_call_target="tpu_custom_call" | custom-call | tf_op jit(solution)/shard_map/pallas_call | solution.py:113
  34.6 4.9 %all-to-all-start.1 = ((bf16[64,32,512]{2,1,0:T(8,128)(2,1)}), bf16[64,32,512]{2,1,0:T(8,128)(2,1)S(1)}, u32[]{:S(2)}, u32[]{:S(2)}) async-start(bf16[64,32,512]{2,1,0:T(8,128)(2,1)} %bitcast.7), calls=%async_computation.1 | async-start | bytes 4194304 | tf_op jit(solution)/shard_map/all_to_all | solution.py:17
  39.5 0.8 constant_dynamic-update-slice_fusion.1
  40.4 0.7 constant_dynamic-update-slice_fusion.refs_0_
  41.1 1.3 collective-permute-start.2
  42.4 1.4 collective-permute-start.1
  43.8 1.6 collective-permute-start
  45.5 0.4 convolution_bitcast_fusion
  46.0 0.1 copy.11
  46.1 0.1 broadcast_in_dim.59
  46.2 0.4 convolution_bitcast_fusion.1
  46.6 0.1 copy.10
  46.7 0.1 convert_element_type.72
  46.8 0.7 select_convert_fusion.refs_10_.spread_ref
  47.5 0.9 select_convert_fusion.1.spread_ref
  48.4 12.9 %collective-permute-done.2.refs_2_ = bf16[512,768]{1,0:T(8,128)(2,1)} collective-permute-done((bf16[512,768]{1,0:T(8,128)(2,1)}, bf16[512,768]{1,0:T(8,128)(2,1)}, u32[]{:S(2)}, u32[]{:S(2)}) %collective-permute-start.2) | collective-permute-done | bytes 786464 | tf_op jit(solution)/shard_map/ppermute | solution.py:325
  61.3 18.0 %collective-permute-done.refs_0_ = bf16[512,768]{1,0:T(8,128)(2,1)} collective-permute-done((bf16[512,768]{1,0:T(8,128)(2,1)}, bf16[512,768]{1,0:T(8,128)(2,1)}, u32[]{:S(2)}, u32[]{:S(2)}) %collective-permute-start) | collective-permute-done | bytes 786464 | tf_op jit(solution)/shard_map/ppermute | solution.py:325
  79.2 10.0 %all-to-all-done.1 = bf16[64,32,512]{2,1,0:T(8,128)(2,1)S(1)} async-done(((bf16[64,32,512]{2,1,0:T(8,128)(2,1)}), bf16[64,32,512]{2,1,0:T(8,128)(2,1)S(1)}, u32[]{:S(2)}, u32[]{:S(2)}) %all-to-all-start.1) | async-done | bytes 2097184 | tf_op jit(solution)/shard_map/all_to_all | solution.py:17
  89.2 6.9 %shard_map.80 = (bf16[2048,512]{1,0:T(8,128)(2,1)}, bf16[2048,512]{1,0:T(8,128)(2,1)}, bf16[2048,512]{1,0:T(8,128)(2,1)}, bf16[128,512]{1,0:T(8,128)(2,1)S(1)}, ...) custom-call(s32[1]{0:T(128)} %bitcast.core_ref, bf16[2048,512]{1,0:T(8,128)(2,1)S(1)} %bitcast.20, ...), custom_call_target="tpu_custom_call" | custom-call | flops 4026531840 | bytes 4718592 | tf_op jit(solution)/shard_map/pallas_call | solution.py:240
  96.2 3.0 %collective-permute-start.3 = (bf16[128,512]{1,0:T(8,128)(2,1)S(1)}, bf16[128,512]{1,0:T(8,128)(2,1)S(1)}, u32[]{:S(2)}, u32[]{:S(2)}) collective-permute-start(bf16[128,512]{1,0:T(8,128)(2,1)S(1)} %get-tuple-element.37), channel_id=1, source_target_pairs={{0,2},{1,3},{2,0},{3,1},{4,6},{5,7},{6,4},{7,5},{8,10},{9,11},{10,... | collective-permute-start | bytes 393224 | tf_op jit(solution)/shard_map/ppermute | solution.py:325
  99.2 0.4 collective-permute-start.4
  99.6 2.3 %collective-permute-start.5 = (bf16[128,512]{1,0:T(8,128)(2,1)S(1)}, bf16[128,512]{1,0:T(8,128)(2,1)S(1)}, u32[]{:S(2)}, u32[]{:S(2)}) collective-permute-start(bf16[128,512]{1,0:T(8,128)(2,1)S(1)} %get-tuple-element.39), channel_id=1, source_target_pairs={{0,3},{1,0},{2,1},{3,2},{4,7},{5,4},{6,5},{7,6},{8,11},{9,8},{10,9... | collective-permute-start | bytes 393224 | tf_op jit(solution)/shard_map/ppermute | solution.py:325
  101.9 3.9 %shard_map.79 = (bf16[2048,512]{1,0:T(8,128)(2,1)}, f32[128,512]{1,0:T(8,128)S(1)}, bf16[512,2048]{1,0:T(8,128)(2,1)}) custom-call(s32[1]{0:T(128)} %bitcast.core_ref, bf16[2048,512]{1,0:T(8,128)(2,1)S(1)} %bitcast.21, bf16[128,2048]{1,0:T(8,128)(2,1)} %select_convert_fusion.1.spread_ref, bf16[512,768]{1,0:T(8,128)(2,1)} %constant_dynamic-update-slice_fusion.refs_0_), custom_call_target="tpu_custom_call" | custom-call | flops 1342177280 | bytes 4718592 | tf_op jit(solution)/shard_map/pallas_call | solution.py:240
  105.8 0.1 add_convert_fusion.4.refs_5_
  105.9 0.2 fusion.20.refs_0_
  106.1 2.6 %collective-permute-start.8 = (f32[128,256]{1,0:T(8,128)S(1)}, f32[128,256]{1,0:T(8,128)S(1)}, u32[]{:S(2)}, u32[]{:S(2)}) collective-permute-start(f32[128,256]{1,0:T(8,128)S(1)} %fusion.20.refs_0_), channel_id=1, source_target_pairs={{0,3},{1,0},{2,1},{3,2},{4,7},{5,4},{6,5},{7,6},{8,11},{9,8},{10,9... | collective-permute-start | bytes 393224 | tf_op jit(solution)/shard_map/ppermute | solution.py:325
  108.6 1.3 collective-permute-start.6
  109.9 1.0 slice.40.refs_8_
  110.9 1.0 slice.39.refs_7_
  111.8 1.0 slice.38.refs_6_
  112.8 2.2 %collective-permute-done.7.refs_2_ = f32[128,256]{1,0:T(8,128)S(1)} collective-permute-done((f32[128,256]{1,0:T(8,128)S(1)}, f32[128,256]{1,0:T(8,128)S(1)}, u32[]{:S(2)}, u32[]{:S(2)}) %collective-permute-start.7) | collective-permute-done | bytes 131104 | tf_op jit(solution)/shard_map/ppermute | solution.py:325
  115.1 2.3 %shard_map.81 = (f32[256,512]{1,0:T(8,128)S(1)}, bf16[256,512]{1,0:T(8,128)(2,1)S(1)}, f32[256,256]{1,0:T(8,128)S(1)}, bf16[256,256]{1,0:T(8,128)(2,1)S(1)}, bf1...) custom-call(s32[1]{0:T(128)} %bitcast.core_ref, ...), custom_call_target="tpu_custom_call" | custom-call | flops 167772160 | bytes 4194304 | tf_op jit(solution)/shard_map/pallas_call | solution.py:167
  117.4 4.1 %collective-permute-start.9 = (bf16[256,512]{1,0:T(8,128)(2,1)S(1)}, bf16[256,512]{1,0:T(8,128)(2,1)S(1)}, u32[]{:S(2)}, u32[]{:S(2)}) collective-permute-start(bf16[256,512]{1,0:T(8,128)(2,1)S(1)} %get-tuple-element.44), channel_id=1, source_target_pairs={{0,4},{4,0},{8,12},{12,8},{16,20},{20,16},{24,28},{28,24},{1,5},{5... | collective-permute-start | bytes 786440 | tf_op jit(solution)/shard_map/ppermute | solution.py:378
  121.5 0.1 collective-permute-start.17
  121.6 1.8 shard_map.83
  123.4 0.5 collective-permute-start.11
  123.9 0.1 add_convert_fusion.1
  124.0 0.1 collective-permute-start.12
  124.1 2.7 %collective-permute-start.15 = (bf16[128,512]{1,0:T(8,128)(2,1)S(1)}, bf16[128,512]{1,0:T(8,128)(2,1)S(1)}, u32[]{:S(2)}, u32[]{:S(2)}) collective-permute-start(bf16[128,512]{1,0:T(8,128)(2,1)S(1)} %get-tuple-element.63), channel_id=1, source_target_pairs={{0,3},{1,0},{2,1},{3,2},{4,7},{5,4},{6,5},{7,6},{8,11},{9,8},{10,9... | collective-permute-start | bytes 393224 | tf_op jit(solution)/shard_map/ppermute | solution.py:325
  126.7 1.8 shard_map.82
  128.5 1.0 collective-permute-start.10
  129.5 0.1 convert_add_fusion.1
  129.6 1.8 shard_map.84
  131.4 0.1 collective-permute-start.14
  131.5 0.1 collective-permute-start.13
  131.6 1.4 collective-permute-done.14
  133.0 0.1 convert_add_fusion
  133.2 1.4 collective-permute-start.16
  134.6 5.6 %collective-permute-done.13 = bf16[256,512]{1,0:T(8,128)(2,1)S(1)} collective-permute-done((bf16[256,512]{1,0:T(8,128)(2,1)S(1)}, bf16[256,512]{1,0:T(8,128)(2,1)S(1)}, u32[]{:S(2)}, u32[]{:S(2)}) %collective-permute-start.13) | collective-permute-done | bytes 262176 | tf_op jit(solution)/shard_map/ppermute | solution.py:325
  140.2 0.8 collective-permute-done.16
  141.0 0.1 fusion.12
  141.2 18.9 %all_to_all.24 = bf16[32,8,768]{2,1,0:T(8,128)(2,1)S(1)} all-to-all(bf16[32,8,768]{2,1,0:T(8,128)(2,1)S(1)} %pad_maximum_fusion), channel_id=1, replica_groups={{0,8,16,24,32,40,48,56,64,72,80,88,96,104,112,120,128,136,144,152,160,1..., dimensions={0} | all-to-all | bytes 786432 | tf_op jit(solution)/shard_map/all_to_all | solution.py:17
  160.1 0.1 reduce_sum.12
  160.2 17.8 %all_to_all.25 = bf16[32,8,768]{2,1,0:T(8,128)(2,1)S(1)} all-to-all(bf16[32,8,768]{2,1,0:T(8,128)(2,1)S(1)} %broadcast_in_dim.65), channel_id=1, replica_groups={{0,8,16,24,32,40,48,56,64,72,80,88,96,104,112,120,128,136,144,152,160,1..., dimensions={0} | all-to-all | bytes 786432 | tf_op jit(solution)/shard_map/all_to_all | solution.py:17
  178.0 3.3 %collective-permute-start.18 = (bf16[256,768]{1,0:T(8,128)(2,1)S(1)}, bf16[256,768]{1,0:T(8,128)(2,1)S(1)}, u32[]{:S(2)}, u32[]{:S(2)}) collective-permute-start(bf16[256,768]{1,0:T(8,128)(2,1)S(1)} %bitcast.22), channel_id=1, source_target_pairs={{0,4},{4,0},{8,12},{12,8},{16,20},{20,16},{24,28},{28,24},{1,5},{5... | collective-permute-start | bytes 1179656 | tf_op jit(solution)/shard_map/ppermute | solution.py:378
  181.3 1.3 collective-permute-done.18.other_ref
  182.7 1.2 shard_map.85
  (47 shorter events, 0.4 us)
Async XLA Ops:
  0.6 0.7 copy-start.6
  3.5 22.3 %all-to-all-start = ((s32[64,1,128]{2,1,0:T(1,128)}), s32[64,1,128]{2,1,0:T(1,128)S(1)}, u32[]{:S(2)}, u32[]{:S(2)}) async-start(s32[64,1,128]{2,1,0:T(1,128)} %bitcast.6), calls=%async_computation | async-start | bytes 65536 | tf_op jit(solution)/shard_map/all_to_all | solution.py:17
  34.5 5.0 %copy-start.9 = (bf16[512,512]{1,0:T(8,128)(2,1)S(1)}, bf16[512,512]{1,0:T(8,128)(2,1)}, u32[]{:S(2)}) copy-start(bf16[512,512]{1,0:T(8,128)(2,1)} %param.10) | copy-start | bytes 1572868
  34.5 5.8 %copy-start.1 = (bf16[512,256]{1,0:T(8,128)(2,1)S(1)}, bf16[512,256]{1,0:T(8,128)(2,1)}, u32[]{:S(2)}) copy-start(bf16[512,256]{1,0:T(8,128)(2,1)} %refs_9_.1) | copy-start | bytes 786436
  34.6 10.9 %copy-start.7 = (s32[128,32]{0,1:T(8,128)S(1)}, s32[128,32]{0,1:T(8,128)}, u32[]{:S(2)}) copy-start(s32[128,32]{0,1:T(8,128)} %param.7) | copy-start | bytes 49156
  34.6 10.9 %copy-start.10 = (bf16[128,32]{0,1:T(8,128)(2,1)S(1)}, bf16[128,32]{0,1:T(8,128)(2,1)}, u32[]{:S(2)}) copy-start(bf16[128,32]{0,1:T(8,128)(2,1)} %param.8) | copy-start | bytes 24580
  34.6 54.7 %all-to-all-start.1 = ((bf16[64,32,512]{2,1,0:T(8,128)(2,1)}), bf16[64,32,512]{2,1,0:T(8,128)(2,1)S(1)}, u32[]{:S(2)}, u32[]{:S(2)}) async-start(bf16[64,32,512]{2,1,0:T(8,128)(2,1)} %bitcast.7), calls=%async_computation.1 | async-start | bytes 4194304 | tf_op jit(solution)/shard_map/all_to_all | solution.py:17
  41.1 20.2 %collective-permute-start.2 = (bf16[512,768]{1,0:T(8,128)(2,1)}, bf16[512,768]{1,0:T(8,128)(2,1)}, u32[]{:S(2)}, u32[]{:S(2)}) collective-permute-start(bf16[512,768]{1,0:T(8,128)(2,1)} %constant_dynamic-update-slice_fusion.refs_0_), channel_id=1, source_target_pairs={{0,1},{1,2},{2,3},{3,0},{4,5},{5,6},{6,7},{7,4},{8,9},{9,10},{10,1... | collective-permute-start | bytes 2359304 | tf_op jit(solution)/shard_map/ppermute | solution.py:325
  42.4 18.9 %collective-permute-start.1 = (bf16[512,768]{1,0:T(8,128)(2,1)}, bf16[512,768]{1,0:T(8,128)(2,1)}, u32[]{:S(2)}, u32[]{:S(2)}) collective-permute-start(bf16[512,768]{1,0:T(8,128)(2,1)} %constant_dynamic-update-slice_fusion.refs_0_), channel_id=1, source_target_pairs={{0,3},{1,0},{2,1},{3,2},{4,7},{5,4},{6,5},{7,6},{8,11},{9,8},{10,9... | collective-permute-start | bytes 2359304 | tf_op jit(solution)/shard_map/ppermute | solution.py:325
  43.8 35.4 %collective-permute-start = (bf16[512,768]{1,0:T(8,128)(2,1)}, bf16[512,768]{1,0:T(8,128)(2,1)}, u32[]{:S(2)}, u32[]{:S(2)}) collective-permute-start(bf16[512,768]{1,0:T(8,128)(2,1)} %constant_dynamic-update-slice_fusion.refs_0_), channel_id=1, source_target_pairs={{0,2},{1,3},{2,0},{3,1},{4,6},{5,7},{6,4},{7,5},{8,10},{9,11},{10,... | collective-permute-start | bytes 2359304 | tf_op jit(solution)/shard_map/ppermute | solution.py:325
  96.2 9.6 %collective-permute-start.3 = (bf16[128,512]{1,0:T(8,128)(2,1)S(1)}, bf16[128,512]{1,0:T(8,128)(2,1)S(1)}, u32[]{:S(2)}, u32[]{:S(2)}) collective-permute-start(bf16[128,512]{1,0:T(8,128)(2,1)S(1)} %get-tuple-element.37), channel_id=1, source_target_pairs={{0,2},{1,3},{2,0},{3,1},{4,6},{5,7},{6,4},{7,5},{8,10},{9,11},{10,... | collective-permute-start | bytes 393224 | tf_op jit(solution)/shard_map/ppermute | solution.py:325
  99.2 6.6 %collective-permute-start.4 = (bf16[128,512]{1,0:T(8,128)(2,1)S(1)}, bf16[128,512]{1,0:T(8,128)(2,1)S(1)}, u32[]{:S(2)}, u32[]{:S(2)}) collective-permute-start(bf16[128,512]{1,0:T(8,128)(2,1)S(1)} %get-tuple-element.38), channel_id=1, source_target_pairs={{0,1},{1,2},{2,3},{3,0},{4,5},{5,6},{6,7},{7,4},{8,9},{9,10},{10,1... | collective-permute-start | bytes 393224 | tf_op jit(solution)/shard_map/ppermute | solution.py:325
  99.6 6.2 %collective-permute-start.5 = (bf16[128,512]{1,0:T(8,128)(2,1)S(1)}, bf16[128,512]{1,0:T(8,128)(2,1)S(1)}, u32[]{:S(2)}, u32[]{:S(2)}) collective-permute-start(bf16[128,512]{1,0:T(8,128)(2,1)S(1)} %get-tuple-element.39), channel_id=1, source_target_pairs={{0,3},{1,0},{2,1},{3,2},{4,7},{5,4},{6,5},{7,6},{8,11},{9,8},{10,9... | collective-permute-start | bytes 393224 | tf_op jit(solution)/shard_map/ppermute | solution.py:325
  101.8 13.2 %copy-start.5 = (bf16[2048,512]{1,0:T(8,128)(2,1)S(1)}, bf16[2048,512]{1,0:T(8,128)(2,1)}, u32[]{:S(2)}) copy-start(bf16[2048,512]{1,0:T(8,128)(2,1)} %get-tuple-element.40.refs_11_) | copy-start | bytes 6291460
  105.7 9.3 %copy-start = (bf16[512,2048]{1,0:T(8,128)(2,1)S(1)}, bf16[512,2048]{1,0:T(8,128)(2,1)}, u32[]{:S(2)}) copy-start(bf16[512,2048]{1,0:T(8,128)(2,1)} %get-tuple-element.41.refs_12_.refs_1_) | copy-start | bytes 6291460
  105.8 9.3 %copy-start.8 = (s32[128]{0:T(128)S(1)}, s32[128]{0:T(128)}, u32[]{:S(2)}) copy-start(s32[128]{0:T(128)} %param.9) | copy-start | bytes 1540
  106.1 6.8 %collective-permute-start.8 = (f32[128,256]{1,0:T(8,128)S(1)}, f32[128,256]{1,0:T(8,128)S(1)}, u32[]{:S(2)}, u32[]{:S(2)}) collective-permute-start(f32[128,256]{1,0:T(8,128)S(1)} %fusion.20.refs_0_), channel_id=1, source_target_pairs={{0,3},{1,0},{2,1},{3,2},{4,7},{5,4},{6,5},{7,6},{8,11},{9,8},{10,9... | collective-permute-start | bytes 393224 | tf_op jit(solution)/shard_map/ppermute | solution.py:325
  108.6 6.4 %collective-permute-start.7 = (f32[128,256]{1,0:T(8,128)S(1)}, f32[128,256]{1,0:T(8,128)S(1)}, u32[]{:S(2)}, u32[]{:S(2)}) collective-permute-start(f32[128,256]{1,0:T(8,128)S(1)} %fusion.20.refs_0_), channel_id=1, source_target_pairs={{0,1},{1,2},{2,3},{3,0},{4,5},{5,6},{6,7},{7,4},{8,9},{9,10},{10,1... | collective-permute-start | bytes 393224 | tf_op jit(solution)/shard_map/ppermute | solution.py:325
  108.6 6.4 %collective-permute-start.6 = (f32[128,256]{1,0:T(8,128)S(1)}, f32[128,256]{1,0:T(8,128)S(1)}, u32[]{:S(2)}, u32[]{:S(2)}) collective-permute-start(f32[128,256]{1,0:T(8,128)S(1)} %fusion.20.refs_0_), channel_id=1, source_target_pairs={{0,2},{1,3},{2,0},{3,1},{4,6},{5,7},{6,4},{7,5},{8,10},{9,11},{10,... | collective-permute-start | bytes 393224 | tf_op jit(solution)/shard_map/ppermute | solution.py:325
  115.1 6.5 %copy-start.4 = (bf16[2048,512]{1,0:T(8,128)(2,1)S(1)}, bf16[2048,512]{1,0:T(8,128)(2,1)}, u32[]{:S(2)}) copy-start(bf16[2048,512]{1,0:T(8,128)(2,1)} %get-tuple-element.51.refs_0_) | copy-start | bytes 6291460
  117.4 6.4 %collective-permute-start.9 = (bf16[256,512]{1,0:T(8,128)(2,1)S(1)}, bf16[256,512]{1,0:T(8,128)(2,1)S(1)}, u32[]{:S(2)}, u32[]{:S(2)}) collective-permute-start(bf16[256,512]{1,0:T(8,128)(2,1)S(1)} %get-tuple-element.44), channel_id=1, source_target_pairs={{0,4},{4,0},{8,12},{12,8},{16,20},{20,16},{24,28},{28,24},{1,5},{5... | collective-permute-start | bytes 786440 | tf_op jit(solution)/shard_map/ppermute | solution.py:378
  121.5 13.1 %collective-permute-start.17 = (bf16[256,256]{1,0:T(8,128)(2,1)S(1)}, bf16[256,256]{1,0:T(8,128)(2,1)S(1)}, u32[]{:S(2)}, u32[]{:S(2)}) collective-permute-start(bf16[256,256]{1,0:T(8,128)(2,1)S(1)} %get-tuple-element.61), channel_id=1, source_target_pairs={{0,4},{4,0},{8,12},{12,8},{16,20},{20,16},{24,28},{28,24},{1,5},{5... | collective-permute-start | bytes 393224 | tf_op jit(solution)/shard_map/ppermute | solution.py:378
  121.6 5.2 %copy-start.3 = (bf16[2048,512]{1,0:T(8,128)(2,1)S(1)}, bf16[2048,512]{1,0:T(8,128)(2,1)}, u32[]{:S(2)}) copy-start(bf16[2048,512]{1,0:T(8,128)(2,1)} %get-tuple-element.46.refs_0_) | copy-start | bytes 6291460
  123.4 6.1 %collective-permute-start.11 = (bf16[256,512]{1,0:T(8,128)(2,1)S(1)}, bf16[256,512]{1,0:T(8,128)(2,1)S(1)}, u32[]{:S(2)}, u32[]{:S(2)}) collective-permute-start(bf16[256,512]{1,0:T(8,128)(2,1)S(1)} %get-tuple-element.53), channel_id=1, source_target_pairs={{0,4},{4,0},{8,12},{12,8},{16,20},{20,16},{24,28},{28,24},{1,5},{5... | collective-permute-start | bytes 786440 | tf_op jit(solution)/shard_map/ppermute | solution.py:378
  124.0 7.5 %collective-permute-start.12 = (bf16[128,512]{1,0:T(8,128)(2,1)S(1)}, bf16[128,512]{1,0:T(8,128)(2,1)S(1)}, u32[]{:S(2)}, u32[]{:S(2)}) collective-permute-start(bf16[128,512]{1,0:T(8,128)(2,1)S(1)} %get-tuple-element.62), channel_id=1, source_target_pairs={{0,1},{1,2},{2,3},{3,0},{4,5},{5,6},{6,7},{7,4},{8,9},{9,10},{10,1... | collective-permute-start | bytes 393224 | tf_op jit(solution)/shard_map/ppermute | solution.py:325
  124.1 9.1 %collective-permute-start.15 = (bf16[128,512]{1,0:T(8,128)(2,1)S(1)}, bf16[128,512]{1,0:T(8,128)(2,1)S(1)}, u32[]{:S(2)}, u32[]{:S(2)}) collective-permute-start(bf16[128,512]{1,0:T(8,128)(2,1)S(1)} %get-tuple-element.63), channel_id=1, source_target_pairs={{0,3},{1,0},{2,1},{3,2},{4,7},{5,4},{6,5},{7,6},{8,11},{9,8},{10,9... | collective-permute-start | bytes 393224 | tf_op jit(solution)/shard_map/ppermute | solution.py:325
  126.7 2.8 %copy-start.2 = (bf16[2048,512]{1,0:T(8,128)(2,1)S(1)}, bf16[2048,512]{1,0:T(8,128)(2,1)}, u32[]{:S(2)}) copy-start(bf16[2048,512]{1,0:T(8,128)(2,1)} %get-tuple-element.57.refs_0_) | copy-start | bytes 6291460
  128.5 6.1 %collective-permute-start.10 = (bf16[256,512]{1,0:T(8,128)(2,1)S(1)}, bf16[256,512]{1,0:T(8,128)(2,1)S(1)}, u32[]{:S(2)}, u32[]{:S(2)}) collective-permute-start(bf16[256,512]{1,0:T(8,128)(2,1)S(1)} %get-tuple-element.48), channel_id=1, source_target_pairs={{0,4},{4,0},{8,12},{12,8},{16,20},{20,16},{24,28},{28,24},{1,5},{5... | collective-permute-start | bytes 786440 | tf_op jit(solution)/shard_map/ppermute | solution.py:378
  131.4 1.6 collective-permute-start.14
  131.5 8.7 %collective-permute-start.13 = (bf16[256,512]{1,0:T(8,128)(2,1)S(1)}, bf16[256,512]{1,0:T(8,128)(2,1)S(1)}, u32[]{:S(2)}, u32[]{:S(2)}) collective-permute-start(bf16[256,512]{1,0:T(8,128)(2,1)S(1)} %pad_maximum_fusion.1), channel_id=1, source_target_pairs={{0,1},{1,2},{2,3},{3,0},{4,5},{5,6},{6,7},{7,4},{8,9},{9,10},{10,1... | collective-permute-start | bytes 786440 | tf_op jit(solution)/shard_map/ppermute | solution.py:325
  133.2 7.8 %collective-permute-start.16 = (bf16[256,512]{1,0:T(8,128)(2,1)S(1)}, bf16[256,512]{1,0:T(8,128)(2,1)S(1)}, u32[]{:S(2)}, u32[]{:S(2)}) collective-permute-start(bf16[256,512]{1,0:T(8,128)(2,1)S(1)} %pad_maximum_fusion.2), channel_id=1, source_target_pairs={{0,3},{1,0},{2,1},{3,2},{4,7},{5,4},{6,5},{7,6},{8,11},{9,8},{10,9... | collective-permute-start | bytes 786440 | tf_op jit(solution)/shard_map/ppermute | solution.py:325
  178.0 4.7 %collective-permute-start.18 = (bf16[256,768]{1,0:T(8,128)(2,1)S(1)}, bf16[256,768]{1,0:T(8,128)(2,1)S(1)}, u32[]{:S(2)}, u32[]{:S(2)}) collective-permute-start(bf16[256,768]{1,0:T(8,128)(2,1)S(1)} %bitcast.22), channel_id=1, source_target_pairs={{0,4},{4,0},{8,12},{12,8},{16,20},{20,16},{24,28},{28,24},{1,5},{5... | collective-permute-start | bytes 1179656 | tf_op jit(solution)/shard_map/ppermute | solution.py:378

commit v8 on v7

--- a/solution.py
+++ b/solution.py
@@ -87,10 +87,11 @@
     rows_dev, width_f = features.shape
     (count,) = asked.shape
     group = 32
+    parts = 4
     chunk = 512
     chunks = rows_dev // chunk
 
-    def kernel(asked_ref, features_ref, out_ref, wide, narrow, sems):
+    def kernel(asked_ref, features_ref, out_ref, wide, narrow, out, sems, out_sems):
         copies = []
         for i in range(chunks):
             at = pl.ds(i * chunk, chunk)
@@ -104,21 +105,33 @@
             at = pl.ds(i * chunk, chunk)
             wide[at, :] = narrow[at, :].astype(F32)
 
-        @pl.loop(0, count // group)
-        def _(i):
-            base = pl.multiple_of(i * group, group)
-            rows = [wide[pl.ds(asked_ref[base + j], 1), :] for j in range(group)]
-            out_ref[pl.ds(base, group), :] = jnp.concatenate(rows, axis=0).astype(BF)
-
-    return pl.pallas_call(
-        kernel,
-        out_shape=jax.ShapeDtypeStruct((count, width_f), BF),
+        copies = []
+        part = count // parts
+        for p in range(parts):
+
+            @pl.loop(0, part // group)
+            def _(i, p=p):
+                base = pl.multiple_of(p * part + i * group, group)
+                rows = [wide[pl.ds(asked_ref[base + j], 1), :] for j in range(group)]
+                out[pl.ds(base, group), :] = jnp.concatenate(rows, axis=0).astype(BF)
+
+            at = pl.ds(p * part, part)
+            copies.append(pltpu.make_async_copy(out.at[at, :], out_ref.at[at, :], out_sems.at[p]))
+            copies[-1].start()
+        for copy in copies:
+            copy.wait()
+
+    return pl.pallas_call(
+        kernel,
+        out_shape=pltpu.HBM((count, width_f), BF),
         in_specs=[SMEM, HBM],
-        out_specs=VMEM,
+        out_specs=HBM,
         scratch_shapes=[
             pltpu.VMEM((rows_dev, width_f), F32),
             pltpu.VMEM((rows_dev, width_f), BF),
+            pltpu.VMEM((count, width_f), BF),
             pltpu.SemaphoreType.DMA((chunks,)),
+            pltpu.SemaphoreType.DMA((parts,)),
         ],
         compiler_params=pltpu.CompilerParams(vmem_limit_bytes=32 * 2**20),
     )(asked, pltpu.with_memory_space_constraint(features, pltpu.HBM))
@@ -148,7 +161,7 @@
         d_hidden_refs = refs[7:]
         logits = part_refs[0][...]
         for part in part_refs[1:]:
-            logits += part[...]
+            logits += part[...].astype(F32)
         exponent = jnp.exp(logits)
         probability = exponent / jnp.sum(exponent, axis=1, keepdims=True)
         ids = lax.broadcasted_iota(jnp.int32, (targets, classes), 1)
@@ -184,13 +197,13 @@
     )(core, *parts, labels, hidden, *w_twos, spread_t, active, rows_t)
 
 
-def forward(rows, w_boths, spread, core, out_type, turn):
+def forward(rows, w_ones, spread, core, out_type, turn):
     slots, width_f = rows.shape
     targets = spread.shape[0]
     units = width_f
     half = width_f // 2
     block = 512
-    count = len(w_boths)
+    count = len(w_ones)
 
     def kernel(core_ref, rows_ref, spread_ref, *refs):
         w_refs, refs = refs[:count], refs[count:]
@@ -201,7 +214,7 @@
         turned, turned_sems = refs[6 : 6 + turn], refs[6 + turn :]
         for i in range(count):
             pltpu.make_async_copy(
-                w_refs[i].at[:, pl.ds(0, units)], w_all.at[i], w_sems.at[i]
+                w_refs[i], w_all.at[i], w_sems.at[i]
             ).start()
         spread_copy = pltpu.make_async_copy(spread_ref, spread_all, spread_sem)
         spread_copy.start()
@@ -219,7 +232,7 @@
             pltpu.make_async_copy(source, target, sem).start()
         for i in range(count):
             pltpu.make_async_copy(
-                w_refs[i].at[:, pl.ds(0, units)], w_all.at[i], w_sems.at[i]
+                w_refs[i], w_all.at[i], w_sems.at[i]
             ).wait()
 
             active_all[i] = jnp.maximum(dot(rows_ref[...], w_all[i]), 0.0).astype(BF)
@@ -258,15 +271,15 @@
             bytes_accessed=2 * slots * (width_f + units + targets),
             transcendentals=0,
         ),
-    )(core, rows, *(pltpu.with_memory_space_constraint(x, pltpu.HBM) for x in (spread, *w_boths)))
-
-
-def backward(spread_t, d_hidden, active, rows_t):
+    )(core, rows, *(pltpu.with_memory_space_constraint(x, pltpu.HBM) for x in (spread, *w_ones)))
+
+
+def backward(spread_t, d_hidden, active, rows_t, earlier):
     units = d_hidden.shape[1]
     half = rows_t.shape[0] // 2
 
-    def kernel(spread_ref, d_hidden_ref, *refs):
-        slice_grad(spread_ref, d_hidden_ref[...], *refs)
+    def kernel(spread_ref, d_hidden_ref, active_ref, rows_ref, *refs):
+        slice_grad(spread_ref, d_hidden_ref[...], active_ref, rows_ref, *refs[-2:])
 
     return pl.pallas_call(
         kernel,
@@ -274,13 +287,13 @@
             jax.ShapeDtypeStruct((half, units), F32),
             jax.ShapeDtypeStruct((half, units), BF),
         ],
-        in_specs=[VMEM] * 4,
+        in_specs=[VMEM] * 4 + [pl.BlockSpec(memory_space=pl.ANY)] * len(earlier),
         out_specs=[VMEM] * 2,
         compiler_params=pltpu.CompilerParams(vmem_limit_bytes=24 * 2**20),
         cost_estimate=pl.CostEstimate(
             flops=2 * units, bytes_accessed=2 * units, transcendentals=0
         ),
-    )(spread_t, d_hidden, active, rows_t)
+    )(spread_t, d_hidden, active, rows_t, *earlier)
 
 
 def outputs(own, other, core, units):
@@ -325,10 +338,11 @@
         return lax.ppermute(x, "mlp", [(j, (j + step) % mlp_n) for j in range(mlp_n)])
 
     steps = (2, 1, 3, 0)
-    w_both = jnp.concatenate([w_one, w_two], axis=1)
-    w_boths = {0: w_both}
+    w_ones, w_twos = {0: w_one}, {0: w_two}
     for step in steps[:-1]:
-        w_boths[step] = to_mlp(w_both, -step)
+        w_ones[step] = to_mlp(w_one, -step)
+        w_twos[step] = to_mlp(w_two, -step)
+    w_ones, w_twos = lax.optimization_barrier((w_ones, w_twos))
 
     requests, slot_ids = slots_of(nbr_page.T, rows_dev, owners, capacity)
     asked = exchange(requests, ("own", "col"))
@@ -360,17 +374,17 @@
 
     core_id = core.reshape(1)
     first = steps[:-1]
-    out = forward(received, [w_boths[s] for s in first], spread, core_id, BF, 0)
+    out = forward(received, [w_ones[s] for s in first], spread, core_id, BF, 0)
     active = dict(zip(first, out))
     shares = [to_mlp(part, step) for part, step in zip(out[len(first) :], first)]
-    active[0], hidden, rows_t = forward(received, [w_both], spread, core_id, F32, 1)
+    active[0], hidden, rows_t = forward(received, [w_one], spread, core_id, F32, 1)
     for share_in in shares:
         hidden += share_in.astype(F32)
     hidden = hidden.astype(BF)
     half = width_f // 2
 
     part = dot(hidden, w_two)
-    parts = [part] + [to_mlp(part, step) for step in steps[:-1]]
+    parts = [part] + [to_mlp(part.astype(BF), step) for step in steps[:-1]]
 
     pairs = [(i, i ^ 1) for i in range(col_n)]
 
@@ -381,24 +395,20 @@
         parts,
         labels[None],
         hidden,
-        [w_both[:, units:] for w_both in (w_boths[s] for s in steps)],
+        [w_twos[s] for s in steps],
         core_id,
         spread_t,
         active[2],
         rows_t,
     )
     far = (mine + partner(other).astype(F32)).astype(BF)
-    upward, downward = to_mlp(far[: half // 2], 1), to_mlp(far[half // 2 :], -1)
+    far = (far[: half // 2], far[half // 2 :])
+    upward, downward = to_mlp(far[0], 1), to_mlp(far[1], -1)
     near = {}
-    d_hidden = dict(zip(steps[1:], d_hidden))
     for step in (1, 0, 3):
-        d_slice = d_hidden[step]
-        if step == 0:
-            d_slice, far = lax.optimization_barrier((d_slice, far))
-            upward, downward = to_mlp(far[: half // 2], 1), to_mlp(far[half // 2 :], -1)
-        if step == 3:
-            d_slice, near[1] = lax.optimization_barrier((d_slice, near[1]))
-        mine, other = backward(spread_t, d_slice, active[step], rows_t)
+        i = steps.index(step) - 1
+        earlier = () if step == 1 else far if step == 0 else (near[1],)
+        mine, other = backward(spread_t, d_hidden[i], active[step], rows_t, earlier)
         near[step] = mine + partner(other).astype(F32)
     top, bottom = near[1][: half // 2], near[1][half // 2 :]
     near[1] = jnp.concatenate([top + upward.astype(F32), bottom], axis=0).astype(BF)

time: 185 us -> 185 us (level)
  starting transfers between devices: 45.1 us -> 48.7 us
  local copies, waits for them, and re-layouts: 5.89 us -> 3.02 us
    all_to_all x2, waiting for transfers between devices: 19.3 us -> 14.1 us  [exchange(): lax.all_to_all(x, axes, split_axis=0, concat_axis=0, tiled=True, axis_ind...]
    ppermute x13 -> x16, waiting for transfers between devices: 39.5 us -> 44.7 us  [to_mlp(): lax.ppermute(x, 'mlp', [(j, (j + step) % mlp_n) for j in range(mlp_n)])]
    ppermute x13 -> x16, starting transfers between devices: 18.1 us -> 21.1 us  [to_mlp(): lax.ppermute(x, 'mlp', [(j, (j + step) % mlp_n) for j in range(mlp_n)])]
    slice x4 -> x1, local copies, waits for them, and re-layouts: 2.92 us -> 0.02 us  [body(): far = (far[:half // 2], far[half // 2:])]
  transfers between devices with their start and end apart: 21 -> 24, of which waited for: 9 -> 10; matrix products, arithmetic and copies ran while one was open for 4% -> 2% of each run, Pallas kernels for 5% -> 5%
where the time goes in v8:
time: 185 us; the launch traced here: 184 us
  waiting for transfers between devices  61.5 us (33%)
  starting transfers between devices  48.7 us (26%)
  blocking collectives  35.7 us (19%)
  Pallas kernels  30.8 us (17%)
  local copies, waits for them, and re-layouts  3.02 us (2%)
  other arithmetic  2.26 us (1%)
    ppermute x16, waiting for transfers between devices, to_mlp(): lax.ppermute(x, 'mlp', [(j, (j + step) % mlp_n) for j in range(mlp_n)])  44.7 us
    all_to_all x2, blocking collectives, exchange(): lax.all_to_all(x, axes, split_axis=0, concat_axis=0, tiled=True, axis_ind...  35.7 us
    ppermute x16, starting transfers between devices, to_mlp(): lax.ppermute(x, 'mlp', [(j, (j + step) % mlp_n) for j in range(mlp_n)])  21.1 us
    all_to_all x2, starting transfers between devices, exchange(): lax.all_to_all(x, axes, split_axis=0, concat_axis=0, tiled=True, axis_ind...  17.9 us
    all_to_all x2, waiting for transfers between devices, exchange(): lax.all_to_all(x, axes, split_axis=0, concat_axis=0, tiled=True, axis_ind...  14.1 us
    pallas_call x2, Pallas kernels, forward(): pl.pallas_call(kernel, out_shape=shapes, in_specs=[SMEM, VMEM, HBM] + [HB...  10.7 us
    ppermute x6, starting transfers between devices, partner(): return lax.ppermute(x, 'col', pairs)  9.74 us
    pallas_call x1, Pallas kernels, gather(): pl.pallas_call(kernel, out_shape=pltpu.HBM((count, width_f), BF), in_spec...  8.03 us
  transfers between devices with their start and end apart: 24, of which 10 were waited for; matrix products, arithmetic and copies ran while one was open for 2% of the time, Pallas kernels for 5%

profile of v8, /device:TPU:1, one launch (start us, length us, event | category | flops | bytes accessed | tf_op | source)
XLA Modules:
  0.0 184.2 jit_solution(16646741519522716862)
XLA Ops:
  0.6 0.0 copy-start.7
  0.6 0.7 copy-done.7
  1.3 2.1 %shard_map.77 = (s32[64,128]{1,0:T(8,128)}, s32[32,128]{1,0:T(8,128)S(1)}) custom-call(s32[32,128]{1,0:T(8,128)S(1)} %bitcast.24), custom_call_target="tpu_custom_call" | custom-call | tf_op jit(solution)/shard_map/pallas_call | solution.py:70
  3.5 13.0 %all-to-all-start = ((s32[64,1,128]{2,1,0:T(1,128)}), s32[64,1,128]{2,1,0:T(1,128)S(1)}, u32[]{:S(2)}, u32[]{:S(2)}) async-start(s32[64,1,128]{2,1,0:T(1,128)} %bitcast.6), calls=%async_computation | async-start | bytes 65536 | tf_op jit(solution)/shard_map/all_to_all | solution.py:17
  16.5 9.3 %all-to-all-done = s32[64,1,128]{2,1,0:T(1,128)S(1)} async-done(((s32[64,1,128]{2,1,0:T(1,128)}), s32[64,1,128]{2,1,0:T(1,128)S(1)}, u32[]{:S(2)}, u32[]{:S(2)}) %all-to-all-start) | async-done | bytes 32800 | tf_op jit(solution)/shard_map/all_to_all | solution.py:17
  25.8 0.2 dynamic-slice_reduce_fusion
  25.9 0.1 reshape.47.asked_ref
  26.0 8.0 %shard_map.78 = bf16[2048,512]{1,0:T(8,128)(2,1)} custom-call(s32[2048]{0:T(1024)S(1)} %reshape.47.asked_ref, bf16[4096,512]{1,0:T(8,128)(2,1)} %features_ref.1), custom_call_target="tpu_custom_call" | custom-call | tf_op jit(solution)/shard_map/pallas_call | solution.py:124
  34.1 4.9 %all-to-all-start.1 = ((bf16[64,32,512]{2,1,0:T(8,128)(2,1)}), bf16[64,32,512]{2,1,0:T(8,128)(2,1)S(1)}, u32[]{:S(2)}, u32[]{:S(2)}) async-start(bf16[64,32,512]{2,1,0:T(8,128)(2,1)} %bitcast.28), calls=%async_computation.1 | async-start | bytes 4194304 | tf_op jit(solution)/shard_map/all_to_all | solution.py:17
  39.1 2.8 %collective-permute-start = (bf16[512,512]{1,0:T(8,128)(2,1)}, bf16[512,512]{1,0:T(8,128)(2,1)}, u32[]{:S(2)}, u32[]{:S(2)}) collective-permute-start(bf16[512,512]{1,0:T(8,128)(2,1)} %refs_0_.1), channel_id=1, source_target_pairs={{0,3},{1,0},{2,1},{3,2},{4,7},{5,4},{6,5},{7,6},{8,11},{9,8},{10,9... | collective-permute-start | bytes 1572872 | tf_op jit(solution)/shard_map/ppermute | solution.py:338
  41.9 0.3 collective-permute-start.1
  42.2 0.7 collective-permute-start.2
  42.9 2.0 %collective-permute-start.3 = (bf16[512,256]{1,0:T(8,128)(2,1)S(1)}, bf16[512,256]{1,0:T(8,128)(2,1)S(1)}, u32[]{:S(2)}, u32[]{:S(2)}) collective-permute-start(bf16[512,256]{1,0:T(8,128)(2,1)S(1)} %copy-done.6), channel_id=1, source_target_pairs={{0,3},{1,0},{2,1},{3,2},{4,7},{5,4},{6,5},{7,6},{8,11},{9,8},{10,9... | collective-permute-start | bytes 786440 | tf_op jit(solution)/shard_map/ppermute | solution.py:338
  44.9 1.4 collective-permute-start.4
  46.3 0.4 convolution_bitcast_fusion.1
  46.8 0.1 copy.10
  46.9 0.1 convert_element_type.77
  46.9 0.4 convolution_bitcast_fusion
  47.4 0.1 copy.11
  47.5 0.1 broadcast_in_dim.59
  47.6 0.7 select_convert_fusion.refs_10_.spread_ref
  48.3 26.8 %collective-permute-done.3.refs_7_ = bf16[512,256]{1,0:T(8,128)(2,1)S(1)} collective-permute-done((bf16[512,256]{1,0:T(8,128)(2,1)S(1)}, bf16[512,256]{1,0:T(8,128)(2,1)S(1)}, u32[]{:S(2)}, u32[]{:S(2)}) %collective-permute-start.3) | collective-permute-done | bytes 262176 | tf_op jit(solution)/shard_map/ppermute | solution.py:338
  75.1 0.9 select_convert_fusion.1.spread_ref
  76.0 7.9 %collective-permute-done.5.refs_8_ = bf16[512,256]{1,0:T(8,128)(2,1)} collective-permute-done((bf16[512,256]{1,0:T(8,128)(2,1)S(1)}, bf16[512,256]{1,0:T(8,128)(2,1)}, u32[]{:S(2)}, u32[]{:S(2)}) %collective-permute-start.5) | collective-permute-done | bytes 262176 | tf_op jit(solution)/shard_map/ppermute | solution.py:338
  84.0 4.8 %all-to-all-done.1 = bf16[64,32,512]{2,1,0:T(8,128)(2,1)S(1)} async-done(((bf16[64,32,512]{2,1,0:T(8,128)(2,1)}), bf16[64,32,512]{2,1,0:T(8,128)(2,1)S(1)}, u32[]{:S(2)}, u32[]{:S(2)}) %all-to-all-start.1) | async-done | bytes 2097184 | tf_op jit(solution)/shard_map/all_to_all | solution.py:17
  88.7 6.9 %shard_map.80 = (bf16[2048,512]{1,0:T(8,128)(2,1)}, bf16[2048,512]{1,0:T(8,128)(2,1)}, bf16[2048,512]{1,0:T(8,128)(2,1)}, bf16[128,512]{1,0:T(8,128)(2,1)S(1)}, ...) custom-call(s32[1]{0:T(128)} %bitcast.core_ref, bf16[2048,512]{1,0:T(8,128)(2,1)S(1)} %bitcast.20, ...), custom_call_target="tpu_custom_call" | custom-call | flops 4026531840 | bytes 4718592 | tf_op jit(solution)/shard_map/pallas_call | solution.py:253
  95.7 3.0 %collective-permute-start.6 = (bf16[128,512]{1,0:T(8,128)(2,1)S(1)}, bf16[128,512]{1,0:T(8,128)(2,1)S(1)}, u32[]{:S(2)}, u32[]{:S(2)}) collective-permute-start(bf16[128,512]{1,0:T(8,128)(2,1)S(1)} %get-tuple-element.43), channel_id=1, source_target_pairs={{0,2},{1,3},{2,0},{3,1},{4,6},{5,7},{6,4},{7,5},{8,10},{9,11},{10,... | collective-permute-start | bytes 393224 | tf_op jit(solution)/shard_map/ppermute | solution.py:338
  98.7 0.4 collective-permute-start.7
  99.1 2.3 %collective-permute-start.8 = (bf16[128,512]{1,0:T(8,128)(2,1)S(1)}, bf16[128,512]{1,0:T(8,128)(2,1)S(1)}, u32[]{:S(2)}, u32[]{:S(2)}) collective-permute-start(bf16[128,512]{1,0:T(8,128)(2,1)S(1)} %get-tuple-element.45), channel_id=1, source_target_pairs={{0,3},{1,0},{2,1},{3,2},{4,7},{5,4},{6,5},{7,6},{8,11},{9,8},{10,9... | collective-permute-start | bytes 393224 | tf_op jit(solution)/shard_map/ppermute | solution.py:338
  101.4 3.7 %shard_map.79 = (bf16[2048,512]{1,0:T(8,128)(2,1)}, f32[128,512]{1,0:T(8,128)S(1)}, bf16[512,2048]{1,0:T(8,128)(2,1)}) custom-call(s32[1]{0:T(128)} %bitcast.core_ref, bf16[2048,512]{1,0:T(8,128)(2,1)S(1)} %bitcast.21, bf16[128,2048]{1,0:T(8,128)(2,1)} %select_convert_fusion.1.spread_ref, bf16[512,512]{1,0:T(8,128)(2,1)} %refs_0_.1), custom_call_target="tpu_custom_call" | custom-call | flops 1342177280 | bytes 4718592 | tf_op jit(solution)/shard_map/pallas_call | solution.py:253
  105.2 0.1 add_convert_fusion.3.refs_5_
  105.2 0.2 fusion.21
  105.4 0.1 collective-permute-start.10
  105.5 2.7 %collective-permute-start.11 = (bf16[128,256]{1,0:T(8,128)(2,1)S(1)}, bf16[128,256]{1,0:T(8,128)(2,1)S(1)}, u32[]{:S(2)}, u32[]{:S(2)}) collective-permute-start(bf16[128,256]{1,0:T(8,128)(2,1)S(1)} %get-tuple-element.70), channel_id=1, source_target_pairs={{0,3},{1,0},{2,1},{3,2},{4,7},{5,4},{6,5},{7,6},{8,11},{9,8},{10,9... | collective-permute-start | bytes 196616 | tf_op jit(solution)/shard_map/ppermute | solution.py:338
  108.2 1.1 collective-permute-start.9
  109.3 0.5 collective-permute-done.10.refs_2_
  109.8 3.1 %collective-permute-done.9.refs_1_ = bf16[128,256]{1,0:T(8,128)(2,1)S(1)} collective-permute-done((bf16[128,256]{1,0:T(8,128)(2,1)S(1)}, bf16[128,256]{1,0:T(8,128)(2,1)S(1)}, u32[]{:S(2)}, u32[]{:S(2)}) %collective-permute-start.9) | collective-permute-done | bytes 65568 | tf_op jit(solution)/shard_map/ppermute | solution.py:338
  112.9 1.6 copy-done
  114.5 3.4 %shard_map.81 = (f32[256,512]{1,0:T(8,128)S(1)}, bf16[256,512]{1,0:T(8,128)(2,1)S(1)}, f32[256,256]{1,0:T(8,128)S(1)}, bf16[256,256]{1,0:T(8,128)(2,1)S(1)}, bf1...) custom-call(s32[1]{0:T(128)} %bitcast.core_ref, ...), custom_call_target="tpu_custom_call" | custom-call | flops 167772160 | bytes 4194304 | tf_op jit(solution)/shard_map/pallas_call | solution.py:180
  117.9 5.0 %collective-permute-start.12 = (bf16[256,512]{1,0:T(8,128)(2,1)S(1)}, bf16[256,512]{1,0:T(8,128)(2,1)S(1)}, u32[]{:S(2)}, u32[]{:S(2)}) collective-permute-start(bf16[256,512]{1,0:T(8,128)(2,1)S(1)} %get-tuple-element.55), channel_id=1, source_target_pairs={{0,4},{4,0},{8,12},{12,8},{16,20},{20,16},{24,28},{28,24},{1,5},{5... | collective-permute-start | bytes 786440 | tf_op jit(solution)/shard_map/ppermute | solution.py:392
  122.9 1.8 shard_map.83
  124.7 0.1 collective-permute-start.14
  124.8 0.5 collective-permute-start.20
  125.3 0.1 add_convert_fusion.1
  125.4 0.1 collective-permute-start.15
  125.4 2.7 %collective-permute-start.18 = (bf16[128,512]{1,0:T(8,128)(2,1)S(1)}, bf16[128,512]{1,0:T(8,128)(2,1)S(1)}, u32[]{:S(2)}, u32[]{:S(2)}) collective-permute-start(bf16[128,512]{1,0:T(8,128)(2,1)S(1)} %get-tuple-element.69.refs_1_), channel_id=1, source_target_pairs={{0,3},{1,0},{2,1},{3,2},{4,7},{5,4},{6,5},{7,6},{8,11},{9,8},{10,9... | collective-permute-start | bytes 393224 | tf_op jit(solution)/shard_map/ppermute | solution.py:338
  128.1 1.8 shard_map.82
  129.9 0.7 collective-permute-start.13
  130.6 0.1 convert_add_fusion.1.refs_0_
  130.7 1.8 shard_map.84
  132.5 0.1 collective-permute-start.17
  132.7 0.1 collective-permute-start.16
  132.8 1.4 collective-permute-done.17
  134.1 0.1 convert_add_fusion
  134.3 1.4 collective-permute-start.19
  135.8 5.6 %collective-permute-done.16 = bf16[256,512]{1,0:T(8,128)(2,1)S(1)} collective-permute-done((bf16[256,512]{1,0:T(8,128)(2,1)S(1)}, bf16[256,512]{1,0:T(8,128)(2,1)S(1)}, u32[]{:S(2)}, u32[]{:S(2)}) %collective-permute-start.16) | collective-permute-done | bytes 262176 | tf_op jit(solution)/shard_map/ppermute | solution.py:338
  141.4 0.8 collective-permute-done.19
  142.2 0.1 fusion.12
  142.3 17.9 %all_to_all.24 = bf16[32,8,768]{2,1,0:T(8,128)(2,1)S(1)} all-to-all(bf16[32,8,768]{2,1,0:T(8,128)(2,1)S(1)} %pad_maximum_fusion), channel_id=1, replica_groups={{0,8,16,24,32,40,48,56,64,72,80,88,96,104,112,120,128,136,144,152,160,1..., dimensions={0} | all-to-all | bytes 786432 | tf_op jit(solution)/shard_map/all_to_all | solution.py:17
  160.3 0.1 reduce_sum.12
  160.4 17.8 %all_to_all.25 = bf16[32,8,768]{2,1,0:T(8,128)(2,1)S(1)} all-to-all(bf16[32,8,768]{2,1,0:T(8,128)(2,1)S(1)} %broadcast_in_dim.65), channel_id=1, replica_groups={{0,8,16,24,32,40,48,56,64,72,80,88,96,104,112,120,128,136,144,152,160,1..., dimensions={0} | all-to-all | bytes 786432 | tf_op jit(solution)/shard_map/all_to_all | solution.py:17
  178.2 3.3 %collective-permute-start.21 = (bf16[256,768]{1,0:T(8,128)(2,1)S(1)}, bf16[256,768]{1,0:T(8,128)(2,1)S(1)}, u32[]{:S(2)}, u32[]{:S(2)}) collective-permute-start(bf16[256,768]{1,0:T(8,128)(2,1)S(1)} %bitcast.22), channel_id=1, source_target_pairs={{0,4},{4,0},{8,12},{12,8},{16,20},{20,16},{24,28},{28,24},{1,5},{5... | collective-permute-start | bytes 1179656 | tf_op jit(solution)/shard_map/ppermute | solution.py:392
  181.5 1.3 collective-permute-done.21.other_ref
  182.8 1.2 shard_map.85
  (48 shorter events, 0.4 us)
Async XLA Ops:
  0.6 0.7 copy-start.7
  3.5 22.3 %all-to-all-start = ((s32[64,1,128]{2,1,0:T(1,128)}), s32[64,1,128]{2,1,0:T(1,128)S(1)}, u32[]{:S(2)}, u32[]{:S(2)}) async-start(s32[64,1,128]{2,1,0:T(1,128)} %bitcast.6), calls=%async_computation | async-start | bytes 65536 | tf_op jit(solution)/shard_map/all_to_all | solution.py:17
  34.1 8.8 %copy-start.6 = (bf16[512,256]{1,0:T(8,128)(2,1)S(1)}, bf16[512,256]{1,0:T(8,128)(2,1)}, u32[]{:S(2)}) copy-start(bf16[512,256]{1,0:T(8,128)(2,1)} %refs_9_) | copy-start | bytes 786436
  34.1 12.2 %copy-start.8 = (s32[128,32]{0,1:T(8,128)S(1)}, s32[128,32]{0,1:T(8,128)}, u32[]{:S(2)}) copy-start(s32[128,32]{0,1:T(8,128)} %param.7) | copy-start | bytes 49156
  34.1 54.7 %all-to-all-start.1 = ((bf16[64,32,512]{2,1,0:T(8,128)(2,1)}), bf16[64,32,512]{2,1,0:T(8,128)(2,1)S(1)}, u32[]{:S(2)}, u32[]{:S(2)}) async-start(bf16[64,32,512]{2,1,0:T(8,128)(2,1)} %bitcast.28), calls=%async_computation.1 | async-start | bytes 4194304 | tf_op jit(solution)/shard_map/all_to_all | solution.py:17
  39.0 7.9 %copy-start.10 = (bf16[128,32]{0,1:T(8,128)(2,1)S(1)}, bf16[128,32]{0,1:T(8,128)(2,1)}, u32[]{:S(2)}) copy-start(bf16[128,32]{0,1:T(8,128)(2,1)} %param.8) | copy-start | bytes 24580
  39.1 44.9 %collective-permute-start = (bf16[512,512]{1,0:T(8,128)(2,1)}, bf16[512,512]{1,0:T(8,128)(2,1)}, u32[]{:S(2)}, u32[]{:S(2)}) collective-permute-start(bf16[512,512]{1,0:T(8,128)(2,1)} %refs_0_.1), channel_id=1, source_target_pairs={{0,3},{1,0},{2,1},{3,2},{4,7},{5,4},{6,5},{7,6},{8,11},{9,8},{10,9... | collective-permute-start | bytes 1572872 | tf_op jit(solution)/shard_map/ppermute | solution.py:338
  41.9 42.1 %collective-permute-start.1 = (bf16[512,512]{1,0:T(8,128)(2,1)}, bf16[512,512]{1,0:T(8,128)(2,1)}, u32[]{:S(2)}, u32[]{:S(2)}) collective-permute-start(bf16[512,512]{1,0:T(8,128)(2,1)} %refs_0_.1), channel_id=1, source_target_pairs={{0,2},{1,3},{2,0},{3,1},{4,6},{5,7},{6,4},{7,5},{8,10},{9,11},{10,... | collective-permute-start | bytes 1572872 | tf_op jit(solution)/shard_map/ppermute | solution.py:338
  42.2 41.8 %collective-permute-start.2 = (bf16[512,512]{1,0:T(8,128)(2,1)}, bf16[512,512]{1,0:T(8,128)(2,1)}, u32[]{:S(2)}, u32[]{:S(2)}) collective-permute-start(bf16[512,512]{1,0:T(8,128)(2,1)} %refs_0_.1), channel_id=1, source_target_pairs={{0,1},{1,2},{2,3},{3,0},{4,5},{5,6},{6,7},{7,4},{8,9},{9,10},{10,1... | collective-permute-start | bytes 1572872 | tf_op jit(solution)/shard_map/ppermute | solution.py:338
  42.9 32.2 %collective-permute-start.3 = (bf16[512,256]{1,0:T(8,128)(2,1)S(1)}, bf16[512,256]{1,0:T(8,128)(2,1)S(1)}, u32[]{:S(2)}, u32[]{:S(2)}) collective-permute-start(bf16[512,256]{1,0:T(8,128)(2,1)S(1)} %copy-done.6), channel_id=1, source_target_pairs={{0,3},{1,0},{2,1},{3,2},{4,7},{5,4},{6,5},{7,6},{8,11},{9,8},{10,9... | collective-permute-start | bytes 786440 | tf_op jit(solution)/shard_map/ppermute | solution.py:338
  44.9 31.1 %collective-permute-start.4 = (bf16[512,256]{1,0:T(8,128)(2,1)S(1)}, bf16[512,256]{1,0:T(8,128)(2,1)S(1)}, u32[]{:S(2)}, u32[]{:S(2)}) collective-permute-start(bf16[512,256]{1,0:T(8,128)(2,1)S(1)} %copy-done.6), channel_id=1, source_target_pairs={{0,2},{1,3},{2,0},{3,1},{4,6},{5,7},{6,4},{7,5},{8,10},{9,11},{10,... | collective-permute-start | bytes 786440 | tf_op jit(solution)/shard_map/ppermute | solution.py:338
  75.1 8.8 %collective-permute-start.5 = (bf16[512,256]{1,0:T(8,128)(2,1)S(1)}, bf16[512,256]{1,0:T(8,128)(2,1)}, u32[]{:S(2)}, u32[]{:S(2)}) collective-permute-start(bf16[512,256]{1,0:T(8,128)(2,1)S(1)} %copy-done.6), channel_id=1, source_target_pairs={{0,1},{1,2},{2,3},{3,0},{4,5},{5,6},{6,7},{7,4},{8,9},{9,10},{10,1... | collective-permute-start | bytes 786440 | tf_op jit(solution)/shard_map/ppermute | solution.py:338
  95.7 9.4 %collective-permute-start.6 = (bf16[128,512]{1,0:T(8,128)(2,1)S(1)}, bf16[128,512]{1,0:T(8,128)(2,1)S(1)}, u32[]{:S(2)}, u32[]{:S(2)}) collective-permute-start(bf16[128,512]{1,0:T(8,128)(2,1)S(1)} %get-tuple-element.43), channel_id=1, source_target_pairs={{0,2},{1,3},{2,0},{3,1},{4,6},{5,7},{6,4},{7,5},{8,10},{9,11},{10,... | collective-permute-start | bytes 393224 | tf_op jit(solution)/shard_map/ppermute | solution.py:338
  98.7 6.4 %collective-permute-start.7 = (bf16[128,512]{1,0:T(8,128)(2,1)S(1)}, bf16[128,512]{1,0:T(8,128)(2,1)S(1)}, u32[]{:S(2)}, u32[]{:S(2)}) collective-permute-start(bf16[128,512]{1,0:T(8,128)(2,1)S(1)} %get-tuple-element.44), channel_id=1, source_target_pairs={{0,1},{1,2},{2,3},{3,0},{4,5},{5,6},{6,7},{7,4},{8,9},{9,10},{10,1... | collective-permute-start | bytes 393224 | tf_op jit(solution)/shard_map/ppermute | solution.py:338
  99.1 13.8 %copy-start.2 = (bf16[2048,512]{1,0:T(8,128)(2,1)S(1)}, bf16[2048,512]{1,0:T(8,128)(2,1)}, u32[]{:S(2)}) copy-start(bf16[2048,512]{1,0:T(8,128)(2,1)} %get-tuple-element.50.refs_11_) | copy-start | bytes 6291460
  99.1 13.8 %copy-start.9 = (s32[128]{0:T(128)S(1)}, s32[128]{0:T(128)}, u32[]{:S(2)}) copy-start(s32[128]{0:T(128)} %param.9) | copy-start | bytes 1540
  99.1 6.0 %collective-permute-start.8 = (bf16[128,512]{1,0:T(8,128)(2,1)S(1)}, bf16[128,512]{1,0:T(8,128)(2,1)S(1)}, u32[]{:S(2)}, u32[]{:S(2)}) collective-permute-start(bf16[128,512]{1,0:T(8,128)(2,1)S(1)} %get-tuple-element.45), channel_id=1, source_target_pairs={{0,3},{1,0},{2,1},{3,2},{4,7},{5,4},{6,5},{7,6},{8,11},{9,8},{10,9... | collective-permute-start | bytes 393224 | tf_op jit(solution)/shard_map/ppermute | solution.py:338
  105.4 4.4 %collective-permute-start.10 = (bf16[128,256]{1,0:T(8,128)(2,1)S(1)}, bf16[128,256]{1,0:T(8,128)(2,1)S(1)}, u32[]{:S(2)}, u32[]{:S(2)}) collective-permute-start(bf16[128,256]{1,0:T(8,128)(2,1)S(1)} %get-tuple-element.70), channel_id=1, source_target_pairs={{0,1},{1,2},{2,3},{3,0},{4,5},{5,6},{6,7},{7,4},{8,9},{9,10},{10,1... | collective-permute-start | bytes 196616 | tf_op jit(solution)/shard_map/ppermute | solution.py:338
  105.5 4.3 %collective-permute-start.11 = (bf16[128,256]{1,0:T(8,128)(2,1)S(1)}, bf16[128,256]{1,0:T(8,128)(2,1)S(1)}, u32[]{:S(2)}, u32[]{:S(2)}) collective-permute-start(bf16[128,256]{1,0:T(8,128)(2,1)S(1)} %get-tuple-element.70), channel_id=1, source_target_pairs={{0,3},{1,0},{2,1},{3,2},{4,7},{5,4},{6,5},{7,6},{8,11},{9,8},{10,9... | collective-permute-start | bytes 196616 | tf_op jit(solution)/shard_map/ppermute | solution.py:338
  108.2 4.6 %collective-permute-start.9 = (bf16[128,256]{1,0:T(8,128)(2,1)S(1)}, bf16[128,256]{1,0:T(8,128)(2,1)S(1)}, u32[]{:S(2)}, u32[]{:S(2)}) collective-permute-start(bf16[128,256]{1,0:T(8,128)(2,1)S(1)} %get-tuple-element.70), channel_id=1, source_target_pairs={{0,2},{1,3},{2,0},{3,1},{4,6},{5,7},{6,4},{7,5},{8,10},{9,11},{10,... | collective-permute-start | bytes 196616 | tf_op jit(solution)/shard_map/ppermute | solution.py:338
  112.9 1.6 copy-start
  114.5 8.4 %copy-start.1 = (bf16[512,2048]{1,0:T(8,128)(2,1)S(1)}, bf16[512,2048]{1,0:T(8,128)(2,1)}, u32[]{:S(2)}) copy-start(bf16[512,2048]{1,0:T(8,128)(2,1)} %get-tuple-element.51.refs_12_.rows_ref) | copy-start | bytes 6291460
  114.5 8.4 %copy-start.3 = (bf16[2048,512]{1,0:T(8,128)(2,1)S(1)}, bf16[2048,512]{1,0:T(8,128)(2,1)}, u32[]{:S(2)}) copy-start(bf16[2048,512]{1,0:T(8,128)(2,1)} %get-tuple-element.59.active_ref) | copy-start | bytes 6291460
  117.9 7.4 %collective-permute-start.12 = (bf16[256,512]{1,0:T(8,128)(2,1)S(1)}, bf16[256,512]{1,0:T(8,128)(2,1)S(1)}, u32[]{:S(2)}, u32[]{:S(2)}) collective-permute-start(bf16[256,512]{1,0:T(8,128)(2,1)S(1)} %get-tuple-element.55), channel_id=1, source_target_pairs={{0,4},{4,0},{8,12},{12,8},{16,20},{20,16},{24,28},{28,24},{1,5},{5... | collective-permute-start | bytes 786440 | tf_op jit(solution)/shard_map/ppermute | solution.py:392
  122.9 5.3 %copy-start.4 = (bf16[2048,512]{1,0:T(8,128)(2,1)S(1)}, bf16[2048,512]{1,0:T(8,128)(2,1)}, u32[]{:S(2)}) copy-start(bf16[2048,512]{1,0:T(8,128)(2,1)} %get-tuple-element.53.active_ref) | copy-start | bytes 6291460
  124.7 6.0 %collective-permute-start.14 = (bf16[256,512]{1,0:T(8,128)(2,1)S(1)}, bf16[256,512]{1,0:T(8,128)(2,1)S(1)}, u32[]{:S(2)}, u32[]{:S(2)}) collective-permute-start(bf16[256,512]{1,0:T(8,128)(2,1)S(1)} %get-tuple-element.61), channel_id=1, source_target_pairs={{0,4},{4,0},{8,12},{12,8},{16,20},{20,16},{24,28},{28,24},{1,5},{5... | collective-permute-start | bytes 786440 | tf_op jit(solution)/shard_map/ppermute | solution.py:392
  124.8 10.9 %collective-permute-start.20 = (bf16[256,256]{1,0:T(8,128)(2,1)S(1)}, bf16[256,256]{1,0:T(8,128)(2,1)S(1)}, u32[]{:S(2)}, u32[]{:S(2)}) collective-permute-start(bf16[256,256]{1,0:T(8,128)(2,1)S(1)} %get-tuple-element.67), channel_id=1, source_target_pairs={{0,4},{4,0},{8,12},{12,8},{16,20},{20,16},{24,28},{28,24},{1,5},{5... | collective-permute-start | bytes 393224 | tf_op jit(solution)/shard_map/ppermute | solution.py:392
  125.4 7.3 %collective-permute-start.15 = (bf16[128,512]{1,0:T(8,128)(2,1)S(1)}, bf16[128,512]{1,0:T(8,128)(2,1)S(1)}, u32[]{:S(2)}, u32[]{:S(2)}) collective-permute-start(bf16[128,512]{1,0:T(8,128)(2,1)S(1)} %get-tuple-element.68.refs_0_), channel_id=1, source_target_pairs={{0,1},{1,2},{2,3},{3,0},{4,5},{5,6},{6,7},{7,4},{8,9},{9,10},{10,1... | collective-permute-start | bytes 393224 | tf_op jit(solution)/shard_map/ppermute | solution.py:338
  125.4 8.8 %collective-permute-start.18 = (bf16[128,512]{1,0:T(8,128)(2,1)S(1)}, bf16[128,512]{1,0:T(8,128)(2,1)S(1)}, u32[]{:S(2)}, u32[]{:S(2)}) collective-permute-start(bf16[128,512]{1,0:T(8,128)(2,1)S(1)} %get-tuple-element.69.refs_1_), channel_id=1, source_target_pairs={{0,3},{1,0},{2,1},{3,2},{4,7},{5,4},{6,5},{7,6},{8,11},{9,8},{10,9... | collective-permute-start | bytes 393224 | tf_op jit(solution)/shard_map/ppermute | solution.py:338
  128.1 2.6 %copy-start.5 = (bf16[2048,512]{1,0:T(8,128)(2,1)S(1)}, bf16[2048,512]{1,0:T(8,128)(2,1)}, u32[]{:S(2)}) copy-start(bf16[2048,512]{1,0:T(8,128)(2,1)} %get-tuple-element.63.active_ref) | copy-start | bytes 6291460
  129.9 5.8 %collective-permute-start.13 = (bf16[256,512]{1,0:T(8,128)(2,1)S(1)}, bf16[256,512]{1,0:T(8,128)(2,1)S(1)}, u32[]{:S(2)}, u32[]{:S(2)}) collective-permute-start(bf16[256,512]{1,0:T(8,128)(2,1)S(1)} %get-tuple-element.57), channel_id=1, source_target_pairs={{0,4},{4,0},{8,12},{12,8},{16,20},{20,16},{24,28},{28,24},{1,5},{5... | collective-permute-start | bytes 786440 | tf_op jit(solution)/shard_map/ppermute | solution.py:392
  132.5 1.6 collective-permute-start.17
  132.7 8.7 %collective-permute-start.16 = (bf16[256,512]{1,0:T(8,128)(2,1)S(1)}, bf16[256,512]{1,0:T(8,128)(2,1)S(1)}, u32[]{:S(2)}, u32[]{:S(2)}) collective-permute-start(bf16[256,512]{1,0:T(8,128)(2,1)S(1)} %pad_maximum_fusion.1), channel_id=1, source_target_pairs={{0,1},{1,2},{2,3},{3,0},{4,5},{5,6},{6,7},{7,4},{8,9},{9,10},{10,1... | collective-permute-start | bytes 786440 | tf_op jit(solution)/shard_map/ppermute | solution.py:338
  134.3 7.8 %collective-permute-start.19 = (bf16[256,512]{1,0:T(8,128)(2,1)S(1)}, bf16[256,512]{1,0:T(8,128)(2,1)S(1)}, u32[]{:S(2)}, u32[]{:S(2)}) collective-permute-start(bf16[256,512]{1,0:T(8,128)(2,1)S(1)} %pad_maximum_fusion.2), channel_id=1, source_target_pairs={{0,3},{1,0},{2,1},{3,2},{4,7},{5,4},{6,5},{7,6},{8,11},{9,8},{10,9... | collective-permute-start | bytes 786440 | tf_op jit(solution)/shard_map/ppermute | solution.py:338
  178.2 4.7 %collective-permute-start.21 = (bf16[256,768]{1,0:T(8,128)(2,1)S(1)}, bf16[256,768]{1,0:T(8,128)(2,1)S(1)}, u32[]{:S(2)}, u32[]{:S(2)}) collective-permute-start(bf16[256,768]{1,0:T(8,128)(2,1)S(1)} %bitcast.22), channel_id=1, source_target_pairs={{0,4},{4,0},{8,12},{12,8},{16,20},{20,16},{24,28},{28,24},{1,5},{5... | collective-permute-start | bytes 1179656 | tf_op jit(solution)/shard_map/ppermute | solution.py:392

commit v9 on v8

--- a/solution.py
+++ b/solution.py
@@ -137,13 +137,18 @@
     )(asked, pltpu.with_memory_space_constraint(features, pltpu.HBM))
 
 
-def slice_grad(spread_ref, d_hidden, active_ref, rows_ref, own_ref, other_ref):
+def slice_grad(core, spread, d_hidden, active, rows, hidden, d_logits, own_ref, other_ref):
     half = own_ref.shape[0]
-    scattered = dot(spread_ref[...], d_hidden).astype(BF)
-    d_pre = jnp.where(active_ref[...] > 0, scattered, jnp.zeros_like(scattered))
-    total = dot(rows_ref[...], d_pre)
-    own_ref[...] = total[:half]
-    other_ref[...] = total[half:].astype(BF)
+    units = d_hidden.shape[1]
+    scattered = dot(spread[...], d_hidden).astype(BF)
+    d_pre = jnp.where(active[...] > 0, scattered, jnp.zeros_like(scattered))
+    total = dot(rows[...], d_pre)
+    own_ref[:, :units] = total[:half]
+    other_ref[:, :units] = total[half:].astype(BF)
+    mine = hidden[:, pl.ds(pl.multiple_of(core * half, half), half)]
+    other = hidden[:, pl.ds(pl.multiple_of((1 - core) * half, half), half)]
+    own_ref[:, units:] = dot(mine, d_logits, 0, 0)
+    other_ref[:, units:] = dot(other, d_logits, 0, 0).astype(BF)
 
 
 def middle(parts, labels, hidden, w_twos, core, spread_t, active, rows_t):
@@ -151,14 +156,20 @@
     targets, classes = parts[0].shape
     units = hidden.shape[1]
     half = units // 2
-    half_f = rows_t.shape[0] // 2
 
     def kernel(core_ref, *refs):
         part_refs, refs = refs[:count], refs[count:]
         labels_ref, hidden_ref = refs[:2]
-        w_refs, refs = refs[2 : 2 + count], refs[2 + count :]
-        spread_ref, active_ref, rows_ref, own_ref, other_ref, own_two, other_two = refs[:7]
-        d_hidden_refs = refs[7:]
+        sources, refs = refs[2 : 5 + count], refs[5 + count :]
+        own_ref, other_ref, d_logits_ref = refs[:3]
+        d_hidden_refs, refs = refs[3 : 2 + count], refs[2 + count :]
+        scratch, sems = refs[:-1], refs[-1]
+        copies = [
+            pltpu.make_async_copy(source, target, sems.at[i])
+            for i, (source, target) in enumerate(zip(sources, scratch))
+        ]
+        for copy in copies:
+            copy.start()
         logits = part_refs[0][...]
         for part in part_refs[1:]:
             logits += part[...].astype(F32)
@@ -167,133 +178,165 @@
         ids = lax.broadcasted_iota(jnp.int32, (targets, classes), 1)
         label = jnp.broadcast_to(labels_ref[...], (targets, targets)).T[:, :1]
         d_logits = (probability - (label == ids).astype(F32)).astype(BF)
-        d_first = dot(d_logits, w_refs[0][...], 1, 1).astype(BF)
-        for w_ref, out in zip(w_refs[1:], d_hidden_refs):
-            out[...] = dot(d_logits, w_ref[...], 1, 1).astype(BF)
-        slice_grad(spread_ref, d_first, active_ref, rows_ref, own_ref, other_ref)
-        both = dot(hidden_ref[...], d_logits, 0, 0)
-        swap = core_ref[0] != 0
-        low, high = both[:half], both[half:]
-        own_two[...] = jnp.where(swap, high, low)
-        other_two[...] = jnp.where(swap, low, high).astype(BF)
-
+        d_logits_ref[...] = d_logits
+        copies[0].wait()
+        d_first = dot(d_logits, scratch[0][...], 1, 1).astype(BF)
+        for copy in copies[1:4]:
+            copy.wait()
+        slice_grad(
+            core_ref[0],
+            scratch[1],
+            d_first,
+            scratch[2],
+            scratch[3],
+            hidden_ref,
+            d_logits,
+            own_ref,
+            other_ref,
+        )
+        for copy, w_two, out in zip(copies[4:], scratch[4:], d_hidden_refs):
+            copy.wait()
+            out[...] = dot(d_logits, w_two[...], 1, 1).astype(BF)
+
+    moved = [w_twos[0], spread_t, active, rows_t, *w_twos[1:]]
+    moved = [pltpu.with_memory_space_constraint(x, pltpu.HBM) for x in moved]
     return pl.pallas_call(
         kernel,
         out_shape=[
-            jax.ShapeDtypeStruct((half_f, units), F32),
-            jax.ShapeDtypeStruct((half_f, units), BF),
-            jax.ShapeDtypeStruct((half, classes), F32),
-            jax.ShapeDtypeStruct((half, classes), BF),
+            jax.ShapeDtypeStruct((half, units + classes), F32),
+            jax.ShapeDtypeStruct((half, units + classes), BF),
+            jax.ShapeDtypeStruct((targets, classes), BF),
         ]
         + [jax.ShapeDtypeStruct((targets, units), BF)] * (count - 1),
-        in_specs=[SMEM] + [VMEM] * (2 * count + 5),
-        out_specs=[VMEM] * (3 + count),
+        in_specs=[SMEM] + [VMEM] * (count + 2) + [HBM] * len(moved),
+        out_specs=[VMEM] * (2 + count),
+        scratch_shapes=[pltpu.VMEM(x.shape, BF) for x in moved]
+        + [pltpu.SemaphoreType.DMA((len(moved),))],
         compiler_params=pltpu.CompilerParams(vmem_limit_bytes=24 * 2**20),
         cost_estimate=pl.CostEstimate(
             flops=2 * targets * classes * units * (count + 1),
             bytes_accessed=4 * 2**20,
             transcendentals=targets * classes,
         ),
-    )(core, *parts, labels, hidden, *w_twos, spread_t, active, rows_t)
-
-
-def forward(rows, w_ones, spread, core, out_type, turn):
+    )(core, *parts, labels, hidden, *moved)
+
+
+def forward(rows, w_ones, w_twos, spread, core):
     slots, width_f = rows.shape
     targets = spread.shape[0]
-    units = width_f
+    units, classes = w_twos[0].shape
     half = width_f // 2
     block = 512
     count = len(w_ones)
 
     def kernel(core_ref, rows_ref, spread_ref, *refs):
-        w_refs, refs = refs[:count], refs[count:]
-        active_refs, refs = refs[:count], refs[count:]
-        hidden_refs, refs = refs[:count], refs[count:]
-        turned_refs, refs = refs[:turn], refs[turn:]
-        w_all, active_all, spread_all, w_sems, out_sems, spread_sem = refs[:6]
-        turned, turned_sems = refs[6 : 6 + turn], refs[6 + turn :]
-        for i in range(count):
-            pltpu.make_async_copy(
-                w_refs[i], w_all.at[i], w_sems.at[i]
-            ).start()
-        spread_copy = pltpu.make_async_copy(spread_ref, spread_all, spread_sem)
+        w_refs, refs = refs[: 2 * count], refs[2 * count :]
+        active_refs, hidden_refs = refs[:count], refs[count : 2 * count]
+        logits_ref, narrow_ref, turned_ref = refs[2 * count : 2 * count + 3]
+        refs = refs[2 * count + 3 :]
+        w_one_all, w_two_all, active_all, spread_all, turned, w_sems, out_sems, sem = refs
+
+        def w_copy(i):
+            target = w_one_all.at[i] if i < count else w_two_all.at[i - count]
+            return pltpu.make_async_copy(w_refs[i], target, w_sems.at[i])
+
+        for i in range(2 * count):
+            w_copy(i).start()
+        spread_copy = pltpu.make_async_copy(spread_ref, spread_all, sem)
         spread_copy.start()
         mine = pl.multiple_of(core_ref[0] * half, half)
         other = pl.multiple_of((1 - core_ref[0]) * half, half)
-        for source, target, sem in zip(turned, turned_refs, turned_sems):
-
-            @pl.loop(0, slots // block)
-            def _(j, source=source):
-                at = pl.ds(pl.multiple_of(j * block, block), block)
-                flat = rows_ref[at, :].T
-                source[pl.ds(mine, half), at] = flat[:half]
-                source[pl.ds(other, half), at] = flat[half:]
-
-            pltpu.make_async_copy(source, target, sem).start()
+
+        @pl.loop(0, slots // block)
+        def _(j):
+            at = pl.ds(pl.multiple_of(j * block, block), block)
+            flat = rows_ref[at, :].T
+            turned[pl.ds(mine, half), at] = flat[:half]
+            turned[pl.ds(other, half), at] = flat[half:]
+
+        turned_copy = pltpu.make_async_copy(turned, turned_ref, out_sems.at[count])
+        turned_copy.start()
+        out_copies = [
+            pltpu.make_async_copy(active_all.at[i], active_refs[i], out_sems.at[i])
+            for i in range(count)
+        ]
+        spread_copy.wait()
+        logits = jnp.zeros((targets, classes), F32)
         for i in range(count):
-            pltpu.make_async_copy(
-                w_refs[i], w_all.at[i], w_sems.at[i]
-            ).wait()
-
-            active_all[i] = jnp.maximum(dot(rows_ref[...], w_all[i]), 0.0).astype(BF)
-            pltpu.make_async_copy(active_all.at[i], active_refs[i], out_sems.at[i]).start()
-            if i == 0:
-                spread_copy.wait()
-            hidden_refs[i][...] = dot(spread_all[...], active_all[i]).astype(out_type)
-        for i in range(count):
-            pltpu.make_async_copy(active_all.at[i], active_refs[i], out_sems.at[i]).wait()
-        for source, target, sem in zip(turned, turned_refs, turned_sems):
-            pltpu.make_async_copy(source, target, sem).wait()
-
-    shapes = (
-        [pltpu.HBM((slots, units), BF)] * count
-        + [jax.ShapeDtypeStruct((targets, units), out_type)] * count
-        + [pltpu.HBM((width_f, slots), BF)] * turn
-    )
-    return pl.pallas_call(
-        kernel,
-        out_shape=shapes,
-        in_specs=[SMEM, VMEM, HBM] + [HBM] * count,
-        out_specs=[HBM] * count + [VMEM] * count + [HBM] * turn,
+            w_copy(i).wait()
+            active_all[i] = jnp.maximum(dot(rows_ref[...], w_one_all[i]), 0.0).astype(BF)
+            out_copies[i].start()
+            hidden = dot(spread_all[...], active_all[i]).astype(BF)
+            hidden_refs[i][...] = hidden
+            w_copy(count + i).wait()
+            logits += dot(hidden, w_two_all[i])
+        logits_ref[...] = logits
+        narrow_ref[...] = logits.astype(BF)
+        for copy in out_copies:
+            copy.wait()
+        turned_copy.wait()
+
+    w_all = [pltpu.with_memory_space_constraint(x, pltpu.HBM) for x in (*w_ones, *w_twos)]
+    return pl.pallas_call(
+        kernel,
+        out_shape=[pltpu.HBM((slots, units), BF)] * count
+        + [jax.ShapeDtypeStruct((targets, units), BF)] * count
+        + [
+            jax.ShapeDtypeStruct((targets, classes), F32),
+            jax.ShapeDtypeStruct((targets, classes), BF),
+            pltpu.HBM((width_f, slots), BF),
+        ],
+        in_specs=[SMEM, VMEM, HBM] + [HBM] * (2 * count),
+        out_specs=[HBM] * count + [VMEM] * (count + 2) + [HBM],
         scratch_shapes=[
             pltpu.VMEM((count, width_f, units), BF),
+            pltpu.VMEM((count, units, classes), BF),
             pltpu.VMEM((count, slots, units), BF),
             pltpu.VMEM((targets, slots), BF),
-            pltpu.SemaphoreType.DMA((count,)),
-            pltpu.SemaphoreType.DMA((count,)),
+            pltpu.VMEM((width_f, slots), BF),
+            pltpu.SemaphoreType.DMA((2 * count,)),
+            pltpu.SemaphoreType.DMA((count + 1,)),
             pltpu.SemaphoreType.DMA,
-        ]
-        + [pltpu.VMEM((width_f, slots), BF)] * turn
-        + [pltpu.SemaphoreType.DMA] * turn,
-        compiler_params=pltpu.CompilerParams(vmem_limit_bytes=24 * 2**20),
+        ],
+        compiler_params=pltpu.CompilerParams(vmem_limit_bytes=32 * 2**20),
         cost_estimate=pl.CostEstimate(
             flops=2 * count * slots * units * (width_f + targets),
             bytes_accessed=2 * slots * (width_f + units + targets),
             transcendentals=0,
         ),
-    )(core, rows, *(pltpu.with_memory_space_constraint(x, pltpu.HBM) for x in (spread, *w_ones)))
-
-
-def backward(spread_t, d_hidden, active, rows_t, earlier):
+    )(core, rows, pltpu.with_memory_space_constraint(spread, pltpu.HBM), *w_all)
+
+
+def backward(core, spread_t, d_hidden, active, rows_t, hidden, d_logits, earlier):
     units = d_hidden.shape[1]
     half = rows_t.shape[0] // 2
-
-    def kernel(spread_ref, d_hidden_ref, active_ref, rows_ref, *refs):
-        slice_grad(spread_ref, d_hidden_ref[...], active_ref, rows_ref, *refs[-2:])
+    width = units + d_logits.shape[1]
+
+    def kernel(core_ref, spread_ref, d_hidden_ref, active_ref, rows_ref, hidden_ref, logits_ref, *refs):
+        slice_grad(
+            core_ref[0],
+            spread_ref,
+            d_hidden_ref[...],
+            active_ref,
+            rows_ref,
+            hidden_ref,
+            logits_ref[...],
+            *refs[-2:],
+        )
 
     return pl.pallas_call(
         kernel,
         out_shape=[
-            jax.ShapeDtypeStruct((half, units), F32),
-            jax.ShapeDtypeStruct((half, units), BF),
-        ],
-        in_specs=[VMEM] * 4 + [pl.BlockSpec(memory_space=pl.ANY)] * len(earlier),
+            jax.ShapeDtypeStruct((half, width), F32),
+            jax.ShapeDtypeStruct((half, width), BF),
+        ],
+        in_specs=[SMEM] + [VMEM] * 6 + [pl.BlockSpec(memory_space=pl.ANY)] * len(earlier),
         out_specs=[VMEM] * 2,
         compiler_params=pltpu.CompilerParams(vmem_limit_bytes=24 * 2**20),
         cost_estimate=pl.CostEstimate(
             flops=2 * units, bytes_accessed=2 * units, transcendentals=0
         ),
-    )(spread_t, d_hidden, active, rows_t, *earlier)
+    )(core, spread_t, d_hidden, active, rows_t, hidden, d_logits, *earlier)
 
 
 def outputs(own, other, core, units):
@@ -373,28 +416,23 @@
     spread, spread_t = lax.optimization_barrier((spread, spread.T))
 
     core_id = core.reshape(1)
-    first = steps[:-1]
-    out = forward(received, [w_ones[s] for s in first], spread, core_id, BF, 0)
-    active = dict(zip(first, out))
-    shares = [to_mlp(part, step) for part, step in zip(out[len(first) :], first)]
-    active[0], hidden, rows_t = forward(received, [w_one], spread, core_id, F32, 1)
-    for share_in in shares:
-        hidden += share_in.astype(F32)
-    hidden = hidden.astype(BF)
     half = width_f // 2
-
-    part = dot(hidden, w_two)
-    parts = [part] + [to_mlp(part.astype(BF), step) for step in steps[:-1]]
+    out = forward(
+        received, [w_ones[s] for s in steps], [w_twos[s] for s in steps], spread, core_id
+    )
+    active, hidden = dict(zip(steps, out)), dict(zip(steps, out[mlp_n:]))
+    part, narrow, rows_t = out[2 * mlp_n :]
+    parts = [part] + [to_mlp(narrow, step) for step in steps[:-1]]
 
     pairs = [(i, i ^ 1) for i in range(col_n)]
 
     def partner(x):
         return lax.ppermute(x, "col", pairs)
 
-    mine, other, own_two, other_two, *d_hidden = middle(
+    mine, other, d_logits, *d_hidden = middle(
         parts,
         labels[None],
-        hidden,
+        hidden[2],
         [w_twos[s] for s in steps],
         core_id,
         spread_t,
@@ -408,15 +446,16 @@
     for step in (1, 0, 3):
         i = steps.index(step) - 1
         earlier = () if step == 1 else far if step == 0 else (near[1],)
-        mine, other = backward(spread_t, d_hidden[i], active[step], rows_t, earlier)
+        mine, other = backward(
+            core_id, spread_t, d_hidden[i], active[step], rows_t, hidden[step], d_logits, earlier
+        )
         near[step] = mine + partner(other).astype(F32)
     top, bottom = near[1][: half // 2], near[1][half // 2 :]
     near[1] = jnp.concatenate([top + upward.astype(F32), bottom], axis=0).astype(BF)
     top, bottom = near[3][: half // 2], near[3][half // 2 :]
     near[3] = jnp.concatenate([top, bottom + downward.astype(F32)], axis=0).astype(BF)
-    grad_one = near[0] + to_mlp(near[1], 1).astype(F32) + to_mlp(near[3], -1).astype(F32)
-    grad_two = own_two + partner(other_two).astype(F32)
-    both = jnp.concatenate([grad_one, grad_two], axis=1).astype(BF)
+    both = near[0] + to_mlp(near[1], 1).astype(F32) + to_mlp(near[3], -1).astype(F32)
+    both = both.astype(BF)
     chips = owners // 2
     groups = [[2 * i + c for i in range(chips)] for c in (0, 1)]
     width = units + classes

time: 185 us -> 182 us (0.984)
  starting transfers between devices: 48.7 us -> 45.8 us
  blocking collectives: 35.7 us -> 33.7 us
  Pallas kernels: 30.8 us -> 32.7 us
    all_to_all x2, waiting for transfers between devices: 14.1 us -> 21.1 us  [exchange(): lax.all_to_all(x, axes, split_axis=0, concat_axis=0, tiled=True, axis_ind...]
    ppermute x16 -> x13, waiting for transfers between devices: 44.7 us -> 38.9 us  [to_mlp(): lax.ppermute(x, 'mlp', [(j, (j + step) % mlp_n) for j in range(mlp_n)])]
    ppermute x16 -> x13, starting transfers between devices: 21.1 us -> 18.4 us  [to_mlp(): lax.ppermute(x, 'mlp', [(j, (j + step) % mlp_n) for j in range(mlp_n)])]
    all_to_all x2, blocking collectives: 35.7 us -> 33.7 us  [exchange(): lax.all_to_all(x, axes, split_axis=0, concat_axis=0, tiled=True, axis_ind...]
    pallas_call x6 -> x5, Pallas kernels: 19.4 us -> 21.3 us  [the longest x1 10.6 us: forward(): pl.pallas_call(kernel, out_shape=[pltpu.HBM((slots, units), BF)] * count...]
    ppermute x6 -> x5, starting transfers between devices: 9.74 us -> 9.5 us  [partner(): return lax.ppermute(x, 'col', pairs)]
  transfers between devices with their start and end apart: 24 -> 20, of which waited for: 10 -> 10; matrix products, arithmetic and copies ran while one was open for 2% -> 2% of each run, Pallas kernels for 5% -> 3%
where the time goes in v9:
time: 182 us; the launch traced here: 181 us
  waiting for transfers between devices  62.6 us (34%)
  starting transfers between devices  45.8 us (25%)
  blocking collectives  33.7 us (19%)
  Pallas kernels  32.7 us (18%)
  other arithmetic  2.9 us (2%)
    ppermute x13, waiting for transfers between devices, to_mlp(): lax.ppermute(x, 'mlp', [(j, (j + step) % mlp_n) for j in range(mlp_n)])  38.9 us
    all_to_all x2, blocking collectives, exchange(): lax.all_to_all(x, axes, split_axis=0, concat_axis=0, tiled=True, axis_ind...  33.7 us
    all_to_all x2, waiting for transfers between devices, exchange(): lax.all_to_all(x, axes, split_axis=0, concat_axis=0, tiled=True, axis_ind...  21.1 us
    ppermute x13, starting transfers between devices, to_mlp(): lax.ppermute(x, 'mlp', [(j, (j + step) % mlp_n) for j in range(mlp_n)])  18.4 us
    all_to_all x2, starting transfers between devices, exchange(): lax.all_to_all(x, axes, split_axis=0, concat_axis=0, tiled=True, axis_ind...  17.9 us
    pallas_call x1, Pallas kernels, forward(): pl.pallas_call(kernel, out_shape=[pltpu.HBM((slots, units), BF)] * count...  10.6 us
    ppermute x5, starting transfers between devices, partner(): return lax.ppermute(x, 'col', pairs)  9.5 us
    pallas_call x1, Pallas kernels, gather(): pl.pallas_call(kernel, out_shape=pltpu.HBM((count, width_f), BF), in_spec...  8.01 us
  transfers between devices with their start and end apart: 20, of which 10 were waited for; matrix products, arithmetic and copies ran while one was open for 2% of the time, Pallas kernels for 3%

profile of v9, /device:TPU:1, one launch (start us, length us, event | category | flops | bytes accessed | tf_op | source)
XLA Modules:
  0.0 181.2 jit_solution(9853394796589441452)
XLA Ops:
  0.6 0.0 copy-start.5
  0.6 0.7 copy-done.5
  1.3 2.1 %shard_map.77 = (s32[64,128]{1,0:T(8,128)}, s32[32,128]{1,0:T(8,128)S(1)}) custom-call(s32[32,128]{1,0:T(8,128)S(1)} %bitcast.19), custom_call_target="tpu_custom_call" | custom-call | tf_op jit(solution)/shard_map/pallas_call | solution.py:70
  3.5 13.0 %all-to-all-start = ((s32[64,1,128]{2,1,0:T(1,128)}), s32[64,1,128]{2,1,0:T(1,128)S(1)}, u32[]{:S(2)}, u32[]{:S(2)}) async-start(s32[64,1,128]{2,1,0:T(1,128)} %bitcast.6), calls=%async_computation | async-start | bytes 65536 | tf_op jit(solution)/shard_map/all_to_all | solution.py:17
  16.5 9.3 %all-to-all-done = s32[64,1,128]{2,1,0:T(1,128)S(1)} async-done(((s32[64,1,128]{2,1,0:T(1,128)}), s32[64,1,128]{2,1,0:T(1,128)S(1)}, u32[]{:S(2)}, u32[]{:S(2)}) %all-to-all-start) | async-done | bytes 32800 | tf_op jit(solution)/shard_map/all_to_all | solution.py:17
  25.8 0.2 dynamic-slice_reduce_fusion
  25.9 0.1 reshape.45.asked_ref
  26.0 8.0 %shard_map.78 = bf16[2048,512]{1,0:T(8,128)(2,1)} custom-call(s32[2048]{0:T(1024)S(1)} %reshape.45.asked_ref, bf16[4096,512]{1,0:T(8,128)(2,1)} %features_ref.1), custom_call_target="tpu_custom_call" | custom-call | tf_op jit(solution)/shard_map/pallas_call | solution.py:124
  34.0 0.0 copy-start.8
  34.1 0.0 copy-start.6
  34.1 0.0 copy-start.12
  34.1 4.9 %all-to-all-start.1 = ((bf16[64,32,512]{2,1,0:T(8,128)(2,1)}), bf16[64,32,512]{2,1,0:T(8,128)(2,1)S(1)}, u32[]{:S(2)}, u32[]{:S(2)}) async-start(bf16[64,32,512]{2,1,0:T(8,128)(2,1)} %bitcast.23), calls=%async_computation.1 | async-start | bytes 4194304 | tf_op jit(solution)/shard_map/all_to_all | solution.py:17
  39.0 3.0 %collective-permute-start.4 = (bf16[512,256]{1,0:T(8,128)(2,1)S(1)}, bf16[512,256]{1,0:T(8,128)(2,1)S(1)}, u32[]{:S(2)}, u32[]{:S(2)}) collective-permute-start(bf16[512,256]{1,0:T(8,128)(2,1)S(1)} %copy-done.8), channel_id=1, source_target_pairs={{0,2},{1,3},{2,0},{3,1},{4,6},{5,7},{6,4},{7,5},{8,10},{9,11},{10,... | collective-permute-start | bytes 786440 | tf_op jit(solution)/shard_map/ppermute | solution.py:381
  42.0 0.8 collective-permute-start.3
  42.8 1.4 collective-permute-start.1
  44.2 1.7 collective-permute-start
  45.9 0.0 collective-permute-start.2
  45.9 0.4 convolution_bitcast_fusion
  46.4 0.1 copy.11
  46.5 0.1 broadcast_in_dim.59
  46.6 0.4 convolution_bitcast_fusion.1
  47.1 0.1 copy.10
  47.1 0.1 convert_element_type.58
  47.2 1.4 select_convert_fusion.refs_7_.spread_ref
  48.6 0.7 collective-permute-start.5
  49.3 0.9 select_convert_fusion.1.spread_ref
  50.2 4.0 %collective-permute-done.3.refs_5_.refs_10_ = bf16[512,256]{1,0:T(8,128)(2,1)S(1)} collective-permute-done((bf16[512,256]{1,0:T(8,128)(2,1)S(1)}, bf16[512,256]{1,0:T(8,128)(2,1)S(1)}, u32[]{:S(2)}, u32[]{:S(2)}) %collective-permute-start.3) | collective-permute-done | bytes 262176 | tf_op jit(solution)/shard_map/ppermute | solution.py:381
  54.2 22.8 %collective-permute-done.5.refs_6_.refs_11_ = bf16[512,256]{1,0:T(8,128)(2,1)S(1)} collective-permute-done((bf16[512,256]{1,0:T(8,128)(2,1)S(1)}, bf16[512,256]{1,0:T(8,128)(2,1)S(1)}, u32[]{:S(2)}, u32[]{:S(2)}) %collective-permute-start.5) | collective-permute-done | bytes 262176 | tf_op jit(solution)/shard_map/ppermute | solution.py:381
  77.0 0.0 collective-permute-done.1.refs_0_
  77.0 0.0 collective-permute-done.refs_1_
  77.0 11.8 %all-to-all-done.1 = bf16[64,32,512]{2,1,0:T(8,128)(2,1)S(1)} async-done(((bf16[64,32,512]{2,1,0:T(8,128)(2,1)}), bf16[64,32,512]{2,1,0:T(8,128)(2,1)S(1)}, u32[]{:S(2)}, u32[]{:S(2)}) %all-to-all-start.1) | async-done | bytes 2097184 | tf_op jit(solution)/shard_map/all_to_all | solution.py:17
  88.7 0.0 copy-start.7
  88.8 10.6 %shard_map.79 = (bf16[2048,512]{1,0:T(8,128)(2,1)}, bf16[2048,512]{1,0:T(8,128)(2,1)}, bf16[2048,512]{1,0:T(8,128)(2,1)}, bf16[2048,512]{1,0:T(8,128)(2,1)}, bf1...) custom-call(s32[1]{0:T(128)} %bitcast.core_ref, ...), custom_call_target="tpu_custom_call" | custom-call | flops 5368709120 | bytes 4718592 | tf_op jit(solution)/shard_map/pallas_call | solution.py:280
  99.4 2.8 %collective-permute-start.8 = (bf16[128,256]{1,0:T(8,128)(2,1)S(1)}, bf16[128,256]{1,0:T(8,128)(2,1)S(1)}, u32[]{:S(2)}, u32[]{:S(2)}) collective-permute-start(bf16[128,256]{1,0:T(8,128)(2,1)S(1)} %get-tuple-element.50), channel_id=1, source_target_pairs={{0,3},{1,0},{2,1},{3,2},{4,7},{5,4},{6,5},{7,6},{8,11},{9,8},{10,9... | collective-permute-start | bytes 196616 | tf_op jit(solution)/shard_map/ppermute | solution.py:381
  102.2 0.0 collective-permute-start.7
  102.2 1.6 collective-permute-start.6
  103.8 3.4 %collective-permute-done.7.refs_2_ = bf16[128,256]{1,0:T(8,128)(2,1)S(1)} collective-permute-done((bf16[128,256]{1,0:T(8,128)(2,1)S(1)}, bf16[128,256]{1,0:T(8,128)(2,1)S(1)}, u32[]{:S(2)}, u32[]{:S(2)}) %collective-permute-start.7) | collective-permute-done | bytes 65568 | tf_op jit(solution)/shard_map/ppermute | solution.py:381
  107.2 0.0 copy-start.1
  107.2 5.2 %shard_map.80 = (f32[256,768]{1,0:T(8,128)S(1)}, bf16[256,768]{1,0:T(8,128)(2,1)S(1)}, bf16[128,256]{1,0:T(8,128)(2,1)S(1)}, bf16[128,512]{1,0:T(8,128)(2,1)S(1)...) custom-call(s32[1]{0:T(128)} %bitcast.core_ref, f32[128,256]{1,0:T(8,128)S(1)} %get-tuple-element.49.refs_0_, ...), custom_call_target="tpu_custom_call" | custom-call | flops 167772160 | bytes 4194304 | tf_op jit(solution)/shard_map/pallas_call | solution.py:203
  112.5 3.7 %collective-permute-start.9 = (bf16[256,768]{1,0:T(8,128)(2,1)S(1)}, bf16[256,768]{1,0:T(8,128)(2,1)S(1)}, u32[]{:S(2)}, u32[]{:S(2)}) collective-permute-start(bf16[256,768]{1,0:T(8,128)(2,1)S(1)} %get-tuple-element.59), channel_id=1, source_target_pairs={{0,4},{4,0},{8,12},{12,8},{16,20},{20,16},{24,28},{28,24},{1,5},{5... | collective-permute-start | bytes 1179656 | tf_op jit(solution)/shard_map/ppermute | solution.py:430
  116.2 1.8 %shard_map.82 = (f32[256,768]{1,0:T(8,128)S(1)}, bf16[256,768]{1,0:T(8,128)(2,1)S(1)}) custom-call(s32[1]{0:T(128)} %bitcast.core_ref, bf16[2048,128]{1,0:T(8,128)(2,1)S(1)} %copy-done.1, bf16[128,512]{1,0:T(8,128)(2,1)S(1)} %get-tuple-element.62.d_hidden_ref, bf16[2048,512]{1,0:T(8,128)(2,1)S(1)} %copy-done.4, bf16[512,2048]{1,0:T(8,128)(2,1)S(1)} %copy-done, ...), custom_call_target="tpu_custom_call" | custom-call | flops 1024 | bytes 1024 | tf_op jit(solution)/shard_map/pallas_call | solution.py:327
  118.1 0.1 collective-permute-start.11
  118.2 0.1 add_convert_fusion.1
  118.3 0.3 collective-permute-start.12
  118.6 1.3 collective-permute-done.11
  119.9 0.1 convert_add_fusion.1.refs_0_
  120.0 1.8 %shard_map.83 = (f32[256,768]{1,0:T(8,128)S(1)}, bf16[256,768]{1,0:T(8,128)(2,1)S(1)}) custom-call(s32[1]{0:T(128)} %bitcast.core_ref, bf16[2048,128]{1,0:T(8,128)(2,1)S(1)} %copy-done.1, bf16[128,512]{1,0:T(8,128)(2,1)S(1)} %get-tuple-element.67.d_hidden_ref, bf16[2048,512]{1,0:T(8,128)(2,1)S(1)} %copy-done.2, bf16[512,2048]{1,0:T(8,128)(2,1)S(1)} %copy-done, ...), custom_call_target="tpu_custom_call" | custom-call | flops 1024 | bytes 1024 | tf_op jit(solution)/shard_map/pallas_call | solution.py:327
  121.8 0.4 collective-permute-start.14
  122.2 2.5 %collective-permute-start.15 = (bf16[128,768]{1,0:T(8,128)(2,1)S(1)}, bf16[128,768]{1,0:T(8,128)(2,1)S(1)}, u32[]{:S(2)}, u32[]{:S(2)}) collective-permute-start(bf16[128,768]{1,0:T(8,128)(2,1)S(1)} %get-tuple-element.73.refs_1_), channel_id=1, source_target_pairs={{0,3},{1,0},{2,1},{3,2},{4,7},{5,4},{6,5},{7,6},{8,11},{9,8},{10,9... | collective-permute-start | bytes 589832 | tf_op jit(solution)/shard_map/ppermute | solution.py:381
  124.7 1.8 %shard_map.81 = (f32[256,768]{1,0:T(8,128)S(1)}, bf16[256,768]{1,0:T(8,128)(2,1)S(1)}) custom-call(s32[1]{0:T(128)} %bitcast.core_ref, bf16[2048,128]{1,0:T(8,128)(2,1)S(1)} %copy-done.1, bf16[128,512]{1,0:T(8,128)(2,1)S(1)} %get-tuple-element.54.d_hidden_ref, bf16[2048,512]{1,0:T(8,128)(2,1)S(1)} %copy-done.3, bf16[512,2048]{1,0:T(8,128)(2,1)S(1)} %copy-done, ...), custom_call_target="tpu_custom_call" | custom-call | flops 1024 | bytes 1024 | tf_op jit(solution)/shard_map/pallas_call | solution.py:327
  126.6 0.6 collective-permute-start.10
  127.3 0.1 collective-permute-start.13
  127.4 0.1 convert_add_fusion
  127.5 1.3 collective-permute-done.15
  128.9 3.5 %collective-permute-start.16 = (bf16[256,768]{1,0:T(8,128)(2,1)S(1)}, bf16[256,768]{1,0:T(8,128)(2,1)S(1)}, u32[]{:S(2)}, u32[]{:S(2)}) collective-permute-start(bf16[256,768]{1,0:T(8,128)(2,1)S(1)} %pad_maximum_fusion.1), channel_id=1, source_target_pairs={{0,3},{1,0},{2,1},{3,2},{4,7},{5,4},{6,5},{7,6},{8,11},{9,8},{10,9... | collective-permute-start | bytes 1179656 | tf_op jit(solution)/shard_map/ppermute | solution.py:381
  132.4 6.9 %collective-permute-done.13 = bf16[256,768]{1,0:T(8,128)(2,1)S(1)} collective-permute-done((bf16[256,768]{1,0:T(8,128)(2,1)S(1)}, bf16[256,768]{1,0:T(8,128)(2,1)S(1)}, u32[]{:S(2)}, u32[]{:S(2)}) %collective-permute-start.13) | collective-permute-done | bytes 393248 | tf_op jit(solution)/shard_map/ppermute | solution.py:381
  139.3 0.5 collective-permute-done.16
  139.8 0.2 fusion.12
  139.9 16.1 %all_to_all.24 = bf16[32,8,768]{2,1,0:T(8,128)(2,1)S(1)} all-to-all(bf16[32,8,768]{2,1,0:T(8,128)(2,1)S(1)} %fusion.12), channel_id=1, replica_groups={{0,8,16,24,32,40,48,56,64,72,80,88,96,104,112,120,128,136,144,152,160,1..., dimensions={0} | all-to-all | bytes 786432 | tf_op jit(solution)/shard_map/all_to_all | solution.py:17
  156.0 0.1 reduce_sum.12
  156.1 17.6 %all_to_all.25 = bf16[32,8,768]{2,1,0:T(8,128)(2,1)S(1)} all-to-all(bf16[32,8,768]{2,1,0:T(8,128)(2,1)S(1)} %broadcast_in_dim.65), channel_id=1, replica_groups={{0,8,16,24,32,40,48,56,64,72,80,88,96,104,112,120,128,136,144,152,160,1..., dimensions={0} | all-to-all | bytes 786432 | tf_op jit(solution)/shard_map/all_to_all | solution.py:17
  173.8 4.7 %collective-permute-start.17 = (bf16[256,768]{1,0:T(8,128)(2,1)S(1)}, bf16[256,768]{1,0:T(8,128)(2,1)S(1)}, u32[]{:S(2)}, u32[]{:S(2)}) collective-permute-start(bf16[256,768]{1,0:T(8,128)(2,1)S(1)} %bitcast.17), channel_id=1, source_target_pairs={{0,4},{4,0},{8,12},{12,8},{16,20},{20,16},{24,28},{28,24},{1,5},{5... | collective-permute-start | bytes 1179656 | tf_op jit(solution)/shard_map/ppermute | solution.py:430
  178.4 1.3 collective-permute-done.17.other_ref
  179.8 1.2 shard_map.84
  (39 shorter events, 0.3 us)
Async XLA Ops:
  0.6 0.7 copy-start.5
  3.5 22.3 %all-to-all-start = ((s32[64,1,128]{2,1,0:T(1,128)}), s32[64,1,128]{2,1,0:T(1,128)S(1)}, u32[]{:S(2)}, u32[]{:S(2)}) async-start(s32[64,1,128]{2,1,0:T(1,128)} %bitcast.6), calls=%async_computation | async-start | bytes 65536 | tf_op jit(solution)/shard_map/all_to_all | solution.py:17
  34.0 5.0 %copy-start.8 = (bf16[512,256]{1,0:T(8,128)(2,1)S(1)}, bf16[512,256]{1,0:T(8,128)(2,1)}, u32[]{:S(2)}) copy-start(bf16[512,256]{1,0:T(8,128)(2,1)} %refs_12_) | copy-start | bytes 786436
  34.1 11.9 %copy-start.6 = (s32[128,32]{0,1:T(8,128)S(1)}, s32[128,32]{0,1:T(8,128)}, u32[]{:S(2)}) copy-start(s32[128,32]{0,1:T(8,128)} %param.7) | copy-start | bytes 49156
  34.1 11.9 %copy-start.12 = (bf16[128,32]{0,1:T(8,128)(2,1)S(1)}, bf16[128,32]{0,1:T(8,128)(2,1)}, u32[]{:S(2)}) copy-start(bf16[128,32]{0,1:T(8,128)(2,1)} %param.8) | copy-start | bytes 24580
  34.1 54.7 %all-to-all-start.1 = ((bf16[64,32,512]{2,1,0:T(8,128)(2,1)}), bf16[64,32,512]{2,1,0:T(8,128)(2,1)S(1)}, u32[]{:S(2)}, u32[]{:S(2)}) async-start(bf16[64,32,512]{2,1,0:T(8,128)(2,1)} %bitcast.23), calls=%async_computation.1 | async-start | bytes 4194304 | tf_op jit(solution)/shard_map/all_to_all | solution.py:17
  39.0 9.6 %collective-permute-start.4 = (bf16[512,256]{1,0:T(8,128)(2,1)S(1)}, bf16[512,256]{1,0:T(8,128)(2,1)S(1)}, u32[]{:S(2)}, u32[]{:S(2)}) collective-permute-start(bf16[512,256]{1,0:T(8,128)(2,1)S(1)} %copy-done.8), channel_id=1, source_target_pairs={{0,2},{1,3},{2,0},{3,1},{4,6},{5,7},{6,4},{7,5},{8,10},{9,11},{10,... | collective-permute-start | bytes 786440 | tf_op jit(solution)/shard_map/ppermute | solution.py:381
  42.0 12.1 %collective-permute-start.3 = (bf16[512,256]{1,0:T(8,128)(2,1)S(1)}, bf16[512,256]{1,0:T(8,128)(2,1)S(1)}, u32[]{:S(2)}, u32[]{:S(2)}) collective-permute-start(bf16[512,256]{1,0:T(8,128)(2,1)S(1)} %copy-done.8), channel_id=1, source_target_pairs={{0,3},{1,0},{2,1},{3,2},{4,7},{5,4},{6,5},{7,6},{8,11},{9,8},{10,9... | collective-permute-start | bytes 786440 | tf_op jit(solution)/shard_map/ppermute | solution.py:381
  42.8 34.1 %collective-permute-start.1 = (bf16[512,512]{1,0:T(8,128)(2,1)}, bf16[512,512]{1,0:T(8,128)(2,1)}, u32[]{:S(2)}, u32[]{:S(2)}) collective-permute-start(bf16[512,512]{1,0:T(8,128)(2,1)} %refs_3_), channel_id=1, source_target_pairs={{0,2},{1,3},{2,0},{3,1},{4,6},{5,7},{6,4},{7,5},{8,10},{9,11},{10,... | collective-permute-start | bytes 1572872 | tf_op jit(solution)/shard_map/ppermute | solution.py:381
  44.2 32.7 %collective-permute-start = (bf16[512,512]{1,0:T(8,128)(2,1)}, bf16[512,512]{1,0:T(8,128)(2,1)}, u32[]{:S(2)}, u32[]{:S(2)}) collective-permute-start(bf16[512,512]{1,0:T(8,128)(2,1)} %refs_3_), channel_id=1, source_target_pairs={{0,3},{1,0},{2,1},{3,2},{4,7},{5,4},{6,5},{7,6},{8,11},{9,8},{10,9... | collective-permute-start | bytes 1572872 | tf_op jit(solution)/shard_map/ppermute | solution.py:381
  45.9 31.1 %collective-permute-start.2 = (bf16[512,512]{1,0:T(8,128)(2,1)}, bf16[512,512]{1,0:T(8,128)(2,1)}, u32[]{:S(2)}, u32[]{:S(2)}) collective-permute-start(bf16[512,512]{1,0:T(8,128)(2,1)} %refs_3_), channel_id=1, source_target_pairs={{0,1},{1,2},{2,3},{3,0},{4,5},{5,6},{6,7},{7,4},{8,9},{9,10},{10,1... | collective-permute-start | bytes 1572872 | tf_op jit(solution)/shard_map/ppermute | solution.py:381
  48.6 40.1 %copy-start.9 = (bf16[512,256]{1,0:T(8,128)(2,1)}, bf16[512,256]{1,0:T(8,128)(2,1)S(1)}, u32[]{:S(2)}) copy-start(bf16[512,256]{1,0:T(8,128)(2,1)S(1)} %collective-permute-done.4.refs_4_.refs_6_) | copy-start | bytes 786436
  48.6 28.3 %collective-permute-start.5 = (bf16[512,256]{1,0:T(8,128)(2,1)S(1)}, bf16[512,256]{1,0:T(8,128)(2,1)S(1)}, u32[]{:S(2)}, u32[]{:S(2)}) collective-permute-start(bf16[512,256]{1,0:T(8,128)(2,1)S(1)} %copy-done.8), channel_id=1, source_target_pairs={{0,1},{1,2},{2,3},{3,0},{4,5},{5,6},{6,7},{7,4},{8,9},{9,10},{10,1... | collective-permute-start | bytes 786440 | tf_op jit(solution)/shard_map/ppermute | solution.py:381
  54.2 34.5 %copy-start.10 = (bf16[512,256]{1,0:T(8,128)(2,1)}, bf16[512,256]{1,0:T(8,128)(2,1)S(1)}, u32[]{:S(2)}) copy-start(bf16[512,256]{1,0:T(8,128)(2,1)S(1)} %collective-permute-done.3.refs_5_.refs_10_) | copy-start | bytes 786436
  77.0 11.8 %copy-start.11 = (bf16[512,256]{1,0:T(8,128)(2,1)}, bf16[512,256]{1,0:T(8,128)(2,1)S(1)}, u32[]{:S(2)}) copy-start(bf16[512,256]{1,0:T(8,128)(2,1)S(1)} %collective-permute-done.5.refs_6_.refs_11_) | copy-start | bytes 786436
  88.7 18.5 %copy-start.7 = (s32[128]{0:T(128)S(1)}, s32[128]{0:T(128)}, u32[]{:S(2)}) copy-start(s32[128]{0:T(128)} %param.9) | copy-start | bytes 1540
  99.4 4.5 %collective-permute-start.8 = (bf16[128,256]{1,0:T(8,128)(2,1)S(1)}, bf16[128,256]{1,0:T(8,128)(2,1)S(1)}, u32[]{:S(2)}, u32[]{:S(2)}) collective-permute-start(bf16[128,256]{1,0:T(8,128)(2,1)S(1)} %get-tuple-element.50), channel_id=1, source_target_pairs={{0,3},{1,0},{2,1},{3,2},{4,7},{5,4},{6,5},{7,6},{8,11},{9,8},{10,9... | collective-permute-start | bytes 196616 | tf_op jit(solution)/shard_map/ppermute | solution.py:381
  102.2 5.0 %collective-permute-start.7 = (bf16[128,256]{1,0:T(8,128)(2,1)S(1)}, bf16[128,256]{1,0:T(8,128)(2,1)S(1)}, u32[]{:S(2)}, u32[]{:S(2)}) collective-permute-start(bf16[128,256]{1,0:T(8,128)(2,1)S(1)} %get-tuple-element.50), channel_id=1, source_target_pairs={{0,1},{1,2},{2,3},{3,0},{4,5},{5,6},{6,7},{7,4},{8,9},{9,10},{10,1... | collective-permute-start | bytes 196616 | tf_op jit(solution)/shard_map/ppermute | solution.py:381
  102.2 5.0 %collective-permute-start.6 = (bf16[128,256]{1,0:T(8,128)(2,1)S(1)}, bf16[128,256]{1,0:T(8,128)(2,1)S(1)}, u32[]{:S(2)}, u32[]{:S(2)}) collective-permute-start(bf16[128,256]{1,0:T(8,128)(2,1)S(1)} %get-tuple-element.50), channel_id=1, source_target_pairs={{0,2},{1,3},{2,0},{3,1},{4,6},{5,7},{6,4},{7,5},{8,10},{9,11},{10,... | collective-permute-start | bytes 196616 | tf_op jit(solution)/shard_map/ppermute | solution.py:381
  107.2 9.0 %copy-start = (bf16[512,2048]{1,0:T(8,128)(2,1)S(1)}, bf16[512,2048]{1,0:T(8,128)(2,1)}, u32[]{:S(2)}) copy-start(bf16[512,2048]{1,0:T(8,128)(2,1)} %get-tuple-element.53.refs_9_.rows_ref) | copy-start | bytes 6291460
  107.2 9.0 %copy-start.1 = (bf16[2048,128]{1,0:T(8,128)(2,1)S(1)}, bf16[2048,128]{1,0:T(8,128)(2,1)}, u32[]{:S(2)}) copy-start(bf16[2048,128]{1,0:T(8,128)(2,1)} %select_convert_fusion.refs_7_.spread_ref) | copy-start | bytes 1572868
  107.2 9.0 %copy-start.4 = (bf16[2048,512]{1,0:T(8,128)(2,1)S(1)}, bf16[2048,512]{1,0:T(8,128)(2,1)}, u32[]{:S(2)}) copy-start(bf16[2048,512]{1,0:T(8,128)(2,1)} %get-tuple-element.63.active_ref) | copy-start | bytes 6291460
  112.5 5.7 %collective-permute-start.9 = (bf16[256,768]{1,0:T(8,128)(2,1)S(1)}, bf16[256,768]{1,0:T(8,128)(2,1)S(1)}, u32[]{:S(2)}, u32[]{:S(2)}) collective-permute-start(bf16[256,768]{1,0:T(8,128)(2,1)S(1)} %get-tuple-element.59), channel_id=1, source_target_pairs={{0,4},{4,0},{8,12},{12,8},{16,20},{20,16},{24,28},{28,24},{1,5},{5... | collective-permute-start | bytes 1179656 | tf_op jit(solution)/shard_map/ppermute | solution.py:430
  118.1 1.8 collective-permute-start.11
  118.2 1.8 copy-start.2
  118.3 8.9 %collective-permute-start.12 = (bf16[128,768]{1,0:T(8,128)(2,1)S(1)}, bf16[128,768]{1,0:T(8,128)(2,1)S(1)}, u32[]{:S(2)}, u32[]{:S(2)}) collective-permute-start(bf16[128,768]{1,0:T(8,128)(2,1)S(1)} %get-tuple-element.72.refs_0_), channel_id=1, source_target_pairs={{0,1},{1,2},{2,3},{3,0},{4,5},{5,6},{6,7},{7,4},{8,9},{9,10},{10,1... | collective-permute-start | bytes 589832 | tf_op jit(solution)/shard_map/ppermute | solution.py:381
  120.0 4.8 %copy-start.3 = (bf16[2048,512]{1,0:T(8,128)(2,1)S(1)}, bf16[2048,512]{1,0:T(8,128)(2,1)}, u32[]{:S(2)}) copy-start(bf16[2048,512]{1,0:T(8,128)(2,1)} %get-tuple-element.55.active_ref) | copy-start | bytes 6291460
  121.8 5.5 %collective-permute-start.14 = (bf16[256,768]{1,0:T(8,128)(2,1)S(1)}, bf16[256,768]{1,0:T(8,128)(2,1)S(1)}, u32[]{:S(2)}, u32[]{:S(2)}) collective-permute-start(bf16[256,768]{1,0:T(8,128)(2,1)S(1)} %get-tuple-element.71), channel_id=1, source_target_pairs={{0,4},{4,0},{8,12},{12,8},{16,20},{20,16},{24,28},{28,24},{1,5},{5... | collective-permute-start | bytes 1179656 | tf_op jit(solution)/shard_map/ppermute | solution.py:430
  122.2 6.6 %collective-permute-start.15 = (bf16[128,768]{1,0:T(8,128)(2,1)S(1)}, bf16[128,768]{1,0:T(8,128)(2,1)S(1)}, u32[]{:S(2)}, u32[]{:S(2)}) collective-permute-start(bf16[128,768]{1,0:T(8,128)(2,1)S(1)} %get-tuple-element.73.refs_1_), channel_id=1, source_target_pairs={{0,3},{1,0},{2,1},{3,2},{4,7},{5,4},{6,5},{7,6},{8,11},{9,8},{10,9... | collective-permute-start | bytes 589832 | tf_op jit(solution)/shard_map/ppermute | solution.py:381
  126.6 5.8 %collective-permute-start.10 = (bf16[256,768]{1,0:T(8,128)(2,1)S(1)}, bf16[256,768]{1,0:T(8,128)(2,1)S(1)}, u32[]{:S(2)}, u32[]{:S(2)}) collective-permute-start(bf16[256,768]{1,0:T(8,128)(2,1)S(1)} %get-tuple-element.61), channel_id=1, source_target_pairs={{0,4},{4,0},{8,12},{12,8},{16,20},{20,16},{24,28},{28,24},{1,5},{5... | collective-permute-start | bytes 1179656 | tf_op jit(solution)/shard_map/ppermute | solution.py:430
  127.3 12.0 %collective-permute-start.13 = (bf16[256,768]{1,0:T(8,128)(2,1)S(1)}, bf16[256,768]{1,0:T(8,128)(2,1)S(1)}, u32[]{:S(2)}, u32[]{:S(2)}) collective-permute-start(bf16[256,768]{1,0:T(8,128)(2,1)S(1)} %pad_maximum_fusion), channel_id=1, source_target_pairs={{0,1},{1,2},{2,3},{3,0},{4,5},{5,6},{6,7},{7,4},{8,9},{9,10},{10,1... | collective-permute-start | bytes 1179656 | tf_op jit(solution)/shard_map/ppermute | solution.py:381
  128.9 10.9 %collective-permute-start.16 = (bf16[256,768]{1,0:T(8,128)(2,1)S(1)}, bf16[256,768]{1,0:T(8,128)(2,1)S(1)}, u32[]{:S(2)}, u32[]{:S(2)}) collective-permute-start(bf16[256,768]{1,0:T(8,128)(2,1)S(1)} %pad_maximum_fusion.1), channel_id=1, source_target_pairs={{0,3},{1,0},{2,1},{3,2},{4,7},{5,4},{6,5},{7,6},{8,11},{9,8},{10,9... | collective-permute-start | bytes 1179656 | tf_op jit(solution)/shard_map/ppermute | solution.py:381
  173.8 6.0 %collective-permute-start.17 = (bf16[256,768]{1,0:T(8,128)(2,1)S(1)}, bf16[256,768]{1,0:T(8,128)(2,1)S(1)}, u32[]{:S(2)}, u32[]{:S(2)}) collective-permute-start(bf16[256,768]{1,0:T(8,128)(2,1)S(1)} %bitcast.17), channel_id=1, source_target_pairs={{0,4},{4,0},{8,12},{12,8},{16,20},{20,16},{24,28},{28,24},{1,5},{5... | collective-permute-start | bytes 1179656 | tf_op jit(solution)/shard_map/ppermute | solution.py:430

commit v10 on v9

--- a/solution.py
+++ b/solution.py
@@ -137,18 +137,27 @@
     )(asked, pltpu.with_memory_space_constraint(features, pltpu.HBM))
 
 
-def slice_grad(core, spread, d_hidden, active, rows, hidden, d_logits, own_ref, other_ref):
+def slice_grad(
+    core, spread, d_hidden, active, rows, hidden, d_logits, own_ref, other_ref, waits=(None,) * 3
+):
+    def arrived(i):
+        if waits[i] is not None:
+            waits[i].wait()
+
     half = own_ref.shape[0]
     units = d_hidden.shape[1]
-    scattered = dot(spread[...], d_hidden).astype(BF)
-    d_pre = jnp.where(active[...] > 0, scattered, jnp.zeros_like(scattered))
-    total = dot(rows[...], d_pre)
-    own_ref[:, :units] = total[:half]
-    other_ref[:, :units] = total[half:].astype(BF)
     mine = hidden[:, pl.ds(pl.multiple_of(core * half, half), half)]
     other = hidden[:, pl.ds(pl.multiple_of((1 - core) * half, half), half)]
     own_ref[:, units:] = dot(mine, d_logits, 0, 0)
     other_ref[:, units:] = dot(other, d_logits, 0, 0).astype(BF)
+    arrived(0)
+    scattered = dot(spread[...], d_hidden).astype(BF)
+    arrived(1)
+    d_pre = jnp.where(active[...] > 0, scattered, jnp.zeros_like(scattered))
+    arrived(2)
+    total = dot(rows[...], d_pre)
+    own_ref[:, :units] = total[:half]
+    other_ref[:, :units] = total[half:].astype(BF)
 
 
 def middle(parts, labels, hidden, w_twos, core, spread_t, active, rows_t):
@@ -181,8 +190,6 @@
         d_logits_ref[...] = d_logits
         copies[0].wait()
         d_first = dot(d_logits, scratch[0][...], 1, 1).astype(BF)
-        for copy in copies[1:4]:
-            copy.wait()
         slice_grad(
             core_ref[0],
             scratch[1],
@@ -193,6 +200,7 @@
             d_logits,
             own_ref,
             other_ref,
+            copies[1:4],
         )
         for copy, w_two, out in zip(copies[4:], scratch[4:], d_hidden_refs):
             copy.wait()
@@ -445,7 +453,7 @@
     near = {}
     for step in (1, 0, 3):
         i = steps.index(step) - 1
-        earlier = () if step == 1 else far if step == 0 else (near[1],)
+        earlier = far if step == 1 else (near[1],) if step == 0 else ()
         mine, other = backward(
             core_id, spread_t, d_hidden[i], active[step], rows_t, hidden[step], d_logits, earlier
         )

time: 182 us -> 179 us (0.984)
  waiting for transfers between devices: 62.6 us -> 58.9 us
  starting transfers between devices: 45.8 us -> 48.4 us
    ppermute x5, starting transfers between devices: 9.5 us -> 12.2 us  [partner(): return lax.ppermute(x, 'col', pairs)]
    ppermute x13, waiting for transfers between devices: 38.9 us -> 36.5 us  [to_mlp(): lax.ppermute(x, 'mlp', [(j, (j + step) % mlp_n) for j in range(mlp_n)])]
  transfers between devices with their start and end apart: 20 -> 20, of which waited for: 10 -> 9; matrix products, arithmetic and copies ran while one was open for 2% -> 2% of each run, Pallas kernels for 3% -> 3%
where the time goes in v10:
time: 179 us
  waiting for transfers between devices  58.9 us (33%)
  starting transfers between devices  48.4 us (27%)
  blocking collectives  32.6 us (18%)
  Pallas kernels  32.3 us (18%)
  other arithmetic  2.89 us (2%)
    ppermute x13, waiting for transfers between devices, to_mlp(): lax.ppermute(x, 'mlp', [(j, (j + step) % mlp_n) for j in range(mlp_n)])  36.5 us
    all_to_all x2, blocking collectives, exchange(): lax.all_to_all(x, axes, split_axis=0, concat_axis=0, tiled=True, axis_ind...  32.6 us
    all_to_all x2, waiting for transfers between devices, exchange(): lax.all_to_all(x, axes, split_axis=0, concat_axis=0, tiled=True, axis_ind...  21.1 us
    ppermute x13, starting transfers between devices, to_mlp(): lax.ppermute(x, 'mlp', [(j, (j + step) % mlp_n) for j in range(mlp_n)])  18.3 us
    all_to_all x2, starting transfers between devices, exchange(): lax.all_to_all(x, axes, split_axis=0, concat_axis=0, tiled=True, axis_ind...  17.9 us
    ppermute x5, starting transfers between devices, partner(): return lax.ppermute(x, 'col', pairs)  12.2 us
    pallas_call x1, Pallas kernels, forward(): pl.pallas_call(kernel, out_shape=[pltpu.HBM((slots, units), BF)] * count...  10.6 us
    pallas_call x1, Pallas kernels, gather(): pl.pallas_call(kernel, out_shape=pltpu.HBM((count, width_f), BF), in_spec...  8.01 us
  transfers between devices with their start and end apart: 20, of which 9 were waited for; matrix products, arithmetic and copies ran while one was open for 2% of the time, Pallas kernels for 3%

profile of v10, /device:TPU:1, one launch (start us, length us, event | category | flops | bytes accessed | tf_op | source)
XLA Modules:
  0.0 178.6 jit_solution(9416445444907001086)
XLA Ops:
  0.6 0.0 copy-start.5
  0.6 0.7 copy-done.5
  1.3 2.1 %shard_map.77 = (s32[64,128]{1,0:T(8,128)}, s32[32,128]{1,0:T(8,128)S(1)}) custom-call(s32[32,128]{1,0:T(8,128)S(1)} %bitcast.19), custom_call_target="tpu_custom_call" | custom-call | tf_op jit(solution)/shard_map/pallas_call | solution.py:70
  3.5 13.0 %all-to-all-start = ((s32[64,1,128]{2,1,0:T(1,128)}), s32[64,1,128]{2,1,0:T(1,128)S(1)}, u32[]{:S(2)}, u32[]{:S(2)}) async-start(s32[64,1,128]{2,1,0:T(1,128)} %bitcast.6), calls=%async_computation | async-start | bytes 65536 | tf_op jit(solution)/shard_map/all_to_all | solution.py:17
  16.5 9.3 %all-to-all-done = s32[64,1,128]{2,1,0:T(1,128)S(1)} async-done(((s32[64,1,128]{2,1,0:T(1,128)}), s32[64,1,128]{2,1,0:T(1,128)S(1)}, u32[]{:S(2)}, u32[]{:S(2)}) %all-to-all-start) | async-done | bytes 32800 | tf_op jit(solution)/shard_map/all_to_all | solution.py:17
  25.8 0.2 dynamic-slice_reduce_fusion
  25.9 0.1 reshape.45.asked_ref
  26.0 8.0 %shard_map.78 = bf16[2048,512]{1,0:T(8,128)(2,1)} custom-call(s32[2048]{0:T(1024)S(1)} %reshape.45.asked_ref, bf16[4096,512]{1,0:T(8,128)(2,1)} %features_ref.1), custom_call_target="tpu_custom_call" | custom-call | tf_op jit(solution)/shard_map/pallas_call | solution.py:124
  34.0 0.0 copy-start.8
  34.1 0.0 copy-start.6
  34.1 0.0 copy-start.12
  34.1 4.9 %all-to-all-start.1 = ((bf16[64,32,512]{2,1,0:T(8,128)(2,1)}), bf16[64,32,512]{2,1,0:T(8,128)(2,1)S(1)}, u32[]{:S(2)}, u32[]{:S(2)}) async-start(bf16[64,32,512]{2,1,0:T(8,128)(2,1)} %bitcast.23), calls=%async_computation.1 | async-start | bytes 4194304 | tf_op jit(solution)/shard_map/all_to_all | solution.py:17
  39.0 3.0 %collective-permute-start.4 = (bf16[512,256]{1,0:T(8,128)(2,1)S(1)}, bf16[512,256]{1,0:T(8,128)(2,1)S(1)}, u32[]{:S(2)}, u32[]{:S(2)}) collective-permute-start(bf16[512,256]{1,0:T(8,128)(2,1)S(1)} %copy-done.8), channel_id=1, source_target_pairs={{0,2},{1,3},{2,0},{3,1},{4,6},{5,7},{6,4},{7,5},{8,10},{9,11},{10,... | collective-permute-start | bytes 786440 | tf_op jit(solution)/shard_map/ppermute | solution.py:389
  42.0 0.8 collective-permute-start.3
  42.8 1.4 collective-permute-start.1
  44.2 1.7 collective-permute-start
  45.9 0.0 collective-permute-start.2
  45.9 0.4 convolution_bitcast_fusion
  46.4 0.1 copy.11
  46.5 0.1 broadcast_in_dim.59
  46.6 0.4 convolution_bitcast_fusion.1
  47.1 0.1 copy.10
  47.1 0.1 convert_element_type.58
  47.2 1.4 select_convert_fusion.refs_7_.spread_ref
  48.6 0.0 collective-permute-done.4.refs_4_.refs_6_
  48.6 0.7 collective-permute-start.5
  49.3 0.9 select_convert_fusion.1.spread_ref
  50.2 4.0 %collective-permute-done.3.refs_5_.refs_10_ = bf16[512,256]{1,0:T(8,128)(2,1)S(1)} collective-permute-done((bf16[512,256]{1,0:T(8,128)(2,1)S(1)}, bf16[512,256]{1,0:T(8,128)(2,1)S(1)}, u32[]{:S(2)}, u32[]{:S(2)}) %collective-permute-start.3) | collective-permute-done | bytes 262176 | tf_op jit(solution)/shard_map/ppermute | solution.py:389
  54.2 22.8 %collective-permute-done.5.refs_6_.refs_11_ = bf16[512,256]{1,0:T(8,128)(2,1)S(1)} collective-permute-done((bf16[512,256]{1,0:T(8,128)(2,1)S(1)}, bf16[512,256]{1,0:T(8,128)(2,1)S(1)}, u32[]{:S(2)}, u32[]{:S(2)}) %collective-permute-start.5) | collective-permute-done | bytes 262176 | tf_op jit(solution)/shard_map/ppermute | solution.py:389
  77.0 0.0 collective-permute-done.2.refs_2_
  77.0 11.8 %all-to-all-done.1 = bf16[64,32,512]{2,1,0:T(8,128)(2,1)S(1)} async-done(((bf16[64,32,512]{2,1,0:T(8,128)(2,1)}), bf16[64,32,512]{2,1,0:T(8,128)(2,1)S(1)}, u32[]{:S(2)}, u32[]{:S(2)}) %all-to-all-start.1) | async-done | bytes 2097184 | tf_op jit(solution)/shard_map/all_to_all | solution.py:17
  88.7 0.0 copy-start.7
  88.8 10.6 %shard_map.79 = (bf16[2048,512]{1,0:T(8,128)(2,1)}, bf16[2048,512]{1,0:T(8,128)(2,1)}, bf16[2048,512]{1,0:T(8,128)(2,1)}, bf16[2048,512]{1,0:T(8,128)(2,1)}, bf1...) custom-call(s32[1]{0:T(128)} %bitcast.core_ref, ...), custom_call_target="tpu_custom_call" | custom-call | flops 5368709120 | bytes 4718592 | tf_op jit(solution)/shard_map/pallas_call | solution.py:288
  99.4 2.8 %collective-permute-start.8 = (bf16[128,256]{1,0:T(8,128)(2,1)S(1)}, bf16[128,256]{1,0:T(8,128)(2,1)S(1)}, u32[]{:S(2)}, u32[]{:S(2)}) collective-permute-start(bf16[128,256]{1,0:T(8,128)(2,1)S(1)} %get-tuple-element.50), channel_id=1, source_target_pairs={{0,3},{1,0},{2,1},{3,2},{4,7},{5,4},{6,5},{7,6},{8,11},{9,8},{10,9... | collective-permute-start | bytes 196616 | tf_op jit(solution)/shard_map/ppermute | solution.py:389
  102.2 1.6 collective-permute-start.6
  103.8 3.4 %collective-permute-done.7.refs_2_ = bf16[128,256]{1,0:T(8,128)(2,1)S(1)} collective-permute-done((bf16[128,256]{1,0:T(8,128)(2,1)S(1)}, bf16[128,256]{1,0:T(8,128)(2,1)S(1)}, u32[]{:S(2)}, u32[]{:S(2)}) %collective-permute-start.7) | collective-permute-done | bytes 65568 | tf_op jit(solution)/shard_map/ppermute | solution.py:389
  107.2 0.0 collective-permute-done.6.refs_1_
  107.2 0.0 copy-start.1
  107.2 4.6 %shard_map.80 = (f32[256,768]{1,0:T(8,128)S(1)}, bf16[256,768]{1,0:T(8,128)(2,1)S(1)}, bf16[128,256]{1,0:T(8,128)(2,1)S(1)}, bf16[128,512]{1,0:T(8,128)(2,1)S(1)...) custom-call(s32[1]{0:T(128)} %bitcast.core_ref, f32[128,256]{1,0:T(8,128)S(1)} %get-tuple-element.49.refs_0_, ...), custom_call_target="tpu_custom_call" | custom-call | flops 167772160 | bytes 4194304 | tf_op jit(solution)/shard_map/pallas_call | solution.py:211
  111.9 3.7 %collective-permute-start.9 = (bf16[256,768]{1,0:T(8,128)(2,1)S(1)}, bf16[256,768]{1,0:T(8,128)(2,1)S(1)}, u32[]{:S(2)}, u32[]{:S(2)}) collective-permute-start(bf16[256,768]{1,0:T(8,128)(2,1)S(1)} %get-tuple-element.62), channel_id=1, source_target_pairs={{0,4},{4,0},{8,12},{12,8},{16,20},{20,16},{24,28},{28,24},{1,5},{5... | collective-permute-start | bytes 1179656 | tf_op jit(solution)/shard_map/ppermute | solution.py:438
  115.6 1.9 %shard_map.83 = (f32[256,768]{1,0:T(8,128)S(1)}, bf16[256,768]{1,0:T(8,128)(2,1)S(1)}) custom-call(s32[1]{0:T(128)} %bitcast.core_ref, bf16[2048,128]{1,0:T(8,128)(2,1)S(1)} %copy-done.1, bf16[128,512]{1,0:T(8,128)(2,1)S(1)} %get-tuple-element.67.d_hidden_ref, bf16[2048,512]{1,0:T(8,128)(2,1)S(1)} %copy-done.4, bf16[512,2048]{1,0:T(8,128)(2,1)S(1)} %copy-done, ...), custom_call_target="tpu_custom_call" | custom-call | flops 1024 | bytes 1024 | tf_op jit(solution)/shard_map/pallas_call | solution.py:335
  117.5 0.3 collective-permute-start.14
  117.9 0.0 collective-permute-done.9
  117.9 0.1 add_convert_fusion.1
  118.0 0.1 collective-permute-start.12
  118.1 2.7 %collective-permute-start.15 = (bf16[128,768]{1,0:T(8,128)(2,1)S(1)}, bf16[128,768]{1,0:T(8,128)(2,1)S(1)}, u32[]{:S(2)}, u32[]{:S(2)}) collective-permute-start(bf16[128,768]{1,0:T(8,128)(2,1)S(1)} %get-tuple-element.73.refs_1_), channel_id=1, source_target_pairs={{0,3},{1,0},{2,1},{3,2},{4,7},{5,4},{6,5},{7,6},{8,11},{9,8},{10,9... | collective-permute-start | bytes 589832 | tf_op jit(solution)/shard_map/ppermute | solution.py:389
  120.8 1.9 %shard_map.81 = (f32[256,768]{1,0:T(8,128)S(1)}, bf16[256,768]{1,0:T(8,128)(2,1)S(1)}) custom-call(s32[1]{0:T(128)} %bitcast.core_ref, bf16[2048,128]{1,0:T(8,128)(2,1)S(1)} %copy-done.1, bf16[128,512]{1,0:T(8,128)(2,1)S(1)} %get-tuple-element.58.d_hidden_ref, bf16[2048,512]{1,0:T(8,128)(2,1)S(1)} %copy-done.3, bf16[512,2048]{1,0:T(8,128)(2,1)S(1)} %copy-done, ...), custom_call_target="tpu_custom_call" | custom-call | flops 1024 | bytes 1024 | tf_op jit(solution)/shard_map/pallas_call | solution.py:335
  122.6 1.1 collective-permute-start.10
  123.8 0.1 convert_add_fusion
  123.9 0.4 collective-permute-done.15
  124.3 3.5 %collective-permute-start.16 = (bf16[256,768]{1,0:T(8,128)(2,1)S(1)}, bf16[256,768]{1,0:T(8,128)(2,1)S(1)}, u32[]{:S(2)}, u32[]{:S(2)}) collective-permute-start(bf16[256,768]{1,0:T(8,128)(2,1)S(1)} %pad_maximum_fusion.1), channel_id=1, source_target_pairs={{0,3},{1,0},{2,1},{3,2},{4,7},{5,4},{6,5},{7,6},{8,11},{9,8},{10,9... | collective-permute-start | bytes 1179656 | tf_op jit(solution)/shard_map/ppermute | solution.py:389
  127.8 0.1 convert_add_fusion.1.refs_0_
  128.0 0.1 collective-permute-start.13
  128.1 1.9 %shard_map.82 = (f32[256,768]{1,0:T(8,128)S(1)}, bf16[256,768]{1,0:T(8,128)(2,1)S(1)}) custom-call(s32[1]{0:T(128)} %bitcast.core_ref, bf16[2048,128]{1,0:T(8,128)(2,1)S(1)} %copy-done.1, bf16[128,512]{1,0:T(8,128)(2,1)S(1)} %get-tuple-element.54.d_hidden_ref, bf16[2048,512]{1,0:T(8,128)(2,1)S(1)} %copy-done.2, bf16[512,2048]{1,0:T(8,128)(2,1)S(1)} %copy-done, ...), custom_call_target="tpu_custom_call" | custom-call | flops 1024 | bytes 1024 | tf_op jit(solution)/shard_map/pallas_call | solution.py:335
  130.0 2.0 %collective-permute-start.11 = (bf16[256,768]{1,0:T(8,128)(2,1)S(1)}, bf16[256,768]{1,0:T(8,128)(2,1)S(1)}, u32[]{:S(2)}, u32[]{:S(2)}) collective-permute-start(bf16[256,768]{1,0:T(8,128)(2,1)S(1)} %get-tuple-element.66), channel_id=1, source_target_pairs={{0,4},{4,0},{8,12},{12,8},{16,20},{20,16},{24,28},{28,24},{1,5},{5... | collective-permute-start | bytes 1179656 | tf_op jit(solution)/shard_map/ppermute | solution.py:438
  132.0 2.6 %collective-permute-done.16 = bf16[256,768]{1,0:T(8,128)(2,1)S(1)} collective-permute-done((bf16[256,768]{1,0:T(8,128)(2,1)S(1)}, bf16[256,768]{1,0:T(8,128)(2,1)S(1)}, u32[]{:S(2)}, u32[]{:S(2)}) %collective-permute-start.16) | collective-permute-done | bytes 393248 | tf_op jit(solution)/shard_map/ppermute | solution.py:389
  134.6 3.4 %collective-permute-done.13 = bf16[256,768]{1,0:T(8,128)(2,1)S(1)} collective-permute-done((bf16[256,768]{1,0:T(8,128)(2,1)S(1)}, bf16[256,768]{1,0:T(8,128)(2,1)S(1)}, u32[]{:S(2)}, u32[]{:S(2)}) %collective-permute-start.13) | collective-permute-done | bytes 393248 | tf_op jit(solution)/shard_map/ppermute | solution.py:389
  138.0 0.2 fusion.12
  138.2 15.8 %all_to_all.24 = bf16[32,8,768]{2,1,0:T(8,128)(2,1)S(1)} all-to-all(bf16[32,8,768]{2,1,0:T(8,128)(2,1)S(1)} %fusion.12), channel_id=1, replica_groups={{0,8,16,24,32,40,48,56,64,72,80,88,96,104,112,120,128,136,144,152,160,1..., dimensions={0} | all-to-all | bytes 786432 | tf_op jit(solution)/shard_map/all_to_all | solution.py:17
  153.9 0.1 reduce_sum.12
  154.0 16.9 %all_to_all.25 = bf16[32,8,768]{2,1,0:T(8,128)(2,1)S(1)} all-to-all(bf16[32,8,768]{2,1,0:T(8,128)(2,1)S(1)} %broadcast_in_dim.65), channel_id=1, replica_groups={{0,8,16,24,32,40,48,56,64,72,80,88,96,104,112,120,128,136,144,152,160,1..., dimensions={0} | all-to-all | bytes 786432 | tf_op jit(solution)/shard_map/all_to_all | solution.py:17
  170.9 5.0 %collective-permute-start.17 = (bf16[256,768]{1,0:T(8,128)(2,1)S(1)}, bf16[256,768]{1,0:T(8,128)(2,1)S(1)}, u32[]{:S(2)}, u32[]{:S(2)}) collective-permute-start(bf16[256,768]{1,0:T(8,128)(2,1)S(1)} %bitcast.17), channel_id=1, source_target_pairs={{0,4},{4,0},{8,12},{12,8},{16,20},{20,16},{24,28},{28,24},{1,5},{5... | collective-permute-start | bytes 1179656 | tf_op jit(solution)/shard_map/ppermute | solution.py:438
  175.9 1.3 collective-permute-done.17.other_ref
  177.2 1.2 shard_map.84
  (39 shorter events, 0.3 us)
Async XLA Ops:
  0.6 0.7 copy-start.5
  3.5 22.3 %all-to-all-start = ((s32[64,1,128]{2,1,0:T(1,128)}), s32[64,1,128]{2,1,0:T(1,128)S(1)}, u32[]{:S(2)}, u32[]{:S(2)}) async-start(s32[64,1,128]{2,1,0:T(1,128)} %bitcast.6), calls=%async_computation | async-start | bytes 65536 | tf_op jit(solution)/shard_map/all_to_all | solution.py:17
  34.0 5.0 %copy-start.8 = (bf16[512,256]{1,0:T(8,128)(2,1)S(1)}, bf16[512,256]{1,0:T(8,128)(2,1)}, u32[]{:S(2)}) copy-start(bf16[512,256]{1,0:T(8,128)(2,1)} %refs_12_) | copy-start | bytes 786436
  34.1 11.9 %copy-start.6 = (s32[128,32]{0,1:T(8,128)S(1)}, s32[128,32]{0,1:T(8,128)}, u32[]{:S(2)}) copy-start(s32[128,32]{0,1:T(8,128)} %param.7) | copy-start | bytes 49156
  34.1 11.9 %copy-start.12 = (bf16[128,32]{0,1:T(8,128)(2,1)S(1)}, bf16[128,32]{0,1:T(8,128)(2,1)}, u32[]{:S(2)}) copy-start(bf16[128,32]{0,1:T(8,128)(2,1)} %param.8) | copy-start | bytes 24580
  34.1 54.7 %all-to-all-start.1 = ((bf16[64,32,512]{2,1,0:T(8,128)(2,1)}), bf16[64,32,512]{2,1,0:T(8,128)(2,1)S(1)}, u32[]{:S(2)}, u32[]{:S(2)}) async-start(bf16[64,32,512]{2,1,0:T(8,128)(2,1)} %bitcast.23), calls=%async_computation.1 | async-start | bytes 4194304 | tf_op jit(solution)/shard_map/all_to_all | solution.py:17
  39.0 9.6 %collective-permute-start.4 = (bf16[512,256]{1,0:T(8,128)(2,1)S(1)}, bf16[512,256]{1,0:T(8,128)(2,1)S(1)}, u32[]{:S(2)}, u32[]{:S(2)}) collective-permute-start(bf16[512,256]{1,0:T(8,128)(2,1)S(1)} %copy-done.8), channel_id=1, source_target_pairs={{0,2},{1,3},{2,0},{3,1},{4,6},{5,7},{6,4},{7,5},{8,10},{9,11},{10,... | collective-permute-start | bytes 786440 | tf_op jit(solution)/shard_map/ppermute | solution.py:389
  42.0 12.1 %collective-permute-start.3 = (bf16[512,256]{1,0:T(8,128)(2,1)S(1)}, bf16[512,256]{1,0:T(8,128)(2,1)S(1)}, u32[]{:S(2)}, u32[]{:S(2)}) collective-permute-start(bf16[512,256]{1,0:T(8,128)(2,1)S(1)} %copy-done.8), channel_id=1, source_target_pairs={{0,3},{1,0},{2,1},{3,2},{4,7},{5,4},{6,5},{7,6},{8,11},{9,8},{10,9... | collective-permute-start | bytes 786440 | tf_op jit(solution)/shard_map/ppermute | solution.py:389
  42.8 34.1 %collective-permute-start.1 = (bf16[512,512]{1,0:T(8,128)(2,1)}, bf16[512,512]{1,0:T(8,128)(2,1)}, u32[]{:S(2)}, u32[]{:S(2)}) collective-permute-start(bf16[512,512]{1,0:T(8,128)(2,1)} %refs_3_), channel_id=1, source_target_pairs={{0,2},{1,3},{2,0},{3,1},{4,6},{5,7},{6,4},{7,5},{8,10},{9,11},{10,... | collective-permute-start | bytes 1572872 | tf_op jit(solution)/shard_map/ppermute | solution.py:389
  44.2 32.7 %collective-permute-start = (bf16[512,512]{1,0:T(8,128)(2,1)}, bf16[512,512]{1,0:T(8,128)(2,1)}, u32[]{:S(2)}, u32[]{:S(2)}) collective-permute-start(bf16[512,512]{1,0:T(8,128)(2,1)} %refs_3_), channel_id=1, source_target_pairs={{0,3},{1,0},{2,1},{3,2},{4,7},{5,4},{6,5},{7,6},{8,11},{9,8},{10,9... | collective-permute-start | bytes 1572872 | tf_op jit(solution)/shard_map/ppermute | solution.py:389
  45.9 31.1 %collective-permute-start.2 = (bf16[512,512]{1,0:T(8,128)(2,1)}, bf16[512,512]{1,0:T(8,128)(2,1)}, u32[]{:S(2)}, u32[]{:S(2)}) collective-permute-start(bf16[512,512]{1,0:T(8,128)(2,1)} %refs_3_), channel_id=1, source_target_pairs={{0,1},{1,2},{2,3},{3,0},{4,5},{5,6},{6,7},{7,4},{8,9},{9,10},{10,1... | collective-permute-start | bytes 1572872 | tf_op jit(solution)/shard_map/ppermute | solution.py:389
  48.6 40.1 %copy-start.9 = (bf16[512,256]{1,0:T(8,128)(2,1)}, bf16[512,256]{1,0:T(8,128)(2,1)S(1)}, u32[]{:S(2)}) copy-start(bf16[512,256]{1,0:T(8,128)(2,1)S(1)} %collective-permute-done.4.refs_4_.refs_6_) | copy-start | bytes 786436
  48.6 28.3 %collective-permute-start.5 = (bf16[512,256]{1,0:T(8,128)(2,1)S(1)}, bf16[512,256]{1,0:T(8,128)(2,1)S(1)}, u32[]{:S(2)}, u32[]{:S(2)}) collective-permute-start(bf16[512,256]{1,0:T(8,128)(2,1)S(1)} %copy-done.8), channel_id=1, source_target_pairs={{0,1},{1,2},{2,3},{3,0},{4,5},{5,6},{6,7},{7,4},{8,9},{9,10},{10,1... | collective-permute-start | bytes 786440 | tf_op jit(solution)/shard_map/ppermute | solution.py:389
  54.2 34.5 %copy-start.10 = (bf16[512,256]{1,0:T(8,128)(2,1)}, bf16[512,256]{1,0:T(8,128)(2,1)S(1)}, u32[]{:S(2)}) copy-start(bf16[512,256]{1,0:T(8,128)(2,1)S(1)} %collective-permute-done.3.refs_5_.refs_10_) | copy-start | bytes 786436
  77.0 11.8 %copy-start.11 = (bf16[512,256]{1,0:T(8,128)(2,1)}, bf16[512,256]{1,0:T(8,128)(2,1)S(1)}, u32[]{:S(2)}) copy-start(bf16[512,256]{1,0:T(8,128)(2,1)S(1)} %collective-permute-done.5.refs_6_.refs_11_) | copy-start | bytes 786436
  88.7 18.5 %copy-start.7 = (s32[128]{0:T(128)S(1)}, s32[128]{0:T(128)}, u32[]{:S(2)}) copy-start(s32[128]{0:T(128)} %param.9) | copy-start | bytes 1540
  99.4 4.5 %collective-permute-start.8 = (bf16[128,256]{1,0:T(8,128)(2,1)S(1)}, bf16[128,256]{1,0:T(8,128)(2,1)S(1)}, u32[]{:S(2)}, u32[]{:S(2)}) collective-permute-start(bf16[128,256]{1,0:T(8,128)(2,1)S(1)} %get-tuple-element.50), channel_id=1, source_target_pairs={{0,3},{1,0},{2,1},{3,2},{4,7},{5,4},{6,5},{7,6},{8,11},{9,8},{10,9... | collective-permute-start | bytes 196616 | tf_op jit(solution)/shard_map/ppermute | solution.py:389
  102.2 5.0 %collective-permute-start.7 = (bf16[128,256]{1,0:T(8,128)(2,1)S(1)}, bf16[128,256]{1,0:T(8,128)(2,1)S(1)}, u32[]{:S(2)}, u32[]{:S(2)}) collective-permute-start(bf16[128,256]{1,0:T(8,128)(2,1)S(1)} %get-tuple-element.50), channel_id=1, source_target_pairs={{0,1},{1,2},{2,3},{3,0},{4,5},{5,6},{6,7},{7,4},{8,9},{9,10},{10,1... | collective-permute-start | bytes 196616 | tf_op jit(solution)/shard_map/ppermute | solution.py:389
  102.2 5.0 %collective-permute-start.6 = (bf16[128,256]{1,0:T(8,128)(2,1)S(1)}, bf16[128,256]{1,0:T(8,128)(2,1)S(1)}, u32[]{:S(2)}, u32[]{:S(2)}) collective-permute-start(bf16[128,256]{1,0:T(8,128)(2,1)S(1)} %get-tuple-element.50), channel_id=1, source_target_pairs={{0,2},{1,3},{2,0},{3,1},{4,6},{5,7},{6,4},{7,5},{8,10},{9,11},{10,... | collective-permute-start | bytes 196616 | tf_op jit(solution)/shard_map/ppermute | solution.py:389
  107.2 8.4 %copy-start = (bf16[512,2048]{1,0:T(8,128)(2,1)S(1)}, bf16[512,2048]{1,0:T(8,128)(2,1)}, u32[]{:S(2)}) copy-start(bf16[512,2048]{1,0:T(8,128)(2,1)} %get-tuple-element.53.refs_9_.rows_ref) | copy-start | bytes 6291460
  107.2 8.4 %copy-start.1 = (bf16[2048,128]{1,0:T(8,128)(2,1)S(1)}, bf16[2048,128]{1,0:T(8,128)(2,1)}, u32[]{:S(2)}) copy-start(bf16[2048,128]{1,0:T(8,128)(2,1)} %select_convert_fusion.refs_7_.spread_ref) | copy-start | bytes 1572868
  107.2 8.4 %copy-start.4 = (bf16[2048,512]{1,0:T(8,128)(2,1)S(1)}, bf16[2048,512]{1,0:T(8,128)(2,1)}, u32[]{:S(2)}) copy-start(bf16[2048,512]{1,0:T(8,128)(2,1)} %get-tuple-element.68.active_ref) | copy-start | bytes 6291460
  111.9 6.0 %collective-permute-start.9 = (bf16[256,768]{1,0:T(8,128)(2,1)S(1)}, bf16[256,768]{1,0:T(8,128)(2,1)S(1)}, u32[]{:S(2)}, u32[]{:S(2)}) collective-permute-start(bf16[256,768]{1,0:T(8,128)(2,1)S(1)} %get-tuple-element.62), channel_id=1, source_target_pairs={{0,4},{4,0},{8,12},{12,8},{16,20},{20,16},{24,28},{28,24},{1,5},{5... | collective-permute-start | bytes 1179656 | tf_op jit(solution)/shard_map/ppermute | solution.py:438
  117.5 3.2 %copy-start.3 = (bf16[2048,512]{1,0:T(8,128)(2,1)S(1)}, bf16[2048,512]{1,0:T(8,128)(2,1)}, u32[]{:S(2)}) copy-start(bf16[2048,512]{1,0:T(8,128)(2,1)} %get-tuple-element.59.active_ref) | copy-start | bytes 6291460
  117.5 6.2 %collective-permute-start.14 = (bf16[256,768]{1,0:T(8,128)(2,1)S(1)}, bf16[256,768]{1,0:T(8,128)(2,1)S(1)}, u32[]{:S(2)}, u32[]{:S(2)}) collective-permute-start(bf16[256,768]{1,0:T(8,128)(2,1)S(1)} %get-tuple-element.71), channel_id=1, source_target_pairs={{0,4},{4,0},{8,12},{12,8},{16,20},{20,16},{24,28},{28,24},{1,5},{5... | collective-permute-start | bytes 1179656 | tf_op jit(solution)/shard_map/ppermute | solution.py:438
  118.0 9.9 %collective-permute-start.12 = (bf16[128,768]{1,0:T(8,128)(2,1)S(1)}, bf16[128,768]{1,0:T(8,128)(2,1)S(1)}, u32[]{:S(2)}, u32[]{:S(2)}) collective-permute-start(bf16[128,768]{1,0:T(8,128)(2,1)S(1)} %get-tuple-element.72.refs_0_), channel_id=1, source_target_pairs={{0,1},{1,2},{2,3},{3,0},{4,5},{5,6},{6,7},{7,4},{8,9},{9,10},{10,1... | collective-permute-start | bytes 589832 | tf_op jit(solution)/shard_map/ppermute | solution.py:389
  118.1 6.1 %collective-permute-start.15 = (bf16[128,768]{1,0:T(8,128)(2,1)S(1)}, bf16[128,768]{1,0:T(8,128)(2,1)S(1)}, u32[]{:S(2)}, u32[]{:S(2)}) collective-permute-start(bf16[128,768]{1,0:T(8,128)(2,1)S(1)} %get-tuple-element.73.refs_1_), channel_id=1, source_target_pairs={{0,3},{1,0},{2,1},{3,2},{4,7},{5,4},{6,5},{7,6},{8,11},{9,8},{10,9... | collective-permute-start | bytes 589832 | tf_op jit(solution)/shard_map/ppermute | solution.py:389
  122.6 5.2 %collective-permute-start.10 = (bf16[256,768]{1,0:T(8,128)(2,1)S(1)}, bf16[256,768]{1,0:T(8,128)(2,1)S(1)}, u32[]{:S(2)}, u32[]{:S(2)}) collective-permute-start(bf16[256,768]{1,0:T(8,128)(2,1)S(1)} %get-tuple-element.64), channel_id=1, source_target_pairs={{0,4},{4,0},{8,12},{12,8},{16,20},{20,16},{24,28},{28,24},{1,5},{5... | collective-permute-start | bytes 1179656 | tf_op jit(solution)/shard_map/ppermute | solution.py:438
  124.3 3.8 %copy-start.2 = (bf16[2048,512]{1,0:T(8,128)(2,1)S(1)}, bf16[2048,512]{1,0:T(8,128)(2,1)}, u32[]{:S(2)}) copy-start(bf16[2048,512]{1,0:T(8,128)(2,1)} %get-tuple-element.55.active_ref) | copy-start | bytes 6291460
  124.3 10.3 %collective-permute-start.16 = (bf16[256,768]{1,0:T(8,128)(2,1)S(1)}, bf16[256,768]{1,0:T(8,128)(2,1)S(1)}, u32[]{:S(2)}, u32[]{:S(2)}) collective-permute-start(bf16[256,768]{1,0:T(8,128)(2,1)S(1)} %pad_maximum_fusion.1), channel_id=1, source_target_pairs={{0,3},{1,0},{2,1},{3,2},{4,7},{5,4},{6,5},{7,6},{8,11},{9,8},{10,9... | collective-permute-start | bytes 1179656 | tf_op jit(solution)/shard_map/ppermute | solution.py:389
  128.0 10.0 %collective-permute-start.13 = (bf16[256,768]{1,0:T(8,128)(2,1)S(1)}, bf16[256,768]{1,0:T(8,128)(2,1)S(1)}, u32[]{:S(2)}, u32[]{:S(2)}) collective-permute-start(bf16[256,768]{1,0:T(8,128)(2,1)S(1)} %pad_maximum_fusion), channel_id=1, source_target_pairs={{0,1},{1,2},{2,3},{3,0},{4,5},{5,6},{6,7},{7,4},{8,9},{9,10},{10,1... | collective-permute-start | bytes 1179656 | tf_op jit(solution)/shard_map/ppermute | solution.py:389
  130.0 8.0 %collective-permute-start.11 = (bf16[256,768]{1,0:T(8,128)(2,1)S(1)}, bf16[256,768]{1,0:T(8,128)(2,1)S(1)}, u32[]{:S(2)}, u32[]{:S(2)}) collective-permute-start(bf16[256,768]{1,0:T(8,128)(2,1)S(1)} %get-tuple-element.66), channel_id=1, source_target_pairs={{0,4},{4,0},{8,12},{12,8},{16,20},{20,16},{24,28},{28,24},{1,5},{5... | collective-permute-start | bytes 1179656 | tf_op jit(solution)/shard_map/ppermute | solution.py:438
  170.9 6.3 %collective-permute-start.17 = (bf16[256,768]{1,0:T(8,128)(2,1)S(1)}, bf16[256,768]{1,0:T(8,128)(2,1)S(1)}, u32[]{:S(2)}, u32[]{:S(2)}) collective-permute-start(bf16[256,768]{1,0:T(8,128)(2,1)S(1)} %bitcast.17), channel_id=1, source_target_pairs={{0,4},{4,0},{8,12},{12,8},{16,20},{20,16},{24,28},{28,24},{1,5},{5... | collective-permute-start | bytes 1179656 | tf_op jit(solution)/shard_map/ppermute | solution.py:438

commit v11 on v10

--- a/solution.py
+++ b/solution.py
@@ -169,16 +169,10 @@
     def kernel(core_ref, *refs):
         part_refs, refs = refs[:count], refs[count:]
         labels_ref, hidden_ref = refs[:2]
-        sources, refs = refs[2 : 5 + count], refs[5 + count :]
+        spread_ref, rows_ref = refs[2:4]
+        sources, refs = refs[4 : 5 + count], refs[5 + count :]
         own_ref, other_ref, d_logits_ref = refs[:3]
-        d_hidden_refs, refs = refs[3 : 2 + count], refs[2 + count :]
-        scratch, sems = refs[:-1], refs[-1]
-        copies = [
-            pltpu.make_async_copy(source, target, sems.at[i])
-            for i, (source, target) in enumerate(zip(sources, scratch))
-        ]
-        for copy in copies:
-            copy.start()
+        d_hidden_refs = refs[3 : 2 + count]
         logits = part_refs[0][...]
         for part in part_refs[1:]:
             logits += part[...].astype(F32)
@@ -188,26 +182,22 @@
         label = jnp.broadcast_to(labels_ref[...], (targets, targets)).T[:, :1]
         d_logits = (probability - (label == ids).astype(F32)).astype(BF)
         d_logits_ref[...] = d_logits
-        copies[0].wait()
-        d_first = dot(d_logits, scratch[0][...], 1, 1).astype(BF)
+        d_first = dot(d_logits, sources[0][...], 1, 1).astype(BF)
         slice_grad(
             core_ref[0],
-            scratch[1],
+            spread_ref,
             d_first,
-            scratch[2],
-            scratch[3],
+            sources[1],
+            rows_ref,
             hidden_ref,
             d_logits,
             own_ref,
             other_ref,
-            copies[1:4],
         )
-        for copy, w_two, out in zip(copies[4:], scratch[4:], d_hidden_refs):
-            copy.wait()
+        for w_two, out in zip(sources[2:], d_hidden_refs):
             out[...] = dot(d_logits, w_two[...], 1, 1).astype(BF)
 
-    moved = [w_twos[0], spread_t, active, rows_t, *w_twos[1:]]
-    moved = [pltpu.with_memory_space_constraint(x, pltpu.HBM) for x in moved]
+    moved = [w_twos[0], active, *w_twos[1:]]
     return pl.pallas_call(
         kernel,
         out_shape=[
@@ -216,33 +206,29 @@
             jax.ShapeDtypeStruct((targets, classes), BF),
         ]
         + [jax.ShapeDtypeStruct((targets, units), BF)] * (count - 1),
-        in_specs=[SMEM] + [VMEM] * (count + 2) + [HBM] * len(moved),
+        in_specs=[SMEM] + [VMEM] * (count + 4 + len(moved)),
         out_specs=[VMEM] * (2 + count),
-        scratch_shapes=[pltpu.VMEM(x.shape, BF) for x in moved]
-        + [pltpu.SemaphoreType.DMA((len(moved),))],
         compiler_params=pltpu.CompilerParams(vmem_limit_bytes=24 * 2**20),
         cost_estimate=pl.CostEstimate(
             flops=2 * targets * classes * units * (count + 1),
             bytes_accessed=4 * 2**20,
             transcendentals=targets * classes,
         ),
-    )(core, *parts, labels, hidden, *moved)
-
-
-def forward(rows, w_ones, w_twos, spread, core):
+    )(core, *parts, labels, hidden, spread_t, rows_t, *moved)
+
+
+def forward(rows, w_ones, w_twos, spread):
     slots, width_f = rows.shape
     targets = spread.shape[0]
     units, classes = w_twos[0].shape
-    half = width_f // 2
-    block = 512
     count = len(w_ones)
 
-    def kernel(core_ref, rows_ref, spread_ref, *refs):
+    def kernel(rows_ref, spread_ref, *refs):
         w_refs, refs = refs[: 2 * count], refs[2 * count :]
         active_refs, hidden_refs = refs[:count], refs[count : 2 * count]
-        logits_ref, narrow_ref, turned_ref = refs[2 * count : 2 * count + 3]
-        refs = refs[2 * count + 3 :]
-        w_one_all, w_two_all, active_all, spread_all, turned, w_sems, out_sems, sem = refs
+        logits_ref, narrow_ref = refs[2 * count : 2 * count + 2]
+        refs = refs[2 * count + 2 :]
+        w_one_all, w_two_all, active_all, spread_all, w_sems, out_sems, sem = refs
 
         def w_copy(i):
             target = w_one_all.at[i] if i < count else w_two_all.at[i - count]
@@ -252,18 +238,6 @@
             w_copy(i).start()
         spread_copy = pltpu.make_async_copy(spread_ref, spread_all, sem)
         spread_copy.start()
-        mine = pl.multiple_of(core_ref[0] * half, half)
-        other = pl.multiple_of((1 - core_ref[0]) * half, half)
-
-        @pl.loop(0, slots // block)
-        def _(j):
-            at = pl.ds(pl.multiple_of(j * block, block), block)
-            flat = rows_ref[at, :].T
-            turned[pl.ds(mine, half), at] = flat[:half]
-            turned[pl.ds(other, half), at] = flat[half:]
-
-        turned_copy = pltpu.make_async_copy(turned, turned_ref, out_sems.at[count])
-        turned_copy.start()
         out_copies = [
             pltpu.make_async_copy(active_all.at[i], active_refs[i], out_sems.at[i])
             for i in range(count)
@@ -282,7 +256,6 @@
         narrow_ref[...] = logits.astype(BF)
         for copy in out_copies:
             copy.wait()
-        turned_copy.wait()
 
     w_all = [pltpu.with_memory_space_constraint(x, pltpu.HBM) for x in (*w_ones, *w_twos)]
     return pl.pallas_call(
@@ -292,18 +265,16 @@
         + [
             jax.ShapeDtypeStruct((targets, classes), F32),
             jax.ShapeDtypeStruct((targets, classes), BF),
-            pltpu.HBM((width_f, slots), BF),
         ],
-        in_specs=[SMEM, VMEM, HBM] + [HBM] * (2 * count),
-        out_specs=[HBM] * count + [VMEM] * (count + 2) + [HBM],
+        in_specs=[VMEM, HBM] + [HBM] * (2 * count),
+        out_specs=[HBM] * count + [VMEM] * (count + 2),
         scratch_shapes=[
             pltpu.VMEM((count, width_f, units), BF),
             pltpu.VMEM((count, units, classes), BF),
             pltpu.VMEM((count, slots, units), BF),
             pltpu.VMEM((targets, slots), BF),
-            pltpu.VMEM((width_f, slots), BF),
             pltpu.SemaphoreType.DMA((2 * count,)),
-            pltpu.SemaphoreType.DMA((count + 1,)),
+            pltpu.SemaphoreType.DMA((count,)),
             pltpu.SemaphoreType.DMA,
         ],
         compiler_params=pltpu.CompilerParams(vmem_limit_bytes=32 * 2**20),
@@ -312,7 +283,52 @@
             bytes_accessed=2 * slots * (width_f + units + targets),
             transcendentals=0,
         ),
-    )(core, rows, pltpu.with_memory_space_constraint(spread, pltpu.HBM), *w_all)
+    )(rows, pltpu.with_memory_space_constraint(spread, pltpu.HBM), *w_all)
+
+
+def prepare(rows, core, moved):
+    slots, width_f = rows.shape
+    half = width_f // 2
+    block = 512
+    count = len(moved)
+
+    def kernel(core_ref, rows_ref, *refs):
+        sources, turned = refs[:count], refs[count]
+        targets, sems = refs[count + 1 : -1], refs[-1]
+        copies = [
+            pltpu.make_async_copy(source, target, sems.at[i])
+            for i, (source, target) in enumerate(zip(sources, targets))
+        ]
+        for copy in copies:
+            copy.start()
+        mine = pl.multiple_of(core_ref[0] * half, half)
+        other = pl.multiple_of((1 - core_ref[0]) * half, half)
+
+        @pl.loop(0, slots // block)
+        def _(j):
+            at = pl.ds(pl.multiple_of(j * block, block), block)
+            flat = rows_ref[at, :].T
+            turned[pl.ds(mine, half), at] = flat[:half]
+            turned[pl.ds(other, half), at] = flat[half:]
+
+        for copy in copies:
+            copy.wait()
+
+    moved = [pltpu.with_memory_space_constraint(x, pltpu.HBM) for x in moved]
+    return pl.pallas_call(
+        kernel,
+        out_shape=[jax.ShapeDtypeStruct((width_f, slots), BF)]
+        + [jax.ShapeDtypeStruct(x.shape, BF) for x in moved],
+        in_specs=[SMEM, VMEM] + [HBM] * count,
+        out_specs=[VMEM] * (1 + count),
+        scratch_shapes=[pltpu.SemaphoreType.DMA((count,))],
+        compiler_params=pltpu.CompilerParams(vmem_limit_bytes=24 * 2**20),
+        cost_estimate=pl.CostEstimate(
+            flops=2 * slots * width_f * width_f,
+            bytes_accessed=8 * slots * width_f,
+            transcendentals=0,
+        ),
+    )(core, rows, *moved)
 
 
 def backward(core, spread_t, d_hidden, active, rows_t, hidden, d_logits, earlier):
@@ -426,11 +442,15 @@
     core_id = core.reshape(1)
     half = width_f // 2
     out = forward(
-        received, [w_ones[s] for s in steps], [w_twos[s] for s in steps], spread, core_id
+        received, [w_ones[s] for s in steps], [w_twos[s] for s in steps], spread
     )
     active, hidden = dict(zip(steps, out)), dict(zip(steps, out[mlp_n:]))
-    part, narrow, rows_t = out[2 * mlp_n :]
+    part, narrow = out[2 * mlp_n :]
     parts = [part] + [to_mlp(narrow, step) for step in steps[:-1]]
+
+    rows_t, first_active, *near_twos = prepare(
+        received, core_id, [active[2]] + [w_twos[s] for s in steps]
+    )
 
     pairs = [(i, i ^ 1) for i in range(col_n)]
 
@@ -441,28 +461,37 @@
         parts,
         labels[None],
         hidden[2],
-        [w_twos[s] for s in steps],
+        near_twos,
         core_id,
         spread_t,
-        active[2],
+        first_active,
         rows_t,
     )
     far = (mine + partner(other).astype(F32)).astype(BF)
     far = (far[: half // 2], far[half // 2 :])
     upward, downward = to_mlp(far[0], 1), to_mlp(far[1], -1)
-    near = {}
-    for step in (1, 0, 3):
-        i = steps.index(step) - 1
-        earlier = far if step == 1 else (near[1],) if step == 0 else ()
+
+    def slice_sum(step, earlier):
         mine, other = backward(
-            core_id, spread_t, d_hidden[i], active[step], rows_t, hidden[step], d_logits, earlier
+            core_id,
+            spread_t,
+            d_hidden[steps.index(step) - 1],
+            active[step],
+            rows_t,
+            hidden[step],
+            d_logits,
+            earlier,
         )
-        near[step] = mine + partner(other).astype(F32)
-    top, bottom = near[1][: half // 2], near[1][half // 2 :]
-    near[1] = jnp.concatenate([top + upward.astype(F32), bottom], axis=0).astype(BF)
-    top, bottom = near[3][: half // 2], near[3][half // 2 :]
-    near[3] = jnp.concatenate([top, bottom + downward.astype(F32)], axis=0).astype(BF)
-    both = near[0] + to_mlp(near[1], 1).astype(F32) + to_mlp(near[3], -1).astype(F32)
+        return mine + partner(other).astype(F32)
+
+    below = slice_sum(3, ())
+    above = slice_sum(1, far)
+    top, bottom = above[: half // 2], above[half // 2 :]
+    above = jnp.concatenate([top + upward.astype(F32), bottom], axis=0).astype(BF)
+    top, bottom = below[: half // 2], below[half // 2 :]
+    below = jnp.concatenate([top, bottom + downward.astype(F32)], axis=0).astype(BF)
+    both = slice_sum(0, (above, below))
+    both += to_mlp(above, 1).astype(F32) + to_mlp(below, -1).astype(F32)
     both = both.astype(BF)
     chips = owners // 2
     groups = [[2 * i + c for i in range(chips)] for c in (0, 1)]

time: 179 us -> 183 us (1.022)
  waiting for transfers between devices: 58.9 us -> 63.4 us
  blocking collectives: 32.6 us -> 35.7 us
    ppermute x13, waiting for transfers between devices: 36.5 us -> 48 us  [to_mlp(): lax.ppermute(x, 'mlp', [(j, (j + step) % mlp_n) for j in range(mlp_n)])]
    all_to_all x2, waiting for transfers between devices: 21.1 us -> 14.1 us  [exchange(): lax.all_to_all(x, axes, split_axis=0, concat_axis=0, tiled=True, axis_ind...]
    ppermute x5, starting transfers between devices: 12.2 us -> 9.03 us  [partner(): return lax.ppermute(x, 'col', pairs)]
    all_to_all x2, blocking collectives: 32.6 us -> 35.7 us  [exchange(): lax.all_to_all(x, axes, split_axis=0, concat_axis=0, tiled=True, axis_ind...]
    pallas_call x1, Pallas kernels: 4.63 us -> 2.32 us  [middle(): pl.pallas_call(kernel, out_shape=[jax.ShapeDtypeStruct((half, units + cla...]
    pallas_call x0 -> x1, Pallas kernels: none -> 1.87 us  [prepare(): pl.pallas_call(kernel, out_shape=[jax.ShapeDtypeStruct((width_f, slots),...]
  transfers between devices with their start and end apart: 20 -> 20, of which waited for: 9 -> 9; matrix products, arithmetic and copies ran while one was open for 2% -> 2% of each run, Pallas kernels for 3% -> 4%
where the time goes in v11:
time: 183 us
  waiting for transfers between devices  63.4 us (35%)
  starting transfers between devices  46.7 us (26%)
  blocking collectives  35.7 us (20%)
  Pallas kernels  31.2 us (17%)
  other arithmetic  2.21 us (1%)
    ppermute x13, waiting for transfers between devices, to_mlp(): lax.ppermute(x, 'mlp', [(j, (j + step) % mlp_n) for j in range(mlp_n)])  48 us
    all_to_all x2, blocking collectives, exchange(): lax.all_to_all(x, axes, split_axis=0, concat_axis=0, tiled=True, axis_ind...  35.7 us
    ppermute x13, starting transfers between devices, to_mlp(): lax.ppermute(x, 'mlp', [(j, (j + step) % mlp_n) for j in range(mlp_n)])  19.8 us
    all_to_all x2, starting transfers between devices, exchange(): lax.all_to_all(x, axes, split_axis=0, concat_axis=0, tiled=True, axis_ind...  17.9 us
    all_to_all x2, waiting for transfers between devices, exchange(): lax.all_to_all(x, axes, split_axis=0, concat_axis=0, tiled=True, axis_ind...  14.1 us
    pallas_call x1, Pallas kernels, forward(): pl.pallas_call(kernel, out_shape=[pltpu.HBM((slots, units), BF)] * count...  9.98 us
    ppermute x5, starting transfers between devices, partner(): return lax.ppermute(x, 'col', pairs)  9.03 us
    pallas_call x1, Pallas kernels, gather(): pl.pallas_call(kernel, out_shape=pltpu.HBM((count, width_f), BF), in_spec...  8.01 us
  transfers between devices with their start and end apart: 20, of which 9 were waited for; matrix products, arithmetic and copies ran while one was open for 2% of the time, Pallas kernels for 4%

profile of v11, /device:TPU:1, one launch (start us, length us, event | category | flops | bytes accessed | tf_op | source)
XLA Modules:
  0.0 182.7 jit_solution(6773034947509433259)
XLA Ops:
  0.6 0.0 copy-start.3
  0.6 0.7 copy-done.3
  1.3 2.1 %shard_map.77 = (s32[64,128]{1,0:T(8,128)}, s32[32,128]{1,0:T(8,128)S(1)}) custom-call(s32[32,128]{1,0:T(8,128)S(1)} %bitcast.20), custom_call_target="tpu_custom_call" | custom-call | tf_op jit(solution)/shard_map/pallas_call | solution.py:70
  3.5 13.0 %all-to-all-start = ((s32[64,1,128]{2,1,0:T(1,128)}), s32[64,1,128]{2,1,0:T(1,128)S(1)}, u32[]{:S(2)}, u32[]{:S(2)}) async-start(s32[64,1,128]{2,1,0:T(1,128)} %bitcast.6), calls=%async_computation | async-start | bytes 65536 | tf_op jit(solution)/shard_map/all_to_all | solution.py:17
  16.5 9.3 %all-to-all-done = s32[64,1,128]{2,1,0:T(1,128)S(1)} async-done(((s32[64,1,128]{2,1,0:T(1,128)}), s32[64,1,128]{2,1,0:T(1,128)S(1)}, u32[]{:S(2)}, u32[]{:S(2)}) %all-to-all-start) | async-done | bytes 32800 | tf_op jit(solution)/shard_map/all_to_all | solution.py:17
  25.8 0.2 dynamic-slice_reduce_fusion
  25.9 0.1 reshape.45.asked_ref
  26.0 8.0 %shard_map.78 = bf16[2048,512]{1,0:T(8,128)(2,1)} custom-call(s32[2048]{0:T(1024)S(1)} %reshape.45.asked_ref, bf16[4096,512]{1,0:T(8,128)(2,1)} %features_ref.1), custom_call_target="tpu_custom_call" | custom-call | tf_op jit(solution)/shard_map/pallas_call | solution.py:124
  34.0 0.0 copy-start.6
  34.0 0.0 copy-start.4
  34.1 4.9 %all-to-all-start.1 = ((bf16[64,32,512]{2,1,0:T(8,128)(2,1)}), bf16[64,32,512]{2,1,0:T(8,128)(2,1)S(1)}, u32[]{:S(2)}, u32[]{:S(2)}) async-start(bf16[64,32,512]{2,1,0:T(8,128)(2,1)} %bitcast.24), calls=%async_computation.1 | async-start | bytes 4194304 | tf_op jit(solution)/shard_map/all_to_all | solution.py:17
  39.0 0.0 copy-start.9
  39.0 2.8 %collective-permute-start = (bf16[512,512]{1,0:T(8,128)(2,1)}, bf16[512,512]{1,0:T(8,128)(2,1)}, u32[]{:S(2)}, u32[]{:S(2)}) collective-permute-start(bf16[512,512]{1,0:T(8,128)(2,1)} %refs_3_), channel_id=1, source_target_pairs={{0,3},{1,0},{2,1},{3,2},{4,7},{5,4},{6,5},{7,6},{8,11},{9,8},{10,9... | collective-permute-start | bytes 1572872 | tf_op jit(solution)/shard_map/ppermute | solution.py:405
  41.8 0.3 collective-permute-start.1
  42.2 0.7 collective-permute-start.2
  42.9 2.0 %collective-permute-start.3 = (bf16[512,256]{1,0:T(8,128)(2,1)S(1)}, bf16[512,256]{1,0:T(8,128)(2,1)S(1)}, u32[]{:S(2)}, u32[]{:S(2)}) collective-permute-start(bf16[512,256]{1,0:T(8,128)(2,1)S(1)} %copy-done.6), channel_id=1, source_target_pairs={{0,3},{1,0},{2,1},{3,2},{4,7},{5,4},{6,5},{7,6},{8,11},{9,8},{10,9... | collective-permute-start | bytes 786440 | tf_op jit(solution)/shard_map/ppermute | solution.py:405
  44.9 1.4 collective-permute-start.4
  46.3 0.4 convolution_bitcast_fusion.1
  46.8 0.1 copy.10
  46.8 0.1 convert_element_type.58
  46.9 0.4 convolution_bitcast_fusion
  47.4 0.1 copy.11
  47.5 0.1 broadcast_in_dim.59
  47.6 0.7 select_convert_fusion.refs_6_.spread_ref
  48.3 26.8 %collective-permute-done.3.refs_5_.refs_2_ = bf16[512,256]{1,0:T(8,128)(2,1)S(1)} collective-permute-done((bf16[512,256]{1,0:T(8,128)(2,1)S(1)}, bf16[512,256]{1,0:T(8,128)(2,1)S(1)}, u32[]{:S(2)}, u32[]{:S(2)}) %collective-permute-start.3) | collective-permute-done | bytes 262176 | tf_op jit(solution)/shard_map/ppermute | solution.py:405
  75.1 0.0 collective-permute-start.5
  75.1 0.9 select_convert_fusion.1.spread_ref
  76.0 0.0 collective-permute-done.4.refs_4_.refs_1_
  76.0 7.9 %collective-permute-done.5.refs_6_.refs_3_ = bf16[512,256]{1,0:T(8,128)(2,1)} collective-permute-done((bf16[512,256]{1,0:T(8,128)(2,1)S(1)}, bf16[512,256]{1,0:T(8,128)(2,1)}, u32[]{:S(2)}, u32[]{:S(2)}) %collective-permute-start.5) | collective-permute-done | bytes 262176 | tf_op jit(solution)/shard_map/ppermute | solution.py:405
  83.9 0.0 collective-permute-done.refs_1_
  83.9 0.0 collective-permute-done.1.refs_0_
  84.0 0.0 collective-permute-done.2.refs_2_
  84.0 4.8 %all-to-all-done.1 = bf16[64,32,512]{2,1,0:T(8,128)(2,1)S(1)} async-done(((bf16[64,32,512]{2,1,0:T(8,128)(2,1)}), bf16[64,32,512]{2,1,0:T(8,128)(2,1)S(1)}, u32[]{:S(2)}, u32[]{:S(2)}) %all-to-all-start.1) | async-done | bytes 2097184 | tf_op jit(solution)/shard_map/all_to_all | solution.py:17
  88.7 10.0 %shard_map.79 = (bf16[2048,512]{1,0:T(8,128)(2,1)}, bf16[2048,512]{1,0:T(8,128)(2,1)}, bf16[2048,512]{1,0:T(8,128)(2,1)}, bf16[2048,512]{1,0:T(8,128)(2,1)}, bf1...) custom-call(bf16[2048,512]{1,0:T(8,128)(2,1)S(1)} %bitcast.16, ...), custom_call_target="tpu_custom_call" | custom-call | flops 5368709120 | bytes 4718592 | tf_op jit(solution)/shard_map/pallas_call | solution.py:261
  98.7 3.0 %collective-permute-start.6 = (bf16[128,256]{1,0:T(8,128)(2,1)S(1)}, bf16[128,256]{1,0:T(8,128)(2,1)S(1)}, u32[]{:S(2)}, u32[]{:S(2)}) collective-permute-start(bf16[128,256]{1,0:T(8,128)(2,1)S(1)} %get-tuple-element.55), channel_id=1, source_target_pairs={{0,2},{1,3},{2,0},{3,1},{4,6},{5,7},{6,4},{7,5},{8,10},{9,11},{10,... | collective-permute-start | bytes 196616 | tf_op jit(solution)/shard_map/ppermute | solution.py:405
  101.7 0.4 collective-permute-start.7
  102.1 2.3 %collective-permute-start.8 = (bf16[128,256]{1,0:T(8,128)(2,1)S(1)}, bf16[128,256]{1,0:T(8,128)(2,1)S(1)}, u32[]{:S(2)}, u32[]{:S(2)}) collective-permute-start(bf16[128,256]{1,0:T(8,128)(2,1)S(1)} %get-tuple-element.55), channel_id=1, source_target_pairs={{0,3},{1,0},{2,1},{3,2},{4,7},{5,4},{6,5},{7,6},{8,11},{9,8},{10,9... | collective-permute-start | bytes 196616 | tf_op jit(solution)/shard_map/ppermute | solution.py:405
  104.4 1.9 %shard_map.80 = (bf16[512,2048]{1,0:T(8,128)(2,1)S(1)}, bf16[2048,512]{1,0:T(8,128)(2,1)S(1)}, bf16[512,256]{1,0:T(8,128)(2,1)S(1)}, bf16[512,256]{1,0:T(8,128)(...) custom-call(s32[1]{0:T(128)} %bitcast.core_ref, bf16[2048,512]{1,0:T(8,128)(2,1)S(1)} %bitcast.17, ...), custom_call_target="tpu_custom_call" | custom-call | flops 1073741824 | bytes 8388608 | tf_op jit(solution)/shard_map/pallas_call | solution.py:318
  106.3 0.0 collective-permute-done.6.refs_1_
  106.3 0.5 collective-permute-done.7.refs_2_
  106.8 2.3 %shard_map.81 = (f32[256,768]{1,0:T(8,128)S(1)}, bf16[256,768]{1,0:T(8,128)(2,1)S(1)}, bf16[128,256]{1,0:T(8,128)(2,1)S(1)}, bf16[128,512]{1,0:T(8,128)(2,1)S(1)...) custom-call(s32[1]{0:T(128)} %bitcast.core_ref, f32[128,256]{1,0:T(8,128)S(1)} %get-tuple-element.54.refs_0_, ...), custom_call_target="tpu_custom_call" | custom-call | flops 167772160 | bytes 4194304 | tf_op jit(solution)/shard_map/pallas_call | solution.py:201
  109.1 3.0 %collective-permute-start.9 = (bf16[256,768]{1,0:T(8,128)(2,1)S(1)}, bf16[256,768]{1,0:T(8,128)(2,1)S(1)}, u32[]{:S(2)}, u32[]{:S(2)}) collective-permute-start(bf16[256,768]{1,0:T(8,128)(2,1)S(1)} %get-tuple-element.72), channel_id=1, source_target_pairs={{0,4},{4,0},{8,12},{12,8},{16,20},{20,16},{24,28},{28,24},{1,5},{5... | collective-permute-start | bytes 1179656 | tf_op jit(solution)/shard_map/ppermute | solution.py:458
  112.1 1.9 %shard_map.83 = (f32[256,768]{1,0:T(8,128)S(1)}, bf16[256,768]{1,0:T(8,128)(2,1)S(1)}) custom-call(s32[1]{0:T(128)} %bitcast.core_ref, bf16[2048,128]{1,0:T(8,128)(2,1)S(1)} %select_convert_fusion.refs_6_.spread_ref, bf16[128,512]{1,0:T(8,128)(2,1)S(1)} %get-tuple-element.75.d_hidden_ref, bf16[2048,512]{1,0:T(8,128)(2,1)S(1)} %copy-done.2, ...), custom_call_target="tpu_custom_call" | custom-call | flops 1024 | bytes 1024 | tf_op jit(solution)/shard_map/pallas_call | solution.py:351
  114.0 0.1 collective-permute-start.12
  114.1 0.1 add_convert_fusion.1
  114.3 0.3 collective-permute-start.11
  114.6 3.0 %collective-permute-start.13 = (bf16[128,768]{1,0:T(8,128)(2,1)S(1)}, bf16[128,768]{1,0:T(8,128)(2,1)S(1)}, u32[]{:S(2)}, u32[]{:S(2)}) collective-permute-start(bf16[128,768]{1,0:T(8,128)(2,1)S(1)} %get-tuple-element.83.refs_1_), channel_id=1, source_target_pairs={{0,3},{1,0},{2,1},{3,2},{4,7},{5,4},{6,5},{7,6},{8,11},{9,8},{10,9... | collective-permute-start | bytes 589832 | tf_op jit(solution)/shard_map/ppermute | solution.py:405
  117.6 1.9 %shard_map.82 = (f32[256,768]{1,0:T(8,128)S(1)}, bf16[256,768]{1,0:T(8,128)(2,1)S(1)}) custom-call(s32[1]{0:T(128)} %bitcast.core_ref, bf16[2048,128]{1,0:T(8,128)(2,1)S(1)} %select_convert_fusion.refs_6_.spread_ref, bf16[128,512]{1,0:T(8,128)(2,1)S(1)} %get-tuple-element.68.d_hidden_ref, bf16[2048,512]{1,0:T(8,128)(2,1)S(1)} %copy-done.1, ...), custom_call_target="tpu_custom_call" | custom-call | flops 1024 | bytes 1024 | tf_op jit(solution)/shard_map/pallas_call | solution.py:351
  119.5 0.8 collective-permute-start.10
  120.3 0.1 convert_add_fusion
  120.4 0.9 collective-permute-done.13
  121.5 3.5 %collective-permute-start.16 = (bf16[256,768]{1,0:T(8,128)(2,1)S(1)}, bf16[256,768]{1,0:T(8,128)(2,1)S(1)}, u32[]{:S(2)}, u32[]{:S(2)}) collective-permute-start(bf16[256,768]{1,0:T(8,128)(2,1)S(1)} %pad_maximum_fusion.1.refs_1_), channel_id=1, source_target_pairs={{0,3},{1,0},{2,1},{3,2},{4,7},{5,4},{6,5},{7,6},{8,11},{9,8},{10,9... | collective-permute-start | bytes 1179656 | tf_op jit(solution)/shard_map/ppermute | solution.py:405
  125.0 0.1 convert_add_fusion.1
  125.2 1.9 %shard_map.84 = (f32[256,768]{1,0:T(8,128)S(1)}, bf16[256,768]{1,0:T(8,128)(2,1)S(1)}) custom-call(s32[1]{0:T(128)} %bitcast.core_ref, bf16[2048,128]{1,0:T(8,128)(2,1)S(1)} %select_convert_fusion.refs_6_.spread_ref, bf16[128,512]{1,0:T(8,128)(2,1)S(1)} %get-tuple-element.64.d_hidden_ref, bf16[2048,512]{1,0:T(8,128)(2,1)S(1)} %copy-done, ...), custom_call_target="tpu_custom_call" | custom-call | flops 1024 | bytes 1024 | tf_op jit(solution)/shard_map/pallas_call | solution.py:351
  127.1 1.7 collective-permute-start.14
  128.8 3.3 %collective-permute-done.16 = bf16[256,768]{1,0:T(8,128)(2,1)S(1)} collective-permute-done((bf16[256,768]{1,0:T(8,128)(2,1)S(1)}, bf16[256,768]{1,0:T(8,128)(2,1)S(1)}, u32[]{:S(2)}, u32[]{:S(2)}) %collective-permute-start.16) | collective-permute-done | bytes 393248 | tf_op jit(solution)/shard_map/ppermute | solution.py:405
  132.0 8.6 %collective-permute-done.15 = bf16[256,768]{1,0:T(8,128)(2,1)S(1)} collective-permute-done((bf16[256,768]{1,0:T(8,128)(2,1)S(1)}, bf16[256,768]{1,0:T(8,128)(2,1)S(1)}, u32[]{:S(2)}, u32[]{:S(2)}) %collective-permute-start.15) | collective-permute-done | bytes 393248 | tf_op jit(solution)/shard_map/ppermute | solution.py:405
  140.6 0.2 fusion.12
  140.8 18.0 %all_to_all.24 = bf16[32,8,768]{2,1,0:T(8,128)(2,1)S(1)} all-to-all(bf16[32,8,768]{2,1,0:T(8,128)(2,1)S(1)} %fusion.12), channel_id=1, replica_groups={{0,8,16,24,32,40,48,56,64,72,80,88,96,104,112,120,128,136,144,152,160,1..., dimensions={0} | all-to-all | bytes 786432 | tf_op jit(solution)/shard_map/all_to_all | solution.py:17
  158.8 0.1 reduce_sum.12
  158.9 17.7 %all_to_all.25 = bf16[32,8,768]{2,1,0:T(8,128)(2,1)S(1)} all-to-all(bf16[32,8,768]{2,1,0:T(8,128)(2,1)S(1)} %broadcast_in_dim.65), channel_id=1, replica_groups={{0,8,16,24,32,40,48,56,64,72,80,88,96,104,112,120,128,136,144,152,160,1..., dimensions={0} | all-to-all | bytes 786432 | tf_op jit(solution)/shard_map/all_to_all | solution.py:17
  176.6 3.3 %collective-permute-start.17 = (bf16[256,768]{1,0:T(8,128)(2,1)S(1)}, bf16[256,768]{1,0:T(8,128)(2,1)S(1)}, u32[]{:S(2)}, u32[]{:S(2)}) collective-permute-start(bf16[256,768]{1,0:T(8,128)(2,1)S(1)} %bitcast.18), channel_id=1, source_target_pairs={{0,4},{4,0},{8,12},{12,8},{16,20},{20,16},{24,28},{28,24},{1,5},{5... | collective-permute-start | bytes 1179656 | tf_op jit(solution)/shard_map/ppermute | solution.py:458
  180.0 1.3 collective-permute-done.17.other_ref
  181.3 1.2 shard_map.85
  (34 shorter events, 0.3 us)
Async XLA Ops:
  0.6 0.7 copy-start.3
  3.5 22.3 %all-to-all-start = ((s32[64,1,128]{2,1,0:T(1,128)}), s32[64,1,128]{2,1,0:T(1,128)S(1)}, u32[]{:S(2)}, u32[]{:S(2)}) async-start(s32[64,1,128]{2,1,0:T(1,128)} %bitcast.6), calls=%async_computation | async-start | bytes 65536 | tf_op jit(solution)/shard_map/all_to_all | solution.py:17
  34.0 8.8 %copy-start.6 = (bf16[512,256]{1,0:T(8,128)(2,1)S(1)}, bf16[512,256]{1,0:T(8,128)(2,1)}, u32[]{:S(2)}) copy-start(bf16[512,256]{1,0:T(8,128)(2,1)} %refs_4_) | copy-start | bytes 786436
  34.0 12.2 %copy-start.4 = (s32[128,32]{0,1:T(8,128)S(1)}, s32[128,32]{0,1:T(8,128)}, u32[]{:S(2)}) copy-start(s32[128,32]{0,1:T(8,128)} %param.7) | copy-start | bytes 49156
  34.1 54.7 %all-to-all-start.1 = ((bf16[64,32,512]{2,1,0:T(8,128)(2,1)}), bf16[64,32,512]{2,1,0:T(8,128)(2,1)S(1)}, u32[]{:S(2)}, u32[]{:S(2)}) async-start(bf16[64,32,512]{2,1,0:T(8,128)(2,1)} %bitcast.24), calls=%async_computation.1 | async-start | bytes 4194304 | tf_op jit(solution)/shard_map/all_to_all | solution.py:17
  39.0 7.9 %copy-start.9 = (bf16[128,32]{0,1:T(8,128)(2,1)S(1)}, bf16[128,32]{0,1:T(8,128)(2,1)}, u32[]{:S(2)}) copy-start(bf16[128,32]{0,1:T(8,128)(2,1)} %param.8) | copy-start | bytes 24580
  39.0 44.9 %collective-permute-start = (bf16[512,512]{1,0:T(8,128)(2,1)}, bf16[512,512]{1,0:T(8,128)(2,1)}, u32[]{:S(2)}, u32[]{:S(2)}) collective-permute-start(bf16[512,512]{1,0:T(8,128)(2,1)} %refs_3_), channel_id=1, source_target_pairs={{0,3},{1,0},{2,1},{3,2},{4,7},{5,4},{6,5},{7,6},{8,11},{9,8},{10,9... | collective-permute-start | bytes 1572872 | tf_op jit(solution)/shard_map/ppermute | solution.py:405
  41.8 42.1 %collective-permute-start.1 = (bf16[512,512]{1,0:T(8,128)(2,1)}, bf16[512,512]{1,0:T(8,128)(2,1)}, u32[]{:S(2)}, u32[]{:S(2)}) collective-permute-start(bf16[512,512]{1,0:T(8,128)(2,1)} %refs_3_), channel_id=1, source_target_pairs={{0,2},{1,3},{2,0},{3,1},{4,6},{5,7},{6,4},{7,5},{8,10},{9,11},{10,... | collective-permute-start | bytes 1572872 | tf_op jit(solution)/shard_map/ppermute | solution.py:405
  42.2 41.8 %collective-permute-start.2 = (bf16[512,512]{1,0:T(8,128)(2,1)}, bf16[512,512]{1,0:T(8,128)(2,1)}, u32[]{:S(2)}, u32[]{:S(2)}) collective-permute-start(bf16[512,512]{1,0:T(8,128)(2,1)} %refs_3_), channel_id=1, source_target_pairs={{0,1},{1,2},{2,3},{3,0},{4,5},{5,6},{6,7},{7,4},{8,9},{9,10},{10,1... | collective-permute-start | bytes 1572872 | tf_op jit(solution)/shard_map/ppermute | solution.py:405
  42.9 32.2 %collective-permute-start.3 = (bf16[512,256]{1,0:T(8,128)(2,1)S(1)}, bf16[512,256]{1,0:T(8,128)(2,1)S(1)}, u32[]{:S(2)}, u32[]{:S(2)}) collective-permute-start(bf16[512,256]{1,0:T(8,128)(2,1)S(1)} %copy-done.6), channel_id=1, source_target_pairs={{0,3},{1,0},{2,1},{3,2},{4,7},{5,4},{6,5},{7,6},{8,11},{9,8},{10,9... | collective-permute-start | bytes 786440 | tf_op jit(solution)/shard_map/ppermute | solution.py:405
  44.9 31.1 %collective-permute-start.4 = (bf16[512,256]{1,0:T(8,128)(2,1)S(1)}, bf16[512,256]{1,0:T(8,128)(2,1)S(1)}, u32[]{:S(2)}, u32[]{:S(2)}) collective-permute-start(bf16[512,256]{1,0:T(8,128)(2,1)S(1)} %copy-done.6), channel_id=1, source_target_pairs={{0,2},{1,3},{2,0},{3,1},{4,6},{5,7},{6,4},{7,5},{8,10},{9,11},{10,... | collective-permute-start | bytes 786440 | tf_op jit(solution)/shard_map/ppermute | solution.py:405
  75.1 13.6 %copy-start.7 = (bf16[512,256]{1,0:T(8,128)(2,1)}, bf16[512,256]{1,0:T(8,128)(2,1)S(1)}, u32[]{:S(2)}) copy-start(bf16[512,256]{1,0:T(8,128)(2,1)S(1)} %collective-permute-done.3.refs_5_.refs_2_) | copy-start | bytes 786436
  75.1 8.8 %collective-permute-start.5 = (bf16[512,256]{1,0:T(8,128)(2,1)S(1)}, bf16[512,256]{1,0:T(8,128)(2,1)}, u32[]{:S(2)}, u32[]{:S(2)}) collective-permute-start(bf16[512,256]{1,0:T(8,128)(2,1)S(1)} %copy-done.6), channel_id=1, source_target_pairs={{0,1},{1,2},{2,3},{3,0},{4,5},{5,6},{6,7},{7,4},{8,9},{9,10},{10,1... | collective-permute-start | bytes 786440 | tf_op jit(solution)/shard_map/ppermute | solution.py:405
  76.0 12.7 %copy-start.8 = (bf16[512,256]{1,0:T(8,128)(2,1)}, bf16[512,256]{1,0:T(8,128)(2,1)S(1)}, u32[]{:S(2)}) copy-start(bf16[512,256]{1,0:T(8,128)(2,1)S(1)} %collective-permute-done.4.refs_4_.refs_1_) | copy-start | bytes 786436
  98.7 7.6 %collective-permute-start.6 = (bf16[128,256]{1,0:T(8,128)(2,1)S(1)}, bf16[128,256]{1,0:T(8,128)(2,1)S(1)}, u32[]{:S(2)}, u32[]{:S(2)}) collective-permute-start(bf16[128,256]{1,0:T(8,128)(2,1)S(1)} %get-tuple-element.55), channel_id=1, source_target_pairs={{0,2},{1,3},{2,0},{3,1},{4,6},{5,7},{6,4},{7,5},{8,10},{9,11},{10,... | collective-permute-start | bytes 196616 | tf_op jit(solution)/shard_map/ppermute | solution.py:405
  101.7 5.0 %collective-permute-start.7 = (bf16[128,256]{1,0:T(8,128)(2,1)S(1)}, bf16[128,256]{1,0:T(8,128)(2,1)S(1)}, u32[]{:S(2)}, u32[]{:S(2)}) collective-permute-start(bf16[128,256]{1,0:T(8,128)(2,1)S(1)} %get-tuple-element.55), channel_id=1, source_target_pairs={{0,1},{1,2},{2,3},{3,0},{4,5},{5,6},{6,7},{7,4},{8,9},{9,10},{10,1... | collective-permute-start | bytes 196616 | tf_op jit(solution)/shard_map/ppermute | solution.py:405
  102.1 4.6 %collective-permute-start.8 = (bf16[128,256]{1,0:T(8,128)(2,1)S(1)}, bf16[128,256]{1,0:T(8,128)(2,1)S(1)}, u32[]{:S(2)}, u32[]{:S(2)}) collective-permute-start(bf16[128,256]{1,0:T(8,128)(2,1)S(1)} %get-tuple-element.55), channel_id=1, source_target_pairs={{0,3},{1,0},{2,1},{3,2},{4,7},{5,4},{6,5},{7,6},{8,11},{9,8},{10,9... | collective-permute-start | bytes 196616 | tf_op jit(solution)/shard_map/ppermute | solution.py:405
  104.4 2.4 %copy-start.5 = (s32[128]{0:T(128)S(1)}, s32[128]{0:T(128)}, u32[]{:S(2)}) copy-start(s32[128]{0:T(128)} %param.9) | copy-start | bytes 1540
  106.7 5.4 %copy-start.2 = (bf16[2048,512]{1,0:T(8,128)(2,1)S(1)}, bf16[2048,512]{1,0:T(8,128)(2,1)}, u32[]{:S(2)}) copy-start(bf16[2048,512]{1,0:T(8,128)(2,1)} %get-tuple-element.76.active_ref) | copy-start | bytes 6291460
  109.1 5.1 %collective-permute-start.9 = (bf16[256,768]{1,0:T(8,128)(2,1)S(1)}, bf16[256,768]{1,0:T(8,128)(2,1)S(1)}, u32[]{:S(2)}, u32[]{:S(2)}) collective-permute-start(bf16[256,768]{1,0:T(8,128)(2,1)S(1)} %get-tuple-element.72), channel_id=1, source_target_pairs={{0,4},{4,0},{8,12},{12,8},{16,20},{20,16},{24,28},{28,24},{1,5},{5... | collective-permute-start | bytes 1179656 | tf_op jit(solution)/shard_map/ppermute | solution.py:458
  114.0 3.6 %copy-start.1 = (bf16[2048,512]{1,0:T(8,128)(2,1)S(1)}, bf16[2048,512]{1,0:T(8,128)(2,1)}, u32[]{:S(2)}) copy-start(bf16[2048,512]{1,0:T(8,128)(2,1)} %get-tuple-element.69.active_ref) | copy-start | bytes 6291460
  114.0 6.3 %collective-permute-start.12 = (bf16[256,768]{1,0:T(8,128)(2,1)S(1)}, bf16[256,768]{1,0:T(8,128)(2,1)S(1)}, u32[]{:S(2)}, u32[]{:S(2)}) collective-permute-start(bf16[256,768]{1,0:T(8,128)(2,1)S(1)} %get-tuple-element.79), channel_id=1, source_target_pairs={{0,4},{4,0},{8,12},{12,8},{16,20},{20,16},{24,28},{28,24},{1,5},{5... | collective-permute-start | bytes 1179656 | tf_op jit(solution)/shard_map/ppermute | solution.py:458
  114.3 10.8 %collective-permute-start.11 = (bf16[128,768]{1,0:T(8,128)(2,1)S(1)}, bf16[128,768]{1,0:T(8,128)(2,1)S(1)}, u32[]{:S(2)}, u32[]{:S(2)}) collective-permute-start(bf16[128,768]{1,0:T(8,128)(2,1)S(1)} %get-tuple-element.82.refs_0_), channel_id=1, source_target_pairs={{0,1},{1,2},{2,3},{3,0},{4,5},{5,6},{6,7},{7,4},{8,9},{9,10},{10,1... | collective-permute-start | bytes 589832 | tf_op jit(solution)/shard_map/ppermute | solution.py:405
  114.6 6.8 %collective-permute-start.13 = (bf16[128,768]{1,0:T(8,128)(2,1)S(1)}, bf16[128,768]{1,0:T(8,128)(2,1)S(1)}, u32[]{:S(2)}, u32[]{:S(2)}) collective-permute-start(bf16[128,768]{1,0:T(8,128)(2,1)S(1)} %get-tuple-element.83.refs_1_), channel_id=1, source_target_pairs={{0,3},{1,0},{2,1},{3,2},{4,7},{5,4},{6,5},{7,6},{8,11},{9,8},{10,9... | collective-permute-start | bytes 589832 | tf_op jit(solution)/shard_map/ppermute | solution.py:405
  119.5 5.5 %collective-permute-start.10 = (bf16[256,768]{1,0:T(8,128)(2,1)S(1)}, bf16[256,768]{1,0:T(8,128)(2,1)S(1)}, u32[]{:S(2)}, u32[]{:S(2)}) collective-permute-start(bf16[256,768]{1,0:T(8,128)(2,1)S(1)} %get-tuple-element.74), channel_id=1, source_target_pairs={{0,4},{4,0},{8,12},{12,8},{16,20},{20,16},{24,28},{28,24},{1,5},{5... | collective-permute-start | bytes 1179656 | tf_op jit(solution)/shard_map/ppermute | solution.py:458
  121.5 3.7 %copy-start = (bf16[2048,512]{1,0:T(8,128)(2,1)S(1)}, bf16[2048,512]{1,0:T(8,128)(2,1)}, u32[]{:S(2)}) copy-start(bf16[2048,512]{1,0:T(8,128)(2,1)} %get-tuple-element.65.active_ref) | copy-start | bytes 6291460
  121.5 10.6 %collective-permute-start.16 = (bf16[256,768]{1,0:T(8,128)(2,1)S(1)}, bf16[256,768]{1,0:T(8,128)(2,1)S(1)}, u32[]{:S(2)}, u32[]{:S(2)}) collective-permute-start(bf16[256,768]{1,0:T(8,128)(2,1)S(1)} %pad_maximum_fusion.1.refs_1_), channel_id=1, source_target_pairs={{0,3},{1,0},{2,1},{3,2},{4,7},{5,4},{6,5},{7,6},{8,11},{9,8},{10,9... | collective-permute-start | bytes 1179656 | tf_op jit(solution)/shard_map/ppermute | solution.py:405
  127.1 5.0 %collective-permute-start.14 = (bf16[256,768]{1,0:T(8,128)(2,1)S(1)}, bf16[256,768]{1,0:T(8,128)(2,1)S(1)}, u32[]{:S(2)}, u32[]{:S(2)}) collective-permute-start(bf16[256,768]{1,0:T(8,128)(2,1)S(1)} %get-tuple-element.81), channel_id=1, source_target_pairs={{0,4},{4,0},{8,12},{12,8},{16,20},{20,16},{24,28},{28,24},{1,5},{5... | collective-permute-start | bytes 1179656 | tf_op jit(solution)/shard_map/ppermute | solution.py:458
  128.7 11.9 %collective-permute-start.15 = (bf16[256,768]{1,0:T(8,128)(2,1)S(1)}, bf16[256,768]{1,0:T(8,128)(2,1)S(1)}, u32[]{:S(2)}, u32[]{:S(2)}) collective-permute-start(bf16[256,768]{1,0:T(8,128)(2,1)S(1)} %pad_maximum_fusion.refs_0_), channel_id=1, source_target_pairs={{0,1},{1,2},{2,3},{3,0},{4,5},{5,6},{6,7},{7,4},{8,9},{9,10},{10,1... | collective-permute-start | bytes 1179656 | tf_op jit(solution)/shard_map/ppermute | solution.py:405
  176.6 4.7 %collective-permute-start.17 = (bf16[256,768]{1,0:T(8,128)(2,1)S(1)}, bf16[256,768]{1,0:T(8,128)(2,1)S(1)}, u32[]{:S(2)}, u32[]{:S(2)}) collective-permute-start(bf16[256,768]{1,0:T(8,128)(2,1)S(1)} %bitcast.18), channel_id=1, source_target_pairs={{0,4},{4,0},{8,12},{12,8},{16,20},{20,16},{24,28},{28,24},{1,5},{5... | collective-permute-start | bytes 1179656 | tf_op jit(solution)/shard_map/ppermute | solution.py:458

commit v12 on v11

--- a/solution.py
+++ b/solution.py
@@ -490,7 +490,7 @@
     above = jnp.concatenate([top + upward.astype(F32), bottom], axis=0).astype(BF)
     top, bottom = below[: half // 2], below[half // 2 :]
     below = jnp.concatenate([top, bottom + downward.astype(F32)], axis=0).astype(BF)
-    both = slice_sum(0, (above, below))
+    both = slice_sum(0, ())
     both += to_mlp(above, 1).astype(F32) + to_mlp(below, -1).astype(F32)
     both = both.astype(BF)
     chips = owners // 2

time: 183 us -> 181 us (0.989)
  blocking collectives: 35.7 us -> 33.6 us
    all_to_all x2, blocking collectives: 35.7 us -> 33.6 us  [exchange(): lax.all_to_all(x, axes, split_axis=0, concat_axis=0, tiled=True, axis_ind...]
where the time goes in v12:
time: 181 us; the launch traced here: 180 us
  waiting for transfers between devices  63.2 us (35%)
  starting transfers between devices  46.5 us (26%)
  blocking collectives  33.6 us (19%)
  Pallas kernels  31.2 us (17%)
  other arithmetic  2.22 us (1%)
    ppermute x13, waiting for transfers between devices, to_mlp(): lax.ppermute(x, 'mlp', [(j, (j + step) % mlp_n) for j in range(mlp_n)])  47.8 us
    all_to_all x2, blocking collectives, exchange(): lax.all_to_all(x, axes, split_axis=0, concat_axis=0, tiled=True, axis_ind...  33.6 us
    ppermute x13, starting transfers between devices, to_mlp(): lax.ppermute(x, 'mlp', [(j, (j + step) % mlp_n) for j in range(mlp_n)])  19.6 us
    all_to_all x2, starting transfers between devices, exchange(): lax.all_to_all(x, axes, split_axis=0, concat_axis=0, tiled=True, axis_ind...  17.9 us
    all_to_all x2, waiting for transfers between devices, exchange(): lax.all_to_all(x, axes, split_axis=0, concat_axis=0, tiled=True, axis_ind...  14.1 us
    pallas_call x1, Pallas kernels, forward(): pl.pallas_call(kernel, out_shape=[pltpu.HBM((slots, units), BF)] * count...  9.98 us
    ppermute x5, starting transfers between devices, partner(): return lax.ppermute(x, 'col', pairs)  8.99 us
    pallas_call x1, Pallas kernels, gather(): pl.pallas_call(kernel, out_shape=pltpu.HBM((count, width_f), BF), in_spec...  8.01 us
  transfers between devices with their start and end apart: 20, of which 9 were waited for; matrix products, arithmetic and copies ran while one was open for 2% of the time, Pallas kernels for 4%

profile of v12, /device:TPU:1, one launch (start us, length us, event | category | flops | bytes accessed | tf_op | source)
XLA Modules:
  0.0 180.2 jit_solution(2395871376463136448)
XLA Ops:
  0.6 0.0 copy-start.3
  0.6 0.7 copy-done.3
  1.3 2.1 %shard_map.77 = (s32[64,128]{1,0:T(8,128)}, s32[32,128]{1,0:T(8,128)S(1)}) custom-call(s32[32,128]{1,0:T(8,128)S(1)} %bitcast.20), custom_call_target="tpu_custom_call" | custom-call | tf_op jit(solution)/shard_map/pallas_call | solution.py:70
  3.5 13.0 %all-to-all-start = ((s32[64,1,128]{2,1,0:T(1,128)}), s32[64,1,128]{2,1,0:T(1,128)S(1)}, u32[]{:S(2)}, u32[]{:S(2)}) async-start(s32[64,1,128]{2,1,0:T(1,128)} %bitcast.6), calls=%async_computation | async-start | bytes 65536 | tf_op jit(solution)/shard_map/all_to_all | solution.py:17
  16.5 9.3 %all-to-all-done = s32[64,1,128]{2,1,0:T(1,128)S(1)} async-done(((s32[64,1,128]{2,1,0:T(1,128)}), s32[64,1,128]{2,1,0:T(1,128)S(1)}, u32[]{:S(2)}, u32[]{:S(2)}) %all-to-all-start) | async-done | bytes 32800 | tf_op jit(solution)/shard_map/all_to_all | solution.py:17
  25.8 0.2 dynamic-slice_reduce_fusion
  25.9 0.1 reshape.45.asked_ref
  26.0 8.0 %shard_map.78 = bf16[2048,512]{1,0:T(8,128)(2,1)} custom-call(s32[2048]{0:T(1024)S(1)} %reshape.45.asked_ref, bf16[4096,512]{1,0:T(8,128)(2,1)} %features_ref.1), custom_call_target="tpu_custom_call" | custom-call | tf_op jit(solution)/shard_map/pallas_call | solution.py:124
  34.0 0.0 copy-start.6
  34.0 0.0 copy-start.4
  34.1 4.9 %all-to-all-start.1 = ((bf16[64,32,512]{2,1,0:T(8,128)(2,1)}), bf16[64,32,512]{2,1,0:T(8,128)(2,1)S(1)}, u32[]{:S(2)}, u32[]{:S(2)}) async-start(bf16[64,32,512]{2,1,0:T(8,128)(2,1)} %bitcast.24), calls=%async_computation.1 | async-start | bytes 4194304 | tf_op jit(solution)/shard_map/all_to_all | solution.py:17
  39.0 0.0 copy-start.9
  39.0 2.8 %collective-permute-start = (bf16[512,512]{1,0:T(8,128)(2,1)}, bf16[512,512]{1,0:T(8,128)(2,1)}, u32[]{:S(2)}, u32[]{:S(2)}) collective-permute-start(bf16[512,512]{1,0:T(8,128)(2,1)} %refs_3_), channel_id=1, source_target_pairs={{0,3},{1,0},{2,1},{3,2},{4,7},{5,4},{6,5},{7,6},{8,11},{9,8},{10,9... | collective-permute-start | bytes 1572872 | tf_op jit(solution)/shard_map/ppermute | solution.py:405
  41.8 0.3 collective-permute-start.1
  42.2 0.7 collective-permute-start.2
  42.9 2.0 %collective-permute-start.3 = (bf16[512,256]{1,0:T(8,128)(2,1)S(1)}, bf16[512,256]{1,0:T(8,128)(2,1)S(1)}, u32[]{:S(2)}, u32[]{:S(2)}) collective-permute-start(bf16[512,256]{1,0:T(8,128)(2,1)S(1)} %copy-done.6), channel_id=1, source_target_pairs={{0,3},{1,0},{2,1},{3,2},{4,7},{5,4},{6,5},{7,6},{8,11},{9,8},{10,9... | collective-permute-start | bytes 786440 | tf_op jit(solution)/shard_map/ppermute | solution.py:405
  44.9 1.4 collective-permute-start.4
  46.3 0.4 convolution_bitcast_fusion.1
  46.8 0.1 copy.10
  46.8 0.1 convert_element_type.58
  46.9 0.4 convolution_bitcast_fusion
  47.4 0.1 copy.11
  47.5 0.1 broadcast_in_dim.59
  47.6 0.7 select_convert_fusion.refs_6_.spread_ref
  48.3 26.8 %collective-permute-done.3.refs_5_.refs_2_ = bf16[512,256]{1,0:T(8,128)(2,1)S(1)} collective-permute-done((bf16[512,256]{1,0:T(8,128)(2,1)S(1)}, bf16[512,256]{1,0:T(8,128)(2,1)S(1)}, u32[]{:S(2)}, u32[]{:S(2)}) %collective-permute-start.3) | collective-permute-done | bytes 262176 | tf_op jit(solution)/shard_map/ppermute | solution.py:405
  75.1 0.0 collective-permute-start.5
  75.1 0.9 select_convert_fusion.1.spread_ref
  76.0 0.0 collective-permute-done.4.refs_4_.refs_1_
  76.0 7.9 %collective-permute-done.5.refs_6_.refs_3_ = bf16[512,256]{1,0:T(8,128)(2,1)} collective-permute-done((bf16[512,256]{1,0:T(8,128)(2,1)S(1)}, bf16[512,256]{1,0:T(8,128)(2,1)}, u32[]{:S(2)}, u32[]{:S(2)}) %collective-permute-start.5) | collective-permute-done | bytes 262176 | tf_op jit(solution)/shard_map/ppermute | solution.py:405
  83.9 0.0 collective-permute-done.refs_1_
  83.9 0.0 collective-permute-done.1.refs_0_
  84.0 0.0 collective-permute-done.2.refs_2_
  84.0 4.8 %all-to-all-done.1 = bf16[64,32,512]{2,1,0:T(8,128)(2,1)S(1)} async-done(((bf16[64,32,512]{2,1,0:T(8,128)(2,1)}), bf16[64,32,512]{2,1,0:T(8,128)(2,1)S(1)}, u32[]{:S(2)}, u32[]{:S(2)}) %all-to-all-start.1) | async-done | bytes 2097184 | tf_op jit(solution)/shard_map/all_to_all | solution.py:17
  88.7 10.0 %shard_map.79 = (bf16[2048,512]{1,0:T(8,128)(2,1)}, bf16[2048,512]{1,0:T(8,128)(2,1)}, bf16[2048,512]{1,0:T(8,128)(2,1)}, bf16[2048,512]{1,0:T(8,128)(2,1)}, bf1...) custom-call(bf16[2048,512]{1,0:T(8,128)(2,1)S(1)} %bitcast.16, ...), custom_call_target="tpu_custom_call" | custom-call | flops 5368709120 | bytes 4718592 | tf_op jit(solution)/shard_map/pallas_call | solution.py:261
  98.7 3.0 %collective-permute-start.6 = (bf16[128,256]{1,0:T(8,128)(2,1)S(1)}, bf16[128,256]{1,0:T(8,128)(2,1)S(1)}, u32[]{:S(2)}, u32[]{:S(2)}) collective-permute-start(bf16[128,256]{1,0:T(8,128)(2,1)S(1)} %get-tuple-element.55), channel_id=1, source_target_pairs={{0,2},{1,3},{2,0},{3,1},{4,6},{5,7},{6,4},{7,5},{8,10},{9,11},{10,... | collective-permute-start | bytes 196616 | tf_op jit(solution)/shard_map/ppermute | solution.py:405
  101.7 0.4 collective-permute-start.7
  102.1 2.3 %collective-permute-start.8 = (bf16[128,256]{1,0:T(8,128)(2,1)S(1)}, bf16[128,256]{1,0:T(8,128)(2,1)S(1)}, u32[]{:S(2)}, u32[]{:S(2)}) collective-permute-start(bf16[128,256]{1,0:T(8,128)(2,1)S(1)} %get-tuple-element.55), channel_id=1, source_target_pairs={{0,3},{1,0},{2,1},{3,2},{4,7},{5,4},{6,5},{7,6},{8,11},{9,8},{10,9... | collective-permute-start | bytes 196616 | tf_op jit(solution)/shard_map/ppermute | solution.py:405
  104.4 1.9 %shard_map.80 = (bf16[512,2048]{1,0:T(8,128)(2,1)S(1)}, bf16[2048,512]{1,0:T(8,128)(2,1)S(1)}, bf16[512,256]{1,0:T(8,128)(2,1)S(1)}, bf16[512,256]{1,0:T(8,128)(...) custom-call(s32[1]{0:T(128)} %bitcast.core_ref, bf16[2048,512]{1,0:T(8,128)(2,1)S(1)} %bitcast.17, ...), custom_call_target="tpu_custom_call" | custom-call | flops 1073741824 | bytes 8388608 | tf_op jit(solution)/shard_map/pallas_call | solution.py:318
  106.3 0.5 collective-permute-done.7.refs_2_
  106.8 2.3 %shard_map.81 = (f32[256,768]{1,0:T(8,128)S(1)}, bf16[256,768]{1,0:T(8,128)(2,1)S(1)}, bf16[128,256]{1,0:T(8,128)(2,1)S(1)}, bf16[128,512]{1,0:T(8,128)(2,1)S(1)...) custom-call(s32[1]{0:T(128)} %bitcast.core_ref, f32[128,256]{1,0:T(8,128)S(1)} %get-tuple-element.54.refs_0_, ...), custom_call_target="tpu_custom_call" | custom-call | flops 167772160 | bytes 4194304 | tf_op jit(solution)/shard_map/pallas_call | solution.py:201
  109.1 3.0 %collective-permute-start.10 = (bf16[256,768]{1,0:T(8,128)(2,1)S(1)}, bf16[256,768]{1,0:T(8,128)(2,1)S(1)}, u32[]{:S(2)}, u32[]{:S(2)}) collective-permute-start(bf16[256,768]{1,0:T(8,128)(2,1)S(1)} %get-tuple-element.74), channel_id=1, source_target_pairs={{0,4},{4,0},{8,12},{12,8},{16,20},{20,16},{24,28},{28,24},{1,5},{5... | collective-permute-start | bytes 1179656 | tf_op jit(solution)/shard_map/ppermute | solution.py:458
  112.1 1.9 %shard_map.82 = (f32[256,768]{1,0:T(8,128)S(1)}, bf16[256,768]{1,0:T(8,128)(2,1)S(1)}) custom-call(s32[1]{0:T(128)} %bitcast.core_ref, bf16[2048,128]{1,0:T(8,128)(2,1)S(1)} %select_convert_fusion.refs_6_.spread_ref, bf16[128,512]{1,0:T(8,128)(2,1)S(1)} %get-tuple-element.64.d_hidden_ref, bf16[2048,512]{1,0:T(8,128)(2,1)S(1)} %copy-done.2, ...), custom_call_target="tpu_custom_call" | custom-call | flops 1024 | bytes 1024 | tf_op jit(solution)/shard_map/pallas_call | solution.py:351
  114.0 0.3 collective-permute-start.9
  114.4 1.9 %shard_map.84 = (f32[256,768]{1,0:T(8,128)S(1)}, bf16[256,768]{1,0:T(8,128)(2,1)S(1)}) custom-call(s32[1]{0:T(128)} %bitcast.core_ref, bf16[2048,128]{1,0:T(8,128)(2,1)S(1)} %select_convert_fusion.refs_6_.spread_ref, bf16[128,512]{1,0:T(8,128)(2,1)S(1)} %get-tuple-element.77.d_hidden_ref, bf16[2048,512]{1,0:T(8,128)(2,1)S(1)} %copy-done.1, ...), custom_call_target="tpu_custom_call" | custom-call | flops 1024 | bytes 1024 | tf_op jit(solution)/shard_map/pallas_call | solution.py:351
  116.3 0.6 collective-permute-start.14
  116.8 0.1 add_convert_fusion.1
  116.9 0.1 collective-permute-start.12
  117.0 3.0 %collective-permute-start.15 = (bf16[128,768]{1,0:T(8,128)(2,1)S(1)}, bf16[128,768]{1,0:T(8,128)(2,1)S(1)}, u32[]{:S(2)}, u32[]{:S(2)}) collective-permute-start(bf16[128,768]{1,0:T(8,128)(2,1)S(1)} %get-tuple-element.83.refs_1_), channel_id=1, source_target_pairs={{0,3},{1,0},{2,1},{3,2},{4,7},{5,4},{6,5},{7,6},{8,11},{9,8},{10,9... | collective-permute-start | bytes 589832 | tf_op jit(solution)/shard_map/ppermute | solution.py:405
  120.1 1.9 %shard_map.83 = (f32[256,768]{1,0:T(8,128)S(1)}, bf16[256,768]{1,0:T(8,128)(2,1)S(1)}) custom-call(s32[1]{0:T(128)} %bitcast.core_ref, bf16[2048,128]{1,0:T(8,128)(2,1)S(1)} %select_convert_fusion.refs_6_.spread_ref, bf16[128,512]{1,0:T(8,128)(2,1)S(1)} %get-tuple-element.70.d_hidden_ref, bf16[2048,512]{1,0:T(8,128)(2,1)S(1)} %copy-done, ...), custom_call_target="tpu_custom_call" | custom-call | flops 1024 | bytes 1024 | tf_op jit(solution)/shard_map/pallas_call | solution.py:351
  122.0 0.4 collective-permute-start.11
  122.4 0.1 convert_add_fusion
  122.5 1.9 %collective-permute-done.15 = bf16[128,768]{1,0:T(8,128)(2,1)S(1)} collective-permute-done((bf16[128,768]{1,0:T(8,128)(2,1)S(1)}, bf16[128,768]{1,0:T(8,128)(2,1)S(1)}, u32[]{:S(2)}, u32[]{:S(2)}) %collective-permute-start.15) | collective-permute-done | bytes 196640 | tf_op jit(solution)/shard_map/ppermute | solution.py:405
  124.4 3.5 %collective-permute-start.16 = (bf16[256,768]{1,0:T(8,128)(2,1)S(1)}, bf16[256,768]{1,0:T(8,128)(2,1)S(1)}, u32[]{:S(2)}, u32[]{:S(2)}) collective-permute-start(bf16[256,768]{1,0:T(8,128)(2,1)S(1)} %pad_maximum_fusion.1), channel_id=1, source_target_pairs={{0,3},{1,0},{2,1},{3,2},{4,7},{5,4},{6,5},{7,6},{8,11},{9,8},{10,9... | collective-permute-start | bytes 1179656 | tf_op jit(solution)/shard_map/ppermute | solution.py:405
  127.9 0.1 convert_add_fusion.1
  128.1 0.1 collective-permute-start.13
  128.2 7.3 %collective-permute-done.16 = bf16[256,768]{1,0:T(8,128)(2,1)S(1)} collective-permute-done((bf16[256,768]{1,0:T(8,128)(2,1)S(1)}, bf16[256,768]{1,0:T(8,128)(2,1)S(1)}, u32[]{:S(2)}, u32[]{:S(2)}) %collective-permute-start.16) | collective-permute-done | bytes 393248 | tf_op jit(solution)/shard_map/ppermute | solution.py:405
  135.5 3.4 %collective-permute-done.13 = bf16[256,768]{1,0:T(8,128)(2,1)S(1)} collective-permute-done((bf16[256,768]{1,0:T(8,128)(2,1)S(1)}, bf16[256,768]{1,0:T(8,128)(2,1)S(1)}, u32[]{:S(2)}, u32[]{:S(2)}) %collective-permute-start.13) | collective-permute-done | bytes 393248 | tf_op jit(solution)/shard_map/ppermute | solution.py:405
  138.9 0.2 fusion.12
  139.1 16.0 %all_to_all.24 = bf16[32,8,768]{2,1,0:T(8,128)(2,1)S(1)} all-to-all(bf16[32,8,768]{2,1,0:T(8,128)(2,1)S(1)} %fusion.12), channel_id=1, replica_groups={{0,8,16,24,32,40,48,56,64,72,80,88,96,104,112,120,128,136,144,152,160,1..., dimensions={0} | all-to-all | bytes 786432 | tf_op jit(solution)/shard_map/all_to_all | solution.py:17
  155.1 0.1 reduce_sum.12
  155.2 17.6 %all_to_all.25 = bf16[32,8,768]{2,1,0:T(8,128)(2,1)S(1)} all-to-all(bf16[32,8,768]{2,1,0:T(8,128)(2,1)S(1)} %broadcast_in_dim.65), channel_id=1, replica_groups={{0,8,16,24,32,40,48,56,64,72,80,88,96,104,112,120,128,136,144,152,160,1..., dimensions={0} | all-to-all | bytes 786432 | tf_op jit(solution)/shard_map/all_to_all | solution.py:17
  172.8 4.6 %collective-permute-start.17 = (bf16[256,768]{1,0:T(8,128)(2,1)S(1)}, bf16[256,768]{1,0:T(8,128)(2,1)S(1)}, u32[]{:S(2)}, u32[]{:S(2)}) collective-permute-start(bf16[256,768]{1,0:T(8,128)(2,1)S(1)} %bitcast.18), channel_id=1, source_target_pairs={{0,4},{4,0},{8,12},{12,8},{16,20},{20,16},{24,28},{28,24},{1,5},{5... | collective-permute-start | bytes 1179656 | tf_op jit(solution)/shard_map/ppermute | solution.py:458
  177.4 1.3 collective-permute-done.17.other_ref
  178.8 1.2 shard_map.85
  (34 shorter events, 0.3 us)
Async XLA Ops:
  0.6 0.7 copy-start.3
  3.5 22.3 %all-to-all-start = ((s32[64,1,128]{2,1,0:T(1,128)}), s32[64,1,128]{2,1,0:T(1,128)S(1)}, u32[]{:S(2)}, u32[]{:S(2)}) async-start(s32[64,1,128]{2,1,0:T(1,128)} %bitcast.6), calls=%async_computation | async-start | bytes 65536 | tf_op jit(solution)/shard_map/all_to_all | solution.py:17
  34.0 8.8 %copy-start.6 = (bf16[512,256]{1,0:T(8,128)(2,1)S(1)}, bf16[512,256]{1,0:T(8,128)(2,1)}, u32[]{:S(2)}) copy-start(bf16[512,256]{1,0:T(8,128)(2,1)} %refs_4_) | copy-start | bytes 786436
  34.0 12.2 %copy-start.4 = (s32[128,32]{0,1:T(8,128)S(1)}, s32[128,32]{0,1:T(8,128)}, u32[]{:S(2)}) copy-start(s32[128,32]{0,1:T(8,128)} %param.7) | copy-start | bytes 49156
  34.1 54.7 %all-to-all-start.1 = ((bf16[64,32,512]{2,1,0:T(8,128)(2,1)}), bf16[64,32,512]{2,1,0:T(8,128)(2,1)S(1)}, u32[]{:S(2)}, u32[]{:S(2)}) async-start(bf16[64,32,512]{2,1,0:T(8,128)(2,1)} %bitcast.24), calls=%async_computation.1 | async-start | bytes 4194304 | tf_op jit(solution)/shard_map/all_to_all | solution.py:17
  39.0 7.9 %copy-start.9 = (bf16[128,32]{0,1:T(8,128)(2,1)S(1)}, bf16[128,32]{0,1:T(8,128)(2,1)}, u32[]{:S(2)}) copy-start(bf16[128,32]{0,1:T(8,128)(2,1)} %param.8) | copy-start | bytes 24580
  39.0 44.9 %collective-permute-start = (bf16[512,512]{1,0:T(8,128)(2,1)}, bf16[512,512]{1,0:T(8,128)(2,1)}, u32[]{:S(2)}, u32[]{:S(2)}) collective-permute-start(bf16[512,512]{1,0:T(8,128)(2,1)} %refs_3_), channel_id=1, source_target_pairs={{0,3},{1,0},{2,1},{3,2},{4,7},{5,4},{6,5},{7,6},{8,11},{9,8},{10,9... | collective-permute-start | bytes 1572872 | tf_op jit(solution)/shard_map/ppermute | solution.py:405
  41.8 42.1 %collective-permute-start.1 = (bf16[512,512]{1,0:T(8,128)(2,1)}, bf16[512,512]{1,0:T(8,128)(2,1)}, u32[]{:S(2)}, u32[]{:S(2)}) collective-permute-start(bf16[512,512]{1,0:T(8,128)(2,1)} %refs_3_), channel_id=1, source_target_pairs={{0,2},{1,3},{2,0},{3,1},{4,6},{5,7},{6,4},{7,5},{8,10},{9,11},{10,... | collective-permute-start | bytes 1572872 | tf_op jit(solution)/shard_map/ppermute | solution.py:405
  42.2 41.8 %collective-permute-start.2 = (bf16[512,512]{1,0:T(8,128)(2,1)}, bf16[512,512]{1,0:T(8,128)(2,1)}, u32[]{:S(2)}, u32[]{:S(2)}) collective-permute-start(bf16[512,512]{1,0:T(8,128)(2,1)} %refs_3_), channel_id=1, source_target_pairs={{0,1},{1,2},{2,3},{3,0},{4,5},{5,6},{6,7},{7,4},{8,9},{9,10},{10,1... | collective-permute-start | bytes 1572872 | tf_op jit(solution)/shard_map/ppermute | solution.py:405
  42.9 32.2 %collective-permute-start.3 = (bf16[512,256]{1,0:T(8,128)(2,1)S(1)}, bf16[512,256]{1,0:T(8,128)(2,1)S(1)}, u32[]{:S(2)}, u32[]{:S(2)}) collective-permute-start(bf16[512,256]{1,0:T(8,128)(2,1)S(1)} %copy-done.6), channel_id=1, source_target_pairs={{0,3},{1,0},{2,1},{3,2},{4,7},{5,4},{6,5},{7,6},{8,11},{9,8},{10,9... | collective-permute-start | bytes 786440 | tf_op jit(solution)/shard_map/ppermute | solution.py:405
  44.9 31.1 %collective-permute-start.4 = (bf16[512,256]{1,0:T(8,128)(2,1)S(1)}, bf16[512,256]{1,0:T(8,128)(2,1)S(1)}, u32[]{:S(2)}, u32[]{:S(2)}) collective-permute-start(bf16[512,256]{1,0:T(8,128)(2,1)S(1)} %copy-done.6), channel_id=1, source_target_pairs={{0,2},{1,3},{2,0},{3,1},{4,6},{5,7},{6,4},{7,5},{8,10},{9,11},{10,... | collective-permute-start | bytes 786440 | tf_op jit(solution)/shard_map/ppermute | solution.py:405
  75.1 13.6 %copy-start.7 = (bf16[512,256]{1,0:T(8,128)(2,1)}, bf16[512,256]{1,0:T(8,128)(2,1)S(1)}, u32[]{:S(2)}) copy-start(bf16[512,256]{1,0:T(8,128)(2,1)S(1)} %collective-permute-done.3.refs_5_.refs_2_) | copy-start | bytes 786436
  75.1 8.8 %collective-permute-start.5 = (bf16[512,256]{1,0:T(8,128)(2,1)S(1)}, bf16[512,256]{1,0:T(8,128)(2,1)}, u32[]{:S(2)}, u32[]{:S(2)}) collective-permute-start(bf16[512,256]{1,0:T(8,128)(2,1)S(1)} %copy-done.6), channel_id=1, source_target_pairs={{0,1},{1,2},{2,3},{3,0},{4,5},{5,6},{6,7},{7,4},{8,9},{9,10},{10,1... | collective-permute-start | bytes 786440 | tf_op jit(solution)/shard_map/ppermute | solution.py:405
  76.0 12.7 %copy-start.8 = (bf16[512,256]{1,0:T(8,128)(2,1)}, bf16[512,256]{1,0:T(8,128)(2,1)S(1)}, u32[]{:S(2)}) copy-start(bf16[512,256]{1,0:T(8,128)(2,1)S(1)} %collective-permute-done.4.refs_4_.refs_1_) | copy-start | bytes 786436
  98.7 7.6 %collective-permute-start.6 = (bf16[128,256]{1,0:T(8,128)(2,1)S(1)}, bf16[128,256]{1,0:T(8,128)(2,1)S(1)}, u32[]{:S(2)}, u32[]{:S(2)}) collective-permute-start(bf16[128,256]{1,0:T(8,128)(2,1)S(1)} %get-tuple-element.55), channel_id=1, source_target_pairs={{0,2},{1,3},{2,0},{3,1},{4,6},{5,7},{6,4},{7,5},{8,10},{9,11},{10,... | collective-permute-start | bytes 196616 | tf_op jit(solution)/shard_map/ppermute | solution.py:405
  101.7 5.0 %collective-permute-start.7 = (bf16[128,256]{1,0:T(8,128)(2,1)S(1)}, bf16[128,256]{1,0:T(8,128)(2,1)S(1)}, u32[]{:S(2)}, u32[]{:S(2)}) collective-permute-start(bf16[128,256]{1,0:T(8,128)(2,1)S(1)} %get-tuple-element.55), channel_id=1, source_target_pairs={{0,1},{1,2},{2,3},{3,0},{4,5},{5,6},{6,7},{7,4},{8,9},{9,10},{10,1... | collective-permute-start | bytes 196616 | tf_op jit(solution)/shard_map/ppermute | solution.py:405
  102.1 4.6 %collective-permute-start.8 = (bf16[128,256]{1,0:T(8,128)(2,1)S(1)}, bf16[128,256]{1,0:T(8,128)(2,1)S(1)}, u32[]{:S(2)}, u32[]{:S(2)}) collective-permute-start(bf16[128,256]{1,0:T(8,128)(2,1)S(1)} %get-tuple-element.55), channel_id=1, source_target_pairs={{0,3},{1,0},{2,1},{3,2},{4,7},{5,4},{6,5},{7,6},{8,11},{9,8},{10,9... | collective-permute-start | bytes 196616 | tf_op jit(solution)/shard_map/ppermute | solution.py:405
  104.4 2.4 %copy-start.5 = (s32[128]{0:T(128)S(1)}, s32[128]{0:T(128)}, u32[]{:S(2)}) copy-start(s32[128]{0:T(128)} %param.9) | copy-start | bytes 1540
  106.7 5.4 %copy-start.2 = (bf16[2048,512]{1,0:T(8,128)(2,1)S(1)}, bf16[2048,512]{1,0:T(8,128)(2,1)}, u32[]{:S(2)}) copy-start(bf16[2048,512]{1,0:T(8,128)(2,1)} %get-tuple-element.65.active_ref) | copy-start | bytes 6291460
  109.1 7.8 %collective-permute-start.10 = (bf16[256,768]{1,0:T(8,128)(2,1)S(1)}, bf16[256,768]{1,0:T(8,128)(2,1)S(1)}, u32[]{:S(2)}, u32[]{:S(2)}) collective-permute-start(bf16[256,768]{1,0:T(8,128)(2,1)S(1)} %get-tuple-element.74), channel_id=1, source_target_pairs={{0,4},{4,0},{8,12},{12,8},{16,20},{20,16},{24,28},{28,24},{1,5},{5... | collective-permute-start | bytes 1179656 | tf_op jit(solution)/shard_map/ppermute | solution.py:458
  112.1 2.2 %copy-start.1 = (bf16[2048,512]{1,0:T(8,128)(2,1)S(1)}, bf16[2048,512]{1,0:T(8,128)(2,1)}, u32[]{:S(2)}) copy-start(bf16[2048,512]{1,0:T(8,128)(2,1)} %get-tuple-element.78.active_ref) | copy-start | bytes 6291460
  114.0 14.2 %collective-permute-start.9 = (bf16[256,768]{1,0:T(8,128)(2,1)S(1)}, bf16[256,768]{1,0:T(8,128)(2,1)S(1)}, u32[]{:S(2)}, u32[]{:S(2)}) collective-permute-start(bf16[256,768]{1,0:T(8,128)(2,1)S(1)} %get-tuple-element.69), channel_id=1, source_target_pairs={{0,4},{4,0},{8,12},{12,8},{16,20},{20,16},{24,28},{28,24},{1,5},{5... | collective-permute-start | bytes 1179656 | tf_op jit(solution)/shard_map/ppermute | solution.py:458
  116.3 3.8 %copy-start = (bf16[2048,512]{1,0:T(8,128)(2,1)S(1)}, bf16[2048,512]{1,0:T(8,128)(2,1)}, u32[]{:S(2)}) copy-start(bf16[2048,512]{1,0:T(8,128)(2,1)} %get-tuple-element.71.active_ref) | copy-start | bytes 6291460
  116.3 6.1 %collective-permute-start.14 = (bf16[256,768]{1,0:T(8,128)(2,1)S(1)}, bf16[256,768]{1,0:T(8,128)(2,1)S(1)}, u32[]{:S(2)}, u32[]{:S(2)}) collective-permute-start(bf16[256,768]{1,0:T(8,128)(2,1)S(1)} %get-tuple-element.81), channel_id=1, source_target_pairs={{0,4},{4,0},{8,12},{12,8},{16,20},{20,16},{24,28},{28,24},{1,5},{5... | collective-permute-start | bytes 1179656 | tf_op jit(solution)/shard_map/ppermute | solution.py:458
  116.9 11.1 %collective-permute-start.12 = (bf16[128,768]{1,0:T(8,128)(2,1)S(1)}, bf16[128,768]{1,0:T(8,128)(2,1)S(1)}, u32[]{:S(2)}, u32[]{:S(2)}) collective-permute-start(bf16[128,768]{1,0:T(8,128)(2,1)S(1)} %get-tuple-element.82.refs_0_), channel_id=1, source_target_pairs={{0,1},{1,2},{2,3},{3,0},{4,5},{5,6},{6,7},{7,4},{8,9},{9,10},{10,1... | collective-permute-start | bytes 589832 | tf_op jit(solution)/shard_map/ppermute | solution.py:405
  117.0 7.3 %collective-permute-start.15 = (bf16[128,768]{1,0:T(8,128)(2,1)S(1)}, bf16[128,768]{1,0:T(8,128)(2,1)S(1)}, u32[]{:S(2)}, u32[]{:S(2)}) collective-permute-start(bf16[128,768]{1,0:T(8,128)(2,1)S(1)} %get-tuple-element.83.refs_1_), channel_id=1, source_target_pairs={{0,3},{1,0},{2,1},{3,2},{4,7},{5,4},{6,5},{7,6},{8,11},{9,8},{10,9... | collective-permute-start | bytes 589832 | tf_op jit(solution)/shard_map/ppermute | solution.py:405
  122.0 6.0 %collective-permute-start.11 = (bf16[256,768]{1,0:T(8,128)(2,1)S(1)}, bf16[256,768]{1,0:T(8,128)(2,1)S(1)}, u32[]{:S(2)}, u32[]{:S(2)}) collective-permute-start(bf16[256,768]{1,0:T(8,128)(2,1)S(1)} %get-tuple-element.76), channel_id=1, source_target_pairs={{0,4},{4,0},{8,12},{12,8},{16,20},{20,16},{24,28},{28,24},{1,5},{5... | collective-permute-start | bytes 1179656 | tf_op jit(solution)/shard_map/ppermute | solution.py:458
  124.4 11.1 %collective-permute-start.16 = (bf16[256,768]{1,0:T(8,128)(2,1)S(1)}, bf16[256,768]{1,0:T(8,128)(2,1)S(1)}, u32[]{:S(2)}, u32[]{:S(2)}) collective-permute-start(bf16[256,768]{1,0:T(8,128)(2,1)S(1)} %pad_maximum_fusion.1), channel_id=1, source_target_pairs={{0,3},{1,0},{2,1},{3,2},{4,7},{5,4},{6,5},{7,6},{8,11},{9,8},{10,9... | collective-permute-start | bytes 1179656 | tf_op jit(solution)/shard_map/ppermute | solution.py:405
  128.1 10.8 %collective-permute-start.13 = (bf16[256,768]{1,0:T(8,128)(2,1)S(1)}, bf16[256,768]{1,0:T(8,128)(2,1)S(1)}, u32[]{:S(2)}, u32[]{:S(2)}) collective-permute-start(bf16[256,768]{1,0:T(8,128)(2,1)S(1)} %pad_maximum_fusion), channel_id=1, source_target_pairs={{0,1},{1,2},{2,3},{3,0},{4,5},{5,6},{6,7},{7,4},{8,9},{9,10},{10,1... | collective-permute-start | bytes 1179656 | tf_op jit(solution)/shard_map/ppermute | solution.py:405
  172.8 6.0 %collective-permute-start.17 = (bf16[256,768]{1,0:T(8,128)(2,1)S(1)}, bf16[256,768]{1,0:T(8,128)(2,1)S(1)}, u32[]{:S(2)}, u32[]{:S(2)}) collective-permute-start(bf16[256,768]{1,0:T(8,128)(2,1)S(1)} %bitcast.18), channel_id=1, source_target_pairs={{0,4},{4,0},{8,12},{12,8},{16,20},{20,16},{24,28},{28,24},{1,5},{5... | collective-permute-start | bytes 1179656 | tf_op jit(solution)/shard_map/ppermute | solution.py:458

commit v13 on v12

--- a/solution.py
+++ b/solution.py
@@ -490,8 +490,8 @@
     above = jnp.concatenate([top + upward.astype(F32), bottom], axis=0).astype(BF)
     top, bottom = below[: half // 2], below[half // 2 :]
     below = jnp.concatenate([top, bottom + downward.astype(F32)], axis=0).astype(BF)
-    both = slice_sum(0, ())
-    both += to_mlp(above, 1).astype(F32) + to_mlp(below, -1).astype(F32)
+    from_below, from_above = to_mlp(above, 1), to_mlp(below, -1)
+    both = slice_sum(0, (from_below,)) + from_below.astype(F32) + from_above.astype(F32)
     both = both.astype(BF)
     chips = owners // 2
     groups = [[2 * i + c for i in range(chips)] for c in (0, 1)]

time: 181 us -> 185 us (1.022)
  waiting for transfers between devices: 63.2 us -> 66.1 us
  blocking collectives: 33.6 us -> 35.7 us
    ppermute x5, waiting for transfers between devices: 1.36 us -> 4.05 us  [partner(): return lax.ppermute(x, 'col', pairs)]
    all_to_all x2, blocking collectives: 33.6 us -> 35.7 us  [exchange(): lax.all_to_all(x, axes, split_axis=0, concat_axis=0, tiled=True, axis_ind...]
  transfers between devices with their start and end apart: 20 -> 20, of which waited for: 9 -> 10; matrix products, arithmetic and copies ran while one was open for 2% -> 2% of each run, Pallas kernels for 4% -> 3%
where the time goes in v13:
time: 185 us
  waiting for transfers between devices  66.1 us (36%)
  starting transfers between devices  45.9 us (25%)
  blocking collectives  35.7 us (19%)
  Pallas kernels  31.2 us (17%)
  other arithmetic  2.22 us (1%)
    ppermute x13, waiting for transfers between devices, to_mlp(): lax.ppermute(x, 'mlp', [(j, (j + step) % mlp_n) for j in range(mlp_n)])  48 us
    all_to_all x2, blocking collectives, exchange(): lax.all_to_all(x, axes, split_axis=0, concat_axis=0, tiled=True, axis_ind...  35.7 us
    ppermute x13, starting transfers between devices, to_mlp(): lax.ppermute(x, 'mlp', [(j, (j + step) % mlp_n) for j in range(mlp_n)])  18.7 us
    all_to_all x2, starting transfers between devices, exchange(): lax.all_to_all(x, axes, split_axis=0, concat_axis=0, tiled=True, axis_ind...  17.9 us
    all_to_all x2, waiting for transfers between devices, exchange(): lax.all_to_all(x, axes, split_axis=0, concat_axis=0, tiled=True, axis_ind...  14.1 us
    pallas_call x1, Pallas kernels, forward(): pl.pallas_call(kernel, out_shape=[pltpu.HBM((slots, units), BF)] * count...  9.98 us
    ppermute x5, starting transfers between devices, partner(): return lax.ppermute(x, 'col', pairs)  9.21 us
    pallas_call x1, Pallas kernels, gather(): pl.pallas_call(kernel, out_shape=pltpu.HBM((count, width_f), BF), in_spec...  8.01 us
  transfers between devices with their start and end apart: 20, of which 10 were waited for; matrix products, arithmetic and copies ran while one was open for 2% of the time, Pallas kernels for 3%

profile of v13, /device:TPU:1, one launch (start us, length us, event | category | flops | bytes accessed | tf_op | source)
XLA Modules:
  0.0 184.6 jit_solution(10662521477438254271)
XLA Ops:
  0.6 0.0 copy-start.3
  0.6 0.7 copy-done.3
  1.3 2.1 %shard_map.77 = (s32[64,128]{1,0:T(8,128)}, s32[32,128]{1,0:T(8,128)S(1)}) custom-call(s32[32,128]{1,0:T(8,128)S(1)} %bitcast.20), custom_call_target="tpu_custom_call" | custom-call | tf_op jit(solution)/shard_map/pallas_call | solution.py:70
  3.5 13.0 %all-to-all-start = ((s32[64,1,128]{2,1,0:T(1,128)}), s32[64,1,128]{2,1,0:T(1,128)S(1)}, u32[]{:S(2)}, u32[]{:S(2)}) async-start(s32[64,1,128]{2,1,0:T(1,128)} %bitcast.6), calls=%async_computation | async-start | bytes 65536 | tf_op jit(solution)/shard_map/all_to_all | solution.py:17
  16.5 9.3 %all-to-all-done = s32[64,1,128]{2,1,0:T(1,128)S(1)} async-done(((s32[64,1,128]{2,1,0:T(1,128)}), s32[64,1,128]{2,1,0:T(1,128)S(1)}, u32[]{:S(2)}, u32[]{:S(2)}) %all-to-all-start) | async-done | bytes 32800 | tf_op jit(solution)/shard_map/all_to_all | solution.py:17
  25.8 0.2 dynamic-slice_reduce_fusion
  25.9 0.1 reshape.45.asked_ref
  26.0 8.0 %shard_map.78 = bf16[2048,512]{1,0:T(8,128)(2,1)} custom-call(s32[2048]{0:T(1024)S(1)} %reshape.45.asked_ref, bf16[4096,512]{1,0:T(8,128)(2,1)} %features_ref.1), custom_call_target="tpu_custom_call" | custom-call | tf_op jit(solution)/shard_map/pallas_call | solution.py:124
  34.0 0.0 copy-start.6
  34.0 0.0 copy-start.4
  34.1 4.9 %all-to-all-start.1 = ((bf16[64,32,512]{2,1,0:T(8,128)(2,1)}), bf16[64,32,512]{2,1,0:T(8,128)(2,1)S(1)}, u32[]{:S(2)}, u32[]{:S(2)}) async-start(bf16[64,32,512]{2,1,0:T(8,128)(2,1)} %bitcast.24), calls=%async_computation.1 | async-start | bytes 4194304 | tf_op jit(solution)/shard_map/all_to_all | solution.py:17
  39.0 0.0 copy-start.9
  39.0 2.8 %collective-permute-start = (bf16[512,512]{1,0:T(8,128)(2,1)}, bf16[512,512]{1,0:T(8,128)(2,1)}, u32[]{:S(2)}, u32[]{:S(2)}) collective-permute-start(bf16[512,512]{1,0:T(8,128)(2,1)} %refs_3_), channel_id=1, source_target_pairs={{0,3},{1,0},{2,1},{3,2},{4,7},{5,4},{6,5},{7,6},{8,11},{9,8},{10,9... | collective-permute-start | bytes 1572872 | tf_op jit(solution)/shard_map/ppermute | solution.py:405
  41.8 0.3 collective-permute-start.1
  42.2 0.7 collective-permute-start.2
  42.9 2.0 %collective-permute-start.3 = (bf16[512,256]{1,0:T(8,128)(2,1)S(1)}, bf16[512,256]{1,0:T(8,128)(2,1)S(1)}, u32[]{:S(2)}, u32[]{:S(2)}) collective-permute-start(bf16[512,256]{1,0:T(8,128)(2,1)S(1)} %copy-done.6), channel_id=1, source_target_pairs={{0,3},{1,0},{2,1},{3,2},{4,7},{5,4},{6,5},{7,6},{8,11},{9,8},{10,9... | collective-permute-start | bytes 786440 | tf_op jit(solution)/shard_map/ppermute | solution.py:405
  44.9 1.4 collective-permute-start.4
  46.3 0.4 convolution_bitcast_fusion.1
  46.8 0.1 copy.10
  46.8 0.1 convert_element_type.58
  46.9 0.4 convolution_bitcast_fusion
  47.4 0.1 copy.11
  47.5 0.1 broadcast_in_dim.59
  47.6 0.7 select_convert_fusion.refs_6_.spread_ref
  48.3 26.8 %collective-permute-done.3.refs_5_.refs_2_ = bf16[512,256]{1,0:T(8,128)(2,1)S(1)} collective-permute-done((bf16[512,256]{1,0:T(8,128)(2,1)S(1)}, bf16[512,256]{1,0:T(8,128)(2,1)S(1)}, u32[]{:S(2)}, u32[]{:S(2)}) %collective-permute-start.3) | collective-permute-done | bytes 262176 | tf_op jit(solution)/shard_map/ppermute | solution.py:405
  75.1 0.0 collective-permute-start.5
  75.1 0.9 select_convert_fusion.1.spread_ref
  76.0 0.0 collective-permute-done.4.refs_4_.refs_1_
  76.0 7.9 %collective-permute-done.5.refs_6_.refs_3_ = bf16[512,256]{1,0:T(8,128)(2,1)} collective-permute-done((bf16[512,256]{1,0:T(8,128)(2,1)S(1)}, bf16[512,256]{1,0:T(8,128)(2,1)}, u32[]{:S(2)}, u32[]{:S(2)}) %collective-permute-start.5) | collective-permute-done | bytes 262176 | tf_op jit(solution)/shard_map/ppermute | solution.py:405
  83.9 0.0 collective-permute-done.refs_1_
  83.9 0.0 collective-permute-done.1.refs_0_
  84.0 0.0 collective-permute-done.2.refs_2_
  84.0 4.8 %all-to-all-done.1 = bf16[64,32,512]{2,1,0:T(8,128)(2,1)S(1)} async-done(((bf16[64,32,512]{2,1,0:T(8,128)(2,1)}), bf16[64,32,512]{2,1,0:T(8,128)(2,1)S(1)}, u32[]{:S(2)}, u32[]{:S(2)}) %all-to-all-start.1) | async-done | bytes 2097184 | tf_op jit(solution)/shard_map/all_to_all | solution.py:17
  88.7 10.0 %shard_map.79 = (bf16[2048,512]{1,0:T(8,128)(2,1)}, bf16[2048,512]{1,0:T(8,128)(2,1)}, bf16[2048,512]{1,0:T(8,128)(2,1)}, bf16[2048,512]{1,0:T(8,128)(2,1)}, bf1...) custom-call(bf16[2048,512]{1,0:T(8,128)(2,1)S(1)} %bitcast.16, ...), custom_call_target="tpu_custom_call" | custom-call | flops 5368709120 | bytes 4718592 | tf_op jit(solution)/shard_map/pallas_call | solution.py:261
  98.7 3.0 %collective-permute-start.6 = (bf16[128,256]{1,0:T(8,128)(2,1)S(1)}, bf16[128,256]{1,0:T(8,128)(2,1)S(1)}, u32[]{:S(2)}, u32[]{:S(2)}) collective-permute-start(bf16[128,256]{1,0:T(8,128)(2,1)S(1)} %get-tuple-element.55), channel_id=1, source_target_pairs={{0,2},{1,3},{2,0},{3,1},{4,6},{5,7},{6,4},{7,5},{8,10},{9,11},{10,... | collective-permute-start | bytes 196616 | tf_op jit(solution)/shard_map/ppermute | solution.py:405
  101.7 0.4 collective-permute-start.7
  102.1 2.3 %collective-permute-start.8 = (bf16[128,256]{1,0:T(8,128)(2,1)S(1)}, bf16[128,256]{1,0:T(8,128)(2,1)S(1)}, u32[]{:S(2)}, u32[]{:S(2)}) collective-permute-start(bf16[128,256]{1,0:T(8,128)(2,1)S(1)} %get-tuple-element.55), channel_id=1, source_target_pairs={{0,3},{1,0},{2,1},{3,2},{4,7},{5,4},{6,5},{7,6},{8,11},{9,8},{10,9... | collective-permute-start | bytes 196616 | tf_op jit(solution)/shard_map/ppermute | solution.py:405
  104.4 1.9 %shard_map.80 = (bf16[512,2048]{1,0:T(8,128)(2,1)S(1)}, bf16[2048,512]{1,0:T(8,128)(2,1)S(1)}, bf16[512,256]{1,0:T(8,128)(2,1)S(1)}, bf16[512,256]{1,0:T(8,128)(...) custom-call(s32[1]{0:T(128)} %bitcast.core_ref, bf16[2048,512]{1,0:T(8,128)(2,1)S(1)} %bitcast.17, ...), custom_call_target="tpu_custom_call" | custom-call | flops 1073741824 | bytes 8388608 | tf_op jit(solution)/shard_map/pallas_call | solution.py:318
  106.3 0.5 collective-permute-done.7.refs_2_
  106.7 2.3 %shard_map.81 = (f32[256,768]{1,0:T(8,128)S(1)}, bf16[256,768]{1,0:T(8,128)(2,1)S(1)}, bf16[128,256]{1,0:T(8,128)(2,1)S(1)}, bf16[128,512]{1,0:T(8,128)(2,1)S(1)...) custom-call(s32[1]{0:T(128)} %bitcast.core_ref, f32[128,256]{1,0:T(8,128)S(1)} %get-tuple-element.54.refs_0_, ...), custom_call_target="tpu_custom_call" | custom-call | flops 167772160 | bytes 4194304 | tf_op jit(solution)/shard_map/pallas_call | solution.py:201
  109.1 3.0 %collective-permute-start.9 = (bf16[256,768]{1,0:T(8,128)(2,1)S(1)}, bf16[256,768]{1,0:T(8,128)(2,1)S(1)}, u32[]{:S(2)}, u32[]{:S(2)}) collective-permute-start(bf16[256,768]{1,0:T(8,128)(2,1)S(1)} %get-tuple-element.72), channel_id=1, source_target_pairs={{0,4},{4,0},{8,12},{12,8},{16,20},{20,16},{24,28},{28,24},{1,5},{5... | collective-permute-start | bytes 1179656 | tf_op jit(solution)/shard_map/ppermute | solution.py:458
  112.1 1.3 collective-permute-done.9
  113.5 0.1 add_convert_fusion.1
  113.6 1.9 %shard_map.82 = (f32[256,768]{1,0:T(8,128)S(1)}, bf16[256,768]{1,0:T(8,128)(2,1)S(1)}) custom-call(s32[1]{0:T(128)} %bitcast.core_ref, bf16[2048,128]{1,0:T(8,128)(2,1)S(1)} %select_convert_fusion.refs_6_.spread_ref, bf16[128,512]{1,0:T(8,128)(2,1)S(1)} %get-tuple-element.68.d_hidden_ref, bf16[2048,512]{1,0:T(8,128)(2,1)S(1)} %copy-done.1, ...), custom_call_target="tpu_custom_call" | custom-call | flops 1024 | bytes 1024 | tf_op jit(solution)/shard_map/pallas_call | solution.py:351
  115.5 0.7 collective-permute-start.10
  116.2 1.9 %shard_map.84 = (f32[256,768]{1,0:T(8,128)S(1)}, bf16[256,768]{1,0:T(8,128)(2,1)S(1)}) custom-call(s32[1]{0:T(128)} %bitcast.core_ref, bf16[2048,128]{1,0:T(8,128)(2,1)S(1)} %select_convert_fusion.refs_6_.spread_ref, bf16[128,512]{1,0:T(8,128)(2,1)S(1)} %get-tuple-element.77.d_hidden_ref, bf16[2048,512]{1,0:T(8,128)(2,1)S(1)} %copy-done.2, ...), custom_call_target="tpu_custom_call" | custom-call | flops 1024 | bytes 1024 | tf_op jit(solution)/shard_map/pallas_call | solution.py:351
  118.1 0.2 collective-permute-start.14
  118.3 3.0 %collective-permute-start.15 = (bf16[128,768]{1,0:T(8,128)(2,1)S(1)}, bf16[128,768]{1,0:T(8,128)(2,1)S(1)}, u32[]{:S(2)}, u32[]{:S(2)}) collective-permute-start(bf16[128,768]{1,0:T(8,128)(2,1)S(1)} %get-tuple-element.83.refs_1_), channel_id=1, source_target_pairs={{0,3},{1,0},{2,1},{3,2},{4,7},{5,4},{6,5},{7,6},{8,11},{9,8},{10,9... | collective-permute-start | bytes 589832 | tf_op jit(solution)/shard_map/ppermute | solution.py:405
  121.3 0.1 convert_add_fusion.1
  121.4 4.8 %collective-permute-done.11 = bf16[128,768]{1,0:T(8,128)(2,1)S(1)} collective-permute-done((bf16[128,768]{1,0:T(8,128)(2,1)S(1)}, bf16[128,768]{1,0:T(8,128)(2,1)S(1)}, u32[]{:S(2)}, u32[]{:S(2)}) %collective-permute-start.11) | collective-permute-done | bytes 196640 | tf_op jit(solution)/shard_map/ppermute | solution.py:405
  126.3 0.1 collective-permute-start.12
  126.4 0.1 convert_add_fusion
  126.6 2.7 %collective-permute-start.16 = (bf16[256,768]{1,0:T(8,128)(2,1)S(1)}, bf16[256,768]{1,0:T(8,128)(2,1)S(1)}, u32[]{:S(2)}, u32[]{:S(2)}) collective-permute-start(bf16[256,768]{1,0:T(8,128)(2,1)S(1)} %pad_maximum_fusion.1), channel_id=1, source_target_pairs={{0,3},{1,0},{2,1},{3,2},{4,7},{5,4},{6,5},{7,6},{8,11},{9,8},{10,9... | collective-permute-start | bytes 1179656 | tf_op jit(solution)/shard_map/ppermute | solution.py:405
  129.3 8.0 %collective-permute-done.12.refs_0_ = bf16[256,768]{1,0:T(8,128)(2,1)S(1)} collective-permute-done((bf16[256,768]{1,0:T(8,128)(2,1)S(1)}, bf16[256,768]{1,0:T(8,128)(2,1)S(1)}, u32[]{:S(2)}, u32[]{:S(2)}) %collective-permute-start.12) | collective-permute-done | bytes 393248 | tf_op jit(solution)/shard_map/ppermute | solution.py:405
  137.3 1.9 %shard_map.83 = (f32[256,768]{1,0:T(8,128)S(1)}, bf16[256,768]{1,0:T(8,128)(2,1)S(1)}) custom-call(s32[1]{0:T(128)} %bitcast.core_ref, bf16[2048,128]{1,0:T(8,128)(2,1)S(1)} %select_convert_fusion.refs_6_.spread_ref, bf16[128,512]{1,0:T(8,128)(2,1)S(1)} %get-tuple-element.64.d_hidden_ref, bf16[2048,512]{1,0:T(8,128)(2,1)S(1)} %copy-done, ...), custom_call_target="tpu_custom_call" | custom-call | flops 1024 | bytes 1024 | tf_op jit(solution)/shard_map/pallas_call | solution.py:351
  139.2 1.9 %collective-permute-start.13 = (bf16[256,768]{1,0:T(8,128)(2,1)S(1)}, bf16[256,768]{1,0:T(8,128)(2,1)S(1)}, u32[]{:S(2)}, u32[]{:S(2)}) collective-permute-start(bf16[256,768]{1,0:T(8,128)(2,1)S(1)} %get-tuple-element.76), channel_id=1, source_target_pairs={{0,4},{4,0},{8,12},{12,8},{16,20},{20,16},{24,28},{28,24},{1,5},{5... | collective-permute-start | bytes 1179656 | tf_op jit(solution)/shard_map/ppermute | solution.py:458
  141.1 1.3 collective-permute-done.13
  142.5 0.2 fusion.12
  142.6 18.1 %all_to_all.24 = bf16[32,8,768]{2,1,0:T(8,128)(2,1)S(1)} all-to-all(bf16[32,8,768]{2,1,0:T(8,128)(2,1)S(1)} %fusion.12), channel_id=1, replica_groups={{0,8,16,24,32,40,48,56,64,72,80,88,96,104,112,120,128,136,144,152,160,1..., dimensions={0} | all-to-all | bytes 786432 | tf_op jit(solution)/shard_map/all_to_all | solution.py:17
  160.7 0.1 reduce_sum.12
  160.8 17.6 %all_to_all.25 = bf16[32,8,768]{2,1,0:T(8,128)(2,1)S(1)} all-to-all(bf16[32,8,768]{2,1,0:T(8,128)(2,1)S(1)} %broadcast_in_dim.65), channel_id=1, replica_groups={{0,8,16,24,32,40,48,56,64,72,80,88,96,104,112,120,128,136,144,152,160,1..., dimensions={0} | all-to-all | bytes 786432 | tf_op jit(solution)/shard_map/all_to_all | solution.py:17
  178.5 3.4 %collective-permute-start.17 = (bf16[256,768]{1,0:T(8,128)(2,1)S(1)}, bf16[256,768]{1,0:T(8,128)(2,1)S(1)}, u32[]{:S(2)}, u32[]{:S(2)}) collective-permute-start(bf16[256,768]{1,0:T(8,128)(2,1)S(1)} %bitcast.18), channel_id=1, source_target_pairs={{0,4},{4,0},{8,12},{12,8},{16,20},{20,16},{24,28},{28,24},{1,5},{5... | collective-permute-start | bytes 1179656 | tf_op jit(solution)/shard_map/ppermute | solution.py:458
  181.9 1.3 collective-permute-done.17.other_ref
  183.2 1.2 shard_map.85
  (34 shorter events, 0.3 us)
Async XLA Ops:
  0.6 0.7 copy-start.3
  3.5 22.3 %all-to-all-start = ((s32[64,1,128]{2,1,0:T(1,128)}), s32[64,1,128]{2,1,0:T(1,128)S(1)}, u32[]{:S(2)}, u32[]{:S(2)}) async-start(s32[64,1,128]{2,1,0:T(1,128)} %bitcast.6), calls=%async_computation | async-start | bytes 65536 | tf_op jit(solution)/shard_map/all_to_all | solution.py:17
  34.0 8.8 %copy-start.6 = (bf16[512,256]{1,0:T(8,128)(2,1)S(1)}, bf16[512,256]{1,0:T(8,128)(2,1)}, u32[]{:S(2)}) copy-start(bf16[512,256]{1,0:T(8,128)(2,1)} %refs_4_) | copy-start | bytes 786436
  34.0 12.2 %copy-start.4 = (s32[128,32]{0,1:T(8,128)S(1)}, s32[128,32]{0,1:T(8,128)}, u32[]{:S(2)}) copy-start(s32[128,32]{0,1:T(8,128)} %param.7) | copy-start | bytes 49156
  34.1 54.7 %all-to-all-start.1 = ((bf16[64,32,512]{2,1,0:T(8,128)(2,1)}), bf16[64,32,512]{2,1,0:T(8,128)(2,1)S(1)}, u32[]{:S(2)}, u32[]{:S(2)}) async-start(bf16[64,32,512]{2,1,0:T(8,128)(2,1)} %bitcast.24), calls=%async_computation.1 | async-start | bytes 4194304 | tf_op jit(solution)/shard_map/all_to_all | solution.py:17
  39.0 7.9 %copy-start.9 = (bf16[128,32]{0,1:T(8,128)(2,1)S(1)}, bf16[128,32]{0,1:T(8,128)(2,1)}, u32[]{:S(2)}) copy-start(bf16[128,32]{0,1:T(8,128)(2,1)} %param.8) | copy-start | bytes 24580
  39.0 44.9 %collective-permute-start = (bf16[512,512]{1,0:T(8,128)(2,1)}, bf16[512,512]{1,0:T(8,128)(2,1)}, u32[]{:S(2)}, u32[]{:S(2)}) collective-permute-start(bf16[512,512]{1,0:T(8,128)(2,1)} %refs_3_), channel_id=1, source_target_pairs={{0,3},{1,0},{2,1},{3,2},{4,7},{5,4},{6,5},{7,6},{8,11},{9,8},{10,9... | collective-permute-start | bytes 1572872 | tf_op jit(solution)/shard_map/ppermute | solution.py:405
  41.8 42.1 %collective-permute-start.1 = (bf16[512,512]{1,0:T(8,128)(2,1)}, bf16[512,512]{1,0:T(8,128)(2,1)}, u32[]{:S(2)}, u32[]{:S(2)}) collective-permute-start(bf16[512,512]{1,0:T(8,128)(2,1)} %refs_3_), channel_id=1, source_target_pairs={{0,2},{1,3},{2,0},{3,1},{4,6},{5,7},{6,4},{7,5},{8,10},{9,11},{10,... | collective-permute-start | bytes 1572872 | tf_op jit(solution)/shard_map/ppermute | solution.py:405
  42.2 41.8 %collective-permute-start.2 = (bf16[512,512]{1,0:T(8,128)(2,1)}, bf16[512,512]{1,0:T(8,128)(2,1)}, u32[]{:S(2)}, u32[]{:S(2)}) collective-permute-start(bf16[512,512]{1,0:T(8,128)(2,1)} %refs_3_), channel_id=1, source_target_pairs={{0,1},{1,2},{2,3},{3,0},{4,5},{5,6},{6,7},{7,4},{8,9},{9,10},{10,1... | collective-permute-start | bytes 1572872 | tf_op jit(solution)/shard_map/ppermute | solution.py:405
  42.9 32.2 %collective-permute-start.3 = (bf16[512,256]{1,0:T(8,128)(2,1)S(1)}, bf16[512,256]{1,0:T(8,128)(2,1)S(1)}, u32[]{:S(2)}, u32[]{:S(2)}) collective-permute-start(bf16[512,256]{1,0:T(8,128)(2,1)S(1)} %copy-done.6), channel_id=1, source_target_pairs={{0,3},{1,0},{2,1},{3,2},{4,7},{5,4},{6,5},{7,6},{8,11},{9,8},{10,9... | collective-permute-start | bytes 786440 | tf_op jit(solution)/shard_map/ppermute | solution.py:405
  44.9 31.1 %collective-permute-start.4 = (bf16[512,256]{1,0:T(8,128)(2,1)S(1)}, bf16[512,256]{1,0:T(8,128)(2,1)S(1)}, u32[]{:S(2)}, u32[]{:S(2)}) collective-permute-start(bf16[512,256]{1,0:T(8,128)(2,1)S(1)} %copy-done.6), channel_id=1, source_target_pairs={{0,2},{1,3},{2,0},{3,1},{4,6},{5,7},{6,4},{7,5},{8,10},{9,11},{10,... | collective-permute-start | bytes 786440 | tf_op jit(solution)/shard_map/ppermute | solution.py:405
  75.1 13.6 %copy-start.7 = (bf16[512,256]{1,0:T(8,128)(2,1)}, bf16[512,256]{1,0:T(8,128)(2,1)S(1)}, u32[]{:S(2)}) copy-start(bf16[512,256]{1,0:T(8,128)(2,1)S(1)} %collective-permute-done.3.refs_5_.refs_2_) | copy-start | bytes 786436
  75.1 8.8 %collective-permute-start.5 = (bf16[512,256]{1,0:T(8,128)(2,1)S(1)}, bf16[512,256]{1,0:T(8,128)(2,1)}, u32[]{:S(2)}, u32[]{:S(2)}) collective-permute-start(bf16[512,256]{1,0:T(8,128)(2,1)S(1)} %copy-done.6), channel_id=1, source_target_pairs={{0,1},{1,2},{2,3},{3,0},{4,5},{5,6},{6,7},{7,4},{8,9},{9,10},{10,1... | collective-permute-start | bytes 786440 | tf_op jit(solution)/shard_map/ppermute | solution.py:405
  76.0 12.7 %copy-start.8 = (bf16[512,256]{1,0:T(8,128)(2,1)}, bf16[512,256]{1,0:T(8,128)(2,1)S(1)}, u32[]{:S(2)}) copy-start(bf16[512,256]{1,0:T(8,128)(2,1)S(1)} %collective-permute-done.4.refs_4_.refs_1_) | copy-start | bytes 786436
  98.7 7.6 %collective-permute-start.6 = (bf16[128,256]{1,0:T(8,128)(2,1)S(1)}, bf16[128,256]{1,0:T(8,128)(2,1)S(1)}, u32[]{:S(2)}, u32[]{:S(2)}) collective-permute-start(bf16[128,256]{1,0:T(8,128)(2,1)S(1)} %get-tuple-element.55), channel_id=1, source_target_pairs={{0,2},{1,3},{2,0},{3,1},{4,6},{5,7},{6,4},{7,5},{8,10},{9,11},{10,... | collective-permute-start | bytes 196616 | tf_op jit(solution)/shard_map/ppermute | solution.py:405
  101.7 5.0 %collective-permute-start.7 = (bf16[128,256]{1,0:T(8,128)(2,1)S(1)}, bf16[128,256]{1,0:T(8,128)(2,1)S(1)}, u32[]{:S(2)}, u32[]{:S(2)}) collective-permute-start(bf16[128,256]{1,0:T(8,128)(2,1)S(1)} %get-tuple-element.55), channel_id=1, source_target_pairs={{0,1},{1,2},{2,3},{3,0},{4,5},{5,6},{6,7},{7,4},{8,9},{9,10},{10,1... | collective-permute-start | bytes 196616 | tf_op jit(solution)/shard_map/ppermute | solution.py:405
  102.1 4.6 %collective-permute-start.8 = (bf16[128,256]{1,0:T(8,128)(2,1)S(1)}, bf16[128,256]{1,0:T(8,128)(2,1)S(1)}, u32[]{:S(2)}, u32[]{:S(2)}) collective-permute-start(bf16[128,256]{1,0:T(8,128)(2,1)S(1)} %get-tuple-element.55), channel_id=1, source_target_pairs={{0,3},{1,0},{2,1},{3,2},{4,7},{5,4},{6,5},{7,6},{8,11},{9,8},{10,9... | collective-permute-start | bytes 196616 | tf_op jit(solution)/shard_map/ppermute | solution.py:405
  104.4 2.4 %copy-start.5 = (s32[128]{0:T(128)S(1)}, s32[128]{0:T(128)}, u32[]{:S(2)}) copy-start(s32[128]{0:T(128)} %param.9) | copy-start | bytes 1540
  109.1 4.5 %copy-start.1 = (bf16[2048,512]{1,0:T(8,128)(2,1)S(1)}, bf16[2048,512]{1,0:T(8,128)(2,1)}, u32[]{:S(2)}) copy-start(bf16[2048,512]{1,0:T(8,128)(2,1)} %get-tuple-element.69.active_ref) | copy-start | bytes 6291460
  109.1 4.4 %collective-permute-start.9 = (bf16[256,768]{1,0:T(8,128)(2,1)S(1)}, bf16[256,768]{1,0:T(8,128)(2,1)S(1)}, u32[]{:S(2)}, u32[]{:S(2)}) collective-permute-start(bf16[256,768]{1,0:T(8,128)(2,1)S(1)} %get-tuple-element.72), channel_id=1, source_target_pairs={{0,4},{4,0},{8,12},{12,8},{16,20},{20,16},{24,28},{28,24},{1,5},{5... | collective-permute-start | bytes 1179656 | tf_op jit(solution)/shard_map/ppermute | solution.py:458
  113.6 2.6 %copy-start.2 = (bf16[2048,512]{1,0:T(8,128)(2,1)S(1)}, bf16[2048,512]{1,0:T(8,128)(2,1)}, u32[]{:S(2)}) copy-start(bf16[2048,512]{1,0:T(8,128)(2,1)} %get-tuple-element.78.active_ref) | copy-start | bytes 6291460
  115.5 5.8 %collective-permute-start.10 = (bf16[256,768]{1,0:T(8,128)(2,1)S(1)}, bf16[256,768]{1,0:T(8,128)(2,1)S(1)}, u32[]{:S(2)}, u32[]{:S(2)}) collective-permute-start(bf16[256,768]{1,0:T(8,128)(2,1)S(1)} %get-tuple-element.74), channel_id=1, source_target_pairs={{0,4},{4,0},{8,12},{12,8},{16,20},{20,16},{24,28},{28,24},{1,5},{5... | collective-permute-start | bytes 1179656 | tf_op jit(solution)/shard_map/ppermute | solution.py:458
  118.1 8.3 %collective-permute-start.14 = (bf16[256,768]{1,0:T(8,128)(2,1)S(1)}, bf16[256,768]{1,0:T(8,128)(2,1)S(1)}, u32[]{:S(2)}, u32[]{:S(2)}) collective-permute-start(bf16[256,768]{1,0:T(8,128)(2,1)S(1)} %get-tuple-element.81), channel_id=1, source_target_pairs={{0,4},{4,0},{8,12},{12,8},{16,20},{20,16},{24,28},{28,24},{1,5},{5... | collective-permute-start | bytes 1179656 | tf_op jit(solution)/shard_map/ppermute | solution.py:458
  118.3 7.9 %collective-permute-start.11 = (bf16[128,768]{1,0:T(8,128)(2,1)S(1)}, bf16[128,768]{1,0:T(8,128)(2,1)S(1)}, u32[]{:S(2)}, u32[]{:S(2)}) collective-permute-start(bf16[128,768]{1,0:T(8,128)(2,1)S(1)} %get-tuple-element.82.refs_0_), channel_id=1, source_target_pairs={{0,1},{1,2},{2,3},{3,0},{4,5},{5,6},{6,7},{7,4},{8,9},{9,10},{10,1... | collective-permute-start | bytes 589832 | tf_op jit(solution)/shard_map/ppermute | solution.py:405
  118.3 8.2 %collective-permute-start.15 = (bf16[128,768]{1,0:T(8,128)(2,1)S(1)}, bf16[128,768]{1,0:T(8,128)(2,1)S(1)}, u32[]{:S(2)}, u32[]{:S(2)}) collective-permute-start(bf16[128,768]{1,0:T(8,128)(2,1)S(1)} %get-tuple-element.83.refs_1_), channel_id=1, source_target_pairs={{0,3},{1,0},{2,1},{3,2},{4,7},{5,4},{6,5},{7,6},{8,11},{9,8},{10,9... | collective-permute-start | bytes 589832 | tf_op jit(solution)/shard_map/ppermute | solution.py:405
  126.3 11.0 %copy-start = (bf16[2048,512]{1,0:T(8,128)(2,1)S(1)}, bf16[2048,512]{1,0:T(8,128)(2,1)}, u32[]{:S(2)}) copy-start(bf16[2048,512]{1,0:T(8,128)(2,1)} %get-tuple-element.65.active_ref) | copy-start | bytes 6291460
  126.3 11.0 %collective-permute-start.12 = (bf16[256,768]{1,0:T(8,128)(2,1)S(1)}, bf16[256,768]{1,0:T(8,128)(2,1)S(1)}, u32[]{:S(2)}, u32[]{:S(2)}) collective-permute-start(bf16[256,768]{1,0:T(8,128)(2,1)S(1)} %pad_maximum_fusion), channel_id=1, source_target_pairs={{0,1},{1,2},{2,3},{3,0},{4,5},{5,6},{6,7},{7,4},{8,9},{9,10},{10,1... | collective-permute-start | bytes 1179656 | tf_op jit(solution)/shard_map/ppermute | solution.py:405
  126.6 14.5 %collective-permute-start.16 = (bf16[256,768]{1,0:T(8,128)(2,1)S(1)}, bf16[256,768]{1,0:T(8,128)(2,1)S(1)}, u32[]{:S(2)}, u32[]{:S(2)}) collective-permute-start(bf16[256,768]{1,0:T(8,128)(2,1)S(1)} %pad_maximum_fusion.1), channel_id=1, source_target_pairs={{0,3},{1,0},{2,1},{3,2},{4,7},{5,4},{6,5},{7,6},{8,11},{9,8},{10,9... | collective-permute-start | bytes 1179656 | tf_op jit(solution)/shard_map/ppermute | solution.py:405
  139.2 3.2 %collective-permute-start.13 = (bf16[256,768]{1,0:T(8,128)(2,1)S(1)}, bf16[256,768]{1,0:T(8,128)(2,1)S(1)}, u32[]{:S(2)}, u32[]{:S(2)}) collective-permute-start(bf16[256,768]{1,0:T(8,128)(2,1)S(1)} %get-tuple-element.76), channel_id=1, source_target_pairs={{0,4},{4,0},{8,12},{12,8},{16,20},{20,16},{24,28},{28,24},{1,5},{5... | collective-permute-start | bytes 1179656 | tf_op jit(solution)/shard_map/ppermute | solution.py:458
  178.5 4.7 %collective-permute-start.17 = (bf16[256,768]{1,0:T(8,128)(2,1)S(1)}, bf16[256,768]{1,0:T(8,128)(2,1)S(1)}, u32[]{:S(2)}, u32[]{:S(2)}) collective-permute-start(bf16[256,768]{1,0:T(8,128)(2,1)S(1)} %bitcast.18), channel_id=1, source_target_pairs={{0,4},{4,0},{8,12},{12,8},{16,20},{20,16},{24,28},{28,24},{1,5},{5... | collective-permute-start | bytes 1179656 | tf_op jit(solution)/shard_map/ppermute | solution.py:458
